TPU v7x, 32 devices: a whole 2x2x4 slice. The times are simulated.
32 devices in a mesh: region: 4 (over x, core), patch: 8 (over z, y).
Axes of the slice: x: 2, y: 2, z: 4, core: 2. Of those that a mesh axis runs over, the one named last changes fastest.
Arguments:
- nodes: bfloat16 [8192, 512], P(('region', 'patch')), may hold values from -6 to 6
- edges: bfloat16 [32768, 512], P(('region', 'patch')), may hold values from -6 to 6
- node_cotan: bfloat16 [8192, 512], P(('region', 'patch')), may hold values from -6 to 6
- edge_cotan: bfloat16 [32768, 512], P(('region', 'patch')), may hold values from -6 to 6
- edge_inner: bfloat16 [1536, 512], replicated, may hold values from -0.15625 to 0.15625
- edge_outer: bfloat16 [512, 512], replicated, may hold values from -0.25 to 0.25
- node_inner: bfloat16 [1024, 512], replicated, may hold values from -0.1875 to 0.1875
- node_outer: bfloat16 [512, 512], replicated, may hold values from -0.25 to 0.25
- edge_shift: float32 [512], replicated, may hold values from -4 to 4
- edge_offset: float32 [512], replicated, may hold values from -4 to 4
- edge_gain: float32 [512], replicated, may hold values from 0.5 to 1.5
- node_shift: float32 [512], replicated, may hold values from -4 to 4
- node_offset: float32 [512], replicated, may hold values from -4 to 4
- node_gain: float32 [512], replicated, may hold values from 0.5 to 1.5
- send_rows: int32 [4, 8, 2, 32], P('region', 'patch'), may hold values from -1 to 255, as said below
- senders: int32 [32768], P(('region', 'patch')), may hold values from 0 to 319, as said below
- receivers: int32 [32768], P(('region', 'patch')), may hold values from 0 to 255
Outputs:
- grad_nodes: float32 [8192, 512], P(('region', 'patch'))
- grad_edges: bfloat16 [32768, 512], P(('region', 'patch'))
- grad_weights: float32 [1835008], P(('region', 'patch'))
- grad_vectors: float32 [3072], replicated
Inputs may be any that keep to these rules, and one draw needn't show every extreme that they name: `send_rows`: list 0 of a patch goes to the patch one index below, list 1 to the one above, cyclically within its region. Live entries are distinct own-node indices and stand first, the rest are -1; each list has half of 32 to 32 live entries, and some list is full. `senders`: below 256 a sender is an own node; 256 + j is the j-th row received from the patch below, 288 + j the j-th from the patch above; only live rows are named.
All inputs are finite; a program needn't handle non-finite values.
Results may differ from a plain program's by a relative error of at most 0.0063.
Values may be sent and summed in bfloat16 or wider, within the bound.
No kernel may reach another device: no remote copies, remote signals or barrier semaphores. Data moves between devices by JAX's collectives and lax.ppermute only.
A program may use at most 128 MiB of HBM per device.

v0:
```python
import math

import jax
import jax.numpy as jnp
from jax import lax
from jax.sharding import PartitionSpec as P


def extended(block, sides, width):
    for axis, dim in sides:
        count = lax.axis_size(axis)
        forward = [(i, i + 1) for i in range(count - 1)]
        forward.append((count - 1, 0))
        backward = [(target, source) for source, target in forward]
        low = lax.ppermute(
            lax.slice_in_dim(block, block.shape[dim] - width, None, axis=dim), axis, forward
        )
        high = lax.ppermute(lax.slice_in_dim(block, 0, width, axis=dim), axis, backward)
        block = jnp.concatenate([low, block, high], axis=dim)
    return block


def layer_norm(values):
    centred = values - jnp.mean(values, axis=-1, keepdims=True)
    invstd = lax.rsqrt(jnp.mean(centred * centred, axis=-1, keepdims=True) + 1e-05)
    return (centred * invstd, invstd)


def norm_back(upstream, normed, invstd, gains):
    scaled = upstream * gains
    return invstd * (
        scaled
        - jnp.mean(scaled, axis=-1, keepdims=True)
        - normed * jnp.mean(scaled * normed, axis=-1, keepdims=True)
    )


def activation_grad(preact):
    sigmoid_val = jax.nn.sigmoid(preact)
    return sigmoid_val * (1.0 + preact * (1.0 - sigmoid_val))


def contract_rows(left, right):
    return lax.dot_general(
        left, right, (((0,), (0,)), ((), ())), preferred_element_type=jnp.float32
    )


def per_device(
    nodes,
    edges,
    node_cotan,
    edge_cotan,
    edge_inner,
    edge_outer,
    node_inner,
    node_outer,
    edge_shift,
    edge_offset,
    edge_gain,
    node_shift,
    node_offset,
    node_gain,
    send_rows,
    senders,
    receivers,
):
    node_count = nodes.shape[0]
    edge_count = edges.shape[0]
    feature_width = nodes.shape[1]
    send_lists = send_rows.reshape(-1)
    slot_count = send_lists.shape[0] // 2
    devices_all = lax.axis_size("region") * lax.axis_size("patch")
    edge_norm = 1.0 / math.sqrt(edge_count * devices_all)
    node_norm = 1.0 / math.sqrt(node_count * devices_all)
    node_ids = jnp.arange(node_count, dtype=jnp.int32)
    pick_send = (send_lists[:, None] == node_ids[None, :]).astype(jnp.bfloat16)
    outgoing = jnp.dot(pick_send, nodes, preferred_element_type=jnp.float32).astype(jnp.bfloat16)
    received = extended(outgoing.reshape(2, slot_count, feature_width), (("patch", 0),), 1)
    lookup = jnp.concatenate([nodes, received[0], received[3]], axis=0)
    lookup_ids = jnp.arange(lookup.shape[0], dtype=jnp.int32)
    pick_sender = (senders[:, None] == lookup_ids[None, :]).astype(jnp.bfloat16)
    pick_receiver = (receivers[:, None] == node_ids[None, :]).astype(jnp.bfloat16)
    sender_rows = jnp.dot(pick_sender, lookup, preferred_element_type=jnp.float32).astype(
        jnp.bfloat16
    )
    receiver_rows = jnp.dot(pick_receiver, nodes, preferred_element_type=jnp.float32).astype(
        jnp.bfloat16
    )
    edge_inputs = jnp.concatenate([edges, sender_rows, receiver_rows], axis=1)
    edge_preact = jnp.dot(edge_inputs, edge_inner, preferred_element_type=jnp.float32) + edge_shift
    edge_hidden = jax.nn.silu(edge_preact).astype(jnp.bfloat16)
    edge_linear = jnp.dot(edge_hidden, edge_outer, preferred_element_type=jnp.float32) + edge_offset
    edge_normed, edge_invstd = layer_norm(edge_linear)
    edge_fresh = (edges.astype(jnp.float32) + edge_gain * edge_normed).astype(jnp.bfloat16)
    aggregate = contract_rows(pick_receiver, edge_fresh).astype(jnp.bfloat16)
    node_inputs = jnp.concatenate([nodes, aggregate], axis=1)
    node_preact = jnp.dot(node_inputs, node_inner, preferred_element_type=jnp.float32) + node_shift
    node_hidden = jax.nn.silu(node_preact).astype(jnp.bfloat16)
    node_linear = jnp.dot(node_hidden, node_outer, preferred_element_type=jnp.float32) + node_offset
    node_normed, node_invstd = layer_norm(node_linear)
    cotan_node = node_cotan.astype(jnp.float32)
    linear_back = norm_back(cotan_node, node_normed, node_invstd, node_gain)
    linear_half = linear_back.astype(jnp.bfloat16)
    preact_back = jnp.dot(
        linear_half, node_outer.T, preferred_element_type=jnp.float32
    ) * activation_grad(node_preact)
    preact_half = preact_back.astype(jnp.bfloat16)
    inputs_back = jnp.dot(preact_half, node_inner.T, preferred_element_type=jnp.float32)
    aggregate_half = inputs_back[:, feature_width:].astype(jnp.bfloat16)
    fresh_back = edge_cotan.astype(jnp.float32) + jnp.dot(
        pick_receiver, aggregate_half, preferred_element_type=jnp.float32
    )
    elinear_back = norm_back(fresh_back, edge_normed, edge_invstd, edge_gain)
    elinear_half = elinear_back.astype(jnp.bfloat16)
    epreact_back = jnp.dot(
        elinear_half, edge_outer.T, preferred_element_type=jnp.float32
    ) * activation_grad(edge_preact)
    epreact_half = epreact_back.astype(jnp.bfloat16)
    einputs_back = jnp.dot(epreact_half, edge_inner.T, preferred_element_type=jnp.float32)
    grad_edges = (fresh_back + einputs_back[:, :feature_width]).astype(jnp.bfloat16)
    sender_half = einputs_back[:, feature_width : 2 * feature_width].astype(jnp.bfloat16)
    receiver_half = einputs_back[:, 2 * feature_width :].astype(jnp.bfloat16)
    lookup_back = contract_rows(pick_sender, sender_half)
    rim_back = lookup_back[node_count:].reshape(2, slot_count, feature_width)
    returned = extended(rim_back.astype(jnp.bfloat16), (("patch", 0),), 1).astype(rim_back.dtype)
    back_rows = jnp.concatenate([returned[0], returned[3]], axis=0)
    from_rims = lax.dot_general(
        pick_send.astype(jnp.float32),
        back_rows,
        (((0,), (0,)), ((), ())),
        precision=lax.Precision.HIGHEST,
        preferred_element_type=jnp.float32,
    )
    grad_nodes = (
        cotan_node
        + inputs_back[:, :feature_width]
        + lookup_back[:node_count]
        + contract_rows(pick_receiver, receiver_half)
        + from_rims
    )
    flat_terms = jnp.concatenate(
        [
            (contract_rows(edge_inputs, epreact_half) * edge_norm).reshape(-1),
            (contract_rows(edge_hidden, elinear_half) * edge_norm).reshape(-1),
            (contract_rows(node_inputs, preact_half) * node_norm).reshape(-1),
            (contract_rows(node_hidden, linear_half) * node_norm).reshape(-1),
        ]
    )
    vector_terms = jnp.concatenate(
        [
            jnp.sum(epreact_back, axis=0) * edge_norm,
            jnp.sum(elinear_back, axis=0) * edge_norm,
            jnp.sum(fresh_back * edge_normed, axis=0) * edge_norm,
            jnp.sum(preact_back, axis=0) * node_norm,
            jnp.sum(linear_back, axis=0) * node_norm,
            jnp.sum(cotan_node * node_normed, axis=0) * node_norm,
        ]
    )
    grad_vectors = lax.psum(vector_terms, ("region", "patch"))
    grad_weights = lax.psum_scatter(
        flat_terms, ("region", "patch"), scatter_dimension=0, tiled=True
    )
    return (grad_nodes, grad_edges, grad_weights, grad_vectors)


def solution(mesh):
    in_specs = (
        P(("region", "patch"), None),
        P(("region", "patch"), None),
        P(("region", "patch"), None),
        P(("region", "patch"), None),
        P(),
        P(),
        P(),
        P(),
        P(),
        P(),
        P(),
        P(),
        P(),
        P(),
        P("region", "patch", None, None),
        P(("region", "patch")),
        P(("region", "patch")),
    )
    out_specs = (
        P(("region", "patch"), None),
        P(("region", "patch"), None),
        P(("region", "patch")),
        P(),
    )
    return jax.shard_map(
        per_device, mesh=mesh, in_specs=in_specs, out_specs=out_specs, check_vma=False
    )
```

profile of v0, /device:TPU:0, one launch (start us, length us, event | category | flops | bytes accessed | tf_op | source)
XLA Modules:
  0.0 229.2 jit_solution(12831472627072938143)
XLA Ops:
  7.2 0.9 eq.47
  8.1 1.1 convolution_convert_fusion.2
  9.3 3.0 %collective-permute-start = (bf16[1,32,512]{2,1,0:T(8,128)(2,1)S(1)}, bf16[1,32,512]{2,1,0:T(8,128)(2,1)S(1)}, u32[]{:S(2)}, u32[]{:S(2)}) collective-permute-start(bf16[1,32,512]{2,1,0:T(8,128)(2,1)S(1)} %get-tuple-element.26), channel_id=1, source_target_pairs={{0,1},{1,2},{2,3},{3,4},{4,5},{5,6},{6,7},{7,0},{8,9},{9,10},{10,1... | collective-permute-start | bytes 98312 | tf_op jit(solution)/shard_map/ppermute | solution.py:15
  12.3 3.1 %collective-permute-start.1 = (bf16[1,32,512]{2,1,0:T(8,128)(2,1)S(1)}, bf16[1,32,512]{2,1,0:T(8,128)(2,1)S(1)}, u32[]{:S(2)}, u32[]{:S(2)}) collective-permute-start(bf16[1,32,512]{2,1,0:T(8,128)(2,1)S(1)} %get-tuple-element.27), channel_id=1, source_target_pairs={{1,0},{2,1},{3,2},{4,3},{5,4},{6,5},{7,6},{0,7},{9,8},{10,9},{11,1... | collective-permute-start | bytes 98312 | tf_op jit(solution)/shard_map/ppermute | solution.py:18
  15.4 1.6 convolution_convert_fusion
  17.0 2.7 %copy.27 = bf16[1024,512]{0,1:T(8,128)(2,1)} copy(bf16[1024,512]{1,0:T(8,128)(2,1)} %param.18) | data formatting | bytes 2097152 | tf_op args[1]
  19.7 2.3 copy.29
  22.0 0.9 fusion.3
  23.2 1.8 fusion.6
  25.0 0.9 add_reduce_fusion
  26.7 1.0 convolution_convert_fusion.1
  28.3 0.6 copy-done.15
  31.4 0.7 copy-done.10
  32.1 1.3 multiply_reduce_fusion
  33.5 1.0 fusion.57
  34.8 1.3 fusion.61
  36.1 0.8 fusion.4
  37.8 0.8 copy-done.7
  38.6 2.0 fusion
  40.7 0.8 copy.35
  42.6 10.8 %pad_maximum_fusion = f32[1835008]{0:T(1024)} fusion(f32[262144]{0:T(1024)S(1)} %bitcast.48, f32[524288]{0:T(1024)S(1)} %bitcast.46, f32[262144]{0:T(1024)S(1)} %bitcast.47, f32[786432]{0:T(1024)S(1)} %bitcast.45), kind=kLoop, calls=%fused_computation | loop fusion | flops 5505024 | bytes 14680064 | tf_op jit(solution)/shard_map/concatenate | solution.py:142
  53.4 3.5 %fusion.59 = (bf16[1024,1536]{1,0:T(8,128)(2,1)}, f32[1024,1536]{1,0:T(8,128)S(1)}) fusion(bf16[1536,512]{1,0:T(8,128)(2,1)S(1)} %copy-done, bf16[1024,512]{1,0:T(8,128)(2,1)S(1)} %get-tuple-element.38), kind=kOutput, calls=%fused_computation.117 | convolution fusion | flops 1612185600 | bytes 12058624 | tf_op jit(solution)/shard_map/dot_general | solution.py:120
  56.9 1.5 slice.84
  58.4 3.0 %copy.34 = f32[1024,512]{0,1:T(8,128)} copy(f32[1024,512]{1,0:T(8,128)} %slice.84) | data formatting | bytes 4194304
  61.4 3.1 %fusion.60 = (bf16[320,512]{1,0:T(8,128)(2,1)S(1)}, f32[320,512]{1,0:T(8,128)}) fusion(bf16[1024,1536]{1,0:T(8,128)(2,1)} %get-tuple-element.33, s32[1024]{0:T(1024)S(1)} %copy-done.17), kind=kOutput, calls=%fused_computation.118 | convolution fusion | flops 336035840 | bytes 2035712 | tf_op jit(solution)/shard_map/dot_general | solution.py:44
  64.5 4.7 %collective-permute-start.3 = (bf16[1,32,512]{2,1,0:T(8,128)(2,1)S(1)}, bf16[1,32,512]{2,1,0:T(8,128)(2,1)S(1)}, u32[]{:S(2)}, u32[]{:S(2)}) collective-permute-start(bf16[1,32,512]{2,1,0:T(8,128)(2,1)S(1)} %get-tuple-element.23), channel_id=1, source_target_pairs={{1,0},{2,1},{3,2},{4,3},{5,4},{6,5},{7,6},{0,7},{9,8},{10,9},{11,1... | collective-permute-start | bytes 98312 | tf_op jit(solution)/shard_map/ppermute | solution.py:18
  69.3 1.9 add_convert_fusion
  71.2 1.3 copy.32
  72.5 37.9 %psum.7 = f32[3072]{0:T(1024)} all-reduce(f32[3072]{0:T(1024)S(1)} %constant_dynamic-update-slice_fusion), channel_id=1, replica_groups=mesh['region'=4,'patch'=8] {'region','patch'}, use_global_device_ids=true, to_apply=%region_15.16 | all-reduce | flops 3072 | bytes 24576 | tf_op jit(solution)/shard_map/psum | solution.py:160
  111.0 3.1 %fusion.7 = f32[256,512]{1,0:T(8,128)} fusion(f32[256,512]{1,0:T(8,128)S(1)} %fusion.37, bf16[1024,1536]{1,0:T(8,128)(2,1)} %get-tuple-element.33, bf16[256,512]{1,0:T(8,128)(2,1)S(1)} %copy-done.5, f32[320,512]{1,0:T(8,128)} %get-tuple-element.36, f32[256,1024]{1,0:T(8,128)} %copy-done.3, s32[1024]{0:T(1024)S(1)} %copy-done.11), kind=kOutput, calls=%fused_computation.30 | convolution fusion | flops 269352960 | bytes 3411968 | tf_op jit(solution)/shard_map/dot_general | solution.py:44
  114.1 106.6 %all-reduce.3.cloned.1.call-done = f32[1835008]{0:T(1024)} async-done(((f32[1835008]{0:T(1024)}), f32[1835008]{0:T(1024)}) %all-reduce.3.cloned.1.call-update) | async-done | bytes 7340048
  220.7 1.6 dynamic-slice
  (78 shorter events, 6.9 us)
Async XLA Ops:
  7.2 15.7 %copy-start = (bf16[1536,512]{1,0:T(8,128)(2,1)S(1)}, bf16[1536,512]{1,0:T(8,128)(2,1)}, u32[]{:S(2)}) copy-start(bf16[1536,512]{1,0:T(8,128)(2,1)} %param.21) | copy-start | bytes 4718596
  7.2 213.5 %all-reduce.3.cloned.1.call-start = ((), (), s32[]{:S(2)}) async-start(), calls=%async_computation | async-start | bytes 14680064
  9.3 12.7 %collective-permute-start = (bf16[1,32,512]{2,1,0:T(8,128)(2,1)S(1)}, bf16[1,32,512]{2,1,0:T(8,128)(2,1)S(1)}, u32[]{:S(2)}, u32[]{:S(2)}) collective-permute-start(bf16[1,32,512]{2,1,0:T(8,128)(2,1)S(1)} %get-tuple-element.26), channel_id=1, source_target_pairs={{0,1},{1,2},{2,3},{3,4},{4,5},{5,6},{6,7},{7,0},{8,9},{9,10},{10,1... | collective-permute-start | bytes 98312 | tf_op jit(solution)/shard_map/ppermute | solution.py:15
  12.3 9.7 %collective-permute-start.1 = (bf16[1,32,512]{2,1,0:T(8,128)(2,1)S(1)}, bf16[1,32,512]{2,1,0:T(8,128)(2,1)S(1)}, u32[]{:S(2)}, u32[]{:S(2)}) collective-permute-start(bf16[1,32,512]{2,1,0:T(8,128)(2,1)S(1)} %get-tuple-element.27), channel_id=1, source_target_pairs={{1,0},{2,1},{3,2},{4,3},{5,4},{6,5},{7,6},{0,7},{9,8},{10,9},{11,1... | collective-permute-start | bytes 98312 | tf_op jit(solution)/shard_map/ppermute | solution.py:18
  17.0 5.9 %copy-start.6 = (bf16[1024,512]{0,1:T(8,128)(2,1)}, bf16[1024,512]{0,1:T(8,128)(2,1)S(1)}, u32[]{:S(2)}) copy-start(bf16[1024,512]{0,1:T(8,128)(2,1)S(1)} %convolution_convert_fusion) | copy-start | bytes 3145732
  17.0 5.0 %copy-start.4 = (bf16[256,512]{1,0:T(8,128)(2,1)S(1)}, bf16[256,512]{1,0:T(8,128)(2,1)}, u32[]{:S(2)}) copy-start(bf16[256,512]{1,0:T(8,128)(2,1)} %param.17) | copy-start | bytes 786436
  17.0 5.0 %copy-start.17 = (s32[1024]{0:T(1024)S(1)}, s32[1024]{0:T(1024)}, u32[]{:S(2)}) copy-start(s32[1024]{0:T(1024)} %param.32) | copy-start | bytes 12292
  21.9 1.2 copy-start.9
  23.2 1.8 copy-start.13
  23.2 1.9 copy-start.16
  23.2 1.9 copy-start.20
  26.0 0.7 copy-start.11
  26.0 0.7 copy-start.14
  26.7 1.2 copy-start.8
  26.7 1.2 copy-start.18
  27.9 1.0 copy-start.15
  27.9 1.0 copy-start.19
  28.9 1.0 copy-start.5
  28.9 1.0 copy-start.12
  30.9 1.2 copy-start.10
  32.1 1.3 copy-start.3
  33.4 1.4 copy-start.1
  37.4 1.2 copy-start.7
  61.4 7.9 %copy-start.2 = (f32[1024,512]{0,1:T(8,128)S(1)}, f32[1024,512]{0,1:T(8,128)}, u32[]{:S(2)}) copy-start(f32[1024,512]{0,1:T(8,128)} %copy-done.1) | copy-start | bytes 6291460
  64.5 46.0 %collective-permute-start.2 = (bf16[1,32,512]{2,1,0:T(8,128)(2,1)S(1)}, bf16[1,32,512]{2,1,0:T(8,128)(2,1)S(1)}, u32[]{:S(2)}, u32[]{:S(2)}) collective-permute-start(bf16[1,32,512]{2,1,0:T(8,128)(2,1)S(1)} %get-tuple-element.22), channel_id=1, source_target_pairs={{0,1},{1,2},{2,3},{3,4},{4,5},{5,6},{6,7},{7,0},{8,9},{9,10},{10,1... | collective-permute-start | bytes 98312 | tf_op jit(solution)/shard_map/ppermute | solution.py:15
  64.5 46.0 %collective-permute-start.3 = (bf16[1,32,512]{2,1,0:T(8,128)(2,1)S(1)}, bf16[1,32,512]{2,1,0:T(8,128)(2,1)S(1)}, u32[]{:S(2)}, u32[]{:S(2)}) collective-permute-start(bf16[1,32,512]{2,1,0:T(8,128)(2,1)S(1)} %get-tuple-element.23), channel_id=1, source_target_pairs={{1,0},{2,1},{3,2},{4,3},{5,4},{6,5},{7,6},{0,7},{9,8},{10,9},{11,1... | collective-permute-start | bytes 98312 | tf_op jit(solution)/shard_map/ppermute | solution.py:18
Sparse Core Ops, SparseCore 0:
  53.5 167.1 all-reduce.2
where the time goes:
time: 230 us; the launch traced here: 229 us
  waiting for transfers between devices  107 us (47%)
  blocking collectives  37.9 us (16%)
  matrix products  25.5 us (11%)
  local copies, waits for them, and re-layouts  18.9 us (8%)
  other arithmetic  14.9 us (6%)
  between operations  14.4 us (6%)
  starting transfers between devices  10.9 us (5%)
    unnamed x2, waiting for transfers between devices  107 us
    psum x1, blocking collectives, per_device(): grad_vectors = lax.psum(vector_terms, ('region', 'patch'))  37.9 us
    unnamed x51, local copies, waits for them, and re-layouts  16.4 us
    dot_general x7, matrix products, contract_rows(): lax.dot_general(left, right, (((0,), (0,)), ((), ())), preferred_element_...  10.8 us
    concatenate x1, other arithmetic, per_device(): jnp.concatenate([(contract_rows(edge_inputs, epreact_half) * edge_norm).r...  10.8 us
    ppermute x2, starting transfers between devices, extended(): lax.ppermute(lax.slice_in_dim(block, 0, width, axis=dim), axis, backward)  7.82 us
  transfers between devices with their start and end apart: 5, of which 1 were waited for; matrix products, arithmetic and copies ran while one was open for 11% of the time, Pallas kernels for 0%

commit v1 on v0

--- a/solution.py
+++ b/solution.py
@@ -44,6 +44,48 @@
     return lax.dot_general(
         left, right, (((0,), (0,)), ((), ())), preferred_element_type=jnp.float32
     )
+
+
+def halving_orders():
+    core_bit = lax.axis_size("patch")
+    high = [core_bit << k for k in range(1, (lax.axis_size("region")).bit_length() - 1)]
+    low = [1 << k for k in range(core_bit.bit_length() - 1)]
+    return core_bit, high + low, low[:-1] + high + low[-1:]
+
+
+def permute_by(values, first, second, core_bit):
+    count = lax.axis_size("region") * lax.axis_size("patch")
+    pairs = [(i, i ^ (second if i & core_bit else first)) for i in range(count)]
+    return lax.ppermute(values, ("region", "patch"), pairs)
+
+
+def reduce_all(flat, vectors):
+    core_bit, first, second = halving_orders()
+    count = lax.axis_size("region") * lax.axis_size("patch")
+    me = lax.axis_index(("region", "patch"))
+    core = (me & core_bit) // core_bit
+    depth = count.bit_length() - 1
+    flat = flat.reshape((2,) * depth + (-1, flat.shape[1]))
+
+    def ordered(order):
+        axes = [depth - bit.bit_length() for bit in [core_bit] + order]
+        return jnp.transpose(flat, axes + [depth, depth + 1])
+
+    blocks = jnp.stack([ordered(first)[0], ordered(second)[1]]).reshape(2, -1, flat.shape[-1])
+    kept = lax.dynamic_index_in_dim(blocks, core, 0, keepdims=False)
+    sent = lax.dynamic_index_in_dim(blocks, 1 - core, 0, keepdims=False).astype(jnp.bfloat16)
+    got = permute_by(sent, core_bit, core_bit, core_bit)
+    total = kept + got.astype(jnp.float32)
+    for one, two in zip(first, second):
+        bit = jnp.where(core == 1, (me & two) // two, (me & one) // one)
+        halves = total.reshape(2, -1, flat.shape[-1])
+        kept = lax.dynamic_index_in_dim(halves, bit, 0, keepdims=False)
+        sent = lax.dynamic_index_in_dim(halves, 1 - bit, 0, keepdims=False).astype(jnp.bfloat16)
+        got = permute_by(sent, one, two, core_bit)
+        vectors = vectors + permute_by(vectors, one, two, core_bit)
+        total = kept + got.astype(jnp.float32)
+    vectors = vectors + permute_by(vectors, core_bit, core_bit, core_bit)
+    return total.reshape(-1), vectors.reshape(-1)
 
 
 def per_device(
@@ -141,10 +183,10 @@
     )
     flat_terms = jnp.concatenate(
         [
-            (contract_rows(edge_inputs, epreact_half) * edge_norm).reshape(-1),
-            (contract_rows(edge_hidden, elinear_half) * edge_norm).reshape(-1),
-            (contract_rows(node_inputs, preact_half) * node_norm).reshape(-1),
-            (contract_rows(node_hidden, linear_half) * node_norm).reshape(-1),
+            contract_rows(edge_inputs, epreact_half) * edge_norm,
+            contract_rows(edge_hidden, elinear_half) * edge_norm,
+            contract_rows(node_inputs, preact_half) * node_norm,
+            contract_rows(node_hidden, linear_half) * node_norm,
         ]
     )
     vector_terms = jnp.concatenate(
@@ -157,10 +199,7 @@
             jnp.sum(cotan_node * node_normed, axis=0) * node_norm,
         ]
     )
-    grad_vectors = lax.psum(vector_terms, ("region", "patch"))
-    grad_weights = lax.psum_scatter(
-        flat_terms, ("region", "patch"), scatter_dimension=0, tiled=True
-    )
+    grad_weights, grad_vectors = reduce_all(flat_terms, vector_terms.reshape(-1, feature_width))
     return (grad_nodes, grad_edges, grad_weights, grad_vectors)
 
 

time: 230 us -> 102 us (0.44)
  waiting for transfers between devices: 107 us -> 10.4 us
  blocking collectives: 37.9 us -> 0 us
  local copies, waits for them, and re-layouts: 18.9 us -> 32.5 us
  between operations: 14.4 us -> 1.25 us
  starting transfers between devices: 10.9 us -> 20.6 us
  matrix products: 25.5 us -> 22.2 us
    unnamed x2 -> x0, waiting for transfers between devices: 107 us -> none
    psum x1 -> x0, blocking collectives: 37.9 us -> none  [per_device(): grad_vectors = lax.psum(vector_terms, ('region', 'patch'))]
    ppermute x0 -> x10, waiting for transfers between devices: none -> 10.4 us  [permute_by(): return lax.ppermute(values, ('region', 'patch'), pairs)]
    concatenate x1, other arithmetic: 10.8 us -> 0.93 us  [per_device(): jnp.concatenate([contract_rows(edge_inputs, epreact_half) * edge_norm, co...]
    ppermute x0 -> x10, starting transfers between devices: none -> 9.72 us  [permute_by(): return lax.ppermute(values, ('region', 'patch'), pairs)]
    add x0 -> x9, other arithmetic: none -> 8.18 us  [the longest x4 6.72 us: reduce_all(): total = kept + got.astype(jnp.float32)]
    unnamed x51 -> x75, local copies, waits for them, and re-layouts: 16.4 us -> 21.8 us
    reshape x0 -> x4, local copies, waits for them, and re-layouts: none -> 3.33 us  [the longest x2 2.72 us: reduce_all(): flat = flat.reshape((2,) * depth + (-1, flat.shape[1]))]
  transfers between devices with their start and end apart: 5 -> 14, of which waited for: 1 -> 4; matrix products, arithmetic and copies ran while one was open for 11% -> 33% of each run, Pallas kernels for 0% -> 0%
where the time goes in v1:
time: 102 us
  local copies, waits for them, and re-layouts  32.5 us (32%)
  matrix products  22.2 us (22%)
  starting transfers between devices  20.6 us (20%)
  other arithmetic  14.8 us (15%)
  waiting for transfers between devices  10.4 us (10%)
  between operations  1.25 us (1%)
    unnamed x75, local copies, waits for them, and re-layouts  21.8 us
    ppermute x10, waiting for transfers between devices, permute_by(): return lax.ppermute(values, ('region', 'patch'), pairs)  10.4 us
    ppermute x10, starting transfers between devices, permute_by(): return lax.ppermute(values, ('region', 'patch'), pairs)  9.72 us
    dot_general x7, matrix products, contract_rows(): lax.dot_general(left, right, (((0,), (0,)), ((), ())), preferred_element_...  9.12 us
    ppermute x2, starting transfers between devices, extended(): lax.ppermute(lax.slice_in_dim(block, 0, width, axis=dim), axis, backward)  7.83 us
    add x4, other arithmetic, reduce_all(): total = kept + got.astype(jnp.float32)  6.72 us
    ppermute x2, starting transfers between devices, extended(): lax.ppermute(lax.slice_in_dim(block, block.shape[dim] - width, None, axis...  3.02 us
    reshape x2, local copies, waits for them, and re-layouts, reduce_all(): flat = flat.reshape((2,) * depth + (-1, flat.shape[1]))  2.72 us
  transfers between devices with their start and end apart: 14, of which 4 were waited for; matrix products, arithmetic and copies ran while one was open for 33% of the time, Pallas kernels for 0%

profile of v1, /device:TPU:0, one launch (start us, length us, event | category | flops | bytes accessed | tf_op | source)
XLA Modules:
  0.0 101.7 jit_solution(5971773552370708268)
XLA Ops:
  2.7 3.0 %collective-permute-start = (bf16[1,32,512]{2,1,0:T(8,128)(2,1)S(1)}, bf16[1,32,512]{2,1,0:T(8,128)(2,1)S(1)}, u32[]{:S(2)}, u32[]{:S(2)}) collective-permute-start(bf16[1,32,512]{2,1,0:T(8,128)(2,1)S(1)} %get-tuple-element.26), channel_id=1, source_target_pairs={{0,1},{1,2},{2,3},{3,4},{4,5},{5,6},{6,7},{7,0},{8,9},{9,10},{10,1... | collective-permute-start | bytes 98312 | tf_op jit(solution)/shard_map/ppermute | solution.py:15
  5.7 3.1 %collective-permute-start.1 = (bf16[1,32,512]{2,1,0:T(8,128)(2,1)S(1)}, bf16[1,32,512]{2,1,0:T(8,128)(2,1)S(1)}, u32[]{:S(2)}, u32[]{:S(2)}) collective-permute-start(bf16[1,32,512]{2,1,0:T(8,128)(2,1)S(1)} %get-tuple-element.27), channel_id=1, source_target_pairs={{1,0},{2,1},{3,2},{4,3},{5,4},{6,5},{7,6},{0,7},{9,8},{10,9},{11,1... | collective-permute-start | bytes 98312 | tf_op jit(solution)/shard_map/ppermute | solution.py:18
  8.8 1.6 %convolution_convert_fusion = bf16[1024,512]{0,1:T(8,128)(2,1)S(1)} fusion(bf16[256,512]{1,0:T(8,128)(2,1)} %param.17, s32[1024]{0:T(1024)} %param.33), kind=kOutput, calls=%fused_computation.28 | convolution fusion | flops 269221888 | bytes 1314816 | tf_op jit(solution)/shard_map/dot_general | solution.py:129
  10.5 2.7 %copy.28 = bf16[1024,512]{0,1:T(8,128)(2,1)} copy(bf16[1024,512]{1,0:T(8,128)(2,1)} %param.18) | data formatting | bytes 2097152 | tf_op args[1]
  13.1 2.3 %copy.30 = bf16[1024,512]{0,1:T(8,128)(2,1)} copy(bf16[1024,512]{1,0:T(8,128)(2,1)} %param.20) | data formatting | bytes 2097152 | tf_op args[3]
  16.6 1.8 %fusion.4 = f32[1024,512]{1,0:T(8,128)S(1)} fusion(bf16[1536,512]{1,0:T(8,128)(2,1)S(1)} %copy-done, bf16[1024,512]{0,1:T(8,128)(2,1)S(1)} %convolution_convert_fusion, bf16[1024,512]{0,1:T(8,128)(2,1)S(1)} %fusion.3, bf16[1024,512]{0,1:T(8,128)(2,1)S(1)} %copy-done.15), kind=kOutput, calls=%fused_computation.32 | convolution fusion | flops 1620049920 | bytes 6815744 | tf_op jit(solution)/shard_map/dot_general | solution.py:133
  28.2 1.3 %fusion.64 = (f32[512]{0:T(512)S(1)}, bf16[1024,512]{1,0:T(8,128)(2,1)S(1)}) fusion(f32[1024,512]{1,0:T(8,128)S(1)} %fusion.4, f32[512]{0:T(512)S(1)} %copy-done.34, bf16[512,512]{1,0:T(8,128)(2,1)S(1)} %copy-done.29, bf16[1024,512]{0,1:T(8,128)(2,1)S(1)} %get-tuple-element.21), kind=kOutput, calls=%fused_computation.135 | convolution fusion | flops 542637568 | bytes 4722688 | tf_op jit(solution)/shard_map/dot_general | solution.py:158
  32.1 2.0 %convolution_multiply_fusion = f32[1536,512]{1,0:T(8,128)S(1)} fusion(bf16[1024,512]{0,1:T(8,128)(2,1)S(1)} %copy-done.13, bf16[1024,512]{0,1:T(8,128)(2,1)S(1)} %fusion.3, bf16[1024,512]{0,1:T(8,128)(2,1)S(1)} %copy-done.15, bf16[1024,512]{1,0:T(8,128)(2,1)S(1)} %get-tuple-element.38), kind=kOutput, calls=%fused_computation.6 | convolution fusion | flops 1620836352 | bytes 7340032 | tf_op jit(solution)/shard_map/dot_general | solution.py:44
  35.1 1.4 %copy.42 = f32[2,2,2,2,2,112,512]{6,5,2,3,4,0,1:T(8,128)S(1)} copy(f32[2,2,2,2,2,112,512]{6,5,4,3,2,1,0:T(8,128)S(1)} %bitcast.70) | data formatting | bytes 14680064 | tf_op jit(solution)/shard_map/reshape | solution.py:68
  36.4 1.4 %copy.41 = f32[2,2,2,2,2,112,512]{6,5,2,0,3,4,1:T(8,128)S(1)} copy(f32[2,2,2,2,2,112,512]{6,5,4,3,2,1,0:T(8,128)S(1)} %bitcast.71) | data formatting | bytes 14680064 | tf_op jit(solution)/shard_map/reshape | solution.py:68
  38.8 1.4 %pad_maximum_fusion.1 = f32[2,2,2,2,2,112,512]{6,5,4,3,2,1,0:T(8,128)S(1)} fusion(f32[1,2,2,2,2,112,512]{6,5,4,3,2,1,0:T(8,128)S(1)} %slice.94, f32[1,2,2,2,2,112,512]{6,5,4,3,2,1,0:T(8,128)S(1)} %slice.93), kind=kLoop, calls=%fused_computation.1 | loop fusion | flops 1835008 | bytes 14680064 | tf_op jit(solution)/shard_map/stack | solution.py:74
  40.2 3.0 %copy-done.1 = f32[2,2,2,2,2,112,512]{6,5,4,3,2,1,0:T(8,128)} copy-done((f32[2,2,2,2,2,112,512]{6,5,4,3,2,1,0:T(8,128)}, f32[2,2,2,2,2,112,512]{6,5,4,3,2,1,0:T(8,128)S(1)}, u32[]{:S(2)}) %copy-start.1) | copy-done | bytes 7340056
  43.2 1.5 %fusion = bf16[1792,512]{1,0:T(8,128)(2,1)} fusion(f32[2,1792,512]{2,1,0:T(8,128)S(1)} %bitcast.72, s32[]{:T(128)S(6)} %select_n.66), kind=kLoop, calls=%fused_computation.21 | loop fusion | bytes 3670020 | tf_op jit(solution)/shard_map/convert_element_type | solution.py:76
  44.8 1.6 %collective-permute-start.9 = (f32[6,512]{1,0:T(8,128)S(1)}, f32[6,512]{1,0:T(8,128)}, u32[]{:S(2)}, u32[]{:S(2)}) collective-permute-start(f32[6,512]{1,0:T(8,128)S(1)} %reshape.103), channel_id=1, source_target_pairs={{0,16},{1,17},{2,18},{3,19},{4,20},{5,21},{6,22},{7,23},{8,9},{9,8... | collective-permute-start | bytes 36872 | tf_op jit(solution)/shard_map/ppermute | solution.py:59
  46.4 2.4 %collective-permute-done.4 = bf16[1792,512]{1,0:T(8,128)(2,1)} collective-permute-done((bf16[1792,512]{1,0:T(8,128)(2,1)}, bf16[1792,512]{1,0:T(8,128)(2,1)}, u32[]{:S(2)}, u32[]{:S(2)}) %collective-permute-start.4) | collective-permute-done | bytes 1835040 | tf_op jit(solution)/shard_map/ppermute | solution.py:59
  48.8 3.2 %bitcast_add_fusion = f32[1792,512]{1,0:T(8,128)S(1)} fusion(bf16[1792,512]{1,0:T(8,128)(2,1)} %collective-permute-done.4, f32[2,1792,512]{2,1,0:T(8,128)} %bitcast.73, s32[]{:T(128)S(6)} %select_n.65), kind=kLoop, calls=%fused_computation.4 | loop fusion | flops 1835008 | bytes 9175044 | tf_op jit(solution)/shard_map/add | solution.py:78
  52.1 1.8 %copy-done.2 = f32[1792,512]{1,0:T(8,128)} copy-done((f32[1792,512]{1,0:T(8,128)}, f32[1792,512]{1,0:T(8,128)S(1)}, u32[]{:S(2)}) %copy-start.2) | copy-done | bytes 3670040
  53.9 1.6 %collective-permute-start.5 = (bf16[896,512]{1,0:T(8,128)(2,1)S(1)}, bf16[896,512]{1,0:T(8,128)(2,1)}, u32[]{:S(2)}, u32[]{:S(2)}) collective-permute-start(bf16[896,512]{1,0:T(8,128)(2,1)S(1)} %fusion.10), channel_id=1, source_target_pairs={{0,16},{1,17},{2,18},{3,19},{4,20},{5,21},{6,22},{7,23},{8,9},{9,8... | collective-permute-start | bytes 2752520 | tf_op jit(solution)/shard_map/ppermute | solution.py:59
  55.5 1.8 %fusion.62 = (bf16[1024,1536]{1,0:T(8,128)(2,1)S(1)}, f32[1024,1536]{1,0:T(8,128)S(1)}) fusion(bf16[1536,512]{1,0:T(8,128)(2,1)S(1)} %copy-done, bf16[1024,512]{1,0:T(8,128)(2,1)S(1)} %get-tuple-element.38), kind=kOutput, calls=%fused_computation.133 | convolution fusion | flops 1612185600 | bytes 12058624 | tf_op jit(solution)/shard_map/dot_general | solution.py:162
  57.3 1.6 %copy-done.3 = bf16[1024,1536]{1,0:T(8,128)(2,1)} copy-done((bf16[1024,1536]{1,0:T(8,128)(2,1)}, bf16[1024,1536]{1,0:T(8,128)(2,1)S(1)}, u32[]{:S(2)}) %copy-start.3) | copy-done | bytes 3145752
  59.0 1.7 %fusion.63 = (bf16[320,512]{1,0:T(8,128)(2,1)S(1)}, f32[320,512]{1,0:T(8,128)}) fusion(bf16[1024,1536]{1,0:T(8,128)(2,1)S(1)} %get-tuple-element.33, s32[1024]{0:T(1024)S(1)} %copy-done.31), kind=kOutput, calls=%fused_computation.134 | convolution fusion | flops 336035840 | bytes 2035712 | tf_op jit(solution)/shard_map/dot_general | solution.py:44
  62.1 1.5 %slice.92 = f32[1024,512]{1,0:T(8,128)} slice(f32[1024,1536]{1,0:T(8,128)S(1)} %get-tuple-element.34), slice={[0:1024], [0:512]} | slice | bytes 4194304 | tf_op jit(solution)/shard_map/slice | solution.py:163
  63.6 3.0 %copy.37 = f32[1024,512]{0,1:T(8,128)} copy(f32[1024,512]{1,0:T(8,128)} %slice.92) | data formatting | bytes 4194304
  66.6 4.7 %collective-permute-start.3 = (bf16[1,32,512]{2,1,0:T(8,128)(2,1)}, bf16[1,32,512]{2,1,0:T(8,128)(2,1)}, u32[]{:S(2)}, u32[]{:S(2)}) collective-permute-start(bf16[1,32,512]{2,1,0:T(8,128)(2,1)} %get-tuple-element.23), channel_id=1, source_target_pairs={{1,0},{2,1},{3,2},{4,3},{5,4},{6,5},{7,6},{0,7},{9,8},{10,9},{11,1... | collective-permute-start | bytes 98312 | tf_op jit(solution)/shard_map/ppermute | solution.py:18
  72.0 2.2 %bitcast_add_fusion.1 = f32[896,512]{1,0:T(8,128)S(1)} fusion(bf16[896,512]{1,0:T(8,128)(2,1)} %collective-permute-done.5, f32[2,896,512]{2,1,0:T(8,128)} %bitcast.77, s32[]{:T(128)S(6)} %select_n.69), kind=kLoop, calls=%fused_computation.22 | loop fusion | flops 917504 | bytes 4587524 | tf_op jit(solution)/shard_map/add | solution.py:86
  75.1 1.8 %collective-permute-start.6 = (bf16[448,512]{1,0:T(8,128)(2,1)}, bf16[448,512]{1,0:T(8,128)(2,1)}, u32[]{:S(2)}, u32[]{:S(2)}) collective-permute-start(bf16[448,512]{1,0:T(8,128)(2,1)} %fusion.31), channel_id=1, source_target_pairs={{0,1},{1,0},{2,3},{3,2},{4,5},{5,4},{6,7},{7,6},{8,10},{9,11},{10,... | collective-permute-start | bytes 1376264 | tf_op jit(solution)/shard_map/ppermute | solution.py:59
  79.1 2.3 %copy.35 = bf16[1024,512]{1,0:T(8,128)(2,1)} copy(bf16[1024,512]{0,1:T(8,128)(2,1)} %add_convert_fusion) | data formatting | bytes 2097152
  82.9 2.9 %collective-permute-done.11 = f32[6,512]{1,0:T(8,128)S(1)} collective-permute-done((f32[6,512]{1,0:T(8,128)S(1)}, f32[6,512]{1,0:T(8,128)S(1)}, u32[]{:S(2)}, u32[]{:S(2)}) %collective-permute-start.11) | collective-permute-done | bytes 12320 | tf_op jit(solution)/shard_map/ppermute | solution.py:59
  88.3 2.3 %collective-permute-done.12 = f32[6,512]{1,0:T(8,128)S(1)} collective-permute-done((f32[6,512]{1,0:T(8,128)S(1)}, f32[6,512]{1,0:T(8,128)S(1)}, u32[]{:S(2)}, u32[]{:S(2)}) %collective-permute-start.12) | collective-permute-done | bytes 12320 | tf_op jit(solution)/shard_map/ppermute | solution.py:59
  90.6 2.8 %collective-permute-done.7 = bf16[224,512]{1,0:T(8,128)(2,1)S(1)} collective-permute-done((bf16[224,512]{1,0:T(8,128)(2,1)S(1)}, bf16[224,512]{1,0:T(8,128)(2,1)S(1)}, u32[]{:S(2)}, u32[]{:S(2)}) %collective-permute-start.7) | collective-permute-done | bytes 229408 | tf_op jit(solution)/shard_map/ppermute | solution.py:59
  93.5 4.1 %collective-permute-start.8 = (bf16[112,512]{1,0:T(8,128)(2,1)S(1)}, bf16[112,512]{1,0:T(8,128)(2,1)S(1)}, u32[]{:S(2)}, u32[]{:S(2)}) collective-permute-start(bf16[112,512]{1,0:T(8,128)(2,1)S(1)} %fusion.48), channel_id=1, source_target_pairs={{0,4},{1,5},{2,6},{3,7},{4,0},{5,1},{6,2},{7,3},{8,12},{9,13},{10,... | collective-permute-start | bytes 344072 | tf_op jit(solution)/shard_map/ppermute | solution.py:59
  97.6 2.7 %fusion.5 = f32[256,512]{1,0:T(8,128)} fusion(f32[256,512]{1,0:T(8,128)S(1)} %fusion.39, bf16[1024,1536]{1,0:T(8,128)(2,1)} %copy-done.3, bf16[256,512]{1,0:T(8,128)(2,1)S(1)} %copy-done.11, f32[320,512]{1,0:T(8,128)S(1)} %copy-done.17, f32[256,1024]{1,0:T(8,128)S(1)} %copy-done.8, s32[1024]{0:T(1024)S(1)} %copy-done.22), kind=kOutput, calls=%fused_computation.35 | convolution fusion | flops 269352960 | bytes 3411968 | tf_op jit(solution)/shard_map/dot_general | solution.py:44
  (140 shorter events, 27.9 us)
Async XLA Ops:
  0.6 15.7 %copy-start = (bf16[1536,512]{1,0:T(8,128)(2,1)S(1)}, bf16[1536,512]{1,0:T(8,128)(2,1)}, u32[]{:S(2)}) copy-start(bf16[1536,512]{1,0:T(8,128)(2,1)} %param.21) | copy-start | bytes 4718596
  1.5 4.2 %copy-start.26 = (s32[64]{0:T(128)}, s32[64]{0:T(128)S(1)}, u32[]{:S(2)}) copy-start(s32[64]{0:T(128)S(1)} %eq.53) | copy-start | bytes 772
  2.7 12.7 %collective-permute-start = (bf16[1,32,512]{2,1,0:T(8,128)(2,1)S(1)}, bf16[1,32,512]{2,1,0:T(8,128)(2,1)S(1)}, u32[]{:S(2)}, u32[]{:S(2)}) collective-permute-start(bf16[1,32,512]{2,1,0:T(8,128)(2,1)S(1)} %get-tuple-element.26), channel_id=1, source_target_pairs={{0,1},{1,2},{2,3},{3,4},{4,5},{5,6},{6,7},{7,0},{8,9},{9,10},{10,1... | collective-permute-start | bytes 98312 | tf_op jit(solution)/shard_map/ppermute | solution.py:15
  5.7 9.7 %collective-permute-start.1 = (bf16[1,32,512]{2,1,0:T(8,128)(2,1)S(1)}, bf16[1,32,512]{2,1,0:T(8,128)(2,1)S(1)}, u32[]{:S(2)}, u32[]{:S(2)}) collective-permute-start(bf16[1,32,512]{2,1,0:T(8,128)(2,1)S(1)} %get-tuple-element.27), channel_id=1, source_target_pairs={{1,0},{2,1},{3,2},{4,3},{5,4},{6,5},{7,6},{0,7},{9,8},{10,9},{11,1... | collective-permute-start | bytes 98312 | tf_op jit(solution)/shard_map/ppermute | solution.py:18
  10.4 5.9 %copy-start.12 = (bf16[1024,512]{0,1:T(8,128)(2,1)}, bf16[1024,512]{0,1:T(8,128)(2,1)S(1)}, u32[]{:S(2)}) copy-start(bf16[1024,512]{0,1:T(8,128)(2,1)S(1)} %convolution_convert_fusion) | copy-start | bytes 3145732
  10.4 4.9 %copy-start.9 = (bf16[256,512]{1,0:T(8,128)(2,1)S(1)}, bf16[256,512]{1,0:T(8,128)(2,1)}, u32[]{:S(2)}) copy-start(bf16[256,512]{1,0:T(8,128)(2,1)} %param.17) | copy-start | bytes 786436
  10.4 4.9 %copy-start.30 = (s32[1024]{0:T(1024)S(1)}, s32[1024]{0:T(1024)}, u32[]{:S(2)}) copy-start(s32[1024]{0:T(1024)} %param.32) | copy-start | bytes 12292
  16.6 1.9 %copy-start.34 = (f32[512]{0:T(512)S(1)}, f32[512]{0:T(512)}, u32[]{:S(2)}) copy-start(f32[512]{0:T(512)} %param.25) | copy-start | bytes 6148
  40.2 3.0 %copy-start.1 = (f32[2,2,2,2,2,112,512]{6,5,4,3,2,1,0:T(8,128)}, f32[2,2,2,2,2,112,512]{6,5,4,3,2,1,0:T(8,128)S(1)}, u32[]{:S(2)}) copy-start(f32[2,2,2,2,2,112,512]{6,5,4,3,2,1,0:T(8,128)S(1)} %pad_maximum_fusion.1) | copy-start | bytes 22020100
  44.7 4.1 %collective-permute-start.4 = (bf16[1792,512]{1,0:T(8,128)(2,1)}, bf16[1792,512]{1,0:T(8,128)(2,1)}, u32[]{:S(2)}, u32[]{:S(2)}) collective-permute-start(bf16[1792,512]{1,0:T(8,128)(2,1)} %fusion), channel_id=1, source_target_pairs={{0,8},{1,9},{2,10},{3,11},{4,12},{5,13},{6,14},{7,15},{8,0},{9,1},... | collective-permute-start | bytes 5505032 | tf_op jit(solution)/shard_map/ppermute | solution.py:59
  44.8 7.2 %copy-start.18 = (f32[6,512]{1,0:T(8,128)}, f32[6,512]{1,0:T(8,128)S(1)}, u32[]{:S(2)}) copy-start(f32[6,512]{1,0:T(8,128)S(1)} %reshape.103) | copy-start | bytes 36868
  44.8 26.5 %collective-permute-start.9 = (f32[6,512]{1,0:T(8,128)S(1)}, f32[6,512]{1,0:T(8,128)}, u32[]{:S(2)}, u32[]{:S(2)}) collective-permute-start(f32[6,512]{1,0:T(8,128)S(1)} %reshape.103), channel_id=1, source_target_pairs={{0,16},{1,17},{2,18},{3,19},{4,20},{5,21},{6,22},{7,23},{8,9},{9,8... | collective-permute-start | bytes 36872 | tf_op jit(solution)/shard_map/ppermute | solution.py:59
  52.0 1.9 %copy-start.2 = (f32[1792,512]{1,0:T(8,128)}, f32[1792,512]{1,0:T(8,128)S(1)}, u32[]{:S(2)}) copy-start(f32[1792,512]{1,0:T(8,128)S(1)} %bitcast_add_fusion) | copy-start | bytes 11010052
  53.9 5.1 %copy-start.31 = (s32[1024]{0:T(1024)S(1)}, s32[1024]{0:T(1024)}, u32[]{:S(2)}) copy-start(s32[1024]{0:T(1024)} %param.32) | copy-start | bytes 12292
  53.9 18.1 %collective-permute-start.5 = (bf16[896,512]{1,0:T(8,128)(2,1)S(1)}, bf16[896,512]{1,0:T(8,128)(2,1)}, u32[]{:S(2)}, u32[]{:S(2)}) collective-permute-start(bf16[896,512]{1,0:T(8,128)(2,1)S(1)} %fusion.10), channel_id=1, source_target_pairs={{0,16},{1,17},{2,18},{3,19},{4,20},{5,21},{6,22},{7,23},{8,9},{9,8... | collective-permute-start | bytes 2752520 | tf_op jit(solution)/shard_map/ppermute | solution.py:59
  63.6 7.7 %copy-start.19 = (f32[6,512]{1,0:T(8,128)S(1)}, f32[6,512]{1,0:T(8,128)}, u32[]{:S(2)}) copy-start(f32[6,512]{1,0:T(8,128)} %copy-done.18) | copy-start | bytes 36868
  66.6 15.6 %collective-permute-start.2 = (bf16[1,32,512]{2,1,0:T(8,128)(2,1)}, bf16[1,32,512]{2,1,0:T(8,128)(2,1)}, u32[]{:S(2)}, u32[]{:S(2)}) collective-permute-start(bf16[1,32,512]{2,1,0:T(8,128)(2,1)} %get-tuple-element.22), channel_id=1, source_target_pairs={{0,1},{1,2},{2,3},{3,4},{4,5},{5,6},{6,7},{7,0},{8,9},{9,10},{10,1... | collective-permute-start | bytes 98312 | tf_op jit(solution)/shard_map/ppermute | solution.py:15
  66.6 15.6 %collective-permute-start.3 = (bf16[1,32,512]{2,1,0:T(8,128)(2,1)}, bf16[1,32,512]{2,1,0:T(8,128)(2,1)}, u32[]{:S(2)}, u32[]{:S(2)}) collective-permute-start(bf16[1,32,512]{2,1,0:T(8,128)(2,1)} %get-tuple-element.23), channel_id=1, source_target_pairs={{1,0},{2,1},{3,2},{4,3},{5,4},{6,5},{7,6},{0,7},{9,8},{10,9},{11,1... | collective-permute-start | bytes 98312 | tf_op jit(solution)/shard_map/ppermute | solution.py:18
  72.0 4.9 %copy-start.5 = (f32[1024,512]{0,1:T(8,128)S(1)}, f32[1024,512]{0,1:T(8,128)}, u32[]{:S(2)}) copy-start(f32[1024,512]{0,1:T(8,128)} %copy-done.4) | copy-start | bytes 6291460
  72.0 4.9 %copy-start.6 = (f32[1024,512]{0,1:T(8,128)S(1)}, f32[1024,512]{0,1:T(8,128)}, u32[]{:S(2)}) copy-start(f32[1024,512]{0,1:T(8,128)} %copy.37) | copy-start | bytes 6291460
  72.0 9.4 %collective-permute-start.10 = (f32[6,512]{1,0:T(8,128)S(1)}, f32[6,512]{1,0:T(8,128)}, u32[]{:S(2)}, u32[]{:S(2)}) collective-permute-start(f32[6,512]{1,0:T(8,128)S(1)} %add.208), channel_id=1, source_target_pairs={{0,1},{1,0},{2,3},{3,2},{4,5},{5,4},{6,7},{7,6},{8,10},{9,11},{10,... | collective-permute-start | bytes 36872 | tf_op jit(solution)/shard_map/ppermute | solution.py:59
  75.1 10.9 %collective-permute-start.6 = (bf16[448,512]{1,0:T(8,128)(2,1)}, bf16[448,512]{1,0:T(8,128)(2,1)}, u32[]{:S(2)}, u32[]{:S(2)}) collective-permute-start(bf16[448,512]{1,0:T(8,128)(2,1)} %fusion.31), channel_id=1, source_target_pairs={{0,1},{1,0},{2,3},{3,2},{4,5},{5,4},{6,7},{7,6},{8,10},{9,11},{10,... | collective-permute-start | bytes 1376264 | tf_op jit(solution)/shard_map/ppermute | solution.py:59
  79.1 8.7 %copy-start.27 = (s32[64]{0:T(128)S(1)}, s32[64]{0:T(128)}, u32[]{:S(2)}) copy-start(s32[64]{0:T(128)} %copy-done.26) | copy-start | bytes 772
  82.1 3.7 %collective-permute-start.11 = (f32[6,512]{1,0:T(8,128)S(1)}, f32[6,512]{1,0:T(8,128)S(1)}, u32[]{:S(2)}, u32[]{:S(2)}) collective-permute-start(f32[6,512]{1,0:T(8,128)S(1)} %add.209), channel_id=1, source_target_pairs={{0,2},{1,3},{2,0},{3,1},{4,6},{5,7},{6,4},{7,5},{8,24},{9,25},{10,... | collective-permute-start | bytes 36872 | tf_op jit(solution)/shard_map/ppermute | solution.py:59
  85.9 11.7 %copy-start.8 = (f32[256,1024]{1,0:T(8,128)S(1)}, f32[256,1024]{1,0:T(8,128)}, u32[]{:S(2)}) copy-start(f32[256,1024]{1,0:T(8,128)} %copy-done.7) | copy-start | bytes 3145732
  85.9 11.7 %copy-start.11 = (bf16[256,512]{1,0:T(8,128)(2,1)S(1)}, bf16[256,512]{1,0:T(8,128)(2,1)}, u32[]{:S(2)}) copy-start(bf16[256,512]{1,0:T(8,128)(2,1)} %param.19) | copy-start | bytes 786436
  85.9 11.7 %copy-start.17 = (f32[320,512]{1,0:T(8,128)S(1)}, f32[320,512]{1,0:T(8,128)}, u32[]{:S(2)}) copy-start(f32[320,512]{1,0:T(8,128)} %get-tuple-element.36) | copy-start | bytes 1966084
  85.9 11.7 %copy-start.22 = (s32[1024]{0:T(1024)S(1)}, s32[1024]{0:T(1024)}, u32[]{:S(2)}) copy-start(s32[1024]{0:T(1024)} %param.33) | copy-start | bytes 12292
  85.9 4.7 %collective-permute-start.12 = (f32[6,512]{1,0:T(8,128)S(1)}, f32[6,512]{1,0:T(8,128)S(1)}, u32[]{:S(2)}, u32[]{:S(2)}) collective-permute-start(f32[6,512]{1,0:T(8,128)S(1)} %add.210), channel_id=1, source_target_pairs={{0,4},{1,5},{2,6},{3,7},{4,0},{5,1},{6,2},{7,3},{8,12},{9,13},{10,... | collective-permute-start | bytes 36872 | tf_op jit(solution)/shard_map/ppermute | solution.py:59
  87.3 6.1 %collective-permute-start.7 = (bf16[224,512]{1,0:T(8,128)(2,1)S(1)}, bf16[224,512]{1,0:T(8,128)(2,1)S(1)}, u32[]{:S(2)}, u32[]{:S(2)}) collective-permute-start(bf16[224,512]{1,0:T(8,128)(2,1)S(1)} %fusion.37), channel_id=1, source_target_pairs={{0,2},{1,3},{2,0},{3,1},{4,6},{5,7},{6,4},{7,5},{8,24},{9,25},{10,... | collective-permute-start | bytes 688136 | tf_op jit(solution)/shard_map/ppermute | solution.py:59
  90.6 9.7 %collective-permute-start.13 = (f32[6,512]{1,0:T(8,128)S(1)}, f32[6,512]{1,0:T(8,128)S(1)}, u32[]{:S(2)}, u32[]{:S(2)}) collective-permute-start(f32[6,512]{1,0:T(8,128)S(1)} %add.211), channel_id=1, source_target_pairs={{0,8},{1,9},{2,10},{3,11},{4,12},{5,13},{6,14},{7,15},{8,0},{9,1},... | collective-permute-start | bytes 36872 | tf_op jit(solution)/shard_map/ppermute | solution.py:59
  93.5 7.4 %collective-permute-start.8 = (bf16[112,512]{1,0:T(8,128)(2,1)S(1)}, bf16[112,512]{1,0:T(8,128)(2,1)S(1)}, u32[]{:S(2)}, u32[]{:S(2)}) collective-permute-start(bf16[112,512]{1,0:T(8,128)(2,1)S(1)} %fusion.48), channel_id=1, source_target_pairs={{0,4},{1,5},{2,6},{3,7},{4,0},{5,1},{6,2},{7,3},{8,12},{9,13},{10,... | collective-permute-start | bytes 344072 | tf_op jit(solution)/shard_map/ppermute | solution.py:59
  (17 other events, 20.2 us)

commit v2 on v1

v2 whole, which is shorter than its diff:
```python
import functools
import math

import jax
import jax.numpy as jnp
from jax import lax
from jax.experimental import pallas as pl
from jax.experimental.pallas import tpu as pltpu
from jax.sharding import PartitionSpec as P

BF = jnp.bfloat16
F32 = jnp.float32
LANES = 128
VMEM = pltpu.VMEM
AXES = ("region", "patch")


def pinned(shape, dtype):
    return pltpu.VMEM(shape, dtype)


def mm(a, b):
    return jnp.dot(a, b, preferred_element_type=F32)


def mm_nt(a, b):
    return lax.dot_general(a, b, (((1,), (1,)), ((), ())), preferred_element_type=F32)


def mm_tn(a, b):
    return lax.dot_general(a, b, (((0,), (0,)), ((), ())), preferred_element_type=F32)


def call(body, outs, *args, scalars=0, flops=0, limit=24 << 20, name=None, outs_plain=()):
    vmem = pl.BlockSpec(memory_space=pltpu.VMEM)
    smem = pl.BlockSpec(memory_space=pltpu.SMEM)
    held = [
        a if i < scalars else pltpu.with_memory_space_constraint(a, pltpu.VMEM)
        for i, a in enumerate(args)
    ]
    shapes = [
        jax.ShapeDtypeStruct(s, d) if i in outs_plain else pinned(s, d)
        for i, (s, d) in enumerate(outs)
    ]
    moved = sum(math.prod(s) * jnp.dtype(d).itemsize for s, d in outs)
    return pl.pallas_call(
        body,
        out_shape=shapes,
        in_specs=[smem if i < scalars else vmem for i in range(len(args))],
        out_specs=[vmem] * len(outs),
        compiler_params=pltpu.CompilerParams(vmem_limit_bytes=limit),
        cost_estimate=pl.CostEstimate(flops=flops, bytes_accessed=moved, transcendentals=0),
        name=name,
    )(*held)


def layer_norm(values):
    centred = values - jnp.mean(values, axis=-1, keepdims=True)
    invstd = lax.rsqrt(jnp.mean(centred * centred, axis=-1, keepdims=True) + 1e-05)
    return centred * invstd, invstd


def norm_back(upstream, normed, invstd, gains):
    scaled = upstream * gains
    return invstd * (
        scaled
        - jnp.mean(scaled, axis=-1, keepdims=True)
        - normed * jnp.mean(scaled * normed, axis=-1, keepdims=True)
    )


def silu_and_slope(preact):
    gate = 1.0 / (1.0 + jnp.exp(-preact))
    hidden = preact * gate
    return hidden, gate + hidden * (1.0 - gate)


def column_sum(values):
    return jnp.sum(values, axis=0, keepdims=True)


def pick_kernel(lists_ref, nodes_ref, out_ref):
    slots, count = lists_ref.shape[1], nodes_ref.shape[0]
    rows = lax.broadcasted_iota(jnp.int32, (count, slots), 0)
    pick = jnp.where(rows == lists_ref[...], 1.0, 0.0).astype(BF)
    out_ref[...] = mm_tn(pick, nodes_ref[...]).astype(BF)


def table_kernel(
    senders_ref, receivers_ref, edges_ref, nodes_ref, inner_ref, shift_ref,
    part_ref, own_ref, pick_ref, turned_ref,
):
    edge_count, width = edges_ref.shape
    count = nodes_ref.shape[0]
    senders = senders_ref[...]
    receivers = receivers_ref[...] + count
    senders = jnp.where(senders < count, senders, senders + count)
    wide_send = jnp.transpose(jnp.broadcast_to(senders, (LANES, edge_count)))
    wide_recv = jnp.transpose(jnp.broadcast_to(receivers, (LANES, edge_count)))
    lane = lax.broadcasted_iota(jnp.int32, (edge_count, LANES), 1)
    row = lax.broadcasted_iota(jnp.int32, (LANES, edge_count), 0)
    for start in range(0, pick_ref.shape[1], LANES):
        own_part = count <= start < 2 * count
        tall = wide_recv if own_part else wide_send
        flat = receivers if own_part else senders
        pick_ref[:, start : start + LANES] = jnp.where(tall == lane + start, 1.0, 0.0).astype(BF)
        turned_ref[start : start + LANES, :] = jnp.where(flat == row + start, 1.0, 0.0).astype(BF)
    nodes = nodes_ref[...]
    own_ref[:count, :] = mm(nodes, inner_ref[width : 2 * width, :]).astype(BF)
    own_ref[count:, :] = mm(nodes, inner_ref[2 * width :, :]).astype(BF)
    tile = edge_count // 4
    for start in range(0, edge_count, tile):
        part_ref[start : start + tile, :] = (
            mm(edges_ref[start : start + tile, :], inner_ref[:width, :]) + shift_ref[...]
        )


def forward_kernel(
    part_ref, own_ref, pick_ref, turned_ref, low_ref, high_ref, edges_ref, nodes_ref, cotan_ref,
    einner_ref, eouter_ref, ninner_ref, nouter_ref, eoffset_ref, egain_ref, nshift_ref, noffset_ref,
    ngain_ref,
    hidden_ref, slope_ref, normed_ref, invstd_ref, pulled_ref, partial_ref, weights_ref, sums_ref,
    *, scale,
):
    edge_count, width = edges_ref.shape
    count = nodes_ref.shape[0]
    rim = jnp.concatenate([low_ref[...], high_ref[...]], axis=0)
    far = mm(rim, einner_ref[width : 2 * width, :]).astype(BF)
    slots = rim.shape[0]
    tile = edge_count // 4
    total = jnp.zeros((count, width), F32)
    for start in range(0, edge_count, tile):
        rows = slice(start, start + tile)
        preact = (
            part_ref[rows, :]
            + mm(pick_ref[rows, : 2 * count], own_ref[...])
            + mm(pick_ref[rows, 2 * count : 2 * count + slots], far)
        )
        hidden, slope = silu_and_slope(preact)
        hidden = hidden.astype(BF)
        hidden_ref[rows, :] = hidden
        slope_ref[rows, :] = slope
        normed, invstd = layer_norm(mm(hidden, eouter_ref[...]) + eoffset_ref[...])
        normed_ref[rows, :] = normed
        invstd_ref[rows, :] = invstd
        fresh = (edges_ref[rows, :].astype(F32) + egain_ref[...] * normed).astype(BF)
        total += mm(turned_ref[count : 2 * count, rows], fresh)
    aggregate = total.astype(BF)
    nodes = nodes_ref[...]
    preact = (
        mm(nodes, ninner_ref[:width, :]) + mm(aggregate, ninner_ref[width:, :]) + nshift_ref[...]
    )
    hidden, slope = silu_and_slope(preact)
    hidden = hidden.astype(BF)
    normed, invstd = layer_norm(mm(hidden, nouter_ref[...]) + noffset_ref[...])
    cotan = cotan_ref[...].astype(F32)
    linear_back = norm_back(cotan, normed, invstd, ngain_ref[...])
    linear_half = linear_back.astype(BF)
    preact_back = mm_nt(linear_half, nouter_ref[...]) * slope
    preact_half = preact_back.astype(BF)
    pulled_ref[...] = mm_nt(preact_half, ninner_ref[width:, :]).astype(BF)
    partial_ref[...] = cotan + mm_nt(preact_half, ninner_ref[:width, :])
    hidden_width = preact.shape[1]
    weights_ref[:width, :] = mm_tn(nodes, preact_half) * scale
    weights_ref[width : 2 * width, :] = mm_tn(aggregate, preact_half) * scale
    weights_ref[2 * width : 2 * width + hidden_width, :] = mm_tn(hidden, linear_half) * scale
    sums_ref[0:1, :] = column_sum(preact_back) * scale
    sums_ref[1:2, :] = column_sum(linear_back) * scale
    sums_ref[2:3, :] = column_sum(cotan * normed) * scale


def backward_kernel(
    pick_ref, turned_ref, edges_ref, ecotan_ref, nodes_ref, low_ref, high_ref, hidden_ref, slope_ref,
    normed_ref, invstd_ref, pulled_ref, eouter_ref, egain_ref,
    fresh_ref, preact_ref, spread_ref, weights_ref, sums_ref,
    linear_ref,
    *, scale,
):
    edge_count, width = edges_ref.shape
    count = nodes_ref.shape[0]
    tile = edge_count // 4
    sums = [0.0, 0.0, 0.0]
    for start in range(0, edge_count, tile):
        rows = slice(start, start + tile)
        fresh_back = ecotan_ref[rows, :].astype(F32) + mm(
            pick_ref[rows, count : 2 * count], pulled_ref[...]
        )
        fresh_ref[rows, :] = fresh_back
        normed = normed_ref[rows, :]
        linear_back = norm_back(fresh_back, normed, invstd_ref[rows, :], egain_ref[...])
        linear_half = linear_back.astype(BF)
        linear_ref[rows, :] = linear_half
        preact_back = mm_nt(linear_half, eouter_ref[...]) * slope_ref[rows, :]
        preact_ref[rows, :] = preact_back.astype(BF)
        sums[0] += column_sum(preact_back)
        sums[1] += column_sum(linear_back)
        sums[2] += column_sum(fresh_back * normed)
    for k in range(3):
        sums_ref[k : k + 1, :] = sums[k] * scale
    used = spread_ref.shape[0]
    spread = mm(turned_ref[:used, :], preact_ref[...]).astype(BF)
    spread_ref[...] = spread
    weights_ref[:width, :] = mm_tn(edges_ref[...], preact_ref[...]) * scale
    rim = jnp.concatenate([low_ref[...], high_ref[...]], axis=0)
    nodes = nodes_ref[...]
    weights_ref[width : 2 * width, :] = (
        mm_tn(nodes, spread[:count]) + mm_tn(rim, spread[2 * count :])
    ) * scale
    weights_ref[2 * width : 3 * width, :] = mm_tn(nodes, spread[count : 2 * count]) * scale
    weights_ref[3 * width :, :] = mm_tn(hidden_ref[...], linear_ref[...]) * scale


def rim_kernel(spread_ref, inner_ref, out_ref, *, count):
    width = spread_ref.shape[1]
    out_ref[...] = mm_nt(spread_ref[2 * count :, :], inner_ref[width : 2 * width, :]).astype(BF)


def grads_kernel(spread_ref, inner_ref, partial_ref, fresh_ref, preact_ref, nodes_ref, edges_ref):
    count, width = partial_ref.shape
    nodes_ref[...] = (
        partial_ref[...]
        + mm_nt(spread_ref[:count, :], inner_ref[width : 2 * width, :])
        + mm_nt(spread_ref[count : 2 * count, :], inner_ref[2 * width :, :])
    )
    edge_count = preact_ref.shape[0]
    tile = edge_count // 4
    for start in range(0, edge_count, tile):
        rows = slice(start, start + tile)
        edges_ref[rows, :] = (
            fresh_ref[rows, :] + mm_nt(preact_ref[rows, :], inner_ref[:width, :])
        ).astype(BF)


def rims_kernel(lists_ref, partial_ref, low_ref, high_ref, out_ref):
    count, slots = partial_ref.shape[0], lists_ref.shape[1]
    rows = lax.broadcasted_iota(jnp.int32, (count, slots), 0)
    pick = jnp.where(rows == lists_ref[...], 1.0, 0.0).astype(BF)
    back = jnp.concatenate([low_ref[...], high_ref[...]], axis=0)
    out_ref[...] = partial_ref[...] + mm(pick, back)


def ring(values, step):
    count = lax.axis_size("patch")
    return lax.ppermute(values, "patch", [(i, (i + step) % count) for i in range(count)])


def halving_orders():
    core_bit = lax.axis_size("patch")
    high = [core_bit << k for k in range(1, lax.axis_size("region").bit_length() - 1)]
    low = [1 << k for k in range(core_bit.bit_length() - 1)]
    return core_bit, high + low, low[:-1] + high + low[-1:]


def permute_by(values, first, second, core_bit):
    count = lax.axis_size("region") * lax.axis_size("patch")
    pairs = [(i, i ^ (second if i & core_bit else first)) for i in range(count)]
    return lax.ppermute(values, AXES, pairs)


def reduce_all(flat, vectors):
    core_bit, first, second = halving_orders()
    count = lax.axis_size("region") * lax.axis_size("patch")
    me = lax.axis_index(AXES)
    core = (me & core_bit) // core_bit
    depth = count.bit_length() - 1
    flat = flat.reshape((2,) * depth + (-1, flat.shape[1]))

    def ordered(order):
        axes = [depth - bit.bit_length() for bit in [core_bit] + order]
        return jnp.transpose(flat, axes + [depth, depth + 1])

    blocks = jnp.stack([ordered(first)[0], ordered(second)[1]]).reshape(2, -1, flat.shape[-1])
    kept = lax.dynamic_index_in_dim(blocks, core, 0, keepdims=False)
    sent = lax.dynamic_index_in_dim(blocks, 1 - core, 0, keepdims=False).astype(BF)
    got = permute_by(sent, core_bit, core_bit, core_bit)
    total = kept + got
    for one, two in zip(first, second):
        bit = jnp.where(core == 1, (me & two) // two, (me & one) // one)
        halves = total.reshape(2, -1, flat.shape[-1])
        kept = lax.dynamic_index_in_dim(halves, bit, 0, keepdims=False)
        sent = lax.dynamic_index_in_dim(halves, 1 - bit, 0, keepdims=False).astype(BF)
        got = permute_by(sent, one, two, core_bit)
        vectors = vectors + permute_by(vectors, one, two, core_bit)
        total = kept + got
    vectors = vectors + permute_by(vectors, core_bit, core_bit, core_bit)
    return total.reshape(-1), vectors.reshape(-1)


def per_device(
    nodes, edges, node_cotan, edge_cotan, edge_inner, edge_outer, node_inner, node_outer, edge_shift,
    edge_offset, edge_gain, node_shift, node_offset, node_gain, send_rows, senders, receivers,
):
    count, width = nodes.shape
    edge_count = edges.shape[0]
    hidden_width = edge_outer.shape[0]
    lists = send_rows.reshape(1, -1)
    slots = lists.shape[1]
    half = slots // 2
    devices_all = lax.axis_size("region") * lax.axis_size("patch")
    edge_norm = 1.0 / math.sqrt(edge_count * devices_all)
    node_norm = 1.0 / math.sqrt(count * devices_all)
    picked = 2 * count + -(-slots // LANES) * LANES
    edge_shift, edge_offset, edge_gain, node_shift, node_offset, node_gain = (
        v.reshape(1, -1)
        for v in (edge_shift, edge_offset, edge_gain, node_shift, node_offset, node_gain)
    )

    (outgoing,) = call(
        pick_kernel, [((slots, width), BF)], lists, nodes, name="pick", limit=4 << 20
    )
    low = ring(outgoing[half:], 1)
    high = ring(outgoing[:half], -1)

    part, own, pick, turned = call(
        table_kernel,
        [
            ((edge_count, hidden_width), F32),
            ((2 * count, hidden_width), BF),
            ((edge_count, picked), BF),
            ((picked, edge_count), BF),
        ],
        senders.reshape(1, -1), receivers.reshape(1, -1), edges, nodes, edge_inner, edge_shift,
        name="table", flops=2 * (edge_count + 2 * count) * width * hidden_width,
    )
    hidden, slope, normed, invstd, pulled, partial, node_weights, node_sums = call(
        functools.partial(forward_kernel, scale=node_norm),
        [
            ((edge_count, hidden_width), BF),
            ((edge_count, hidden_width), F32),
            ((edge_count, width), F32),
            ((edge_count, 1), F32),
            ((count, width), BF),
            ((count, width), F32),
            ((2 * width + hidden_width, hidden_width), F32),
            ((3, width), F32),
        ],
        part, own, pick, turned, low, high, edges, nodes, node_cotan, edge_inner, edge_outer,
        node_inner, node_outer, edge_offset, edge_gain, node_shift, node_offset, node_gain,
        name="forward", flops=5 << 30,
    )
    fresh, preact, spread, edge_weights, edge_sums, _ = call(
        functools.partial(backward_kernel, scale=edge_norm),
        [
            ((edge_count, width), F32),
            ((edge_count, hidden_width), BF),
            ((2 * count + slots, hidden_width), BF),
            ((3 * width + hidden_width, hidden_width), F32),
            ((3, width), F32),
            ((edge_count, width), BF),
        ],
        pick, turned, edges, edge_cotan, nodes, low, high, hidden, slope, normed, invstd, pulled,
        edge_outer, edge_gain,
        name="backward", flops=5 << 30,
    )
    (rim_back,) = call(
        functools.partial(rim_kernel, count=count), [((slots, width), BF)], spread, edge_inner,
        name="rim", limit=4 << 20,
    )
    back_low = ring(rim_back[half:], 1)
    back_high = ring(rim_back[:half], -1)
    grad_weights, grad_vectors = reduce_all(
        jnp.concatenate([edge_weights, node_weights]), jnp.concatenate([edge_sums, node_sums])
    )
    nodes_part, grad_edges = call(
        grads_kernel,
        [((count, width), F32), ((edge_count, width), BF)],
        spread, edge_inner, partial, fresh, preact,
        name="grads", flops=2 << 30, outs_plain=(1,),
    )
    (grad_nodes,) = call(
        rims_kernel, [((count, width), F32)], lists, nodes_part, back_low, back_high, name="rims",
        outs_plain=(0,), limit=4 << 20,
    )
    return (grad_nodes, grad_edges, grad_weights, grad_vectors)


def solution(mesh):
    in_specs = (
        P(AXES, None), P(AXES, None), P(AXES, None), P(AXES, None),
        P(), P(), P(), P(), P(), P(), P(), P(), P(), P(),
        P("region", "patch", None, None), P(AXES), P(AXES),
    )
    out_specs = (P(AXES, None), P(AXES, None), P(AXES), P())
    return jax.shard_map(
        per_device, mesh=mesh, in_specs=in_specs, out_specs=out_specs, check_vma=False
    )
```

time: 102 us -> 120 us (1.18); the launches traced: 102 us -> 118 us
  matrix products: 22.2 us -> 0 us
  Pallas kernels: 0 us -> 15.2 us
  waiting for transfers between devices: 10.4 us -> 25.3 us
  local copies, waits for them, and re-layouts: 32.5 us -> 38.8 us
  other arithmetic: 14.8 us -> 17.9 us
    dot_general x20 -> x0, matrix products: 22.2 us -> none  [the longest x7 9.12 us: contract_rows(): lax.dot_general(left, right, (((0,), (0,)), ((), ())), preferred_element_...]
    pallas_call x0 -> x7, Pallas kernels: none -> 15.2 us  [call(): pl.pallas_call(body, out_shape=shapes, in_specs=[smem if i < scalars else...]
    ppermute x14, waiting for transfers between devices: 10.4 us -> 25.3 us  [the longest x10 25.3 us: permute_by(): return lax.ppermute(values, AXES, pairs)]
    convert_element_type x5, local copies, waits for them, and re-layouts: 2.5 us -> 9.34 us  [the longest x4 5.74 us: reduce_all(): lax.dynamic_index_in_dim(halves, 1 - bit, 0, keepdims=False).astype(BF)]
    add x4, other arithmetic: 6.72 us -> 11.8 us  [reduce_all(): total = kept + got]
    another operation x1, other arithmetic: 1.36 us -> 4.26 us  [reduce_all(): jnp.stack([ordered(first)[0], ordered(second)[1]])]
    unnamed x75 -> x67, local copies, waits for them, and re-layouts: 21.8 us -> 24.5 us
    slice x4 -> x2, local copies, waits for them, and re-layouts: 2.97 us -> 0.63 us  [the longest x1 0.62 us: per_device(): high = ring(outgoing[:half], -1)]
  transfers between devices with their start and end apart: 14 -> 14, of which waited for: 4 -> 5; matrix products, arithmetic and copies ran while one was open for 33% -> 5% of each run, Pallas kernels for 0% -> 4%
where the time goes in v2:
time: 120 us; the launch traced here: 118 us
  local copies, waits for them, and re-layouts  38.8 us (32%)
  waiting for transfers between devices  25.3 us (21%)
  starting transfers between devices  20.5 us (17%)
  other arithmetic  17.9 us (15%)
  Pallas kernels  15.2 us (13%)
    ppermute x10, waiting for transfers between devices, permute_by(): return lax.ppermute(values, AXES, pairs)  25.3 us
    unnamed x67, local copies, waits for them, and re-layouts  24.5 us
    pallas_call x7, Pallas kernels, call(): pl.pallas_call(body, out_shape=shapes, in_specs=[smem if i < scalars else...  15.2 us
    add x4, other arithmetic, reduce_all(): total = kept + got  11.8 us
    ppermute x4, starting transfers between devices, ring(): lax.ppermute(values, 'patch', [(i, (i + step) % count) for i in range(cou...  10.7 us
    ppermute x10, starting transfers between devices, permute_by(): return lax.ppermute(values, AXES, pairs)  9.74 us
    convert_element_type x4, local copies, waits for them, and re-layouts, reduce_all(): lax.dynamic_index_in_dim(halves, 1 - bit, 0, keepdims=False).astype(BF)  5.74 us
    another operation x1, other arithmetic, reduce_all(): jnp.stack([ordered(first)[0], ordered(second)[1]])  4.26 us
  transfers between devices with their start and end apart: 14, of which 5 were waited for; matrix products, arithmetic and copies ran while one was open for 5% of the time, Pallas kernels for 4%

profile of v2, /device:TPU:0, one launch (start us, length us, event | category | flops | bytes accessed | tf_op | source)
XLA Modules:
  0.0 118.5 jit_solution(4133508804081834622)
XLA Ops:
  3.2 3.0 %collective-permute-start = (bf16[32,512]{1,0:T(8,128)(2,1)}, bf16[32,512]{1,0:T(8,128)(2,1)S(1)}, u32[]{:S(2)}, u32[]{:S(2)}) collective-permute-start(bf16[32,512]{1,0:T(8,128)(2,1)} %get-tuple-element.45), channel_id=1, source_target_pairs={{0,1},{1,2},{2,3},{3,4},{4,5},{5,6},{6,7},{7,0},{8,9},{9,10},{10,1... | collective-permute-start | bytes 98312 | tf_op jit(solution)/shard_map/ppermute | solution.py:244
  6.1 3.0 %collective-permute-start.1 = (bf16[32,512]{1,0:T(8,128)(2,1)S(1)}, bf16[32,512]{1,0:T(8,128)(2,1)S(1)}, u32[]{:S(2)}, u32[]{:S(2)}) collective-permute-start(bf16[32,512]{1,0:T(8,128)(2,1)S(1)} %get-tuple-element.44), channel_id=1, source_target_pairs={{0,7},{1,0},{2,1},{3,2},{4,3},{5,4},{6,5},{7,6},{8,15},{9,8},{10,9... | collective-permute-start | bytes 98312 | tf_op jit(solution)/shard_map/ppermute | solution.py:244
  9.2 1.4 %copy-done = bf16[1536,512]{1,0:T(8,128)(2,1)S(1)} copy-done((bf16[1536,512]{1,0:T(8,128)(2,1)S(1)}, bf16[1536,512]{1,0:T(8,128)(2,1)}, u32[]{:S(2)}) %copy-start) | copy-done | bytes 1572888
  11.5 1.2 %copy-done.7 = bf16[1024,512]{1,0:T(8,128)(2,1)S(1)} copy-done((bf16[1024,512]{1,0:T(8,128)(2,1)S(1)}, bf16[1024,512]{1,0:T(8,128)(2,1)}, u32[]{:S(2)}) %copy-start.7) | copy-done | bytes 1048600
  14.8 1.4 %table.1 = (f32[1024,512]{1,0:T(8,128)S(1)}, bf16[512,512]{1,0:T(8,128)(2,1)S(1)}, bf16[1024,640]{1,0:T(8,128)(2,1)S(1)}, bf16[640,1024]{1,0:T(8,128)(2,1)S(1)}) custom-call(s32[1,1024]{1,0:T(1,128)S(1)} %bitcast.45, s32[1,1024]{1,0:T(1,128)S(1)} %bitcast.46, bf16[1024,512]{1,0:T(8,128)(2,1)S(1)} %copy-done.7, bf16[256,512]{1,0:T(8,128)(2,1)S(1)} %copy-done.4, ...), custom_call_target="tpu_custom_call" | custom-call | flops 805306368 | bytes 5242880 | tf_op jit(solution)/shard_map/table/pallas_call | solution.py:46
  18.1 1.4 %copy-done.1 = bf16[1536,512]{1,0:T(8,128)(2,1)S(1)} copy-done((bf16[1536,512]{1,0:T(8,128)(2,1)S(1)}, bf16[1536,512]{1,0:T(8,128)(2,1)}, u32[]{:S(2)}) %copy-start.1) | copy-done | bytes 1572888
  20.5 1.2 %copy-done.6 = bf16[1024,512]{1,0:T(8,128)(2,1)S(1)} copy-done((bf16[1024,512]{1,0:T(8,128)(2,1)S(1)}, bf16[1024,512]{1,0:T(8,128)(2,1)}, u32[]{:S(2)}) %copy-start.6) | copy-done | bytes 1048600
  21.7 1.2 %copy-done.8 = bf16[1024,512]{1,0:T(8,128)(2,1)S(1)} copy-done((bf16[1024,512]{1,0:T(8,128)(2,1)S(1)}, bf16[1024,512]{1,0:T(8,128)(2,1)}, u32[]{:S(2)}) %copy-start.8) | copy-done | bytes 1048600
  29.4 1.3 %copy-done.23 = bf16[640,1024]{1,0:T(8,128)(2,1)S(1)} copy-done((bf16[640,1024]{1,0:T(8,128)(2,1)S(1)}, bf16[640,1024]{1,0:T(8,128)(2,1)}, u32[]{:S(2)}) %copy-start.23) | copy-done | bytes 1310744
  31.7 5.7 %forward.1 = (bf16[1024,512]{1,0:T(8,128)(2,1)S(1)}, f32[1024,512]{1,0:T(8,128)S(1)}, f32[1024,512]{1,0:T(8,128)S(1)}, f32[1024,1]{1,0:T(8,128)S(1)}, bf16[256,5...) custom-call(f32[1024,512]{1,0:T(8,128)S(1)} %get-tuple-element.25.part_ref, ...), custom_call_target="tpu_custom_call" | custom-call | flops 5368709120 | bytes 9185280 | tf_op jit(solution)/shard_map/forward/pallas_call | solution.py:46
  37.5 4.5 %backward.1 = (f32[1024,512]{1,0:T(8,128)S(1)}, bf16[1024,512]{1,0:T(8,128)(2,1)S(1)}, bf16[576,512]{1,0:T(8,128)(2,1)S(1)}, f32[2048,512]{1,0:T(8,128)S(1)}, f3...) custom-call(bf16[1024,640]{1,0:T(8,128)(2,1)S(1)} %get-tuple-element.23.pick_ref, bf16[640,1024]{1,0:T(8,128)(2,1)S(1)} %copy-done.23, ...), custom_call_target="tpu_custom_call" | custom-call | flops 5368709120 | bytes 8984576 | tf_op jit(solution)/shard_map/backward/pallas_call | solution.py:46
  42.1 1.4 %copy-done.26 = f32[1024,512]{1,0:T(8,128)} copy-done((f32[1024,512]{1,0:T(8,128)}, f32[1024,512]{1,0:T(8,128)S(1)}, u32[]{:S(2)}) %copy-start.26) | copy-done | bytes 2097176
  47.5 4.3 %pad_maximum_fusion.1 = f32[2,2,2,2,2,112,512]{6,5,4,3,2,1,0:T(8,128)} fusion(f32[1,2,2,2,2,112,512]{6,5,4,3,2,1,0:T(8,128)S(1)} %slice.29, f32[1,2,2,2,2,112,512]{6,5,4,3,2,1,0:T(8,128)S(1)} %slice.28), kind=kLoop, calls=%fused_computation.1 | loop fusion | flops 1835008 | bytes 14680064 | tf_op jit(solution)/shard_map/stack | solution.py:272
  51.8 3.6 %fusion = bf16[1792,512]{1,0:T(8,128)(2,1)} fusion(f32[2,1792,512]{2,1,0:T(8,128)} %bitcast.11, s32[]{:T(128)S(6)} %select_n.66), kind=kLoop, calls=%fused_computation.6 | loop fusion | bytes 3670020 | tf_op jit(solution)/shard_map/convert_element_type | solution.py:274
  55.4 4.1 %collective-permute-done.4 = bf16[1792,512]{1,0:T(8,128)(2,1)} collective-permute-done((bf16[1792,512]{1,0:T(8,128)(2,1)}, bf16[1792,512]{1,0:T(8,128)(2,1)}, u32[]{:S(2)}, u32[]{:S(2)}) %collective-permute-start.4) | collective-permute-done | bytes 1835040 | tf_op jit(solution)/shard_map/ppermute | solution.py:257
  59.5 5.1 %bitcast_add_fusion = f32[1792,512]{1,0:T(8,128)} fusion(bf16[1792,512]{1,0:T(8,128)(2,1)} %collective-permute-done.4, f32[2,1792,512]{2,1,0:T(8,128)} %bitcast.11, s32[]{:T(128)S(6)} %select_n.65), kind=kLoop, calls=%fused_computation.4 | loop fusion | flops 1835008 | bytes 9175044 | tf_op jit(solution)/shard_map/add | solution.py:276
  64.6 2.6 %fusion.1 = bf16[896,512]{1,0:T(8,128)(2,1)} fusion(f32[2,896,512]{2,1,0:T(8,128)} %bitcast.14, s32[]{:T(128)S(6)} %select_n.70), kind=kLoop, calls=%fused_computation.9 | loop fusion | bytes 1835012 | tf_op jit(solution)/shard_map/convert_element_type | solution.py:281
  67.2 1.6 %collective-permute-start.5 = (bf16[896,512]{1,0:T(8,128)(2,1)}, bf16[896,512]{1,0:T(8,128)(2,1)S(1)}, u32[]{:S(2)}, u32[]{:S(2)}) collective-permute-start(bf16[896,512]{1,0:T(8,128)(2,1)} %fusion.1), channel_id=1, source_target_pairs={{0,16},{1,17},{2,18},{3,19},{4,20},{5,21},{6,22},{7,23},{8,9},{9,8... | collective-permute-start | bytes 2752520 | tf_op jit(solution)/shard_map/ppermute | solution.py:257
  68.8 12.0 %collective-permute-done.5 = bf16[896,512]{1,0:T(8,128)(2,1)S(1)} collective-permute-done((bf16[896,512]{1,0:T(8,128)(2,1)}, bf16[896,512]{1,0:T(8,128)(2,1)S(1)}, u32[]{:S(2)}, u32[]{:S(2)}) %collective-permute-start.5) | collective-permute-done | bytes 917536 | tf_op jit(solution)/shard_map/ppermute | solution.py:257
  80.8 3.1 %bitcast_add_fusion.1 = f32[896,512]{1,0:T(8,128)} fusion(bf16[896,512]{1,0:T(8,128)(2,1)S(1)} %collective-permute-done.5, f32[2,896,512]{2,1,0:T(8,128)} %bitcast.14, s32[]{:T(128)S(6)} %select_n.69), kind=kLoop, calls=%fused_computation.7 | loop fusion | flops 917504 | bytes 4587524 | tf_op jit(solution)/shard_map/add | solution.py:284
  83.9 2.1 %fusion.2 = bf16[448,512]{1,0:T(8,128)(2,1)} fusion(f32[2,448,512]{2,1,0:T(8,128)} %bitcast.17, s32[]{:T(128)S(6)} %select_n.74), kind=kLoop, calls=%fused_computation.12 | loop fusion | bytes 917508 | tf_op jit(solution)/shard_map/convert_element_type | solution.py:281
  86.0 1.7 %collective-permute-start.9 = (f32[6,512]{1,0:T(8,128)S(1)}, f32[6,512]{1,0:T(8,128)S(1)}, u32[]{:S(2)}, u32[]{:S(2)}) collective-permute-start(f32[6,512]{1,0:T(8,128)S(1)} %pad_maximum_fusion.2), channel_id=1, source_target_pairs={{0,16},{1,17},{2,18},{3,19},{4,20},{5,21},{6,22},{7,23},{8,9},{9,8... | collective-permute-start | bytes 36872 | tf_op jit(solution)/shard_map/ppermute | solution.py:257
  87.7 2.1 %collective-permute-done.9 = f32[6,512]{1,0:T(8,128)S(1)} collective-permute-done((f32[6,512]{1,0:T(8,128)S(1)}, f32[6,512]{1,0:T(8,128)S(1)}, u32[]{:S(2)}, u32[]{:S(2)}) %collective-permute-start.9) | collective-permute-done | bytes 12320 | tf_op jit(solution)/shard_map/ppermute | solution.py:257
  89.8 2.1 %collective-permute-start.10 = (f32[6,512]{1,0:T(8,128)S(1)}, f32[6,512]{1,0:T(8,128)S(1)}, u32[]{:S(2)}, u32[]{:S(2)}) collective-permute-start(f32[6,512]{1,0:T(8,128)S(1)} %fusion.6), channel_id=1, source_target_pairs={{0,1},{1,0},{2,3},{3,2},{4,5},{5,4},{6,7},{7,6},{8,10},{9,11},{10,... | collective-permute-start | bytes 36872 | tf_op jit(solution)/shard_map/ppermute | solution.py:257
  91.9 3.0 %collective-permute-done.10 = f32[6,512]{1,0:T(8,128)S(1)} collective-permute-done((f32[6,512]{1,0:T(8,128)S(1)}, f32[6,512]{1,0:T(8,128)S(1)}, u32[]{:S(2)}, u32[]{:S(2)}) %collective-permute-start.10) | collective-permute-done | bytes 12320 | tf_op jit(solution)/shard_map/ppermute | solution.py:257
  94.9 2.4 %bitcast_add_fusion.2 = f32[448,512]{1,0:T(8,128)} fusion(bf16[448,512]{1,0:T(8,128)(2,1)} %collective-permute-done.6, f32[2,448,512]{2,1,0:T(8,128)} %bitcast.17, s32[]{:T(128)S(6)} %select_n.73), kind=kLoop, calls=%fused_computation.10 | loop fusion | flops 458752 | bytes 2293764 | tf_op jit(solution)/shard_map/add | solution.py:284
  98.4 2.0 %collective-permute-start.7 = (bf16[224,512]{1,0:T(8,128)(2,1)S(1)}, bf16[224,512]{1,0:T(8,128)(2,1)}, u32[]{:S(2)}, u32[]{:S(2)}) collective-permute-start(bf16[224,512]{1,0:T(8,128)(2,1)S(1)} %fusion.3), channel_id=1, source_target_pairs={{0,2},{1,3},{2,0},{3,1},{4,6},{5,7},{6,4},{7,5},{8,24},{9,25},{10,... | collective-permute-start | bytes 688136 | tf_op jit(solution)/shard_map/ppermute | solution.py:257
  102.5 3.9 %collective-permute-start.3 = (bf16[32,512]{1,0:T(8,128)(2,1)S(1)}, bf16[32,512]{1,0:T(8,128)(2,1)S(1)}, u32[]{:S(2)}, u32[]{:S(2)}) collective-permute-start(bf16[32,512]{1,0:T(8,128)(2,1)S(1)} %get-tuple-element.42), channel_id=1, source_target_pairs={{0,7},{1,0},{2,1},{3,2},{4,3},{5,4},{6,5},{7,6},{8,15},{9,8},{10,9... | collective-permute-start | bytes 98312 | tf_op jit(solution)/shard_map/ppermute | solution.py:244
  106.5 1.2 %bitcast_add_fusion.3 = f32[224,512]{1,0:T(8,128)S(1)} fusion(bf16[224,512]{1,0:T(8,128)(2,1)} %collective-permute-done.7, f32[2,224,512]{2,1,0:T(8,128)} %bitcast.20, s32[]{:T(128)S(6)} %select_n.76), kind=kLoop, calls=%fused_computation.13 | loop fusion | flops 229376 | bytes 1146884 | tf_op jit(solution)/shard_map/add | solution.py:284
  107.8 1.1 collective-permute-start.8
  108.9 2.1 %grads.1 = (f32[256,512]{1,0:T(8,128)S(1)}, bf16[1024,512]{1,0:T(8,128)(2,1)}) custom-call(bf16[576,512]{1,0:T(8,128)(2,1)S(1)} %get-tuple-element.32.spread_ref, bf16[1536,512]{1,0:T(8,128)(2,1)S(1)} %copy-done.2, f32[256,512]{1,0:T(8,128)S(1)} %copy-done.31, f32[1024,512]{1,0:T(8,128)S(1)} %copy-done.27, bf16[1024,512]{1,0:T(8,128)(2,1)S(1)} %copy-done.29), custom_call_target="tpu_custom_call" | custom-call | flops 2147483648 | bytes 1572864 | tf_op jit(solution)/shard_map/grads/pallas_call | solution.py:46
  112.6 4.1 %collective-permute-done.8 = bf16[112,512]{1,0:T(8,128)(2,1)S(1)} collective-permute-done((bf16[112,512]{1,0:T(8,128)(2,1)S(1)}, bf16[112,512]{1,0:T(8,128)(2,1)S(1)}, u32[]{:S(2)}, u32[]{:S(2)}) %collective-permute-start.8) | collective-permute-done | bytes 114720 | tf_op jit(solution)/shard_map/ppermute | solution.py:257
  (96 shorter events, 26.6 us)
Async XLA Ops:
  3.2 14.9 %collective-permute-start = (bf16[32,512]{1,0:T(8,128)(2,1)}, bf16[32,512]{1,0:T(8,128)(2,1)S(1)}, u32[]{:S(2)}, u32[]{:S(2)}) collective-permute-start(bf16[32,512]{1,0:T(8,128)(2,1)} %get-tuple-element.45), channel_id=1, source_target_pairs={{0,1},{1,2},{2,3},{3,4},{4,5},{5,6},{6,7},{7,0},{8,9},{9,10},{10,1... | collective-permute-start | bytes 98312 | tf_op jit(solution)/shard_map/ppermute | solution.py:244
  6.1 12.0 %collective-permute-start.1 = (bf16[32,512]{1,0:T(8,128)(2,1)S(1)}, bf16[32,512]{1,0:T(8,128)(2,1)S(1)}, u32[]{:S(2)}, u32[]{:S(2)}) collective-permute-start(bf16[32,512]{1,0:T(8,128)(2,1)S(1)} %get-tuple-element.44), channel_id=1, source_target_pairs={{0,7},{1,0},{2,1},{3,2},{4,3},{5,4},{6,5},{7,6},{8,15},{9,8},{10,9... | collective-permute-start | bytes 98312 | tf_op jit(solution)/shard_map/ppermute | solution.py:244
  9.2 1.4 %copy-start = (bf16[1536,512]{1,0:T(8,128)(2,1)S(1)}, bf16[1536,512]{1,0:T(8,128)(2,1)}, u32[]{:S(2)}) copy-start(bf16[1536,512]{1,0:T(8,128)(2,1)} %inner_ref.5) | copy-start | bytes 4718596
  11.5 1.2 %copy-start.7 = (bf16[1024,512]{1,0:T(8,128)(2,1)S(1)}, bf16[1024,512]{1,0:T(8,128)(2,1)}, u32[]{:S(2)}) copy-start(bf16[1024,512]{1,0:T(8,128)(2,1)} %edges_ref.5) | copy-start | bytes 3145732
  16.2 1.1 copy-start.22
  18.1 1.4 %copy-start.1 = (bf16[1536,512]{1,0:T(8,128)(2,1)S(1)}, bf16[1536,512]{1,0:T(8,128)(2,1)}, u32[]{:S(2)}) copy-start(bf16[1536,512]{1,0:T(8,128)(2,1)} %inner_ref.5) | copy-start | bytes 4718596
  20.5 1.2 %copy-start.6 = (bf16[1024,512]{1,0:T(8,128)(2,1)S(1)}, bf16[1024,512]{1,0:T(8,128)(2,1)}, u32[]{:S(2)}) copy-start(bf16[1024,512]{1,0:T(8,128)(2,1)} %ninner_ref.1) | copy-start | bytes 3145732
  21.7 1.2 %copy-start.8 = (bf16[1024,512]{1,0:T(8,128)(2,1)S(1)}, bf16[1024,512]{1,0:T(8,128)(2,1)}, u32[]{:S(2)}) copy-start(bf16[1024,512]{1,0:T(8,128)(2,1)} %edges_ref.5) | copy-start | bytes 3145732
  22.9 1.0 copy-start.10
  29.4 1.3 %copy-start.23 = (bf16[640,1024]{1,0:T(8,128)(2,1)S(1)}, bf16[640,1024]{1,0:T(8,128)(2,1)}, u32[]{:S(2)}) copy-start(bf16[640,1024]{1,0:T(8,128)(2,1)} %copy-done.22) | copy-start | bytes 3932164
  31.7 5.8 %copy-start.9 = (bf16[1024,512]{1,0:T(8,128)(2,1)S(1)}, bf16[1024,512]{1,0:T(8,128)(2,1)}, u32[]{:S(2)}) copy-start(bf16[1024,512]{1,0:T(8,128)(2,1)} %ecotan_ref.1) | copy-start | bytes 3145732
  31.7 5.8 %copy-start.12 = (bf16[512,512]{1,0:T(8,128)(2,1)S(1)}, bf16[512,512]{1,0:T(8,128)(2,1)}, u32[]{:S(2)}) copy-start(bf16[512,512]{1,0:T(8,128)(2,1)} %eouter_ref.3) | copy-start | bytes 1572868
  37.5 4.6 %copy-start.30 = (f32[256,512]{1,0:T(8,128)}, f32[256,512]{1,0:T(8,128)S(1)}, u32[]{:S(2)}) copy-start(f32[256,512]{1,0:T(8,128)S(1)} %get-tuple-element.33.partial_ref) | copy-start | bytes 1572868
  42.0 1.4 %copy-start.26 = (f32[1024,512]{1,0:T(8,128)}, f32[1024,512]{1,0:T(8,128)S(1)}, u32[]{:S(2)}) copy-start(f32[1024,512]{1,0:T(8,128)S(1)} %get-tuple-element.34.fresh_ref) | copy-start | bytes 6291460
  43.5 1.2 copy-start.28
  55.4 4.1 %collective-permute-start.4 = (bf16[1792,512]{1,0:T(8,128)(2,1)}, bf16[1792,512]{1,0:T(8,128)(2,1)}, u32[]{:S(2)}, u32[]{:S(2)}) collective-permute-start(bf16[1792,512]{1,0:T(8,128)(2,1)} %fusion), channel_id=1, source_target_pairs={{0,8},{1,9},{2,10},{3,11},{4,12},{5,13},{6,14},{7,15},{8,0},{9,1},... | collective-permute-start | bytes 5505032 | tf_op jit(solution)/shard_map/ppermute | solution.py:257
  67.2 13.6 %collective-permute-start.5 = (bf16[896,512]{1,0:T(8,128)(2,1)}, bf16[896,512]{1,0:T(8,128)(2,1)S(1)}, u32[]{:S(2)}, u32[]{:S(2)}) collective-permute-start(bf16[896,512]{1,0:T(8,128)(2,1)} %fusion.1), channel_id=1, source_target_pairs={{0,16},{1,17},{2,18},{3,19},{4,20},{5,21},{6,22},{7,23},{8,9},{9,8... | collective-permute-start | bytes 2752520 | tf_op jit(solution)/shard_map/ppermute | solution.py:257
  68.8 31.6 %copy-start.2 = (bf16[1536,512]{1,0:T(8,128)(2,1)S(1)}, bf16[1536,512]{1,0:T(8,128)(2,1)}, u32[]{:S(2)}) copy-start(bf16[1536,512]{1,0:T(8,128)(2,1)} %inner_ref.5) | copy-start | bytes 4718596
  83.9 25.1 %copy-start.29 = (bf16[1024,512]{1,0:T(8,128)(2,1)S(1)}, bf16[1024,512]{1,0:T(8,128)(2,1)}, u32[]{:S(2)}) copy-start(bf16[1024,512]{1,0:T(8,128)(2,1)} %copy-done.28) | copy-start | bytes 3145732
  86.0 9.0 %collective-permute-start.6 = (bf16[448,512]{1,0:T(8,128)(2,1)}, bf16[448,512]{1,0:T(8,128)(2,1)}, u32[]{:S(2)}, u32[]{:S(2)}) collective-permute-start(bf16[448,512]{1,0:T(8,128)(2,1)} %fusion.2), channel_id=1, source_target_pairs={{0,1},{1,0},{2,3},{3,2},{4,5},{5,4},{6,7},{7,6},{8,10},{9,11},{10,... | collective-permute-start | bytes 1376264 | tf_op jit(solution)/shard_map/ppermute | solution.py:257
  86.0 3.8 %collective-permute-start.9 = (f32[6,512]{1,0:T(8,128)S(1)}, f32[6,512]{1,0:T(8,128)S(1)}, u32[]{:S(2)}, u32[]{:S(2)}) collective-permute-start(f32[6,512]{1,0:T(8,128)S(1)} %pad_maximum_fusion.2), channel_id=1, source_target_pairs={{0,16},{1,17},{2,18},{3,19},{4,20},{5,21},{6,22},{7,23},{8,9},{9,8... | collective-permute-start | bytes 36872 | tf_op jit(solution)/shard_map/ppermute | solution.py:257
  89.8 5.0 %collective-permute-start.10 = (f32[6,512]{1,0:T(8,128)S(1)}, f32[6,512]{1,0:T(8,128)S(1)}, u32[]{:S(2)}, u32[]{:S(2)}) collective-permute-start(f32[6,512]{1,0:T(8,128)S(1)} %fusion.6), channel_id=1, source_target_pairs={{0,1},{1,0},{2,3},{3,2},{4,5},{5,4},{6,7},{7,6},{8,10},{9,11},{10,... | collective-permute-start | bytes 36872 | tf_op jit(solution)/shard_map/ppermute | solution.py:257
  94.9 5.8 %collective-permute-start.11 = (f32[6,512]{1,0:T(8,128)S(1)}, f32[6,512]{1,0:T(8,128)S(1)}, u32[]{:S(2)}, u32[]{:S(2)}) collective-permute-start(f32[6,512]{1,0:T(8,128)S(1)} %add.95), channel_id=1, source_target_pairs={{0,2},{1,3},{2,0},{3,1},{4,6},{5,7},{6,4},{7,5},{8,24},{9,25},{10,... | collective-permute-start | bytes 36872 | tf_op jit(solution)/shard_map/ppermute | solution.py:257
  98.4 8.1 %collective-permute-start.7 = (bf16[224,512]{1,0:T(8,128)(2,1)S(1)}, bf16[224,512]{1,0:T(8,128)(2,1)}, u32[]{:S(2)}, u32[]{:S(2)}) collective-permute-start(bf16[224,512]{1,0:T(8,128)(2,1)S(1)} %fusion.3), channel_id=1, source_target_pairs={{0,2},{1,3},{2,0},{3,1},{4,6},{5,7},{6,4},{7,5},{8,24},{9,25},{10,... | collective-permute-start | bytes 688136 | tf_op jit(solution)/shard_map/ppermute | solution.py:257
  100.4 8.5 %copy-start.27 = (f32[1024,512]{1,0:T(8,128)S(1)}, f32[1024,512]{1,0:T(8,128)}, u32[]{:S(2)}) copy-start(f32[1024,512]{1,0:T(8,128)} %copy-done.26) | copy-start | bytes 6291460
  100.4 8.5 %copy-start.31 = (f32[256,512]{1,0:T(8,128)S(1)}, f32[256,512]{1,0:T(8,128)}, u32[]{:S(2)}) copy-start(f32[256,512]{1,0:T(8,128)} %copy-done.30) | copy-start | bytes 1572868
  100.7 5.7 %collective-permute-start.12 = (f32[6,512]{1,0:T(8,128)S(1)}, f32[6,512]{1,0:T(8,128)S(1)}, u32[]{:S(2)}, u32[]{:S(2)}) collective-permute-start(f32[6,512]{1,0:T(8,128)S(1)} %add.96), channel_id=1, source_target_pairs={{0,4},{1,5},{2,6},{3,7},{4,0},{5,1},{6,2},{7,3},{8,12},{9,13},{10,... | collective-permute-start | bytes 36872 | tf_op jit(solution)/shard_map/ppermute | solution.py:257
  101.7 9.3 %collective-permute-start.2 = (bf16[32,512]{1,0:T(8,128)(2,1)S(1)}, bf16[32,512]{1,0:T(8,128)(2,1)S(1)}, u32[]{:S(2)}, u32[]{:S(2)}) collective-permute-start(bf16[32,512]{1,0:T(8,128)(2,1)S(1)} %get-tuple-element.43), channel_id=1, source_target_pairs={{0,1},{1,2},{2,3},{3,4},{4,5},{5,6},{6,7},{7,0},{8,9},{9,10},{10,1... | collective-permute-start | bytes 98312 | tf_op jit(solution)/shard_map/ppermute | solution.py:244
  102.5 8.5 %collective-permute-start.3 = (bf16[32,512]{1,0:T(8,128)(2,1)S(1)}, bf16[32,512]{1,0:T(8,128)(2,1)S(1)}, u32[]{:S(2)}, u32[]{:S(2)}) collective-permute-start(bf16[32,512]{1,0:T(8,128)(2,1)S(1)} %get-tuple-element.42), channel_id=1, source_target_pairs={{0,7},{1,0},{2,1},{3,2},{4,3},{5,4},{6,5},{7,6},{8,15},{9,8},{10,9... | collective-permute-start | bytes 98312 | tf_op jit(solution)/shard_map/ppermute | solution.py:244
  106.5 5.6 %collective-permute-start.13 = (f32[6,512]{1,0:T(8,128)S(1)}, f32[6,512]{1,0:T(8,128)S(1)}, u32[]{:S(2)}, u32[]{:S(2)}) collective-permute-start(f32[6,512]{1,0:T(8,128)S(1)} %add.97), channel_id=1, source_target_pairs={{0,8},{1,9},{2,10},{3,11},{4,12},{5,13},{6,14},{7,15},{8,0},{9,1},... | collective-permute-start | bytes 36872 | tf_op jit(solution)/shard_map/ppermute | solution.py:257
  107.8 3.2 %copy-start.32 = (f32[224,512]{1,0:T(8,128)}, f32[224,512]{1,0:T(8,128)S(1)}, u32[]{:S(2)}) copy-start(f32[224,512]{1,0:T(8,128)S(1)} %bitcast_add_fusion.3) | copy-start | bytes 1376260
  107.8 9.0 %collective-permute-start.8 = (bf16[112,512]{1,0:T(8,128)(2,1)S(1)}, bf16[112,512]{1,0:T(8,128)(2,1)S(1)}, u32[]{:S(2)}, u32[]{:S(2)}) collective-permute-start(bf16[112,512]{1,0:T(8,128)(2,1)S(1)} %fusion.5), channel_id=1, source_target_pairs={{0,4},{1,5},{2,6},{3,7},{4,0},{5,1},{6,2},{7,3},{8,12},{9,13},{10,... | collective-permute-start | bytes 344072 | tf_op jit(solution)/shard_map/ppermute | solution.py:257
  (15 other events, 12.1 us)

commit v3 on v2

--- a/solution.py
+++ b/solution.py
@@ -31,27 +31,38 @@
     return lax.dot_general(a, b, (((0,), (0,)), ((), ())), preferred_element_type=F32)
 
 
-def call(body, outs, *args, scalars=0, flops=0, limit=24 << 20, name=None, outs_plain=()):
+def call(body, outs, *args, flops=0, limit=24 << 20, name=None, plain=(), hbm=(), scratch=()):
     vmem = pl.BlockSpec(memory_space=pltpu.VMEM)
-    smem = pl.BlockSpec(memory_space=pltpu.SMEM)
-    held = [
-        a if i < scalars else pltpu.with_memory_space_constraint(a, pltpu.VMEM)
-        for i, a in enumerate(args)
-    ]
+    anywhere = pl.BlockSpec(memory_space=pltpu.HBM)
     shapes = [
-        jax.ShapeDtypeStruct(s, d) if i in outs_plain else pinned(s, d)
-        for i, (s, d) in enumerate(outs)
+        jax.ShapeDtypeStruct(s, d) if i in plain else pinned(s, d) for i, (s, d) in enumerate(outs)
     ]
     moved = sum(math.prod(s) * jnp.dtype(d).itemsize for s, d in outs)
     return pl.pallas_call(
         body,
         out_shape=shapes,
-        in_specs=[smem if i < scalars else vmem for i in range(len(args))],
+        in_specs=[anywhere if i in hbm else vmem for i in range(len(args))],
         out_specs=[vmem] * len(outs),
+        scratch_shapes=list(scratch),
         compiler_params=pltpu.CompilerParams(vmem_limit_bytes=limit),
         cost_estimate=pl.CostEstimate(flops=flops, bytes_accessed=moved, transcendentals=0),
         name=name,
-    )(*held)
+    )(*[far(a) if i in hbm else a for i, a in enumerate(args)])
+
+
+def far(array):
+    return pltpu.with_memory_space_constraint(array, pltpu.HBM)
+
+
+def near(array):
+    return pltpu.with_memory_space_constraint(array, pltpu.VMEM)
+
+
+def start_copies(pairs, sems):
+    copies = [pltpu.make_async_copy(a, b, sems.at[i]) for i, (a, b) in enumerate(pairs)]
+    for copy in copies:
+        copy.start()
+    return copies
 
 
 def layer_norm(values):
@@ -79,17 +90,25 @@
     return jnp.sum(values, axis=0, keepdims=True)
 
 
-def pick_kernel(lists_ref, nodes_ref, out_ref):
+def pick_kernel(lists_hbm, nodes_hbm, low_ref, high_ref, lists_ref, nodes_ref, sems):
+    for copy in start_copies([(lists_hbm, lists_ref), (nodes_hbm, nodes_ref)], sems):
+        copy.wait()
     slots, count = lists_ref.shape[1], nodes_ref.shape[0]
     rows = lax.broadcasted_iota(jnp.int32, (count, slots), 0)
-    pick = jnp.where(rows == lists_ref[...], 1.0, 0.0).astype(BF)
-    out_ref[...] = mm_tn(pick, nodes_ref[...]).astype(BF)
+    for k, out_ref in enumerate((low_ref, high_ref)):
+        pick = jnp.where(rows == lists_ref[k : k + 1, :], 1.0, 0.0).astype(BF)
+        out_ref[...] = mm_tn(pick, nodes_ref[...]).astype(BF)
 
 
 def table_kernel(
-    senders_ref, receivers_ref, edges_ref, nodes_ref, inner_ref, shift_ref,
-    part_ref, own_ref, pick_ref, turned_ref,
+    *refs, given,
 ):
+    part_ref, own_ref, pick_ref, turned_ref = refs[given : given + 4]
+    loaded, sems = refs[given + 4 : -1], refs[-1]
+    copies = start_copies(list(zip(refs[:given], loaded)), sems)
+    senders_ref, receivers_ref, shift_ref, nodes_ref, inner_ref, edges_ref = loaded[:6]
+    copies[0].wait()
+    copies[1].wait()
     edge_count, width = edges_ref.shape
     count = nodes_ref.shape[0]
     senders = senders_ref[...]
@@ -105,23 +124,37 @@
         flat = receivers if own_part else senders
         pick_ref[:, start : start + LANES] = jnp.where(tall == lane + start, 1.0, 0.0).astype(BF)
         turned_ref[start : start + LANES, :] = jnp.where(flat == row + start, 1.0, 0.0).astype(BF)
+    copies[3].wait()
+    copies[4].wait()
     nodes = nodes_ref[...]
     own_ref[:count, :] = mm(nodes, inner_ref[width : 2 * width, :]).astype(BF)
     own_ref[count:, :] = mm(nodes, inner_ref[2 * width :, :]).astype(BF)
+    copies[2].wait()
+    copies[5].wait()
     tile = edge_count // 4
     for start in range(0, edge_count, tile):
         part_ref[start : start + tile, :] = (
             mm(edges_ref[start : start + tile, :], inner_ref[:width, :]) + shift_ref[...]
         )
+    for copy in copies[6:]:
+        copy.wait()
 
 
 def forward_kernel(
-    part_ref, own_ref, pick_ref, turned_ref, low_ref, high_ref, edges_ref, nodes_ref, cotan_ref,
-    einner_ref, eouter_ref, ninner_ref, nouter_ref, eoffset_ref, egain_ref, nshift_ref, noffset_ref,
-    ngain_ref,
+    part_ref, own_ref, pick_ref, turned_ref, low_ref, high_ref, edges_ref, nodes_ref,
+    einner_ref, eouter_ref, eoffset_ref, egain_ref, nshift_ref, noffset_ref, ngain_ref,
+    ninner_hbm, nouter_hbm, cotan_hbm, ecotan_hbm,
     hidden_ref, slope_ref, normed_ref, invstd_ref, pulled_ref, partial_ref, weights_ref, sums_ref,
+    ecotan_ref, ninner_ref, nouter_ref, cotan_ref, sems,
     *, scale,
 ):
+    copies = start_copies(
+        [
+            (ninner_hbm, ninner_ref), (nouter_hbm, nouter_ref), (cotan_hbm, cotan_ref),
+            (ecotan_hbm, ecotan_ref),
+        ],
+        sems,
+    )
     edge_count, width = edges_ref.shape
     count = nodes_ref.shape[0]
     rim = jnp.concatenate([low_ref[...], high_ref[...]], axis=0)
@@ -146,6 +179,8 @@
         fresh = (edges_ref[rows, :].astype(F32) + egain_ref[...] * normed).astype(BF)
         total += mm(turned_ref[count : 2 * count, rows], fresh)
     aggregate = total.astype(BF)
+    for copy in copies:
+        copy.wait()
     nodes = nodes_ref[...]
     preact = (
         mm(nodes, ninner_ref[:width, :]) + mm(aggregate, ninner_ref[width:, :]) + nshift_ref[...]
@@ -163,7 +198,7 @@
     hidden_width = preact.shape[1]
     weights_ref[:width, :] = mm_tn(nodes, preact_half) * scale
     weights_ref[width : 2 * width, :] = mm_tn(aggregate, preact_half) * scale
-    weights_ref[2 * width : 2 * width + hidden_width, :] = mm_tn(hidden, linear_half) * scale
+    weights_ref[2 * width :, :] = mm_tn(hidden, linear_half) * scale
     sums_ref[0:1, :] = column_sum(preact_back) * scale
     sums_ref[1:2, :] = column_sum(linear_back) * scale
     sums_ref[2:3, :] = column_sum(cotan * normed) * scale
@@ -171,11 +206,11 @@
 
 def backward_kernel(
     pick_ref, turned_ref, edges_ref, ecotan_ref, nodes_ref, low_ref, high_ref, hidden_ref, slope_ref,
-    normed_ref, invstd_ref, pulled_ref, eouter_ref, egain_ref,
-    fresh_ref, preact_ref, spread_ref, weights_ref, sums_ref,
-    linear_ref,
-    *, scale,
+    normed_ref, invstd_ref, pulled_ref, eouter_ref, egain_ref, node_sums_ref, node_weights_ref,
+    fresh_ref, preact_ref, spread_ref, weights_ref, sums_ref, *rest, scale, split,
 ):
+    linear_ref = rest[-1]
+    weights_ref[weights_ref.shape[0] - node_weights_ref.shape[0] :, :] = node_weights_ref[...]
     edge_count, width = edges_ref.shape
     count = nodes_ref.shape[0]
     tile = edge_count // 4
@@ -197,6 +232,7 @@
         sums[2] += column_sum(fresh_back * normed)
     for k in range(3):
         sums_ref[k : k + 1, :] = sums[k] * scale
+    sums_ref[3:, :] = node_sums_ref[...]
     used = spread_ref.shape[0]
     spread = mm(turned_ref[:used, :], preact_ref[...]).astype(BF)
     spread_ref[...] = spread
@@ -207,15 +243,23 @@
         mm_tn(nodes, spread[:count]) + mm_tn(rim, spread[2 * count :])
     ) * scale
     weights_ref[2 * width : 3 * width, :] = mm_tn(nodes, spread[count : 2 * count]) * scale
-    weights_ref[3 * width :, :] = mm_tn(hidden_ref[...], linear_ref[...]) * scale
-
-
-def rim_kernel(spread_ref, inner_ref, out_ref, *, count):
-    width = spread_ref.shape[1]
-    out_ref[...] = mm_nt(spread_ref[2 * count :, :], inner_ref[width : 2 * width, :]).astype(BF)
-
-
-def grads_kernel(spread_ref, inner_ref, partial_ref, fresh_ref, preact_ref, nodes_ref, edges_ref):
+    weights_ref[3 * width : 3 * width + hidden_ref.shape[1], :] = (
+        mm_tn(hidden_ref[...], linear_ref[...]) * scale
+    )
+    if split is not None:
+        split.first_send(weights_ref, rest[0])
+
+
+def rim_kernel(spread_ref, inner_ref, _, low_ref, high_ref, *, count):
+    width, slots = spread_ref.shape[1], low_ref.shape[0]
+    for k, out_ref in enumerate((low_ref, high_ref)):
+        start = 2 * count + k * slots
+        out_ref[...] = mm_nt(
+            spread_ref[start : start + slots, :], inner_ref[width : 2 * width, :]
+        ).astype(BF)
+
+
+def grads_kernel(spread_ref, inner_ref, partial_ref, fresh_ref, preact_ref, _, nodes_ref, edges_ref):
     count, width = partial_ref.shape
     nodes_ref[...] = (
         partial_ref[...]
@@ -234,9 +278,11 @@
 def rims_kernel(lists_ref, partial_ref, low_ref, high_ref, out_ref):
     count, slots = partial_ref.shape[0], lists_ref.shape[1]
     rows = lax.broadcasted_iota(jnp.int32, (count, slots), 0)
-    pick = jnp.where(rows == lists_ref[...], 1.0, 0.0).astype(BF)
-    back = jnp.concatenate([low_ref[...], high_ref[...]], axis=0)
-    out_ref[...] = partial_ref[...] + mm(pick, back)
+    total = partial_ref[...]
+    for k, back_ref in enumerate((low_ref, high_ref)):
+        pick = jnp.where(rows == lists_ref[k : k + 1, :], 1.0, 0.0).astype(BF)
+        total += mm(pick, back_ref[...])
+    out_ref[...] = total
 
 
 def ring(values, step):
@@ -286,6 +332,120 @@
     return total.reshape(-1), vectors.reshape(-1)
 
 
+class Halving:
+    def __init__(self, rows):
+        self.core_bit, self.first, self.second = halving_orders()
+        self.count = lax.axis_size("region") * lax.axis_size("patch")
+        self.block = rows // self.count
+        self.rows = rows // 2
+        self.steps = len(self.first)
+        self.aligned = rows % (16 * self.count) == 0
+
+    def place(self, order, core, position):
+        block = self.core_bit if core else 0
+        for k, bit in enumerate(order):
+            if (position >> (self.steps - 1 - k)) & 1:
+                block |= bit
+        return block * self.block
+
+    def me(self):
+        return lax.axis_index("region") * self.core_bit + lax.axis_index("patch")
+
+    def core(self):
+        return lax.rem(self.me() // self.core_bit, 2)
+
+    def bit(self, step):
+        me = self.me()
+        one, two = self.first[step], self.second[step]
+        return jnp.where(self.core() == 1, lax.rem(me // two, 2), lax.rem(me // one, 2))
+
+    def source(self, position, core):
+        zero, one = self.place(self.first, 0, position), self.place(self.second, 1, position)
+        return pl.multiple_of(jnp.where(core == 1, one, zero), 8)
+
+    def first_send(self, weights_ref, send_ref):
+        other = 1 - self.core()
+        for position in range(self.count // 2):
+            start = position * self.block
+            send_ref[start : start + self.block, :] = weights_ref[
+                pl.ds(self.source(position, other), self.block), :
+            ].astype(BF)
+
+
+def halve_kernel(src_ref, got_ref, out_ref, *, plan, step, side):
+    half = plan.rows >> (step + 1)
+    bit = plan.bit(step)
+    chosen = 1 - bit if side else bit
+    if step:
+        start = pl.multiple_of(chosen * half, 16)
+        held = src_ref[pl.ds(start, half), :]
+        out_ref[:half, :] = (held + got_ref[pl.ds(start, half), :]).astype(out_ref.dtype)
+        return
+    core = plan.core()
+    per_half = half // plan.block
+    for k in range(per_half):
+        low, high = plan.source(k, core), plan.source(k + per_half, core)
+        held = src_ref[pl.ds(pl.multiple_of(jnp.where(chosen == 1, high, low), 8), plan.block), :]
+        start = pl.multiple_of(chosen * half + k * plan.block, 16)
+        got = got_ref[pl.ds(start, plan.block), :]
+        out_ref[k * plan.block : (k + 1) * plan.block, :] = (held + got).astype(out_ref.dtype)
+
+
+def vector_parts(ref, start, count):
+    return ref[start : start + count, :].astype(F32) + ref[start + 8 : start + 8 + count, :].astype(F32)
+
+
+def send_kernel(src_ref, got_ref, vec_ref, out_ref, new_ref, *, plan, step):
+    halve_kernel(src_ref, got_ref, out_ref, plan=plan, step=step, side=1)
+    half = plan.rows >> (step + 1)
+    count = vec_ref.shape[0]
+    vec = vec_ref[...]
+    if step:
+        vec = vec + vector_parts(got_ref, 2 * half, count)
+    upper = vec.astype(BF)
+    lower = (vec - upper.astype(F32)).astype(BF)
+    out_ref[half:, :] = jnp.zeros_like(out_ref[half:, :])
+    out_ref[half : half + count, :] = upper
+    out_ref[half + 8 : half + 8 + count, :] = lower
+    new_ref[...] = upper.astype(F32) + lower.astype(F32)
+
+
+def last_kernel(src_ref, got_ref, vec_ref, out_ref, new_ref):
+    rows, width = src_ref.shape
+    total = src_ref[...] + got_ref[:rows, :]
+    parts = width // LANES
+    for k in range(parts):
+        out_ref[pl.ds(k, rows, stride=parts), :] = total[:, k * LANES : (k + 1) * LANES]
+    new_ref[...] = vec_ref[...] + vector_parts(got_ref, rows, vec_ref.shape[0])
+
+
+def reduce_kernels(plan, held, sent, vec):
+    width = held.shape[1]
+    vec_shape = (vec.shape, F32)
+    got = permute_by(sent, plan.core_bit, plan.core_bit, plan.core_bit)
+    marks = []
+    for step in range(plan.steps):
+        half = plan.rows >> (step + 1)
+        send, vec = call(
+            functools.partial(send_kernel, plan=plan, step=step),
+            [((half + 16, width), BF), vec_shape], near(held), near(got), near(vec), name=f"send{step}",
+        )
+        marks.append(send)
+        held_late, got_late, send = lax.optimization_barrier((held, got, send))
+        incoming = permute_by(send, plan.first[step], plan.second[step], plan.core_bit)
+        (held,) = call(
+            functools.partial(halve_kernel, plan=plan, step=step, side=0),
+            [((half, width), F32)], near(held_late), near(got_late), name=f"keep{step}",
+        )
+        got = incoming
+    out, vec = call(
+        last_kernel, [((plan.block * width // LANES, LANES), F32), vec_shape], near(held), near(got),
+        near(vec), name="last", plain=(0,),
+    )
+    vec = vec + permute_by(vec, plan.core_bit, plan.core_bit, plan.core_bit)
+    return out.reshape(-1), vec.reshape(-1), marks
+
+
 def per_device(
     nodes, edges, node_cotan, edge_cotan, edge_inner, edge_outer, node_inner, node_outer, edge_shift,
     edge_offset, edge_gain, node_shift, node_offset, node_gain, send_rows, senders, receivers,
@@ -293,36 +453,49 @@
     count, width = nodes.shape
     edge_count = edges.shape[0]
     hidden_width = edge_outer.shape[0]
-    lists = send_rows.reshape(1, -1)
-    slots = lists.shape[1]
-    half = slots // 2
+    lists = send_rows.reshape(send_rows.shape[2:])
+    half = lists.shape[1]
+    slots = 2 * half
     devices_all = lax.axis_size("region") * lax.axis_size("patch")
     edge_norm = 1.0 / math.sqrt(edge_count * devices_all)
     node_norm = 1.0 / math.sqrt(count * devices_all)
     picked = 2 * count + -(-slots // LANES) * LANES
+    edge_rows = 3 * width + hidden_width
+    weight_rows = edge_rows + 2 * width + hidden_width
+    plan = Halving(weight_rows)
     edge_shift, edge_offset, edge_gain, node_shift, node_offset, node_gain = (
         v.reshape(1, -1)
         for v in (edge_shift, edge_offset, edge_gain, node_shift, node_offset, node_gain)
     )
 
-    (outgoing,) = call(
-        pick_kernel, [((slots, width), BF)], lists, nodes, name="pick", limit=4 << 20
-    )
-    low = ring(outgoing[half:], 1)
-    high = ring(outgoing[:half], -1)
-
-    part, own, pick, turned = call(
-        table_kernel,
+    out_low, out_high = call(
+        pick_kernel, [((half, width), BF)] * 2, lists, nodes, name="pick", limit=4 << 20, hbm=(0, 1),
+        scratch=[
+            pltpu.VMEM(lists.shape, jnp.int32), pltpu.VMEM(nodes.shape, BF),
+            pltpu.SemaphoreType.DMA((2,)),
+        ],
+    )
+    low = ring(out_high, 1)
+    high = ring(out_low, -1)
+
+    given = [
+        senders.reshape(1, -1), receivers.reshape(1, -1), edge_shift, nodes, edge_inner, edges,
+        edge_outer, edge_offset, edge_gain, node_shift, node_offset, node_gain,
+    ]
+    part, own, pick, turned, *loaded = call(
+        functools.partial(table_kernel, given=len(given)),
         [
             ((edge_count, hidden_width), F32),
             ((2 * count, hidden_width), BF),
             ((edge_count, picked), BF),
             ((picked, edge_count), BF),
-        ],
-        senders.reshape(1, -1), receivers.reshape(1, -1), edges, nodes, edge_inner, edge_shift,
-        name="table", flops=2 * (edge_count + 2 * count) * width * hidden_width,
-    )
-    hidden, slope, normed, invstd, pulled, partial, node_weights, node_sums = call(
+        ] + [(a.shape, a.dtype) for a in given],
+        *given, name="table", flops=2 * (edge_count + 2 * count) * width * hidden_width,
+        hbm=range(len(given)), scratch=[pltpu.SemaphoreType.DMA((len(given),))],
+    )
+    nodes_near, inner_near, edges_near, outer_near, *vectors = loaded[3:]
+    gain_near = vectors[1]
+    hidden, slope, normed, invstd, pulled, partial, node_weights, node_sums, ecotan_near = call(
         functools.partial(forward_kernel, scale=node_norm),
         [
             ((edge_count, hidden_width), BF),
@@ -331,45 +504,58 @@
             ((edge_count, 1), F32),
             ((count, width), BF),
             ((count, width), F32),
-            ((2 * width + hidden_width, hidden_width), F32),
+            ((weight_rows - edge_rows, hidden_width), F32),
             ((3, width), F32),
+            ((edge_count, width), BF),
         ],
-        part, own, pick, turned, low, high, edges, nodes, node_cotan, edge_inner, edge_outer,
-        node_inner, node_outer, edge_offset, edge_gain, node_shift, node_offset, node_gain,
-        name="forward", flops=5 << 30,
-    )
-    fresh, preact, spread, edge_weights, edge_sums, _ = call(
-        functools.partial(backward_kernel, scale=edge_norm),
+        near(part), near(own), near(pick), near(turned), near(low), near(high), near(edges_near),
+        near(nodes_near), near(inner_near), near(outer_near),
+        *[near(v) for v in vectors],
+        node_inner, node_outer, node_cotan, edge_cotan,
+        name="forward", flops=5 << 30, hbm=(15, 16, 17, 18),
+        scratch=[
+            pltpu.VMEM(node_inner.shape, BF), pltpu.VMEM(node_outer.shape, BF),
+            pltpu.VMEM(node_cotan.shape, BF), pltpu.SemaphoreType.DMA((4,)),
+        ],
+    )
+    sends = [((plan.rows, hidden_width), BF)] if plan.aligned else []
+    fresh, preact, spread, weights, sums, *sent = call(
+        functools.partial(backward_kernel, scale=edge_norm, split=plan if plan.aligned else None),
         [
             ((edge_count, width), F32),
             ((edge_count, hidden_width), BF),
             ((2 * count + slots, hidden_width), BF),
-            ((3 * width + hidden_width, hidden_width), F32),
-            ((3, width), F32),
-            ((edge_count, width), BF),
+            ((weight_rows, hidden_width), F32),
+            ((6, width), F32),
+            *sends,
         ],
-        pick, turned, edges, edge_cotan, nodes, low, high, hidden, slope, normed, invstd, pulled,
-        edge_outer, edge_gain,
+        near(pick), near(turned), near(edges_near), near(ecotan_near), near(nodes_near), near(low),
+        near(high), near(hidden), near(slope), near(normed), near(invstd), near(pulled),
+        near(outer_near), near(gain_near), near(node_sums), near(node_weights),
         name="backward", flops=5 << 30,
-    )
-    (rim_back,) = call(
-        functools.partial(rim_kernel, count=count), [((slots, width), BF)], spread, edge_inner,
-        name="rim", limit=4 << 20,
-    )
-    back_low = ring(rim_back[half:], 1)
-    back_high = ring(rim_back[:half], -1)
-    grad_weights, grad_vectors = reduce_all(
-        jnp.concatenate([edge_weights, node_weights]), jnp.concatenate([edge_sums, node_sums])
-    )
+        scratch=[pltpu.VMEM((edge_count, width), BF)],
+    )
+    if plan.aligned:
+        grad_weights, grad_vectors, marks = reduce_kernels(plan, weights, sent[0], sums)
+        mark = marks[0]
+    else:
+        grad_weights, grad_vectors = reduce_all(weights, sums)
+        mark = sums
+    rim_low, rim_high = call(
+        functools.partial(rim_kernel, count=count), [((half, width), BF)] * 2, near(spread),
+        near(inner_near), near(mark), name="rim", limit=4 << 20,
+    )
+    back_low = ring(rim_high, 1)
+    back_high = ring(rim_low, -1)
     nodes_part, grad_edges = call(
         grads_kernel,
         [((count, width), F32), ((edge_count, width), BF)],
-        spread, edge_inner, partial, fresh, preact,
-        name="grads", flops=2 << 30, outs_plain=(1,),
+        near(spread), near(inner_near), near(partial), near(fresh), near(preact), near(mark),
+        name="grads", flops=2 << 30, plain=(1,),
     )
     (grad_nodes,) = call(
-        rims_kernel, [((count, width), F32)], lists, nodes_part, back_low, back_high, name="rims",
-        outs_plain=(0,), limit=4 << 20,
+        rims_kernel, [((count, width), F32)], lists, near(nodes_part), near(back_low),
+        near(back_high), name="rims", plain=(0,), limit=4 << 20,
     )
     return (grad_nodes, grad_edges, grad_weights, grad_vectors)
 

time: 120 us -> 68.2 us (0.57); the launches traced: 118 us -> 68 us
  local copies, waits for them, and re-layouts: 38.8 us -> 0.61 us
  other arithmetic: 17.9 us -> 0.01 us
  starting transfers between devices: 20.5 us -> 13.7 us
  Pallas kernels: 15.2 us -> 21.7 us
  waiting for transfers between devices: 25.3 us -> 31.2 us
    unnamed x67 -> x2, local copies, waits for them, and re-layouts: 24.5 us -> 0.01 us
    add x9 -> x1, other arithmetic: 11.8 us -> 0.01 us  [reduce_kernels(): vec = vec + permute_by(vec, plan.core_bit, plan.core_bit, plan.core_bit)]
    convert_element_type x5 -> x0, local copies, waits for them, and re-layouts: 9.34 us -> none  [the longest x4 5.74 us: reduce_all(): lax.dynamic_index_in_dim(halves, 1 - bit, 0, keepdims=False).astype(BF)]
    ppermute x10 -> x6, starting transfers between devices: 9.74 us -> 2.83 us  [permute_by(): return lax.ppermute(values, AXES, pairs)]
    pallas_call x7 -> x16, Pallas kernels: 15.2 us -> 21.7 us  [call(): pl.pallas_call(body, out_shape=shapes, in_specs=[anywhere if i in hbm els...]
    ppermute x10 -> x6, waiting for transfers between devices: 25.3 us -> 31.2 us  [permute_by(): return lax.ppermute(values, AXES, pairs)]
    another operation x1 -> x0, other arithmetic: 4.26 us -> none  [reduce_all(): jnp.stack([ordered(first)[0], ordered(second)[1]])]
    reshape x4 -> x1, local copies, waits for them, and re-layouts: 3.06 us -> 0.6 us  [reduce_kernels(): return (out.reshape(-1), vec.reshape(-1), marks)]
  transfers between devices with their start and end apart: 14 -> 10, of which waited for: 5 -> 5; matrix products, arithmetic and copies ran while one was open for 5% -> 0% of each run, Pallas kernels for 4% -> 12%
where the time goes in v3:
time: 68.2 us; the launch traced here: 68 us
  waiting for transfers between devices  31.2 us (46%)
  Pallas kernels  21.7 us (32%)
  starting transfers between devices  13.7 us (20%)
  between operations  0.76 us (1%)
    ppermute x6, waiting for transfers between devices, permute_by(): return lax.ppermute(values, AXES, pairs)  31.2 us
    pallas_call x16, Pallas kernels, call(): pl.pallas_call(body, out_shape=shapes, in_specs=[anywhere if i in hbm els...  21.7 us
    ppermute x4, starting transfers between devices, ring(): lax.ppermute(values, 'patch', [(i, (i + step) % count) for i in range(cou...  10.9 us
    ppermute x6, starting transfers between devices, permute_by(): return lax.ppermute(values, AXES, pairs)  2.83 us
  transfers between devices with their start and end apart: 10, of which 5 were waited for; matrix products, arithmetic and copies ran while one was open for 0% of the time, Pallas kernels for 12%

profile of v3, /device:TPU:0, one launch (start us, length us, event | category | flops | bytes accessed | tf_op | source)
XLA Modules:
  0.0 68.0 jit_solution(7211712505266264197)
XLA Ops:
  0.6 1.2 %pick.1 = (bf16[32,512]{1,0:T(8,128)(2,1)S(1)}, bf16[32,512]{1,0:T(8,128)(2,1)S(1)}) custom-call(s32[2,32]{1,0:T(2,128)} %bitcast.10, bf16[256,512]{1,0:T(8,128)(2,1)} %nodes_hbm.1), custom_call_target="tpu_custom_call" | custom-call | bytes 65536 | tf_op jit(solution)/shard_map/pick/pallas_call | solution.py:41
  1.8 3.0 %collective-permute-start = (bf16[32,512]{1,0:T(8,128)(2,1)S(1)}, bf16[32,512]{1,0:T(8,128)(2,1)S(1)}, u32[]{:S(2)}, u32[]{:S(2)}) collective-permute-start(bf16[32,512]{1,0:T(8,128)(2,1)S(1)} %get-tuple-element.65), channel_id=1, source_target_pairs={{0,1},{1,2},{2,3},{3,4},{4,5},{5,6},{6,7},{7,0},{8,9},{9,10},{10,1... | collective-permute-start | bytes 98312 | tf_op jit(solution)/shard_map/ppermute | solution.py:290
  4.9 3.1 %collective-permute-start.1 = (bf16[32,512]{1,0:T(8,128)(2,1)S(1)}, bf16[32,512]{1,0:T(8,128)(2,1)S(1)}, u32[]{:S(2)}, u32[]{:S(2)}) collective-permute-start(bf16[32,512]{1,0:T(8,128)(2,1)S(1)} %get-tuple-element.66), channel_id=1, source_target_pairs={{0,7},{1,0},{2,1},{3,2},{4,3},{5,4},{6,5},{7,6},{8,15},{9,8},{10,9... | collective-permute-start | bytes 98312 | tf_op jit(solution)/shard_map/ppermute | solution.py:290
  8.0 3.4 %table.1 = (f32[1024,512]{1,0:T(8,128)S(1)}, bf16[512,512]{1,0:T(8,128)(2,1)S(1)}, bf16[1024,640]{1,0:T(8,128)(2,1)S(1)}, bf16[640,1024]{1,0:T(8,128)(2,1)S(1)},...) custom-call(s32[1,1024]{1,0:T(1,128)} %bitcast.12, ...), custom_call_target="tpu_custom_call" | custom-call | flops 805306368 | bytes 8671232 | tf_op jit(solution)/shard_map/table/pallas_call | solution.py:41
  11.4 0.0 collective-permute-done.low_ref
  11.4 0.0 collective-permute-done.1.high_ref
  11.4 7.0 %forward.1 = (bf16[1024,512]{1,0:T(8,128)(2,1)S(1)}, f32[1024,512]{1,0:T(8,128)S(1)}, f32[1024,512]{1,0:T(8,128)S(1)}, f32[1024,1]{1,0:T(8,128)S(1)}, bf16[256,5...) custom-call(f32[1024,512]{1,0:T(8,128)S(1)} %get-tuple-element.63.pa, ...), custom_call_target="tpu_custom_call" | custom-call | flops 5368709120 | bytes 10233856 | tf_op jit(solution)/shard_map/forward/pallas_call | solution.py:41
  18.4 5.2 %backward.1 = (f32[1024,512]{1,0:T(8,128)S(1)}, bf16[1024,512]{1,0:T(8,128)(2,1)S(1)}, bf16[576,512]{1,0:T(8,128)(2,1)S(1)}, f32[3584,512]{1,0:T(8,128)S(1)}, f3...) custom-call(bf16[1024,640]{1,0:T(8,128)(2,1)S(1)} %get-tuple-element.60.pick_ref, ...), custom_call_target="tpu_custom_call" | custom-call | flops 5368709120 | bytes 12922880 | tf_op jit(solution)/shard_map/backward/pallas_call | solution.py:41
  23.7 0.1 collective-permute-start.2
  23.7 3.8 %collective-permute-done.2.got_ref = bf16[1792,512]{1,0:T(8,128)(2,1)S(1)} collective-permute-done((bf16[1792,512]{1,0:T(8,128)(2,1)S(1)}, bf16[1792,512]{1,0:T(8,128)(2,1)S(1)}, u32[]{:S(2)}, u32[]{:S(2)}) %collective-permute-start.2) | collective-permute-done | bytes 1835040 | tf_op jit(solution)/shard_map/ppermute | solution.py:303
  27.5 0.2 send0.1
  27.7 1.7 %collective-permute-start.5 = (bf16[912,512]{1,0:T(8,128)(2,1)S(1)}, bf16[912,512]{1,0:T(8,128)(2,1)S(1)}, u32[]{:S(2)}, u32[]{:S(2)}) collective-permute-start(bf16[912,512]{1,0:T(8,128)(2,1)S(1)} %get-tuple-element.97._), channel_id=1, source_target_pairs={{0,16},{1,17},{2,18},{3,19},{4,20},{5,21},{6,22},{7,23},{8,9},{9,8... | collective-permute-start | bytes 2801672 | tf_op jit(solution)/shard_map/ppermute | solution.py:303
  29.4 0.2 keep0.1.src_ref
  29.5 11.8 %collective-permute-done.5.got_ref = bf16[912,512]{1,0:T(8,128)(2,1)S(1)} collective-permute-done((bf16[912,512]{1,0:T(8,128)(2,1)S(1)}, bf16[912,512]{1,0:T(8,128)(2,1)S(1)}, u32[]{:S(2)}, u32[]{:S(2)}) %collective-permute-start.5) | collective-permute-done | bytes 933920 | tf_op jit(solution)/shard_map/ppermute | solution.py:303
  41.3 0.1 send1.1
  41.4 0.1 collective-permute-start.6
  41.5 0.1 keep1.1.src_ref
  41.6 8.5 %collective-permute-done.6.got_ref = bf16[464,512]{1,0:T(8,128)(2,1)S(1)} collective-permute-done((bf16[464,512]{1,0:T(8,128)(2,1)S(1)}, bf16[464,512]{1,0:T(8,128)(2,1)S(1)}, u32[]{:S(2)}, u32[]{:S(2)}) %collective-permute-start.6) | collective-permute-done | bytes 475168 | tf_op jit(solution)/shard_map/ppermute | solution.py:303
  50.1 0.1 send2.1
  50.2 0.1 collective-permute-start.7
  50.3 0.1 keep2.1.src_ref
  50.4 6.1 %collective-permute-done.7.got_ref = bf16[240,512]{1,0:T(8,128)(2,1)S(1)} collective-permute-done((bf16[240,512]{1,0:T(8,128)(2,1)S(1)}, bf16[240,512]{1,0:T(8,128)(2,1)S(1)}, u32[]{:S(2)}, u32[]{:S(2)}) %collective-permute-start.7) | collective-permute-done | bytes 245792 | tf_op jit(solution)/shard_map/ppermute | solution.py:303
  56.5 1.0 %collective-permute-start.8 = (bf16[128,512]{1,0:T(8,128)(2,1)S(1)}, bf16[128,512]{1,0:T(8,128)(2,1)S(1)}, u32[]{:S(2)}, u32[]{:S(2)}) collective-permute-start(bf16[128,512]{1,0:T(8,128)(2,1)S(1)} %get-tuple-element.112), channel_id=1, source_target_pairs={{0,4},{1,5},{2,6},{3,7},{4,0},{5,1},{6,2},{7,3},{8,12},{9,13},{10,... | collective-permute-start | bytes 393224 | tf_op jit(solution)/shard_map/ppermute | solution.py:303
  57.5 0.4 rim.1
  57.9 1.5 %collective-permute-start.3 = (bf16[32,512]{1,0:T(8,128)(2,1)S(1)}, bf16[32,512]{1,0:T(8,128)(2,1)S(1)}, u32[]{:S(2)}, u32[]{:S(2)}) collective-permute-start(bf16[32,512]{1,0:T(8,128)(2,1)S(1)} %get-tuple-element.92), channel_id=1, source_target_pairs={{0,1},{1,2},{2,3},{3,4},{4,5},{5,6},{6,7},{7,0},{8,9},{9,10},{10,1... | collective-permute-start | bytes 98312 | tf_op jit(solution)/shard_map/ppermute | solution.py:290
  59.4 3.2 %collective-permute-start.4 = (bf16[32,512]{1,0:T(8,128)(2,1)S(1)}, bf16[32,512]{1,0:T(8,128)(2,1)S(1)}, u32[]{:S(2)}, u32[]{:S(2)}) collective-permute-start(bf16[32,512]{1,0:T(8,128)(2,1)S(1)} %get-tuple-element.93), channel_id=1, source_target_pairs={{0,7},{1,0},{2,1},{3,2},{4,3},{5,4},{6,5},{7,6},{8,15},{9,8},{10,9... | collective-permute-start | bytes 98312 | tf_op jit(solution)/shard_map/ppermute | solution.py:290
  62.7 1.0 %collective-permute-done.8.got_ref = bf16[128,512]{1,0:T(8,128)(2,1)S(1)} collective-permute-done((bf16[128,512]{1,0:T(8,128)(2,1)S(1)}, bf16[128,512]{1,0:T(8,128)(2,1)S(1)}, u32[]{:S(2)}, u32[]{:S(2)}) %collective-permute-start.8) | collective-permute-done | bytes 131104 | tf_op jit(solution)/shard_map/ppermute | solution.py:303
  63.6 0.7 %last.1 = (f32[448,128]{1,0:T(8,128)}, f32[6,512]{1,0:T(8,128)S(1)}) custom-call(f32[112,512]{1,0:T(8,128)S(1)} %keep3.1.src_ref, bf16[128,512]{1,0:T(8,128)(2,1)S(1)} %collective-permute-done.8.got_ref, f32[6,512]{1,0:T(8,128)S(1)} %get-tuple-element.113.vec_ref), custom_call_target="tpu_custom_call" | custom-call | bytes 241664 | tf_op jit(solution)/shard_map/last/pallas_call | solution.py:41
  64.3 2.0 %grads.1 = (f32[256,512]{1,0:T(8,128)S(1)}, bf16[1024,512]{1,0:T(8,128)(2,1)}) custom-call(bf16[576,512]{1,0:T(8,128)(2,1)S(1)} %get-tuple-element.83.spread_ref, bf16[1536,512]{1,0:T(8,128)(2,1)S(1)} %get-tuple-element.68.einner_ref.inner_ref, f32[256,512]{1,0:T(8,128)S(1)} %get-tuple-element.84.partial_ref, f32[1024,512]{1,0:T(8,128)S(1)} %get-tuple-element.85.fresh_ref, ...), custom_call_target="tpu_custom_call" | custom-call | flops 2147483648 | bytes 1572864 | tf_op jit(solution)/shard_map/grads/pallas_call | solution.py:41
  66.3 0.0 collective-permute-done.3.low_ref
  66.3 1.1 %rims.1 = f32[256,512]{1,0:T(8,128)} custom-call(s32[2,32]{1,0:T(2,128)S(1)} %bitcast.11, f32[256,512]{1,0:T(8,128)S(1)} %get-tuple-element.91.partial_ref, bf16[32,512]{1,0:T(8,128)(2,1)S(1)} %collective-permute-done.3.low_ref, bf16[32,512]{1,0:T(8,128)(2,1)S(1)} %collective-permute-done.4.high_ref), custom_call_target="tpu_custom_call" | custom-call | bytes 524288 | tf_op jit(solution)/shard_map/rims/pallas_call | solution.py:41
  67.4 0.6 reshape.51
  (8 shorter events, 0.1 us)
Async XLA Ops:
  1.8 9.5 %collective-permute-start = (bf16[32,512]{1,0:T(8,128)(2,1)S(1)}, bf16[32,512]{1,0:T(8,128)(2,1)S(1)}, u32[]{:S(2)}, u32[]{:S(2)}) collective-permute-start(bf16[32,512]{1,0:T(8,128)(2,1)S(1)} %get-tuple-element.65), channel_id=1, source_target_pairs={{0,1},{1,2},{2,3},{3,4},{4,5},{5,6},{6,7},{7,0},{8,9},{9,10},{10,1... | collective-permute-start | bytes 98312 | tf_op jit(solution)/shard_map/ppermute | solution.py:290
  4.9 6.5 %collective-permute-start.1 = (bf16[32,512]{1,0:T(8,128)(2,1)S(1)}, bf16[32,512]{1,0:T(8,128)(2,1)S(1)}, u32[]{:S(2)}, u32[]{:S(2)}) collective-permute-start(bf16[32,512]{1,0:T(8,128)(2,1)S(1)} %get-tuple-element.66), channel_id=1, source_target_pairs={{0,7},{1,0},{2,1},{3,2},{4,3},{5,4},{6,5},{7,6},{8,15},{9,8},{10,9... | collective-permute-start | bytes 98312 | tf_op jit(solution)/shard_map/ppermute | solution.py:290
  23.7 3.9 %collective-permute-start.2 = (bf16[1792,512]{1,0:T(8,128)(2,1)S(1)}, bf16[1792,512]{1,0:T(8,128)(2,1)S(1)}, u32[]{:S(2)}, u32[]{:S(2)}) collective-permute-start(bf16[1792,512]{1,0:T(8,128)(2,1)S(1)} %get-tuple-element.88), channel_id=1, source_target_pairs={{0,8},{1,9},{2,10},{3,11},{4,12},{5,13},{6,14},{7,15},{8,0},{9,1},... | collective-permute-start | bytes 5505032 | tf_op jit(solution)/shard_map/ppermute | solution.py:303
  27.7 13.6 %collective-permute-start.5 = (bf16[912,512]{1,0:T(8,128)(2,1)S(1)}, bf16[912,512]{1,0:T(8,128)(2,1)S(1)}, u32[]{:S(2)}, u32[]{:S(2)}) collective-permute-start(bf16[912,512]{1,0:T(8,128)(2,1)S(1)} %get-tuple-element.97._), channel_id=1, source_target_pairs={{0,16},{1,17},{2,18},{3,19},{4,20},{5,21},{6,22},{7,23},{8,9},{9,8... | collective-permute-start | bytes 2801672 | tf_op jit(solution)/shard_map/ppermute | solution.py:303
  41.4 8.7 %collective-permute-start.6 = (bf16[464,512]{1,0:T(8,128)(2,1)S(1)}, bf16[464,512]{1,0:T(8,128)(2,1)S(1)}, u32[]{:S(2)}, u32[]{:S(2)}) collective-permute-start(bf16[464,512]{1,0:T(8,128)(2,1)S(1)} %get-tuple-element.102), channel_id=1, source_target_pairs={{0,1},{1,0},{2,3},{3,2},{4,5},{5,4},{6,7},{7,6},{8,10},{9,11},{10,... | collective-permute-start | bytes 1425416 | tf_op jit(solution)/shard_map/ppermute | solution.py:303
  50.2 6.3 %collective-permute-start.7 = (bf16[240,512]{1,0:T(8,128)(2,1)S(1)}, bf16[240,512]{1,0:T(8,128)(2,1)S(1)}, u32[]{:S(2)}, u32[]{:S(2)}) collective-permute-start(bf16[240,512]{1,0:T(8,128)(2,1)S(1)} %get-tuple-element.107), channel_id=1, source_target_pairs={{0,2},{1,3},{2,0},{3,1},{4,6},{5,7},{6,4},{7,5},{8,24},{9,25},{10,... | collective-permute-start | bytes 737288 | tf_op jit(solution)/shard_map/ppermute | solution.py:303
  56.5 7.1 %collective-permute-start.8 = (bf16[128,512]{1,0:T(8,128)(2,1)S(1)}, bf16[128,512]{1,0:T(8,128)(2,1)S(1)}, u32[]{:S(2)}, u32[]{:S(2)}) collective-permute-start(bf16[128,512]{1,0:T(8,128)(2,1)S(1)} %get-tuple-element.112), channel_id=1, source_target_pairs={{0,4},{1,5},{2,6},{3,7},{4,0},{5,1},{6,2},{7,3},{8,12},{9,13},{10,... | collective-permute-start | bytes 393224 | tf_op jit(solution)/shard_map/ppermute | solution.py:303
  57.9 8.4 %collective-permute-start.3 = (bf16[32,512]{1,0:T(8,128)(2,1)S(1)}, bf16[32,512]{1,0:T(8,128)(2,1)S(1)}, u32[]{:S(2)}, u32[]{:S(2)}) collective-permute-start(bf16[32,512]{1,0:T(8,128)(2,1)S(1)} %get-tuple-element.92), channel_id=1, source_target_pairs={{0,1},{1,2},{2,3},{3,4},{4,5},{5,6},{6,7},{7,0},{8,9},{9,10},{10,1... | collective-permute-start | bytes 98312 | tf_op jit(solution)/shard_map/ppermute | solution.py:290
  59.4 6.9 %collective-permute-start.4 = (bf16[32,512]{1,0:T(8,128)(2,1)S(1)}, bf16[32,512]{1,0:T(8,128)(2,1)S(1)}, u32[]{:S(2)}, u32[]{:S(2)}) collective-permute-start(bf16[32,512]{1,0:T(8,128)(2,1)S(1)} %get-tuple-element.93), channel_id=1, source_target_pairs={{0,7},{1,0},{2,1},{3,2},{4,3},{5,4},{6,5},{7,6},{8,15},{9,8},{10,9... | collective-permute-start | bytes 98312 | tf_op jit(solution)/shard_map/ppermute | solution.py:290
  64.3 3.1 %collective-permute-start.9 = (f32[6,512]{1,0:T(8,128)S(1)}, f32[6,512]{1,0:T(8,128)S(1)}, u32[]{:S(2)}, u32[]{:S(2)}) collective-permute-start(f32[6,512]{1,0:T(8,128)S(1)} %get-tuple-element.115), channel_id=1, source_target_pairs={{0,8},{1,9},{2,10},{3,11},{4,12},{5,13},{6,14},{7,15},{8,0},{9,1},... | collective-permute-start | bytes 36872 | tf_op jit(solution)/shard_map/ppermute | solution.py:303
  64.3 2.0 %copy-start = (s32[1,1,2,32]{3,2,1,0:T(2,128)S(1)}, s32[1,1,2,32]{3,2,1,0:T(2,128)}, u32[]{:S(2)}) copy-start(s32[1,1,2,32]{3,2,1,0:T(2,128)} %param.31) | copy-start | bytes 772

commit v4 on v3

--- a/solution.py
+++ b/solution.py
@@ -101,14 +101,9 @@
 
 
 def table_kernel(
-    *refs, given,
+    senders_ref, receivers_ref, shift_ref, nodes_ref, inner_ref, edges_ref,
+    part_ref, own_ref, pick_ref, turned_ref,
 ):
-    part_ref, own_ref, pick_ref, turned_ref = refs[given : given + 4]
-    loaded, sems = refs[given + 4 : -1], refs[-1]
-    copies = start_copies(list(zip(refs[:given], loaded)), sems)
-    senders_ref, receivers_ref, shift_ref, nodes_ref, inner_ref, edges_ref = loaded[:6]
-    copies[0].wait()
-    copies[1].wait()
     edge_count, width = edges_ref.shape
     count = nodes_ref.shape[0]
     senders = senders_ref[...]
@@ -124,37 +119,23 @@
         flat = receivers if own_part else senders
         pick_ref[:, start : start + LANES] = jnp.where(tall == lane + start, 1.0, 0.0).astype(BF)
         turned_ref[start : start + LANES, :] = jnp.where(flat == row + start, 1.0, 0.0).astype(BF)
-    copies[3].wait()
-    copies[4].wait()
     nodes = nodes_ref[...]
     own_ref[:count, :] = mm(nodes, inner_ref[width : 2 * width, :]).astype(BF)
     own_ref[count:, :] = mm(nodes, inner_ref[2 * width :, :]).astype(BF)
-    copies[2].wait()
-    copies[5].wait()
     tile = edge_count // 4
     for start in range(0, edge_count, tile):
         part_ref[start : start + tile, :] = (
             mm(edges_ref[start : start + tile, :], inner_ref[:width, :]) + shift_ref[...]
         )
-    for copy in copies[6:]:
-        copy.wait()
 
 
 def forward_kernel(
     part_ref, own_ref, pick_ref, turned_ref, low_ref, high_ref, edges_ref, nodes_ref,
     einner_ref, eouter_ref, eoffset_ref, egain_ref, nshift_ref, noffset_ref, ngain_ref,
-    ninner_hbm, nouter_hbm, cotan_hbm, ecotan_hbm,
+    ninner_ref, nouter_ref, cotan_ref,
     hidden_ref, slope_ref, normed_ref, invstd_ref, pulled_ref, partial_ref, weights_ref, sums_ref,
-    ecotan_ref, ninner_ref, nouter_ref, cotan_ref, sems,
     *, scale,
 ):
-    copies = start_copies(
-        [
-            (ninner_hbm, ninner_ref), (nouter_hbm, nouter_ref), (cotan_hbm, cotan_ref),
-            (ecotan_hbm, ecotan_ref),
-        ],
-        sems,
-    )
     edge_count, width = edges_ref.shape
     count = nodes_ref.shape[0]
     rim = jnp.concatenate([low_ref[...], high_ref[...]], axis=0)
@@ -179,8 +160,6 @@
         fresh = (edges_ref[rows, :].astype(F32) + egain_ref[...] * normed).astype(BF)
         total += mm(turned_ref[count : 2 * count, rows], fresh)
     aggregate = total.astype(BF)
-    for copy in copies:
-        copy.wait()
     nodes = nodes_ref[...]
     preact = (
         mm(nodes, ninner_ref[:width, :]) + mm(aggregate, ninner_ref[width:, :]) + nshift_ref[...]
@@ -207,9 +186,8 @@
 def backward_kernel(
     pick_ref, turned_ref, edges_ref, ecotan_ref, nodes_ref, low_ref, high_ref, hidden_ref, slope_ref,
     normed_ref, invstd_ref, pulled_ref, eouter_ref, egain_ref, node_sums_ref, node_weights_ref,
-    fresh_ref, preact_ref, spread_ref, weights_ref, sums_ref, *rest, scale, split,
+    fresh_ref, preact_ref, spread_ref, weights_ref, sums_ref, linear_ref, *, scale,
 ):
-    linear_ref = rest[-1]
     weights_ref[weights_ref.shape[0] - node_weights_ref.shape[0] :, :] = node_weights_ref[...]
     edge_count, width = edges_ref.shape
     count = nodes_ref.shape[0]
@@ -246,11 +224,9 @@
     weights_ref[3 * width : 3 * width + hidden_ref.shape[1], :] = (
         mm_tn(hidden_ref[...], linear_ref[...]) * scale
     )
-    if split is not None:
-        split.first_send(weights_ref, rest[0])
-
-
-def rim_kernel(spread_ref, inner_ref, _, low_ref, high_ref, *, count):
+
+
+def rim_kernel(spread_ref, inner_ref, low_ref, high_ref, *, count):
     width, slots = spread_ref.shape[1], low_ref.shape[0]
     for k, out_ref in enumerate((low_ref, high_ref)):
         start = 2 * count + k * slots
@@ -259,7 +235,7 @@
         ).astype(BF)
 
 
-def grads_kernel(spread_ref, inner_ref, partial_ref, fresh_ref, preact_ref, _, nodes_ref, edges_ref):
+def grads_kernel(spread_ref, inner_ref, partial_ref, fresh_ref, preact_ref, nodes_ref, edges_ref):
     count, width = partial_ref.shape
     nodes_ref[...] = (
         partial_ref[...]
@@ -333,13 +309,15 @@
 
 
 class Halving:
-    def __init__(self, rows):
-        self.core_bit, self.first, self.second = halving_orders()
+    def __init__(self, rows, columns, orders, carries):
+        self.core_bit, (self.first, self.second) = lax.axis_size("patch"), orders
         self.count = lax.axis_size("region") * lax.axis_size("patch")
         self.block = rows // self.count
         self.rows = rows // 2
+        self.columns = columns
+        self.width = columns.stop - columns.start
         self.steps = len(self.first)
-        self.aligned = rows % (16 * self.count) == 0
+        self.carries = carries
 
     def place(self, order, core, position):
         block = self.core_bit if core else 0
@@ -363,16 +341,21 @@
         zero, one = self.place(self.first, 0, position), self.place(self.second, 1, position)
         return pl.multiple_of(jnp.where(core == 1, one, zero), 8)
 
-    def first_send(self, weights_ref, send_ref):
-        other = 1 - self.core()
-        for position in range(self.count // 2):
-            start = position * self.block
-            send_ref[start : start + self.block, :] = weights_ref[
-                pl.ds(self.source(position, other), self.block), :
-            ].astype(BF)
-
-
-def halve_kernel(src_ref, got_ref, out_ref, *, plan, step, side):
+    def extra(self, vec_width):
+        return 16 * (vec_width // self.width) if self.carries else 0
+
+
+def first_kernel(weights_ref, *refs, plan):
+    send_ref = refs[-1]
+    other = 1 - plan.core()
+    for position in range(plan.count // 2):
+        start = position * plan.block
+        send_ref[start : start + plan.block, :] = weights_ref[
+            pl.ds(plan.source(position, other), plan.block), plan.columns
+        ].astype(BF)
+
+
+def halve(src_ref, got_ref, out_ref, plan, step, side):
     half = plan.rows >> (step + 1)
     bit = plan.bit(step)
     chosen = 1 - bit if side else bit
@@ -385,65 +368,150 @@
     per_half = half // plan.block
     for k in range(per_half):
         low, high = plan.source(k, core), plan.source(k + per_half, core)
-        held = src_ref[pl.ds(pl.multiple_of(jnp.where(chosen == 1, high, low), 8), plan.block), :]
+        row = pl.multiple_of(jnp.where(chosen == 1, high, low), 8)
+        held = src_ref[pl.ds(row, plan.block), plan.columns]
         start = pl.multiple_of(chosen * half + k * plan.block, 16)
         got = got_ref[pl.ds(start, plan.block), :]
         out_ref[k * plan.block : (k + 1) * plan.block, :] = (held + got).astype(out_ref.dtype)
 
 
-def vector_parts(ref, start, count):
-    return ref[start : start + count, :].astype(F32) + ref[start + 8 : start + 8 + count, :].astype(F32)
-
-
-def send_kernel(src_ref, got_ref, vec_ref, out_ref, new_ref, *, plan, step):
-    halve_kernel(src_ref, got_ref, out_ref, plan=plan, step=step, side=1)
+def keep_kernel(src_ref, got_ref, out_ref, *, plan, step):
+    halve(src_ref, got_ref, out_ref, plan, step, 0)
+
+
+def add_vectors(vec_ref, got_ref, start, plan):
+    pieces = vec_ref.shape[1] // plan.width
+    count = vec_ref.shape[0]
+    parts = []
+    for k in range(pieces):
+        low = start + 8 * (pieces + k)
+        high = start + 8 * k
+        parts.append(
+            got_ref[high : high + count, :].astype(F32) + got_ref[low : low + count, :].astype(F32)
+        )
+    return vec_ref[...] + jnp.concatenate(parts, axis=1)
+
+
+def send_kernel(src_ref, got_ref, *refs, plan, step):
+    if not plan.carries:
+        halve(src_ref, got_ref, refs[0], plan, step, 1)
+        return
+    vec_ref, out_ref, new_ref = refs
+    halve(src_ref, got_ref, out_ref, plan, step, 1)
     half = plan.rows >> (step + 1)
     count = vec_ref.shape[0]
-    vec = vec_ref[...]
-    if step:
-        vec = vec + vector_parts(got_ref, 2 * half, count)
+    vec = add_vectors(vec_ref, got_ref, 2 * half, plan) if step else vec_ref[...]
     upper = vec.astype(BF)
     lower = (vec - upper.astype(F32)).astype(BF)
+    pieces = vec.shape[1] // plan.width
     out_ref[half:, :] = jnp.zeros_like(out_ref[half:, :])
-    out_ref[half : half + count, :] = upper
-    out_ref[half + 8 : half + 8 + count, :] = lower
+    for k in range(pieces):
+        cut = slice(k * plan.width, (k + 1) * plan.width)
+        high, low = half + 8 * k, half + 8 * (pieces + k)
+        out_ref[high : high + count, :] = upper[:, cut]
+        out_ref[low : low + count, :] = lower[:, cut]
     new_ref[...] = upper.astype(F32) + lower.astype(F32)
 
 
-def last_kernel(src_ref, got_ref, vec_ref, out_ref, new_ref):
-    rows, width = src_ref.shape
-    total = src_ref[...] + got_ref[:rows, :]
-    parts = width // LANES
-    for k in range(parts):
-        out_ref[pl.ds(k, rows, stride=parts), :] = total[:, k * LANES : (k + 1) * LANES]
-    new_ref[...] = vec_ref[...] + vector_parts(got_ref, rows, vec_ref.shape[0])
-
-
-def reduce_kernels(plan, held, sent, vec):
-    width = held.shape[1]
+def vector_kernel(vec_ref, got_ref, new_ref, *, plan):
+    new_ref[...] = add_vectors(vec_ref, got_ref, plan.block, plan)
+
+
+def sum_kernel(held_ref, got_ref, out_ref):
+    out_ref[...] = held_ref[...] + got_ref[: held_ref.shape[0], :]
+
+
+def join_kernel(*refs, plans):
+    out_ref = refs[-1]
+    pieces = out_ref.shape[0] // plans[0].block
+    for plan, part_ref in zip(plans, refs):
+        for k in range(0, plan.width, LANES):
+            piece = (plan.columns.start + k) // LANES
+            out_ref[pl.ds(piece, plan.block, stride=pieces), :] = part_ref[:, k : k + LANES]
+
+
+def after(marks, *values):
+    return lax.optimization_barrier((*values, *marks))[: len(values)]
+
+
+def reduce_kernels(plans, weights, vec, beside):
     vec_shape = (vec.shape, F32)
-    got = permute_by(sent, plan.core_bit, plan.core_bit, plan.core_bit)
-    marks = []
-    for step in range(plan.steps):
-        half = plan.rows >> (step + 1)
-        send, vec = call(
-            functools.partial(send_kernel, plan=plan, step=step),
-            [((half + 16, width), BF), vec_shape], near(held), near(got), near(vec), name=f"send{step}",
-        )
-        marks.append(send)
-        held_late, got_late, send = lax.optimization_barrier((held, got, send))
-        incoming = permute_by(send, plan.first[step], plan.second[step], plan.core_bit)
-        (held,) = call(
-            functools.partial(halve_kernel, plan=plan, step=step, side=0),
-            [((half, width), F32)], near(held_late), near(got_late), name=f"keep{step}",
-        )
-        got = incoming
-    out, vec = call(
-        last_kernel, [((plan.block * width // LANES, LANES), F32), vec_shape], near(held), near(got),
-        near(vec), name="last", plain=(0,),
-    )
-    vec = vec + permute_by(vec, plan.core_bit, plan.core_bit, plan.core_bit)
-    return out.reshape(-1), vec.reshape(-1), marks
+    held = {plan: weights for plan in plans}
+    got, carrier = {}, None
+    marks = ()
+    for plan in plans:
+        (weights_late,) = after(marks, weights)
+        (sent,) = marks = call(
+            functools.partial(first_kernel, plan=plan), [((plan.rows, plan.width), BF)],
+            near(weights_late), name="first",
+        )
+        got[plan] = permute_by(sent, plan.core_bit, plan.core_bit, plan.core_bit)
+    marks = beside[-1](marks)
+    for step in range(plans[0].steps):
+        for plan in plans:
+            half = plan.rows >> (step + 1)
+            source, came = after(marks, held[plan], got[plan])
+            rows = half + plan.extra(vec.shape[1])
+            vectors = [near(vec)] if plan.carries else []
+            sent, *new = call(
+                functools.partial(send_kernel, plan=plan, step=step),
+                [((rows, plan.width), BF)] + ([vec_shape] if plan.carries else []),
+                near(source), near(came), *vectors, name=f"send{step}",
+            )
+            if plan.carries:
+                (vec,) = new
+            marks = (sent,)
+            source, came = after(marks, source, came)
+            incoming = permute_by(sent, plan.first[step], plan.second[step], plan.core_bit)
+            (held[plan],) = call(
+                functools.partial(keep_kernel, plan=plan, step=step),
+                [((half, plan.width), F32)], near(source), near(came), name=f"keep{step}",
+            )
+            got[plan] = incoming
+        if step in beside:
+            marks = beside[step](marks)
+    for plan in plans:
+        if plan.carries:
+            (vec,) = call(
+                functools.partial(vector_kernel, plan=plan), [vec_shape], near(vec), near(got[plan]),
+                name="vectors",
+            )
+            vec = vec + permute_by(vec, plan.core_bit, plan.core_bit, plan.core_bit)
+    parts = []
+    for plan in plans:
+        source, came = after(marks, held[plan], got[plan])
+        marks = call(
+            sum_kernel, [((plan.block, plan.width), F32)], near(source), near(came), name="sum"
+        )
+        parts.append(near(marks[0]))
+    (out,) = call(
+        functools.partial(join_kernel, plans=plans),
+        [((plans[0].block * weights.shape[1] // LANES, LANES), F32)], *parts, name="join", plain=(0,),
+    )
+    return out.reshape(-1), vec.reshape(-1)
+
+
+def make_plans(rows, width):
+    count = lax.axis_size("region") * lax.axis_size("patch")
+    core_bit, first, second = halving_orders()
+    if rows % (16 * count) or width % (4 * LANES):
+        return []
+    high = [b for b in first if b > core_bit]
+    low = [b for b in first if b < core_bit]
+    turned = low[1:-1] + high + low[:1] + low[-1:]
+    quarter = width // 4
+    chunks = CHUNKS
+    return [
+        Halving(
+            rows, slice(a * quarter, b * quarter),
+            (turned, turned) if kind else (first, second), i == 0,
+        )
+        for i, (a, b, kind) in enumerate(chunks)
+    ]
+
+
+PICK = 20 << 30
+CHUNKS = ((0, 2, 0), (2, 4, 0))
 
 
 def per_device(
@@ -462,14 +530,14 @@
     picked = 2 * count + -(-slots // LANES) * LANES
     edge_rows = 3 * width + hidden_width
     weight_rows = edge_rows + 2 * width + hidden_width
-    plan = Halving(weight_rows)
+    plans = make_plans(weight_rows, hidden_width)
     edge_shift, edge_offset, edge_gain, node_shift, node_offset, node_gain = (
         v.reshape(1, -1)
         for v in (edge_shift, edge_offset, edge_gain, node_shift, node_offset, node_gain)
     )
 
     out_low, out_high = call(
-        pick_kernel, [((half, width), BF)] * 2, lists, nodes, name="pick", limit=4 << 20, hbm=(0, 1),
+        pick_kernel, [((half, width), BF)] * 2, lists, nodes, name="pick", limit=4 << 20, hbm=(0, 1), flops=PICK,
         scratch=[
             pltpu.VMEM(lists.shape, jnp.int32), pltpu.VMEM(nodes.shape, BF),
             pltpu.SemaphoreType.DMA((2,)),
@@ -478,24 +546,18 @@
     low = ring(out_high, 1)
     high = ring(out_low, -1)
 
-    given = [
-        senders.reshape(1, -1), receivers.reshape(1, -1), edge_shift, nodes, edge_inner, edges,
-        edge_outer, edge_offset, edge_gain, node_shift, node_offset, node_gain,
-    ]
-    part, own, pick, turned, *loaded = call(
-        functools.partial(table_kernel, given=len(given)),
+    part, own, pick, turned = call(
+        table_kernel,
         [
             ((edge_count, hidden_width), F32),
             ((2 * count, hidden_width), BF),
             ((edge_count, picked), BF),
             ((picked, edge_count), BF),
-        ] + [(a.shape, a.dtype) for a in given],
-        *given, name="table", flops=2 * (edge_count + 2 * count) * width * hidden_width,
-        hbm=range(len(given)), scratch=[pltpu.SemaphoreType.DMA((len(given),))],
-    )
-    nodes_near, inner_near, edges_near, outer_near, *vectors = loaded[3:]
-    gain_near = vectors[1]
-    hidden, slope, normed, invstd, pulled, partial, node_weights, node_sums, ecotan_near = call(
+        ],
+        senders.reshape(1, -1), receivers.reshape(1, -1), edge_shift, nodes, edge_inner, edges,
+        name="table", flops=2 * (edge_count + 2 * count) * width * hidden_width,
+    )
+    hidden, slope, normed, invstd, pulled, partial, node_weights, node_sums = call(
         functools.partial(forward_kernel, scale=node_norm),
         [
             ((edge_count, hidden_width), BF),
@@ -506,58 +568,61 @@
             ((count, width), F32),
             ((weight_rows - edge_rows, hidden_width), F32),
             ((3, width), F32),
-            ((edge_count, width), BF),
         ],
-        near(part), near(own), near(pick), near(turned), near(low), near(high), near(edges_near),
-        near(nodes_near), near(inner_near), near(outer_near),
-        *[near(v) for v in vectors],
-        node_inner, node_outer, node_cotan, edge_cotan,
-        name="forward", flops=5 << 30, hbm=(15, 16, 17, 18),
-        scratch=[
-            pltpu.VMEM(node_inner.shape, BF), pltpu.VMEM(node_outer.shape, BF),
-            pltpu.VMEM(node_cotan.shape, BF), pltpu.SemaphoreType.DMA((4,)),
-        ],
-    )
-    sends = [((plan.rows, hidden_width), BF)] if plan.aligned else []
-    fresh, preact, spread, weights, sums, *sent = call(
-        functools.partial(backward_kernel, scale=edge_norm, split=plan if plan.aligned else None),
+        near(part), near(own), near(pick), near(turned), near(low), near(high), edges, nodes,
+        edge_inner, edge_outer, edge_offset, edge_gain, node_shift, node_offset, node_gain,
+        node_inner, node_outer, node_cotan, name="forward", flops=5 << 30,
+    )
+    fresh, preact, spread, weights, sums = call(
+        functools.partial(backward_kernel, scale=edge_norm),
         [
             ((edge_count, width), F32),
             ((edge_count, hidden_width), BF),
             ((2 * count + slots, hidden_width), BF),
             ((weight_rows, hidden_width), F32),
             ((6, width), F32),
-            *sends,
         ],
-        near(pick), near(turned), near(edges_near), near(ecotan_near), near(nodes_near), near(low),
+        near(pick), near(turned), edges, edge_cotan, nodes, near(low),
         near(high), near(hidden), near(slope), near(normed), near(invstd), near(pulled),
-        near(outer_near), near(gain_near), near(node_sums), near(node_weights),
+        edge_outer, edge_gain, near(node_sums), near(node_weights),
         name="backward", flops=5 << 30,
         scratch=[pltpu.VMEM((edge_count, width), BF)],
     )
-    if plan.aligned:
-        grad_weights, grad_vectors, marks = reduce_kernels(plan, weights, sent[0], sums)
-        mark = marks[0]
+    results = {}
+
+    def rim_side(marks):
+        (spread_late,) = after(marks, spread)
+        rim_low, rim_high = call(
+            functools.partial(rim_kernel, count=count), [((half, width), BF)] * 2,
+            near(spread_late), edge_inner, name="rim", limit=4 << 20,
+        )
+        results["low"], results["high"] = ring(rim_high, 1), ring(rim_low, -1)
+        return rim_low, rim_high
+
+    def edge_side(marks):
+        spread_late, fresh_late = after(marks, spread, fresh)
+        results["nodes"], results["edges"] = call(
+            grads_kernel,
+            [((count, width), F32), ((edge_count, width), BF)],
+            near(spread_late), edge_inner, near(partial), near(fresh_late), near(preact),
+            name="grads", flops=2 << 30, plain=(1,),
+        )
+        return results["nodes"], results["low"], results["high"]
+
+    def node_side(marks):
+        (part_late,) = after(marks, results["nodes"])
+        (results["nodes"],) = call(
+            rims_kernel, [((count, width), F32)], lists, near(part_late),
+            near(results["low"]), near(results["high"]), name="rims", plain=(0,), limit=4 << 20,
+        )
+        return (results["nodes"],)
+
+    if plans:
+        grad_weights, grad_vectors = reduce_kernels(plans, weights, sums, {-1: rim_side, 0: edge_side, 1: node_side})
     else:
         grad_weights, grad_vectors = reduce_all(weights, sums)
-        mark = sums
-    rim_low, rim_high = call(
-        functools.partial(rim_kernel, count=count), [((half, width), BF)] * 2, near(spread),
-        near(inner_near), near(mark), name="rim", limit=4 << 20,
-    )
-    back_low = ring(rim_high, 1)
-    back_high = ring(rim_low, -1)
-    nodes_part, grad_edges = call(
-        grads_kernel,
-        [((count, width), F32), ((edge_count, width), BF)],
-        near(spread), near(inner_near), near(partial), near(fresh), near(preact), near(mark),
-        name="grads", flops=2 << 30, plain=(1,),
-    )
-    (grad_nodes,) = call(
-        rims_kernel, [((count, width), F32)], lists, near(nodes_part), near(back_low),
-        near(back_high), name="rims", plain=(0,), limit=4 << 20,
-    )
-    return (grad_nodes, grad_edges, grad_weights, grad_vectors)
+        node_side(edge_side(rim_side((sums,))))
+    return (results["nodes"], results["edges"], grad_weights, grad_vectors)
 
 
 def solution(mesh):

time: 68.2 us -> 60 us (0.88)
  waiting for transfers between devices: 31.2 us -> 20 us
  starting transfers between devices: 13.7 us -> 19.2 us
  Pallas kernels: 21.7 us -> 18.8 us
    ppermute x6 -> x11, waiting for transfers between devices: 31.2 us -> 15.1 us  [permute_by(): return lax.ppermute(values, AXES, pairs)]
    ppermute x6 -> x11, starting transfers between devices: 2.83 us -> 8.37 us  [permute_by(): return lax.ppermute(values, AXES, pairs)]
    ppermute x4, waiting for transfers between devices: 0.01 us -> 4.89 us  [ring(): lax.ppermute(values, 'patch', [(i, (i + step) % count) for i in range(cou...]
    pallas_call x16 -> x29, Pallas kernels: 21.7 us -> 18.8 us  [call(): pl.pallas_call(body, out_shape=shapes, in_specs=[anywhere if i in hbm els...]
  transfers between devices with their start and end apart: 10 -> 15, of which waited for: 5 -> 9; matrix products, arithmetic and copies ran while one was open for 0% -> 0% of each run, Pallas kernels for 12% -> 11%
where the time goes in v4:
time: 60 us; the launch traced here: 59.8 us
  waiting for transfers between devices  20 us (33%)
  starting transfers between devices  19.2 us (32%)
  Pallas kernels  18.8 us (31%)
  between operations  1.07 us (2%)
  local copies, waits for them, and re-layouts  0.7 us (1%)
    pallas_call x29, Pallas kernels, call(): pl.pallas_call(body, out_shape=shapes, in_specs=[anywhere if i in hbm els...  18.8 us
    ppermute x11, waiting for transfers between devices, permute_by(): return lax.ppermute(values, AXES, pairs)  15.1 us
    ppermute x4, starting transfers between devices, ring(): lax.ppermute(values, 'patch', [(i, (i + step) % count) for i in range(cou...  10.8 us
    ppermute x11, starting transfers between devices, permute_by(): return lax.ppermute(values, AXES, pairs)  8.37 us
    ppermute x4, waiting for transfers between devices, ring(): lax.ppermute(values, 'patch', [(i, (i + step) % count) for i in range(cou...  4.89 us
  transfers between devices with their start and end apart: 15, of which 9 were waited for; matrix products, arithmetic and copies ran while one was open for 0% of the time, Pallas kernels for 11%

profile of v4, /device:TPU:0, one launch (start us, length us, event | category | flops | bytes accessed | tf_op | source)
XLA Modules:
  0.0 59.8 jit_solution(4849026620515596774)
XLA Ops:
  0.7 1.4 %pick.1 = (bf16[32,512]{1,0:T(8,128)(2,1)S(1)}, bf16[32,512]{1,0:T(8,128)(2,1)S(1)}) custom-call(s32[2,32]{1,0:T(2,128)} %bitcast.10, bf16[256,512]{1,0:T(8,128)(2,1)} %nodes_ref.5), custom_call_target="tpu_custom_call" | custom-call | flops 21474836480 | bytes 65536 | tf_op jit(solution)/shard_map/pick/pallas_call | solution.py:41
  2.2 3.0 %collective-permute-start = (bf16[32,512]{1,0:T(8,128)(2,1)S(1)}, bf16[32,512]{1,0:T(8,128)(2,1)S(1)}, u32[]{:S(2)}, u32[]{:S(2)}) collective-permute-start(bf16[32,512]{1,0:T(8,128)(2,1)S(1)} %get-tuple-element.78), channel_id=1, source_target_pairs={{0,1},{1,2},{2,3},{3,4},{4,5},{5,6},{6,7},{7,0},{8,9},{9,10},{10,1... | collective-permute-start | bytes 98312 | tf_op jit(solution)/shard_map/ppermute | solution.py:266
  5.2 3.1 %collective-permute-start.1 = (bf16[32,512]{1,0:T(8,128)(2,1)S(1)}, bf16[32,512]{1,0:T(8,128)(2,1)S(1)}, u32[]{:S(2)}, u32[]{:S(2)}) collective-permute-start(bf16[32,512]{1,0:T(8,128)(2,1)S(1)} %get-tuple-element.79), channel_id=1, source_target_pairs={{0,7},{1,0},{2,1},{3,2},{4,3},{5,4},{6,5},{7,6},{8,15},{9,8},{10,9... | collective-permute-start | bytes 98312 | tf_op jit(solution)/shard_map/ppermute | solution.py:266
  8.3 1.4 %table.1 = (f32[1024,512]{1,0:T(8,128)S(1)}, bf16[512,512]{1,0:T(8,128)(2,1)S(1)}, bf16[1024,640]{1,0:T(8,128)(2,1)S(1)}, bf16[640,1024]{1,0:T(8,128)(2,1)S(1)}) custom-call(s32[1,1024]{1,0:T(1,128)S(1)} %bitcast.12, s32[1,1024]{1,0:T(1,128)S(1)} %bitcast.13, f32[1,512]{1,0:T(1,128)S(1)} %bitcast.14, bf16[256,512]{1,0:T(8,128)(2,1)S(1)} %copy-done.8, ...), custom_call_target="tpu_custom_call" | custom-call | flops 805306368 | bytes 5242880 | tf_op jit(solution)/shard_map/table/pallas_call | solution.py:41
  9.7 0.4 collective-permute-done.low_ref
  10.2 5.8 %forward.1 = (bf16[1024,512]{1,0:T(8,128)(2,1)S(1)}, f32[1024,512]{1,0:T(8,128)S(1)}, f32[1024,512]{1,0:T(8,128)S(1)}, f32[1024,1]{1,0:T(8,128)S(1)}, bf16[256,5...) custom-call(f32[1024,512]{1,0:T(8,128)S(1)} %get-tuple-element.80.part_ref, ...), custom_call_target="tpu_custom_call" | custom-call | flops 5368709120 | bytes 9185280 | tf_op jit(solution)/shard_map/forward/pallas_call | solution.py:41
  16.1 4.8 %backward.1 = (f32[1024,512]{1,0:T(8,128)S(1)}, bf16[1024,512]{1,0:T(8,128)(2,1)S(1)}, bf16[576,512]{1,0:T(8,128)(2,1)S(1)}, f32[3584,512]{1,0:T(8,128)S(1)}, f32[6,512]{1,0:T(8,128)S(1)}) custom-call(bf16[1024,640]{1,0:T(8,128)(2,1)S(1)} %get-tuple-element.76.pick_ref, bf16[640,1024]{1,0:T(8,128)(2,1)S(1)} %get-tuple-element.77.turned_ref, ...), custom_call_target="tpu_custom_call" | custom-call | flops 5368709120 | bytes 11087872 | tf_op jit(solution)/shard_map/backward/pallas_call | solution.py:41
  20.9 0.1 first.2
  21.1 0.1 first.3
  21.2 0.5 collective-permute-start.2
  21.8 0.4 rim.1
  22.2 1.4 %collective-permute-done.3.got_ref = bf16[1792,256]{1,0:T(8,128)(2,1)S(1)} collective-permute-done((bf16[1792,256]{1,0:T(8,128)(2,1)S(1)}, bf16[1792,256]{1,0:T(8,128)(2,1)S(1)}, u32[]{:S(2)}, u32[]{:S(2)}) %collective-permute-start.3) | collective-permute-done | bytes 917536 | tf_op jit(solution)/shard_map/ppermute | solution.py:279
  23.5 0.1 send0.2
  23.7 1.7 %collective-permute-start.5 = (bf16[928,256]{1,0:T(8,128)(2,1)S(1)}, bf16[928,256]{1,0:T(8,128)(2,1)S(1)}, u32[]{:S(2)}, u32[]{:S(2)}) collective-permute-start(bf16[928,256]{1,0:T(8,128)(2,1)S(1)} %get-tuple-element.99), channel_id=1, source_target_pairs={{0,16},{1,17},{2,18},{3,19},{4,20},{5,21},{6,22},{7,23},{8,9},{9,8... | collective-permute-start | bytes 1425416 | tf_op jit(solution)/shard_map/ppermute | solution.py:279
  25.4 0.1 send0.3
  25.5 1.2 %collective-permute-start.4 = (bf16[896,256]{1,0:T(8,128)(2,1)S(1)}, bf16[896,256]{1,0:T(8,128)(2,1)S(1)}, u32[]{:S(2)}, u32[]{:S(2)}) collective-permute-start(bf16[896,256]{1,0:T(8,128)(2,1)S(1)} %send0.3), channel_id=1, source_target_pairs={{0,16},{1,17},{2,18},{3,19},{4,20},{5,21},{6,22},{7,23},{8,9},{9,8... | collective-permute-start | bytes 1376264 | tf_op jit(solution)/shard_map/ppermute | solution.py:279
  26.7 4.7 %collective-permute-start.7 = (bf16[32,512]{1,0:T(8,128)(2,1)S(1)}, bf16[32,512]{1,0:T(8,128)(2,1)S(1)}, u32[]{:S(2)}, u32[]{:S(2)}) collective-permute-start(bf16[32,512]{1,0:T(8,128)(2,1)S(1)} %get-tuple-element.94), channel_id=1, source_target_pairs={{0,7},{1,0},{2,1},{3,2},{4,3},{5,4},{6,5},{7,6},{8,15},{9,8},{10,9... | collective-permute-start | bytes 98312 | tf_op jit(solution)/shard_map/ppermute | solution.py:266
  31.4 2.0 %grads.1 = (f32[256,512]{1,0:T(8,128)S(1)}, bf16[1024,512]{1,0:T(8,128)(2,1)}) custom-call(bf16[576,512]{1,0:T(8,128)(2,1)S(1)} %get-tuple-element.102.spread_ref, bf16[1536,512]{1,0:T(8,128)(2,1)S(1)} %copy-done, f32[256,512]{1,0:T(8,128)S(1)} %get-tuple-element.103.partial_ref, f32[1024,512]{1,0:T(8,128)S(1)} %get-tuple-element.104.fresh_ref, ...), custom_call_target="tpu_custom_call" | custom-call | flops 2147483648 | bytes 1572864 | tf_op jit(solution)/shard_map/grads/pallas_call | solution.py:41
  33.5 4.5 %collective-permute-done.6.low_ref = bf16[32,512]{1,0:T(8,128)(2,1)S(1)} collective-permute-done((bf16[32,512]{1,0:T(8,128)(2,1)S(1)}, bf16[32,512]{1,0:T(8,128)(2,1)S(1)}, u32[]{:S(2)}, u32[]{:S(2)}) %collective-permute-start.6) | collective-permute-done | bytes 32800 | tf_op jit(solution)/shard_map/ppermute | solution.py:266
  38.2 0.1 keep0.2.src_ref
  38.4 2.0 %collective-permute-start.10 = (bf16[448,256]{1,0:T(8,128)(2,1)S(1)}, bf16[448,256]{1,0:T(8,128)(2,1)S(1)}, u32[]{:S(2)}, u32[]{:S(2)}) collective-permute-start(bf16[448,256]{1,0:T(8,128)(2,1)S(1)} %send1.3), channel_id=1, source_target_pairs={{0,1},{1,0},{2,3},{3,2},{4,5},{5,4},{6,7},{7,6},{8,10},{9,11},{10,... | collective-permute-start | bytes 688136 | tf_op jit(solution)/shard_map/ppermute | solution.py:279
  40.5 1.1 %rims.1 = f32[256,512]{1,0:T(8,128)} custom-call(s32[2,32]{1,0:T(2,128)S(1)} %bitcast.11, f32[256,512]{1,0:T(8,128)S(1)} %get-tuple-element.117.partial_ref, bf16[32,512]{1,0:T(8,128)(2,1)S(1)} %collective-permute-done.6.low_ref, bf16[32,512]{1,0:T(8,128)(2,1)S(1)} %collective-permute-done.7.high_ref), custom_call_target="tpu_custom_call" | custom-call | bytes 524288 | tf_op jit(solution)/shard_map/rims/pallas_call | solution.py:41
  41.6 2.8 %collective-permute-done.8.got_ref = bf16[480,256]{1,0:T(8,128)(2,1)S(1)} collective-permute-done((bf16[480,256]{1,0:T(8,128)(2,1)S(1)}, bf16[480,256]{1,0:T(8,128)(2,1)S(1)}, u32[]{:S(2)}, u32[]{:S(2)}) %collective-permute-start.8) | collective-permute-done | bytes 245792 | tf_op jit(solution)/shard_map/ppermute | solution.py:279
  44.6 2.2 %collective-permute-done.10.got_ref = bf16[448,256]{1,0:T(8,128)(2,1)S(1)} collective-permute-done((bf16[448,256]{1,0:T(8,128)(2,1)S(1)}, bf16[448,256]{1,0:T(8,128)(2,1)S(1)}, u32[]{:S(2)}, u32[]{:S(2)}) %collective-permute-start.10) | collective-permute-done | bytes 229408 | tf_op jit(solution)/shard_map/ppermute | solution.py:279
  47.0 2.5 %collective-permute-done.9.got_ref = bf16[256,256]{1,0:T(8,128)(2,1)S(1)} collective-permute-done((bf16[256,256]{1,0:T(8,128)(2,1)S(1)}, bf16[256,256]{1,0:T(8,128)(2,1)S(1)}, u32[]{:S(2)}, u32[]{:S(2)}) %collective-permute-start.9) | collective-permute-done | bytes 131104 | tf_op jit(solution)/shard_map/ppermute | solution.py:279
  49.6 2.1 %collective-permute-done.12.got_ref = bf16[224,256]{1,0:T(8,128)(2,1)S(1)} collective-permute-done((bf16[224,256]{1,0:T(8,128)(2,1)S(1)}, bf16[224,256]{1,0:T(8,128)(2,1)S(1)}, u32[]{:S(2)}, u32[]{:S(2)}) %collective-permute-start.12) | collective-permute-done | bytes 114720 | tf_op jit(solution)/shard_map/ppermute | solution.py:279
  51.7 0.9 %collective-permute-start.13 = (bf16[112,256]{1,0:T(8,128)(2,1)S(1)}, bf16[112,256]{1,0:T(8,128)(2,1)S(1)}, u32[]{:S(2)}, u32[]{:S(2)}) collective-permute-start(bf16[112,256]{1,0:T(8,128)(2,1)S(1)} %send3.3), channel_id=1, source_target_pairs={{0,4},{1,5},{2,6},{3,7},{4,0},{5,1},{6,2},{7,3},{8,12},{9,13},{10,... | collective-permute-start | bytes 172040 | tf_op jit(solution)/shard_map/ppermute | solution.py:279
  52.6 2.8 %collective-permute-done.11.got_ref = bf16[144,256]{1,0:T(8,128)(2,1)S(1)} collective-permute-done((bf16[144,256]{1,0:T(8,128)(2,1)S(1)}, bf16[144,256]{1,0:T(8,128)(2,1)S(1)}, u32[]{:S(2)}, u32[]{:S(2)}) %collective-permute-start.11) | collective-permute-done | bytes 73760 | tf_op jit(solution)/shard_map/ppermute | solution.py:279
  55.4 1.6 %collective-permute-start.14 = (f32[6,512]{1,0:T(8,128)S(1)}, f32[6,512]{1,0:T(8,128)S(1)}, u32[]{:S(2)}, u32[]{:S(2)}) collective-permute-start(f32[6,512]{1,0:T(8,128)S(1)} %vectors.1), channel_id=1, source_target_pairs={{0,8},{1,9},{2,10},{3,11},{4,12},{5,13},{6,14},{7,15},{8,0},{9,1},... | collective-permute-start | bytes 36872 | tf_op jit(solution)/shard_map/ppermute | solution.py:279
  57.1 1.3 %collective-permute-done.13.got_ref = bf16[112,256]{1,0:T(8,128)(2,1)S(1)} collective-permute-done((bf16[112,256]{1,0:T(8,128)(2,1)S(1)}, bf16[112,256]{1,0:T(8,128)(2,1)S(1)}, u32[]{:S(2)}, u32[]{:S(2)}) %collective-permute-start.13) | collective-permute-done | bytes 57376 | tf_op jit(solution)/shard_map/ppermute | solution.py:279
  58.5 0.7 %join.1 = f32[448,128]{1,0:T(8,128)} custom-call(f32[112,256]{1,0:T(8,128)S(1)} %sum.2.refs_0_, f32[112,256]{1,0:T(8,128)S(1)} %sum.3.refs_1_), custom_call_target="tpu_custom_call" | custom-call | bytes 229376 | tf_op jit(solution)/shard_map/join/pallas_call | solution.py:41
  59.2 0.6 %reshape.51 = f32[3072]{0:T(1024)} reshape(f32[6,512]{1,0:T(8,128)S(1)} %add.3) | data formatting | bytes 24576 | tf_op jit(solution)/shard_map/reshape | solution.py:491
  (63 shorter events, 1.1 us)
Async XLA Ops:
  0.6 7.7 %copy-start = (bf16[1536,512]{1,0:T(8,128)(2,1)S(1)}, bf16[1536,512]{1,0:T(8,128)(2,1)}, u32[]{:S(2)}) copy-start(bf16[1536,512]{1,0:T(8,128)(2,1)} %inner_ref.5) | copy-start | bytes 4718596
  0.6 7.7 %copy-start.3 = (bf16[1024,512]{1,0:T(8,128)(2,1)S(1)}, bf16[1024,512]{1,0:T(8,128)(2,1)}, u32[]{:S(2)}) copy-start(bf16[1024,512]{1,0:T(8,128)(2,1)} %edges_ref.5) | copy-start | bytes 3145732
  0.7 7.6 %copy-start.8 = (bf16[256,512]{1,0:T(8,128)(2,1)S(1)}, bf16[256,512]{1,0:T(8,128)(2,1)}, u32[]{:S(2)}) copy-start(bf16[256,512]{1,0:T(8,128)(2,1)} %nodes_ref.5) | copy-start | bytes 786436
  0.7 7.6 %copy-start.9 = (s32[1024]{0:T(1024)S(1)}, s32[1024]{0:T(1024)}, u32[]{:S(2)}) copy-start(s32[1024]{0:T(1024)} %param.32) | copy-start | bytes 12292
  0.7 7.6 %copy-start.10 = (s32[1024]{0:T(1024)S(1)}, s32[1024]{0:T(1024)}, u32[]{:S(2)}) copy-start(s32[1024]{0:T(1024)} %param.33) | copy-start | bytes 12292
  0.7 7.6 %copy-start.11 = (f32[512]{0:T(512)S(1)}, f32[512]{0:T(512)}, u32[]{:S(2)}) copy-start(f32[512]{0:T(512)} %param.25) | copy-start | bytes 6148
  2.1 8.1 %copy-start.2 = (bf16[1024,512]{1,0:T(8,128)(2,1)S(1)}, bf16[1024,512]{1,0:T(8,128)(2,1)}, u32[]{:S(2)}) copy-start(bf16[1024,512]{1,0:T(8,128)(2,1)} %ninner_ref.1) | copy-start | bytes 3145732
  2.1 8.1 %copy-start.5 = (bf16[512,512]{1,0:T(8,128)(2,1)S(1)}, bf16[512,512]{1,0:T(8,128)(2,1)}, u32[]{:S(2)}) copy-start(bf16[512,512]{1,0:T(8,128)(2,1)} %nouter_ref.1) | copy-start | bytes 1572868
  2.1 8.1 %copy-start.6 = (bf16[512,512]{1,0:T(8,128)(2,1)S(1)}, bf16[512,512]{1,0:T(8,128)(2,1)}, u32[]{:S(2)}) copy-start(bf16[512,512]{1,0:T(8,128)(2,1)} %eouter_ref.3) | copy-start | bytes 1572868
  2.1 8.0 %copy-start.7 = (bf16[256,512]{1,0:T(8,128)(2,1)S(1)}, bf16[256,512]{1,0:T(8,128)(2,1)}, u32[]{:S(2)}) copy-start(bf16[256,512]{1,0:T(8,128)(2,1)} %cotan_ref.1) | copy-start | bytes 786436
  2.1 8.0 %copy-start.12 = (f32[512]{0:T(512)S(1)}, f32[512]{0:T(512)}, u32[]{:S(2)}) copy-start(f32[512]{0:T(512)} %param.26) | copy-start | bytes 6148
  2.1 8.0 %copy-start.13 = (f32[512]{0:T(512)S(1)}, f32[512]{0:T(512)}, u32[]{:S(2)}) copy-start(f32[512]{0:T(512)} %param.28) | copy-start | bytes 6148
  2.1 8.0 %copy-start.14 = (f32[512]{0:T(512)S(1)}, f32[512]{0:T(512)}, u32[]{:S(2)}) copy-start(f32[512]{0:T(512)} %param.29) | copy-start | bytes 6148
  2.1 8.0 %copy-start.15 = (f32[512]{0:T(512)S(1)}, f32[512]{0:T(512)}, u32[]{:S(2)}) copy-start(f32[512]{0:T(512)} %param.30) | copy-start | bytes 6148
  2.2 8.0 %copy-start.16 = (f32[512]{0:T(512)S(1)}, f32[512]{0:T(512)}, u32[]{:S(2)}) copy-start(f32[512]{0:T(512)} %param.27) | copy-start | bytes 6148
  2.2 8.0 %collective-permute-start = (bf16[32,512]{1,0:T(8,128)(2,1)S(1)}, bf16[32,512]{1,0:T(8,128)(2,1)S(1)}, u32[]{:S(2)}, u32[]{:S(2)}) collective-permute-start(bf16[32,512]{1,0:T(8,128)(2,1)S(1)} %get-tuple-element.78), channel_id=1, source_target_pairs={{0,1},{1,2},{2,3},{3,4},{4,5},{5,6},{6,7},{7,0},{8,9},{9,10},{10,1... | collective-permute-start | bytes 98312 | tf_op jit(solution)/shard_map/ppermute | solution.py:266
  5.2 4.9 %collective-permute-start.1 = (bf16[32,512]{1,0:T(8,128)(2,1)S(1)}, bf16[32,512]{1,0:T(8,128)(2,1)S(1)}, u32[]{:S(2)}, u32[]{:S(2)}) collective-permute-start(bf16[32,512]{1,0:T(8,128)(2,1)S(1)} %get-tuple-element.79), channel_id=1, source_target_pairs={{0,7},{1,0},{2,1},{3,2},{4,3},{5,4},{6,5},{7,6},{8,15},{9,8},{10,9... | collective-permute-start | bytes 98312 | tf_op jit(solution)/shard_map/ppermute | solution.py:266
  10.2 5.9 %copy-start.4 = (bf16[1024,512]{1,0:T(8,128)(2,1)S(1)}, bf16[1024,512]{1,0:T(8,128)(2,1)}, u32[]{:S(2)}) copy-start(bf16[1024,512]{1,0:T(8,128)(2,1)} %ecotan_ref.1) | copy-start | bytes 3145732
  21.0 2.5 %collective-permute-start.3 = (bf16[1792,256]{1,0:T(8,128)(2,1)S(1)}, bf16[1792,256]{1,0:T(8,128)(2,1)S(1)}, u32[]{:S(2)}, u32[]{:S(2)}) collective-permute-start(bf16[1792,256]{1,0:T(8,128)(2,1)S(1)} %first.2), channel_id=1, source_target_pairs={{0,8},{1,9},{2,10},{3,11},{4,12},{5,13},{6,14},{7,15},{8,0},{9,1},... | collective-permute-start | bytes 2752520 | tf_op jit(solution)/shard_map/ppermute | solution.py:279
  21.2 4.1 %collective-permute-start.2 = (bf16[1792,256]{1,0:T(8,128)(2,1)S(1)}, bf16[1792,256]{1,0:T(8,128)(2,1)S(1)}, u32[]{:S(2)}, u32[]{:S(2)}) collective-permute-start(bf16[1792,256]{1,0:T(8,128)(2,1)S(1)} %first.3), channel_id=1, source_target_pairs={{0,8},{1,9},{2,10},{3,11},{4,12},{5,13},{6,14},{7,15},{8,0},{9,1},... | collective-permute-start | bytes 2752520 | tf_op jit(solution)/shard_map/ppermute | solution.py:279
  23.7 14.4 %collective-permute-start.5 = (bf16[928,256]{1,0:T(8,128)(2,1)S(1)}, bf16[928,256]{1,0:T(8,128)(2,1)S(1)}, u32[]{:S(2)}, u32[]{:S(2)}) collective-permute-start(bf16[928,256]{1,0:T(8,128)(2,1)S(1)} %get-tuple-element.99), channel_id=1, source_target_pairs={{0,16},{1,17},{2,18},{3,19},{4,20},{5,21},{6,22},{7,23},{8,9},{9,8... | collective-permute-start | bytes 1425416 | tf_op jit(solution)/shard_map/ppermute | solution.py:279
  25.5 12.8 %collective-permute-start.4 = (bf16[896,256]{1,0:T(8,128)(2,1)S(1)}, bf16[896,256]{1,0:T(8,128)(2,1)S(1)}, u32[]{:S(2)}, u32[]{:S(2)}) collective-permute-start(bf16[896,256]{1,0:T(8,128)(2,1)S(1)} %send0.3), channel_id=1, source_target_pairs={{0,16},{1,17},{2,18},{3,19},{4,20},{5,21},{6,22},{7,23},{8,9},{9,8... | collective-permute-start | bytes 1376264 | tf_op jit(solution)/shard_map/ppermute | solution.py:279
  26.7 6.8 %collective-permute-start.7 = (bf16[32,512]{1,0:T(8,128)(2,1)S(1)}, bf16[32,512]{1,0:T(8,128)(2,1)S(1)}, u32[]{:S(2)}, u32[]{:S(2)}) collective-permute-start(bf16[32,512]{1,0:T(8,128)(2,1)S(1)} %get-tuple-element.94), channel_id=1, source_target_pairs={{0,7},{1,0},{2,1},{3,2},{4,3},{5,4},{6,5},{7,6},{8,15},{9,8},{10,9... | collective-permute-start | bytes 98312 | tf_op jit(solution)/shard_map/ppermute | solution.py:266
  31.4 6.6 %collective-permute-start.6 = (bf16[32,512]{1,0:T(8,128)(2,1)S(1)}, bf16[32,512]{1,0:T(8,128)(2,1)S(1)}, u32[]{:S(2)}, u32[]{:S(2)}) collective-permute-start(bf16[32,512]{1,0:T(8,128)(2,1)S(1)} %get-tuple-element.95), channel_id=1, source_target_pairs={{0,1},{1,2},{2,3},{3,4},{4,5},{5,6},{6,7},{7,0},{8,9},{9,10},{10,1... | collective-permute-start | bytes 98312 | tf_op jit(solution)/shard_map/ppermute | solution.py:266
  38.1 6.3 %collective-permute-start.8 = (bf16[480,256]{1,0:T(8,128)(2,1)S(1)}, bf16[480,256]{1,0:T(8,128)(2,1)S(1)}, u32[]{:S(2)}, u32[]{:S(2)}) collective-permute-start(bf16[480,256]{1,0:T(8,128)(2,1)S(1)} %get-tuple-element.114), channel_id=1, source_target_pairs={{0,1},{1,0},{2,3},{3,2},{4,5},{5,4},{6,7},{7,6},{8,10},{9,11},{10,... | collective-permute-start | bytes 737288 | tf_op jit(solution)/shard_map/ppermute | solution.py:279
  38.3 2.2 %copy-start.1 = (s32[1,1,2,32]{3,2,1,0:T(2,128)S(1)}, s32[1,1,2,32]{3,2,1,0:T(2,128)}, u32[]{:S(2)}) copy-start(s32[1,1,2,32]{3,2,1,0:T(2,128)} %param.31) | copy-start | bytes 772
  38.4 8.4 %collective-permute-start.10 = (bf16[448,256]{1,0:T(8,128)(2,1)S(1)}, bf16[448,256]{1,0:T(8,128)(2,1)S(1)}, u32[]{:S(2)}, u32[]{:S(2)}) collective-permute-start(bf16[448,256]{1,0:T(8,128)(2,1)S(1)} %send1.3), channel_id=1, source_target_pairs={{0,1},{1,0},{2,3},{3,2},{4,5},{5,4},{6,7},{7,6},{8,10},{9,11},{10,... | collective-permute-start | bytes 688136 | tf_op jit(solution)/shard_map/ppermute | solution.py:279
  44.4 5.0 %collective-permute-start.9 = (bf16[256,256]{1,0:T(8,128)(2,1)S(1)}, bf16[256,256]{1,0:T(8,128)(2,1)S(1)}, u32[]{:S(2)}, u32[]{:S(2)}) collective-permute-start(bf16[256,256]{1,0:T(8,128)(2,1)S(1)} %get-tuple-element.124), channel_id=1, source_target_pairs={{0,2},{1,3},{2,0},{3,1},{4,6},{5,7},{6,4},{7,5},{8,24},{9,25},{10,... | collective-permute-start | bytes 393224 | tf_op jit(solution)/shard_map/ppermute | solution.py:279
  46.8 4.9 %collective-permute-start.12 = (bf16[224,256]{1,0:T(8,128)(2,1)S(1)}, bf16[224,256]{1,0:T(8,128)(2,1)S(1)}, u32[]{:S(2)}, u32[]{:S(2)}) collective-permute-start(bf16[224,256]{1,0:T(8,128)(2,1)S(1)} %send2.3), channel_id=1, source_target_pairs={{0,2},{1,3},{2,0},{3,1},{4,6},{5,7},{6,4},{7,5},{8,24},{9,25},{10,... | collective-permute-start | bytes 344072 | tf_op jit(solution)/shard_map/ppermute | solution.py:279
  49.5 6.0 %collective-permute-start.11 = (bf16[144,256]{1,0:T(8,128)(2,1)S(1)}, bf16[144,256]{1,0:T(8,128)(2,1)S(1)}, u32[]{:S(2)}, u32[]{:S(2)}) collective-permute-start(bf16[144,256]{1,0:T(8,128)(2,1)S(1)} %get-tuple-element.134), channel_id=1, source_target_pairs={{0,4},{1,5},{2,6},{3,7},{4,0},{5,1},{6,2},{7,3},{8,12},{9,13},{10,... | collective-permute-start | bytes 221192 | tf_op jit(solution)/shard_map/ppermute | solution.py:279
  51.7 6.8 %collective-permute-start.13 = (bf16[112,256]{1,0:T(8,128)(2,1)S(1)}, bf16[112,256]{1,0:T(8,128)(2,1)S(1)}, u32[]{:S(2)}, u32[]{:S(2)}) collective-permute-start(bf16[112,256]{1,0:T(8,128)(2,1)S(1)} %send3.3), channel_id=1, source_target_pairs={{0,4},{1,5},{2,6},{3,7},{4,0},{5,1},{6,2},{7,3},{8,12},{9,13},{10,... | collective-permute-start | bytes 172040 | tf_op jit(solution)/shard_map/ppermute | solution.py:279
  55.4 3.8 %collective-permute-start.14 = (f32[6,512]{1,0:T(8,128)S(1)}, f32[6,512]{1,0:T(8,128)S(1)}, u32[]{:S(2)}, u32[]{:S(2)}) collective-permute-start(f32[6,512]{1,0:T(8,128)S(1)} %vectors.1), channel_id=1, source_target_pairs={{0,8},{1,9},{2,10},{3,11},{4,12},{5,13},{6,14},{7,15},{8,0},{9,1},... | collective-permute-start | bytes 36872 | tf_op jit(solution)/shard_map/ppermute | solution.py:279

commit v5 on v4

--- a/solution.py
+++ b/solution.py
@@ -1,3 +1,4 @@
+import collections
 import functools
 import math
 
@@ -226,13 +227,11 @@
     )
 
 
-def rim_kernel(spread_ref, inner_ref, low_ref, high_ref, *, count):
-    width, slots = spread_ref.shape[1], low_ref.shape[0]
-    for k, out_ref in enumerate((low_ref, high_ref)):
-        start = 2 * count + k * slots
-        out_ref[...] = mm_nt(
-            spread_ref[start : start + slots, :], inner_ref[width : 2 * width, :]
-        ).astype(BF)
+def rim_kernel(spread_ref, inner_ref, out_ref, *, count):
+    width, slots = spread_ref.shape[1], out_ref.shape[0]
+    rows = mm_nt(spread_ref[2 * count :, :], inner_ref[width : 2 * width, :]).astype(BF)
+    out_ref[: slots // 2, :] = rows[slots // 2 :]
+    out_ref[slots // 2 :, :] = rows[: slots // 2]
 
 
 def grads_kernel(spread_ref, inner_ref, partial_ref, fresh_ref, preact_ref, nodes_ref, edges_ref):
@@ -251,13 +250,13 @@
         ).astype(BF)
 
 
-def rims_kernel(lists_ref, partial_ref, low_ref, high_ref, out_ref):
-    count, slots = partial_ref.shape[0], lists_ref.shape[1]
-    rows = lax.broadcasted_iota(jnp.int32, (count, slots), 0)
+def rims_kernel(lists_ref, partial_ref, back_ref, out_ref):
+    count, half = partial_ref.shape[0], lists_ref.shape[1]
+    rows = lax.broadcasted_iota(jnp.int32, (count, half), 0)
     total = partial_ref[...]
-    for k, back_ref in enumerate((low_ref, high_ref)):
+    for k in range(2):
         pick = jnp.where(rows == lists_ref[k : k + 1, :], 1.0, 0.0).astype(BF)
-        total += mm(pick, back_ref[...])
+        total += mm(pick, back_ref[k * half : (k + 1) * half, :])
     out_ref[...] = total
 
 
@@ -308,6 +307,9 @@
     return total.reshape(-1), vectors.reshape(-1)
 
 
+Sides = collections.namedtuple("Sides", ("early", "late", "last"))
+
+
 class Halving:
     def __init__(self, rows, columns, orders, carries):
         self.core_bit, (self.first, self.second) = lax.axis_size("patch"), orders
@@ -341,8 +343,32 @@
         zero, one = self.place(self.first, 0, position), self.place(self.second, 1, position)
         return pl.multiple_of(jnp.where(core == 1, one, zero), 8)
 
-    def extra(self, vec_width):
-        return 16 * (vec_width // self.width) if self.carries else 0
+    def pieces(self, full):
+        return full // self.width
+
+    def extra(self, full):
+        return 16 * self.pieces(full) if self.carries else 0
+
+    def slots(self, step, rows):
+        if not self.carries:
+            return 0
+        bits = (self.first[step], self.second[step])
+        return rows if 1 in bits else rows // 2 if min(bits) < self.core_bit else 0
+
+    def taken(self, step):
+        place = lax.rem(self.me(), self.core_bit)
+        even = lax.rem(place, 2) == 0
+        answers = []
+        for bit in (self.first[step], self.second[step]):
+            if bit == 1 or bit > self.core_bit:
+                answers.append((bit == 1, bit == 1))
+                continue
+            between = lax.rem(place, bit) // 2
+            up = jnp.logical_and(even, between == 0)
+            down = jnp.logical_and(jnp.logical_not(even), between == bit // 2 - 1)
+            answers.append((up, down))
+        core = self.core() == 1
+        return tuple(jnp.where(core, b, a) for a, b in zip(*answers))
 
 
 def first_kernel(weights_ref, *refs, plan):
@@ -379,65 +405,102 @@
     halve(src_ref, got_ref, out_ref, plan, step, 0)
 
 
+def unpack(got_ref, start, rows, plan, full):
+    parts = [
+        got_ref[start + k * rows : start + (k + 1) * rows, :] for k in range(plan.pieces(full))
+    ]
+    return jnp.concatenate(parts, axis=1).astype(F32)
+
+
+def pack(out_ref, start, values, plan):
+    rows = values.shape[0]
+    for k in range(plan.pieces(values.shape[1])):
+        out_ref[start + k * rows : start + (k + 1) * rows, :] = values[
+            :, k * plan.width : (k + 1) * plan.width
+        ].astype(BF)
+
+
 def add_vectors(vec_ref, got_ref, start, plan):
-    pieces = vec_ref.shape[1] // plan.width
-    count = vec_ref.shape[0]
-    parts = []
-    for k in range(pieces):
-        low = start + 8 * (pieces + k)
-        high = start + 8 * k
-        parts.append(
-            got_ref[high : high + count, :].astype(F32) + got_ref[low : low + count, :].astype(F32)
-        )
-    return vec_ref[...] + jnp.concatenate(parts, axis=1)
+    count, full = vec_ref.shape
+    both = unpack(got_ref, start, 16, plan, full)
+    return vec_ref[...] + (both[:count] + both[8 : 8 + count])
+
+
+def move_halo(state_ref, got_ref, start, plan, step):
+    rows, full = state_ref.shape
+    half = rows // 2
+    slots = plan.slots(step, rows)
+    state = state_ref[...].astype(F32)
+    if not slots:
+        return state
+    came = unpack(got_ref, start, slots, plan, full)
+    up, down = plan.taken(step)
+    return jnp.concatenate(
+        [
+            jnp.where(up, came[:half], state[:half]),
+            jnp.where(down, came[slots - half :], state[half:]),
+        ],
+        axis=0,
+    )
 
 
 def send_kernel(src_ref, got_ref, *refs, plan, step):
     if not plan.carries:
         halve(src_ref, got_ref, refs[0], plan, step, 1)
         return
-    vec_ref, out_ref, new_ref = refs
+    vec_ref, state_ref, out_ref, new_ref, moved_ref = refs
     halve(src_ref, got_ref, out_ref, plan, step, 1)
     half = plan.rows >> (step + 1)
-    count = vec_ref.shape[0]
-    vec = add_vectors(vec_ref, got_ref, 2 * half, plan) if step else vec_ref[...]
-    upper = vec.astype(BF)
-    lower = (vec - upper.astype(F32)).astype(BF)
-    pieces = vec.shape[1] // plan.width
-    out_ref[half:, :] = jnp.zeros_like(out_ref[half:, :])
-    for k in range(pieces):
-        cut = slice(k * plan.width, (k + 1) * plan.width)
-        high, low = half + 8 * k, half + 8 * (pieces + k)
-        out_ref[high : high + count, :] = upper[:, cut]
-        out_ref[low : low + count, :] = lower[:, cut]
-    new_ref[...] = upper.astype(F32) + lower.astype(F32)
-
-
-def vector_kernel(vec_ref, got_ref, new_ref, *, plan):
+    count, full = vec_ref.shape
+    vec, state = vec_ref[...], state_ref[...].astype(F32)
+    if step:
+        vec = add_vectors(vec_ref, got_ref, 2 * half, plan)
+        state = move_halo(state_ref, got_ref, 2 * half + plan.extra(full), plan, step - 1)
+    upper = vec.astype(BF).astype(F32)
+    lower = (vec - upper).astype(BF).astype(F32)
+    gap = jnp.zeros((8 - count, full), F32)
+    pack(out_ref, half, jnp.concatenate([upper, gap, lower, gap], axis=0), plan)
+    new_ref[...] = upper + lower
+    moved_ref[...] = state.astype(BF)
+    rows = state.shape[0]
+    slots = plan.slots(step, rows)
+    if slots == rows:
+        pack(out_ref, half + plan.extra(full), state, plan)
+    elif slots:
+        even = lax.rem(plan.me(), 2) == 0
+        pack(
+            out_ref, half + plan.extra(full),
+            jnp.where(even, state[: rows // 2], state[rows // 2 :]), plan,
+        )
+
+
+def carried_kernel(vec_ref, state_ref, got_ref, new_ref, moved_ref, *, plan):
     new_ref[...] = add_vectors(vec_ref, got_ref, plan.block, plan)
-
-
-def sum_kernel(held_ref, got_ref, out_ref):
-    out_ref[...] = held_ref[...] + got_ref[: held_ref.shape[0], :]
-
-
-def join_kernel(*refs, plans):
-    out_ref = refs[-1]
+    start = plan.block + plan.extra(vec_ref.shape[1])
+    moved_ref[...] = move_halo(state_ref, got_ref, start, plan, plan.steps - 1).astype(BF)
+
+
+def close_kernel(vec_ref, other_ref, *refs, plans):
+    out_ref, vectors_ref = refs[-2:]
     pieces = out_ref.shape[0] // plans[0].block
-    for plan, part_ref in zip(plans, refs):
+    for plan, held_ref, got_ref in zip(plans, refs[0:-2:2], refs[1:-2:2]):
+        total = held_ref[...] + got_ref[: plan.block, :]
         for k in range(0, plan.width, LANES):
             piece = (plan.columns.start + k) // LANES
-            out_ref[pl.ds(piece, plan.block, stride=pieces), :] = part_ref[:, k : k + LANES]
+            out_ref[pl.ds(piece, plan.block, stride=pieces), :] = total[:, k : k + LANES]
+    vec = vec_ref[...] + other_ref[...]
+    for k in range(pieces):
+        vectors_ref[pl.ds(k, vec.shape[0], stride=pieces), :] = vec[:, k * LANES : (k + 1) * LANES]
 
 
 def after(marks, *values):
     return lax.optimization_barrier((*values, *marks))[: len(values)]
 
 
-def reduce_kernels(plans, weights, vec, beside):
-    vec_shape = (vec.shape, F32)
+def reduce_kernels(plans, weights, vec, sides):
+    full = vec.shape[1]
     held = {plan: weights for plan in plans}
-    got, carrier = {}, None
+    got = {}
     marks = ()
     for plan in plans:
         (weights_late,) = after(marks, weights)
@@ -446,20 +509,24 @@
             near(weights_late), name="first",
         )
         got[plan] = permute_by(sent, plan.core_bit, plan.core_bit, plan.core_bit)
-    marks = beside[-1](marks)
+    state = sides.early(marks)
+    marks = (state,)
+    shapes = [(vec.shape, F32), (state.shape, BF)]
     for step in range(plans[0].steps):
+        if step == 1:
+            marks = sides.late(marks)
         for plan in plans:
             half = plan.rows >> (step + 1)
             source, came = after(marks, held[plan], got[plan])
-            rows = half + plan.extra(vec.shape[1])
-            vectors = [near(vec)] if plan.carries else []
+            rows = half + plan.extra(full) + plan.slots(step, state.shape[0]) * plan.pieces(full)
+            carried = [near(vec), near(state)] if plan.carries else []
             sent, *new = call(
                 functools.partial(send_kernel, plan=plan, step=step),
-                [((rows, plan.width), BF)] + ([vec_shape] if plan.carries else []),
-                near(source), near(came), *vectors, name=f"send{step}",
+                [((rows, plan.width), BF)] + (shapes if plan.carries else []),
+                near(source), near(came), *carried, name=f"send{step}",
             )
             if plan.carries:
-                (vec,) = new
+                vec, state = new
             marks = (sent,)
             source, came = after(marks, source, came)
             incoming = permute_by(sent, plan.first[step], plan.second[step], plan.core_bit)
@@ -468,33 +535,29 @@
                 [((half, plan.width), F32)], near(source), near(came), name=f"keep{step}",
             )
             got[plan] = incoming
-        if step in beside:
-            marks = beside[step](marks)
-    for plan in plans:
-        if plan.carries:
-            (vec,) = call(
-                functools.partial(vector_kernel, plan=plan), [vec_shape], near(vec), near(got[plan]),
-                name="vectors",
-            )
-            vec = vec + permute_by(vec, plan.core_bit, plan.core_bit, plan.core_bit)
-    parts = []
-    for plan in plans:
-        source, came = after(marks, held[plan], got[plan])
-        marks = call(
-            sum_kernel, [((plan.block, plan.width), F32)], near(source), near(came), name="sum"
-        )
-        parts.append(near(marks[0]))
-    (out,) = call(
-        functools.partial(join_kernel, plans=plans),
-        [((plans[0].block * weights.shape[1] // LANES, LANES), F32)], *parts, name="join", plain=(0,),
-    )
-    return out.reshape(-1), vec.reshape(-1)
-
-
-def make_plans(rows, width):
+    (carrier,) = [plan for plan in plans if plan.carries]
+    vec, state = call(
+        functools.partial(carried_kernel, plan=carrier), shapes, near(vec), near(state),
+        near(got[carrier]), name="carried",
+    )
+    other = permute_by(vec, carrier.core_bit, carrier.core_bit, carrier.core_bit)
+    sides.last(state)
+    pairs = [near(a) for plan in plans for a in (held[plan], got[plan])]
+    out, vectors = call(
+        functools.partial(close_kernel, plans=plans),
+        [
+            ((plans[0].block * weights.shape[1] // LANES, LANES), F32),
+            ((vec.size // LANES, LANES), F32),
+        ],
+        near(vec), near(other), *pairs, name="close", plain=(0, 1),
+    )
+    return out.reshape(-1), vectors.reshape(-1)
+
+
+def make_plans(rows, width, slots):
     count = lax.axis_size("region") * lax.axis_size("patch")
     core_bit, first, second = halving_orders()
-    if rows % (16 * count) or width % (4 * LANES):
+    if rows % (16 * count) or width % (4 * LANES) or slots % 32:
         return []
     high = [b for b in first if b > core_bit]
     low = [b for b in first if b < core_bit]
@@ -530,7 +593,7 @@
     picked = 2 * count + -(-slots // LANES) * LANES
     edge_rows = 3 * width + hidden_width
     weight_rows = edge_rows + 2 * width + hidden_width
-    plans = make_plans(weight_rows, hidden_width)
+    plans = make_plans(weight_rows, hidden_width, slots)
     edge_shift, edge_offset, edge_gain, node_shift, node_offset, node_gain = (
         v.reshape(1, -1)
         for v in (edge_shift, edge_offset, edge_gain, node_shift, node_offset, node_gain)
@@ -592,14 +655,13 @@
 
     def rim_side(marks):
         (spread_late,) = after(marks, spread)
-        rim_low, rim_high = call(
-            functools.partial(rim_kernel, count=count), [((half, width), BF)] * 2,
+        (rims,) = call(
+            functools.partial(rim_kernel, count=count), [((slots, width), BF)],
             near(spread_late), edge_inner, name="rim", limit=4 << 20,
         )
-        results["low"], results["high"] = ring(rim_high, 1), ring(rim_low, -1)
-        return rim_low, rim_high
-
-    def edge_side(marks):
+        return rims
+
+    def grads_side(marks):
         spread_late, fresh_late = after(marks, spread, fresh)
         results["nodes"], results["edges"] = call(
             grads_kernel,
@@ -607,21 +669,23 @@
             near(spread_late), edge_inner, near(partial), near(fresh_late), near(preact),
             name="grads", flops=2 << 30, plain=(1,),
         )
-        return results["nodes"], results["low"], results["high"]
-
-    def node_side(marks):
-        (part_late,) = after(marks, results["nodes"])
+        return (results["nodes"],)
+
+    def halo_side(back):
         (results["nodes"],) = call(
-            rims_kernel, [((count, width), F32)], lists, near(part_late),
-            near(results["low"]), near(results["high"]), name="rims", plain=(0,), limit=4 << 20,
-        )
-        return (results["nodes"],)
+            rims_kernel, [((count, width), F32)], lists, near(results["nodes"]), near(back),
+            name="rims", plain=(0,), limit=4 << 20,
+        )
 
     if plans:
-        grad_weights, grad_vectors = reduce_kernels(plans, weights, sums, {-1: rim_side, 0: edge_side, 1: node_side})
+        sides = Sides(rim_side, grads_side, halo_side)
+        grad_weights, grad_vectors = reduce_kernels(plans, weights, sums, sides)
     else:
         grad_weights, grad_vectors = reduce_all(weights, sums)
-        node_side(edge_side(rim_side((sums,))))
+        rims = rim_side((sums,))
+        back = jnp.concatenate([ring(rims[:half], 1), ring(rims[half:], -1)])
+        grads_side((sums,))
+        halo_side(back)
     return (results["nodes"], results["edges"], grad_weights, grad_vectors)
 
 

time: 60 us -> 57.3 us (0.955)
  waiting for transfers between devices: 20 us -> 18.1 us
  local copies, waits for them, and re-layouts: 0.7 us -> 0.09 us
    ppermute x4 -> x2, starting transfers between devices: 10.8 us -> 6.12 us  [ring(): lax.ppermute(values, 'patch', [(i, (i + step) % count) for i in range(cou...]
    ppermute x11, starting transfers between devices: 8.37 us -> 13.1 us  [permute_by(): return lax.ppermute(values, AXES, pairs)]
    ppermute x4 -> x2, waiting for transfers between devices: 4.89 us -> 0.38 us  [ring(): lax.ppermute(values, 'patch', [(i, (i + step) % count) for i in range(cou...]
    ppermute x11, waiting for transfers between devices: 15.1 us -> 17.7 us  [permute_by(): return lax.ppermute(values, AXES, pairs)]
    reshape x1 -> x0, local copies, waits for them, and re-layouts: 0.6 us -> none  [reduce_kernels(): return (out.reshape(-1), vec.reshape(-1))]
    pallas_call x29 -> x27, Pallas kernels: 18.8 us -> 18.8 us  [call(): pl.pallas_call(body, out_shape=shapes, in_specs=[anywhere if i in hbm els...]
  transfers between devices with their start and end apart: 15 -> 13, of which waited for: 9 -> 9; matrix products, arithmetic and copies ran while one was open for 0% -> 0% of each run, Pallas kernels for 11% -> 10%
where the time goes in v5:
time: 57.3 us; the launch traced here: 57.1 us
  starting transfers between devices  19.2 us (34%)
  Pallas kernels  18.8 us (33%)
  waiting for transfers between devices  18.1 us (32%)
  between operations  1.01 us (2%)
    pallas_call x27, Pallas kernels, call(): pl.pallas_call(body, out_shape=shapes, in_specs=[anywhere if i in hbm els...  18.8 us
    ppermute x11, waiting for transfers between devices, permute_by(): return lax.ppermute(values, AXES, pairs)  17.7 us
    ppermute x11, starting transfers between devices, permute_by(): return lax.ppermute(values, AXES, pairs)  13.1 us
    ppermute x2, starting transfers between devices, ring(): lax.ppermute(values, 'patch', [(i, (i + step) % count) for i in range(cou...  6.12 us
  transfers between devices with their start and end apart: 13, of which 9 were waited for; matrix products, arithmetic and copies ran while one was open for 0% of the time, Pallas kernels for 10%

profile of v5, /device:TPU:0, one launch (start us, length us, event | category | flops | bytes accessed | tf_op | source)
XLA Modules:
  0.0 57.1 jit_solution(1139849122096186849)
XLA Ops:
  0.7 1.4 %pick.1 = (bf16[32,512]{1,0:T(8,128)(2,1)S(1)}, bf16[32,512]{1,0:T(8,128)(2,1)S(1)}) custom-call(s32[2,32]{1,0:T(2,128)} %bitcast.11, bf16[256,512]{1,0:T(8,128)(2,1)} %nodes_ref.5), custom_call_target="tpu_custom_call" | custom-call | flops 21474836480 | bytes 65536 | tf_op jit(solution)/shard_map/pick/pallas_call | solution.py:42
  2.2 3.0 %collective-permute-start = (bf16[32,512]{1,0:T(8,128)(2,1)S(1)}, bf16[32,512]{1,0:T(8,128)(2,1)S(1)}, u32[]{:S(2)}, u32[]{:S(2)}) collective-permute-start(bf16[32,512]{1,0:T(8,128)(2,1)S(1)} %get-tuple-element.79), channel_id=1, source_target_pairs={{0,1},{1,2},{2,3},{3,4},{4,5},{5,6},{6,7},{7,0},{8,9},{9,10},{10,1... | collective-permute-start | bytes 98312 | tf_op jit(solution)/shard_map/ppermute | solution.py:265
  5.2 3.1 %collective-permute-start.1 = (bf16[32,512]{1,0:T(8,128)(2,1)S(1)}, bf16[32,512]{1,0:T(8,128)(2,1)S(1)}, u32[]{:S(2)}, u32[]{:S(2)}) collective-permute-start(bf16[32,512]{1,0:T(8,128)(2,1)S(1)} %get-tuple-element.80), channel_id=1, source_target_pairs={{0,7},{1,0},{2,1},{3,2},{4,3},{5,4},{6,5},{7,6},{8,15},{9,8},{10,9... | collective-permute-start | bytes 98312 | tf_op jit(solution)/shard_map/ppermute | solution.py:265
  8.3 1.4 %table.1 = (f32[1024,512]{1,0:T(8,128)S(1)}, bf16[512,512]{1,0:T(8,128)(2,1)S(1)}, bf16[1024,640]{1,0:T(8,128)(2,1)S(1)}, bf16[640,1024]{1,0:T(8,128)(2,1)S(1)}) custom-call(s32[1,1024]{1,0:T(1,128)S(1)} %bitcast.13, s32[1,1024]{1,0:T(1,128)S(1)} %bitcast.14, f32[1,512]{1,0:T(1,128)S(1)} %bitcast.15, bf16[256,512]{1,0:T(8,128)(2,1)S(1)} %copy-done.8, ...), custom_call_target="tpu_custom_call" | custom-call | flops 805306368 | bytes 5242880 | tf_op jit(solution)/shard_map/table/pallas_call | solution.py:42
  9.7 0.4 collective-permute-done.low_ref
  10.2 5.9 %forward.1 = (bf16[1024,512]{1,0:T(8,128)(2,1)S(1)}, f32[1024,512]{1,0:T(8,128)S(1)}, f32[1024,512]{1,0:T(8,128)S(1)}, f32[1024,1]{1,0:T(8,128)S(1)}, bf16[256,5...) custom-call(f32[1024,512]{1,0:T(8,128)S(1)} %get-tuple-element.81.part_ref, ...), custom_call_target="tpu_custom_call" | custom-call | flops 5368709120 | bytes 9185280 | tf_op jit(solution)/shard_map/forward/pallas_call | solution.py:42
  16.1 4.8 %backward.1 = (f32[1024,512]{1,0:T(8,128)S(1)}, bf16[1024,512]{1,0:T(8,128)(2,1)S(1)}, bf16[576,512]{1,0:T(8,128)(2,1)S(1)}, f32[3584,512]{1,0:T(8,128)S(1)}, f32[6,512]{1,0:T(8,128)S(1)}) custom-call(bf16[1024,640]{1,0:T(8,128)(2,1)S(1)} %get-tuple-element.77.pick_ref, bf16[640,1024]{1,0:T(8,128)(2,1)S(1)} %get-tuple-element.78.turned_ref, ...), custom_call_target="tpu_custom_call" | custom-call | flops 5368709120 | bytes 11087872 | tf_op jit(solution)/shard_map/backward/pallas_call | solution.py:42
  20.9 0.1 first.2
  21.1 0.1 first.3
  21.3 0.5 collective-permute-start.2
  21.8 0.3 rim.1.refs_1_
  22.1 1.5 %collective-permute-done.3.got_ref = bf16[1792,256]{1,0:T(8,128)(2,1)S(1)} collective-permute-done((bf16[1792,256]{1,0:T(8,128)(2,1)S(1)}, bf16[1792,256]{1,0:T(8,128)(2,1)S(1)}, u32[]{:S(2)}, u32[]{:S(2)}) %collective-permute-start.3) | collective-permute-done | bytes 917536 | tf_op jit(solution)/shard_map/ppermute | solution.py:278
  23.6 0.1 send0.2
  23.7 1.7 %collective-permute-start.4 = (bf16[1056,256]{1,0:T(8,128)(2,1)S(1)}, bf16[1056,256]{1,0:T(8,128)(2,1)S(1)}, u32[]{:S(2)}, u32[]{:S(2)}) collective-permute-start(bf16[1056,256]{1,0:T(8,128)(2,1)S(1)} %get-tuple-element.98), channel_id=1, source_target_pairs={{0,16},{1,17},{2,18},{3,19},{4,20},{5,21},{6,22},{7,23},{8,9},{9,8... | collective-permute-start | bytes 1622024 | tf_op jit(solution)/shard_map/ppermute | solution.py:278
  25.4 0.1 send0.3
  25.5 1.2 %collective-permute-start.6 = (bf16[896,256]{1,0:T(8,128)(2,1)S(1)}, bf16[896,256]{1,0:T(8,128)(2,1)S(1)}, u32[]{:S(2)}, u32[]{:S(2)}) collective-permute-start(bf16[896,256]{1,0:T(8,128)(2,1)S(1)} %send0.3), channel_id=1, source_target_pairs={{0,16},{1,17},{2,18},{3,19},{4,20},{5,21},{6,22},{7,23},{8,9},{9,8... | collective-permute-start | bytes 1376264 | tf_op jit(solution)/shard_map/ppermute | solution.py:278
  26.8 2.1 %grads.1 = (f32[256,512]{1,0:T(8,128)S(1)}, bf16[1024,512]{1,0:T(8,128)(2,1)}) custom-call(bf16[576,512]{1,0:T(8,128)(2,1)S(1)} %get-tuple-element.101.spread_ref, bf16[1536,512]{1,0:T(8,128)(2,1)S(1)} %copy-done, f32[256,512]{1,0:T(8,128)S(1)} %get-tuple-element.102.partial_ref, f32[1024,512]{1,0:T(8,128)S(1)} %get-tuple-element.103.fresh_ref, ...), custom_call_target="tpu_custom_call" | custom-call | flops 2147483648 | bytes 1572864 | tf_op jit(solution)/shard_map/grads/pallas_call | solution.py:42
  28.9 4.3 %collective-permute-done.4.got_ref = bf16[1056,256]{1,0:T(8,128)(2,1)S(1)} collective-permute-done((bf16[1056,256]{1,0:T(8,128)(2,1)S(1)}, bf16[1056,256]{1,0:T(8,128)(2,1)S(1)}, u32[]{:S(2)}, u32[]{:S(2)}) %collective-permute-start.4) | collective-permute-done | bytes 540704 | tf_op jit(solution)/shard_map/ppermute | solution.py:278
  33.2 1.4 %collective-permute-start.5 = (bf16[608,256]{1,0:T(8,128)(2,1)S(1)}, bf16[608,256]{1,0:T(8,128)(2,1)S(1)}, u32[]{:S(2)}, u32[]{:S(2)}) collective-permute-start(bf16[608,256]{1,0:T(8,128)(2,1)S(1)} %get-tuple-element.112), channel_id=1, source_target_pairs={{0,1},{1,0},{2,3},{3,2},{4,5},{5,4},{6,7},{7,6},{8,10},{9,11},{10,... | collective-permute-start | bytes 933896 | tf_op jit(solution)/shard_map/ppermute | solution.py:278
  34.8 3.3 %collective-permute-done.6.got_ref = bf16[896,256]{1,0:T(8,128)(2,1)S(1)} collective-permute-done((bf16[896,256]{1,0:T(8,128)(2,1)S(1)}, bf16[896,256]{1,0:T(8,128)(2,1)S(1)}, u32[]{:S(2)}, u32[]{:S(2)}) %collective-permute-start.6) | collective-permute-done | bytes 458784 | tf_op jit(solution)/shard_map/ppermute | solution.py:278
  38.1 1.4 %collective-permute-start.8 = (bf16[448,256]{1,0:T(8,128)(2,1)S(1)}, bf16[448,256]{1,0:T(8,128)(2,1)S(1)}, u32[]{:S(2)}, u32[]{:S(2)}) collective-permute-start(bf16[448,256]{1,0:T(8,128)(2,1)S(1)} %send1.3), channel_id=1, source_target_pairs={{0,1},{1,0},{2,3},{3,2},{4,5},{5,4},{6,7},{7,6},{8,10},{9,11},{10,... | collective-permute-start | bytes 688136 | tf_op jit(solution)/shard_map/ppermute | solution.py:278
  39.6 1.0 %collective-permute-done.5.got_ref = bf16[608,256]{1,0:T(8,128)(2,1)S(1)} collective-permute-done((bf16[608,256]{1,0:T(8,128)(2,1)S(1)}, bf16[608,256]{1,0:T(8,128)(2,1)S(1)}, u32[]{:S(2)}, u32[]{:S(2)}) %collective-permute-start.5) | collective-permute-done | bytes 311328 | tf_op jit(solution)/shard_map/ppermute | solution.py:278
  40.6 1.3 %collective-permute-start.7 = (bf16[320,256]{1,0:T(8,128)(2,1)S(1)}, bf16[320,256]{1,0:T(8,128)(2,1)S(1)}, u32[]{:S(2)}, u32[]{:S(2)}) collective-permute-start(bf16[320,256]{1,0:T(8,128)(2,1)S(1)} %get-tuple-element.123), channel_id=1, source_target_pairs={{0,2},{1,3},{2,0},{3,1},{4,6},{5,7},{6,4},{7,5},{8,24},{9,25},{10,... | collective-permute-start | bytes 491528 | tf_op jit(solution)/shard_map/ppermute | solution.py:278
  42.0 2.2 %collective-permute-done.8.got_ref = bf16[448,256]{1,0:T(8,128)(2,1)S(1)} collective-permute-done((bf16[448,256]{1,0:T(8,128)(2,1)S(1)}, bf16[448,256]{1,0:T(8,128)(2,1)S(1)}, u32[]{:S(2)}, u32[]{:S(2)}) %collective-permute-start.8) | collective-permute-done | bytes 229408 | tf_op jit(solution)/shard_map/ppermute | solution.py:278
  44.2 1.0 %collective-permute-start.11 = (bf16[224,256]{1,0:T(8,128)(2,1)S(1)}, bf16[224,256]{1,0:T(8,128)(2,1)S(1)}, u32[]{:S(2)}, u32[]{:S(2)}) collective-permute-start(bf16[224,256]{1,0:T(8,128)(2,1)S(1)} %send2.3), channel_id=1, source_target_pairs={{0,2},{1,3},{2,0},{3,1},{4,6},{5,7},{6,4},{7,5},{8,24},{9,25},{10,... | collective-permute-start | bytes 344072 | tf_op jit(solution)/shard_map/ppermute | solution.py:278
  45.3 0.8 %collective-permute-done.7.got_ref = bf16[320,256]{1,0:T(8,128)(2,1)S(1)} collective-permute-done((bf16[320,256]{1,0:T(8,128)(2,1)S(1)}, bf16[320,256]{1,0:T(8,128)(2,1)S(1)}, u32[]{:S(2)}, u32[]{:S(2)}) %collective-permute-start.7) | collective-permute-done | bytes 163872 | tf_op jit(solution)/shard_map/ppermute | solution.py:278
  46.1 2.3 %collective-permute-start.9 = (bf16[208,256]{1,0:T(8,128)(2,1)S(1)}, bf16[208,256]{1,0:T(8,128)(2,1)S(1)}, u32[]{:S(2)}, u32[]{:S(2)}) collective-permute-start(bf16[208,256]{1,0:T(8,128)(2,1)S(1)} %get-tuple-element.136), channel_id=1, source_target_pairs={{0,4},{1,5},{2,6},{3,7},{4,0},{5,1},{6,2},{7,3},{8,12},{9,13},{10,... | collective-permute-start | bytes 319496 | tf_op jit(solution)/shard_map/ppermute | solution.py:278
  48.4 1.8 %collective-permute-done.11.got_ref = bf16[224,256]{1,0:T(8,128)(2,1)S(1)} collective-permute-done((bf16[224,256]{1,0:T(8,128)(2,1)S(1)}, bf16[224,256]{1,0:T(8,128)(2,1)S(1)}, u32[]{:S(2)}, u32[]{:S(2)}) %collective-permute-start.11) | collective-permute-done | bytes 114720 | tf_op jit(solution)/shard_map/ppermute | solution.py:278
  50.2 2.0 %collective-permute-start.12 = (bf16[112,256]{1,0:T(8,128)(2,1)S(1)}, bf16[112,256]{1,0:T(8,128)(2,1)S(1)}, u32[]{:S(2)}, u32[]{:S(2)}) collective-permute-start(bf16[112,256]{1,0:T(8,128)(2,1)S(1)} %send3.3), channel_id=1, source_target_pairs={{0,4},{1,5},{2,6},{3,7},{4,0},{5,1},{6,2},{7,3},{8,12},{9,13},{10,... | collective-permute-start | bytes 172040 | tf_op jit(solution)/shard_map/ppermute | solution.py:278
  52.2 2.9 %collective-permute-done.9.got_ref.refs_1_ = bf16[208,256]{1,0:T(8,128)(2,1)S(1)} collective-permute-done((bf16[208,256]{1,0:T(8,128)(2,1)S(1)}, bf16[208,256]{1,0:T(8,128)(2,1)S(1)}, u32[]{:S(2)}, u32[]{:S(2)}) %collective-permute-start.9) | collective-permute-done | bytes 106528 | tf_op jit(solution)/shard_map/ppermute | solution.py:278
  55.3 1.1 %rims.1 = f32[256,512]{1,0:T(8,128)} custom-call(s32[2,32]{1,0:T(2,128)S(1)} %bitcast.12, f32[256,512]{1,0:T(8,128)S(1)} %get-tuple-element.105.partial_ref, bf16[64,512]{1,0:T(8,128)(2,1)S(1)} %get-tuple-element.137.back_ref), custom_call_target="tpu_custom_call" | custom-call | bytes 524288 | tf_op jit(solution)/shard_map/rims/pallas_call | solution.py:42
  56.4 0.7 %close.1 = (f32[448,128]{1,0:T(8,128)}, f32[24,128]{1,0:T(8,128)}) custom-call(f32[6,512]{1,0:T(8,128)S(1)} %get-tuple-element.139.vec_ref, f32[6,512]{1,0:T(8,128)S(1)} %collective-permute-done.10.other_ref, f32[112,256]{1,0:T(8,128)S(1)} %keep3.2.refs_0_, bf16[208,256]{1,0:T(8,128)(2,1)S(1)} %collective-permute-done.9.got_ref.refs_1_, ...), custom_call_target="tpu_custom_call" | custom-call | bytes 241664 | tf_op jit(solution)/shard_map/close/pallas_call | solution.py:42
  (55 shorter events, 0.9 us)
Async XLA Ops:
  0.6 7.7 %copy-start = (bf16[1536,512]{1,0:T(8,128)(2,1)S(1)}, bf16[1536,512]{1,0:T(8,128)(2,1)}, u32[]{:S(2)}) copy-start(bf16[1536,512]{1,0:T(8,128)(2,1)} %inner_ref.5) | copy-start | bytes 4718596
  0.6 7.7 %copy-start.3 = (bf16[1024,512]{1,0:T(8,128)(2,1)S(1)}, bf16[1024,512]{1,0:T(8,128)(2,1)}, u32[]{:S(2)}) copy-start(bf16[1024,512]{1,0:T(8,128)(2,1)} %edges_ref.5) | copy-start | bytes 3145732
  0.7 7.6 %copy-start.8 = (bf16[256,512]{1,0:T(8,128)(2,1)S(1)}, bf16[256,512]{1,0:T(8,128)(2,1)}, u32[]{:S(2)}) copy-start(bf16[256,512]{1,0:T(8,128)(2,1)} %nodes_ref.5) | copy-start | bytes 786436
  0.7 7.6 %copy-start.9 = (s32[1024]{0:T(1024)S(1)}, s32[1024]{0:T(1024)}, u32[]{:S(2)}) copy-start(s32[1024]{0:T(1024)} %param.32) | copy-start | bytes 12292
  0.7 7.6 %copy-start.10 = (s32[1024]{0:T(1024)S(1)}, s32[1024]{0:T(1024)}, u32[]{:S(2)}) copy-start(s32[1024]{0:T(1024)} %param.33) | copy-start | bytes 12292
  0.7 7.6 %copy-start.11 = (f32[512]{0:T(512)S(1)}, f32[512]{0:T(512)}, u32[]{:S(2)}) copy-start(f32[512]{0:T(512)} %param.25) | copy-start | bytes 6148
  2.1 8.1 %copy-start.2 = (bf16[1024,512]{1,0:T(8,128)(2,1)S(1)}, bf16[1024,512]{1,0:T(8,128)(2,1)}, u32[]{:S(2)}) copy-start(bf16[1024,512]{1,0:T(8,128)(2,1)} %ninner_ref.1) | copy-start | bytes 3145732
  2.1 8.1 %copy-start.5 = (bf16[512,512]{1,0:T(8,128)(2,1)S(1)}, bf16[512,512]{1,0:T(8,128)(2,1)}, u32[]{:S(2)}) copy-start(bf16[512,512]{1,0:T(8,128)(2,1)} %nouter_ref.1) | copy-start | bytes 1572868
  2.1 8.1 %copy-start.6 = (bf16[512,512]{1,0:T(8,128)(2,1)S(1)}, bf16[512,512]{1,0:T(8,128)(2,1)}, u32[]{:S(2)}) copy-start(bf16[512,512]{1,0:T(8,128)(2,1)} %eouter_ref.3) | copy-start | bytes 1572868
  2.1 8.0 %copy-start.7 = (bf16[256,512]{1,0:T(8,128)(2,1)S(1)}, bf16[256,512]{1,0:T(8,128)(2,1)}, u32[]{:S(2)}) copy-start(bf16[256,512]{1,0:T(8,128)(2,1)} %cotan_ref.1) | copy-start | bytes 786436
  2.1 8.0 %copy-start.12 = (f32[512]{0:T(512)S(1)}, f32[512]{0:T(512)}, u32[]{:S(2)}) copy-start(f32[512]{0:T(512)} %param.26) | copy-start | bytes 6148
  2.1 8.0 %copy-start.13 = (f32[512]{0:T(512)S(1)}, f32[512]{0:T(512)}, u32[]{:S(2)}) copy-start(f32[512]{0:T(512)} %param.28) | copy-start | bytes 6148
  2.1 8.0 %copy-start.14 = (f32[512]{0:T(512)S(1)}, f32[512]{0:T(512)}, u32[]{:S(2)}) copy-start(f32[512]{0:T(512)} %param.29) | copy-start | bytes 6148
  2.1 8.0 %copy-start.15 = (f32[512]{0:T(512)S(1)}, f32[512]{0:T(512)}, u32[]{:S(2)}) copy-start(f32[512]{0:T(512)} %param.30) | copy-start | bytes 6148
  2.2 8.0 %copy-start.16 = (f32[512]{0:T(512)S(1)}, f32[512]{0:T(512)}, u32[]{:S(2)}) copy-start(f32[512]{0:T(512)} %param.27) | copy-start | bytes 6148
  2.2 8.0 %collective-permute-start = (bf16[32,512]{1,0:T(8,128)(2,1)S(1)}, bf16[32,512]{1,0:T(8,128)(2,1)S(1)}, u32[]{:S(2)}, u32[]{:S(2)}) collective-permute-start(bf16[32,512]{1,0:T(8,128)(2,1)S(1)} %get-tuple-element.79), channel_id=1, source_target_pairs={{0,1},{1,2},{2,3},{3,4},{4,5},{5,6},{6,7},{7,0},{8,9},{9,10},{10,1... | collective-permute-start | bytes 98312 | tf_op jit(solution)/shard_map/ppermute | solution.py:265
  5.2 4.9 %collective-permute-start.1 = (bf16[32,512]{1,0:T(8,128)(2,1)S(1)}, bf16[32,512]{1,0:T(8,128)(2,1)S(1)}, u32[]{:S(2)}, u32[]{:S(2)}) collective-permute-start(bf16[32,512]{1,0:T(8,128)(2,1)S(1)} %get-tuple-element.80), channel_id=1, source_target_pairs={{0,7},{1,0},{2,1},{3,2},{4,3},{5,4},{6,5},{7,6},{8,15},{9,8},{10,9... | collective-permute-start | bytes 98312 | tf_op jit(solution)/shard_map/ppermute | solution.py:265
  10.2 5.9 %copy-start.4 = (bf16[1024,512]{1,0:T(8,128)(2,1)S(1)}, bf16[1024,512]{1,0:T(8,128)(2,1)}, u32[]{:S(2)}) copy-start(bf16[1024,512]{1,0:T(8,128)(2,1)} %ecotan_ref.1) | copy-start | bytes 3145732
  21.1 2.5 %collective-permute-start.3 = (bf16[1792,256]{1,0:T(8,128)(2,1)S(1)}, bf16[1792,256]{1,0:T(8,128)(2,1)S(1)}, u32[]{:S(2)}, u32[]{:S(2)}) collective-permute-start(bf16[1792,256]{1,0:T(8,128)(2,1)S(1)} %first.2), channel_id=1, source_target_pairs={{0,8},{1,9},{2,10},{3,11},{4,12},{5,13},{6,14},{7,15},{8,0},{9,1},... | collective-permute-start | bytes 2752520 | tf_op jit(solution)/shard_map/ppermute | solution.py:278
  21.3 4.1 %collective-permute-start.2 = (bf16[1792,256]{1,0:T(8,128)(2,1)S(1)}, bf16[1792,256]{1,0:T(8,128)(2,1)S(1)}, u32[]{:S(2)}, u32[]{:S(2)}) collective-permute-start(bf16[1792,256]{1,0:T(8,128)(2,1)S(1)} %first.3), channel_id=1, source_target_pairs={{0,8},{1,9},{2,10},{3,11},{4,12},{5,13},{6,14},{7,15},{8,0},{9,1},... | collective-permute-start | bytes 2752520 | tf_op jit(solution)/shard_map/ppermute | solution.py:278
  23.7 9.4 %collective-permute-start.4 = (bf16[1056,256]{1,0:T(8,128)(2,1)S(1)}, bf16[1056,256]{1,0:T(8,128)(2,1)S(1)}, u32[]{:S(2)}, u32[]{:S(2)}) collective-permute-start(bf16[1056,256]{1,0:T(8,128)(2,1)S(1)} %get-tuple-element.98), channel_id=1, source_target_pairs={{0,16},{1,17},{2,18},{3,19},{4,20},{5,21},{6,22},{7,23},{8,9},{9,8... | collective-permute-start | bytes 1622024 | tf_op jit(solution)/shard_map/ppermute | solution.py:278
  25.5 12.5 %collective-permute-start.6 = (bf16[896,256]{1,0:T(8,128)(2,1)S(1)}, bf16[896,256]{1,0:T(8,128)(2,1)S(1)}, u32[]{:S(2)}, u32[]{:S(2)}) collective-permute-start(bf16[896,256]{1,0:T(8,128)(2,1)S(1)} %send0.3), channel_id=1, source_target_pairs={{0,16},{1,17},{2,18},{3,19},{4,20},{5,21},{6,22},{7,23},{8,9},{9,8... | collective-permute-start | bytes 1376264 | tf_op jit(solution)/shard_map/ppermute | solution.py:278
  33.2 7.3 %collective-permute-start.5 = (bf16[608,256]{1,0:T(8,128)(2,1)S(1)}, bf16[608,256]{1,0:T(8,128)(2,1)S(1)}, u32[]{:S(2)}, u32[]{:S(2)}) collective-permute-start(bf16[608,256]{1,0:T(8,128)(2,1)S(1)} %get-tuple-element.112), channel_id=1, source_target_pairs={{0,1},{1,0},{2,3},{3,2},{4,5},{5,4},{6,7},{7,6},{8,10},{9,11},{10,... | collective-permute-start | bytes 933896 | tf_op jit(solution)/shard_map/ppermute | solution.py:278
  38.1 6.1 %collective-permute-start.8 = (bf16[448,256]{1,0:T(8,128)(2,1)S(1)}, bf16[448,256]{1,0:T(8,128)(2,1)S(1)}, u32[]{:S(2)}, u32[]{:S(2)}) collective-permute-start(bf16[448,256]{1,0:T(8,128)(2,1)S(1)} %send1.3), channel_id=1, source_target_pairs={{0,1},{1,0},{2,3},{3,2},{4,5},{5,4},{6,7},{7,6},{8,10},{9,11},{10,... | collective-permute-start | bytes 688136 | tf_op jit(solution)/shard_map/ppermute | solution.py:278
  40.6 5.4 %collective-permute-start.7 = (bf16[320,256]{1,0:T(8,128)(2,1)S(1)}, bf16[320,256]{1,0:T(8,128)(2,1)S(1)}, u32[]{:S(2)}, u32[]{:S(2)}) collective-permute-start(bf16[320,256]{1,0:T(8,128)(2,1)S(1)} %get-tuple-element.123), channel_id=1, source_target_pairs={{0,2},{1,3},{2,0},{3,1},{4,6},{5,7},{6,4},{7,5},{8,24},{9,25},{10,... | collective-permute-start | bytes 491528 | tf_op jit(solution)/shard_map/ppermute | solution.py:278
  44.2 11.1 %copy-start.1 = (s32[1,1,2,32]{3,2,1,0:T(2,128)S(1)}, s32[1,1,2,32]{3,2,1,0:T(2,128)}, u32[]{:S(2)}) copy-start(s32[1,1,2,32]{3,2,1,0:T(2,128)} %param.31) | copy-start | bytes 772
  44.2 6.0 %collective-permute-start.11 = (bf16[224,256]{1,0:T(8,128)(2,1)S(1)}, bf16[224,256]{1,0:T(8,128)(2,1)S(1)}, u32[]{:S(2)}, u32[]{:S(2)}) collective-permute-start(bf16[224,256]{1,0:T(8,128)(2,1)S(1)} %send2.3), channel_id=1, source_target_pairs={{0,2},{1,3},{2,0},{3,1},{4,6},{5,7},{6,4},{7,5},{8,24},{9,25},{10,... | collective-permute-start | bytes 344072 | tf_op jit(solution)/shard_map/ppermute | solution.py:278
  46.1 9.1 %collective-permute-start.9 = (bf16[208,256]{1,0:T(8,128)(2,1)S(1)}, bf16[208,256]{1,0:T(8,128)(2,1)S(1)}, u32[]{:S(2)}, u32[]{:S(2)}) collective-permute-start(bf16[208,256]{1,0:T(8,128)(2,1)S(1)} %get-tuple-element.136), channel_id=1, source_target_pairs={{0,4},{1,5},{2,6},{3,7},{4,0},{5,1},{6,2},{7,3},{8,12},{9,13},{10,... | collective-permute-start | bytes 319496 | tf_op jit(solution)/shard_map/ppermute | solution.py:278
  50.2 6.2 %collective-permute-start.12 = (bf16[112,256]{1,0:T(8,128)(2,1)S(1)}, bf16[112,256]{1,0:T(8,128)(2,1)S(1)}, u32[]{:S(2)}, u32[]{:S(2)}) collective-permute-start(bf16[112,256]{1,0:T(8,128)(2,1)S(1)} %send3.3), channel_id=1, source_target_pairs={{0,4},{1,5},{2,6},{3,7},{4,0},{5,1},{6,2},{7,3},{8,12},{9,13},{10,... | collective-permute-start | bytes 172040 | tf_op jit(solution)/shard_map/ppermute | solution.py:278
  55.2 1.2 %collective-permute-start.10 = (f32[6,512]{1,0:T(8,128)S(1)}, f32[6,512]{1,0:T(8,128)S(1)}, u32[]{:S(2)}, u32[]{:S(2)}) collective-permute-start(f32[6,512]{1,0:T(8,128)S(1)} %get-tuple-element.139.vec_ref), channel_id=1, source_target_pairs={{0,8},{1,9},{2,10},{3,11},{4,12},{5,13},{6,14},{7,15},{8,0},{9,1},... | collective-permute-start | bytes 36872 | tf_op jit(solution)/shard_map/ppermute | solution.py:278

commit v6 on v5

--- a/solution.py
+++ b/solution.py
@@ -102,8 +102,8 @@
 
 
 def table_kernel(
-    senders_ref, receivers_ref, shift_ref, nodes_ref, inner_ref, edges_ref,
-    part_ref, own_ref, pick_ref, turned_ref,
+    senders_ref, receivers_ref, shift_ref, nodes_ref, inner_ref, edges_ref, ninner_ref, nshift_ref,
+    part_ref, npart_ref, pick_ref, turned_ref, own_ref,
 ):
     edge_count, width = edges_ref.shape
     count = nodes_ref.shape[0]
@@ -123,48 +123,55 @@
     nodes = nodes_ref[...]
     own_ref[:count, :] = mm(nodes, inner_ref[width : 2 * width, :]).astype(BF)
     own_ref[count:, :] = mm(nodes, inner_ref[2 * width :, :]).astype(BF)
-    tile = edge_count // 4
+    tile = edge_count // 2
     for start in range(0, edge_count, tile):
-        part_ref[start : start + tile, :] = (
-            mm(edges_ref[start : start + tile, :], inner_ref[:width, :]) + shift_ref[...]
-        )
+        rows = slice(start, start + tile)
+        part_ref[rows, :] = (
+            mm(edges_ref[rows, :], inner_ref[:width, :])
+            + mm(pick_ref[rows, : 2 * count], own_ref[...])
+            + shift_ref[...]
+        )
+    npart_ref[...] = mm(nodes, ninner_ref[:width, :]) + nshift_ref[...]
 
 
 def forward_kernel(
-    part_ref, own_ref, pick_ref, turned_ref, low_ref, high_ref, edges_ref, nodes_ref,
-    einner_ref, eouter_ref, eoffset_ref, egain_ref, nshift_ref, noffset_ref, ngain_ref,
+    part_ref, npart_ref, pick_ref, turned_ref, low_ref, high_ref, edges_ref,
+    einner_ref, eouter_ref, eoffset_ref, egain_ref, noffset_ref, ngain_ref,
     ninner_ref, nouter_ref, cotan_ref,
-    hidden_ref, slope_ref, normed_ref, invstd_ref, pulled_ref, partial_ref, weights_ref, sums_ref,
+    hidden_ref, slope_ref, normed_ref, invstd_ref, pulled_ref, partial_ref, sums_ref,
+    aggregate_ref, node_hidden_ref, node_preact_ref, node_linear_ref,
     *, scale,
 ):
     edge_count, width = edges_ref.shape
-    count = nodes_ref.shape[0]
+    count = cotan_ref.shape[0]
     rim = jnp.concatenate([low_ref[...], high_ref[...]], axis=0)
     far = mm(rim, einner_ref[width : 2 * width, :]).astype(BF)
     slots = rim.shape[0]
-    tile = edge_count // 4
-    total = jnp.zeros((count, width), F32)
-    for start in range(0, edge_count, tile):
-        rows = slice(start, start + tile)
-        preact = (
-            part_ref[rows, :]
-            + mm(pick_ref[rows, : 2 * count], own_ref[...])
-            + mm(pick_ref[rows, 2 * count : 2 * count + slots], far)
-        )
+    tile = edge_count // 2
+    tiles = [slice(start, start + tile) for start in range(0, edge_count, tile)]
+
+    def first(rows):
+        return part_ref[rows, :] + mm(pick_ref[rows, 2 * count : 2 * count + slots], far)
+
+    def second(rows, preact):
         hidden, slope = silu_and_slope(preact)
         hidden = hidden.astype(BF)
         hidden_ref[rows, :] = hidden
         slope_ref[rows, :] = slope
-        normed, invstd = layer_norm(mm(hidden, eouter_ref[...]) + eoffset_ref[...])
+        return mm(hidden, eouter_ref[...]) + eoffset_ref[...]
+
+    def third(rows, linear):
+        normed, invstd = layer_norm(linear)
         normed_ref[rows, :] = normed
         invstd_ref[rows, :] = invstd
         fresh = (edges_ref[rows, :].astype(F32) + egain_ref[...] * normed).astype(BF)
-        total += mm(turned_ref[count : 2 * count, rows], fresh)
+        return mm(turned_ref[count : 2 * count, rows], fresh)
+
+    preacts = [first(rows) for rows in tiles]
+    linears = [second(rows, preact) for rows, preact in zip(tiles, preacts)]
+    total = sum(third(rows, linear) for rows, linear in zip(tiles, linears))
     aggregate = total.astype(BF)
-    nodes = nodes_ref[...]
-    preact = (
-        mm(nodes, ninner_ref[:width, :]) + mm(aggregate, ninner_ref[width:, :]) + nshift_ref[...]
-    )
+    preact = npart_ref[...] + mm(aggregate, ninner_ref[width:, :])
     hidden, slope = silu_and_slope(preact)
     hidden = hidden.astype(BF)
     normed, invstd = layer_norm(mm(hidden, nouter_ref[...]) + noffset_ref[...])
@@ -175,56 +182,86 @@
     preact_half = preact_back.astype(BF)
     pulled_ref[...] = mm_nt(preact_half, ninner_ref[width:, :]).astype(BF)
     partial_ref[...] = cotan + mm_nt(preact_half, ninner_ref[:width, :])
-    hidden_width = preact.shape[1]
-    weights_ref[:width, :] = mm_tn(nodes, preact_half) * scale
-    weights_ref[width : 2 * width, :] = mm_tn(aggregate, preact_half) * scale
-    weights_ref[2 * width :, :] = mm_tn(hidden, linear_half) * scale
+    aggregate_ref[...] = aggregate
+    node_hidden_ref[...] = hidden
+    node_preact_ref[...] = preact_half
+    node_linear_ref[...] = linear_half
     sums_ref[0:1, :] = column_sum(preact_back) * scale
     sums_ref[1:2, :] = column_sum(linear_back) * scale
     sums_ref[2:3, :] = column_sum(cotan * normed) * scale
 
 
 def backward_kernel(
-    pick_ref, turned_ref, edges_ref, ecotan_ref, nodes_ref, low_ref, high_ref, hidden_ref, slope_ref,
-    normed_ref, invstd_ref, pulled_ref, eouter_ref, egain_ref, node_sums_ref, node_weights_ref,
-    fresh_ref, preact_ref, spread_ref, weights_ref, sums_ref, linear_ref, *, scale,
+    pick_ref, turned_ref, ecotan_ref, normed_ref, invstd_ref, slope_ref, pulled_ref, eouter_ref,
+    egain_ref, node_sums_ref,
+    fresh_ref, preact_ref, spread_ref, sums_ref, linear_ref, *, scale,
 ):
-    weights_ref[weights_ref.shape[0] - node_weights_ref.shape[0] :, :] = node_weights_ref[...]
-    edge_count, width = edges_ref.shape
-    count = nodes_ref.shape[0]
-    tile = edge_count // 4
+    edge_count = ecotan_ref.shape[0]
+    count = pulled_ref.shape[0]
+    tile = edge_count // 2
+    tiles = [slice(start, start + tile) for start in range(0, edge_count, tile)]
     sums = [0.0, 0.0, 0.0]
-    for start in range(0, edge_count, tile):
-        rows = slice(start, start + tile)
-        fresh_back = ecotan_ref[rows, :].astype(F32) + mm(
+
+    def first(rows):
+        return ecotan_ref[rows, :].astype(F32) + mm(
             pick_ref[rows, count : 2 * count], pulled_ref[...]
         )
+
+    def second(rows, fresh_back):
         fresh_ref[rows, :] = fresh_back
         normed = normed_ref[rows, :]
         linear_back = norm_back(fresh_back, normed, invstd_ref[rows, :], egain_ref[...])
         linear_half = linear_back.astype(BF)
         linear_ref[rows, :] = linear_half
-        preact_back = mm_nt(linear_half, eouter_ref[...]) * slope_ref[rows, :]
+        sums[1] += column_sum(linear_back)
+        sums[2] += column_sum(fresh_back * normed)
+        return mm_nt(linear_half, eouter_ref[...])
+
+    def third(rows, back):
+        preact_back = back * slope_ref[rows, :]
         preact_ref[rows, :] = preact_back.astype(BF)
         sums[0] += column_sum(preact_back)
-        sums[1] += column_sum(linear_back)
-        sums[2] += column_sum(fresh_back * normed)
+
+    fresh_backs = [first(rows) for rows in tiles]
+    backs = [second(rows, fresh_back) for rows, fresh_back in zip(tiles, fresh_backs)]
+    for rows, back in zip(tiles, backs):
+        third(rows, back)
     for k in range(3):
         sums_ref[k : k + 1, :] = sums[k] * scale
     sums_ref[3:, :] = node_sums_ref[...]
     used = spread_ref.shape[0]
-    spread = mm(turned_ref[:used, :], preact_ref[...]).astype(BF)
-    spread_ref[...] = spread
-    weights_ref[:width, :] = mm_tn(edges_ref[...], preact_ref[...]) * scale
+    spread_ref[...] = mm(turned_ref[:used, :], preact_ref[...]).astype(BF)
+
+
+def weights_kernel(
+    edges_ref, nodes_ref, low_ref, high_ref, hidden_ref, preact_ref, linear_ref, spread_ref,
+    aggregate_ref, node_hidden_ref, node_preact_ref, node_linear_ref,
+    weights_ref, *sends, columns, scales, plan,
+):
+    count = nodes_ref.shape[0]
+    nodes = nodes_ref[...]
     rim = jnp.concatenate([low_ref[...], high_ref[...]], axis=0)
-    nodes = nodes_ref[...]
-    weights_ref[width : 2 * width, :] = (
-        mm_tn(nodes, spread[:count]) + mm_tn(rim, spread[2 * count :])
-    ) * scale
-    weights_ref[2 * width : 3 * width, :] = mm_tn(nodes, spread[count : 2 * count]) * scale
-    weights_ref[3 * width : 3 * width + hidden_ref.shape[1], :] = (
-        mm_tn(hidden_ref[...], linear_ref[...]) * scale
-    )
+    node_preact = node_preact_ref[:, columns]
+    start = 0
+    for scale, terms in (
+        (scales[0], [(edges_ref[...], preact_ref[:, columns])]),
+        (scales[0], [(nodes, spread_ref[:count, columns]), (rim, spread_ref[2 * count :, columns])]),
+        (scales[0], [(nodes, spread_ref[count : 2 * count, columns])]),
+        (scales[0], [(hidden_ref[...], linear_ref[:, columns])]),
+        (scales[1], [(nodes, node_preact)]),
+        (scales[1], [(aggregate_ref[...], node_preact)]),
+        (scales[1], [(node_hidden_ref[...], node_linear_ref[:, columns])]),
+    ):
+        value = sum(mm_tn(a, b) for a, b in terms) * scale
+        weights_ref[start : start + value.shape[0], :] = value
+        start += value.shape[0]
+    for send_ref in sends:
+        other = 1 - plan.core()
+        for position in range(plan.count // 2):
+            row = position * plan.block
+            send_ref[row : row + plan.block, :] = weights_ref[
+                pl.ds(plan.source(position, other), plan.block), :
+            ].astype(BF)
 
 
 def rim_kernel(spread_ref, inner_ref, out_ref, *, count):
@@ -242,7 +279,7 @@
         + mm_nt(spread_ref[count : 2 * count, :], inner_ref[2 * width :, :])
     )
     edge_count = preact_ref.shape[0]
-    tile = edge_count // 4
+    tile = edge_count // 2
     for start in range(0, edge_count, tile):
         rows = slice(start, start + tile)
         edges_ref[rows, :] = (
@@ -307,7 +344,7 @@
     return total.reshape(-1), vectors.reshape(-1)
 
 
-Sides = collections.namedtuple("Sides", ("early", "late", "last"))
+Sides = collections.namedtuple("Sides", ("weights", "early", "late", "last"))
 
 
 class Halving:
@@ -371,16 +408,6 @@
         return tuple(jnp.where(core, b, a) for a, b in zip(*answers))
 
 
-def first_kernel(weights_ref, *refs, plan):
-    send_ref = refs[-1]
-    other = 1 - plan.core()
-    for position in range(plan.count // 2):
-        start = position * plan.block
-        send_ref[start : start + plan.block, :] = weights_ref[
-            pl.ds(plan.source(position, other), plan.block), plan.columns
-        ].astype(BF)
-
-
 def halve(src_ref, got_ref, out_ref, plan, step, side):
     half = plan.rows >> (step + 1)
     bit = plan.bit(step)
@@ -395,7 +422,7 @@
     for k in range(per_half):
         low, high = plan.source(k, core), plan.source(k + per_half, core)
         row = pl.multiple_of(jnp.where(chosen == 1, high, low), 8)
-        held = src_ref[pl.ds(row, plan.block), plan.columns]
+        held = src_ref[pl.ds(row, plan.block), :]
         start = pl.multiple_of(chosen * half + k * plan.block, 16)
         got = got_ref[pl.ds(start, plan.block), :]
         out_ref[k * plan.block : (k + 1) * plan.block, :] = (held + got).astype(out_ref.dtype)
@@ -480,10 +507,11 @@
     moved_ref[...] = move_halo(state_ref, got_ref, start, plan, plan.steps - 1).astype(BF)
 
 
-def close_kernel(vec_ref, other_ref, *refs, plans):
-    out_ref, vectors_ref = refs[-2:]
+def close_kernel(lists_ref, partial_ref, back_ref, vec_ref, other_ref, *refs, plans):
+    *refs, out_ref, vectors_ref, nodes_ref = refs
+    rims_kernel(lists_ref, partial_ref, back_ref, nodes_ref)
     pieces = out_ref.shape[0] // plans[0].block
-    for plan, held_ref, got_ref in zip(plans, refs[0:-2:2], refs[1:-2:2]):
+    for plan, held_ref, got_ref in zip(plans, refs[0::2], refs[1::2]):
         total = held_ref[...] + got_ref[: plan.block, :]
         for k in range(0, plan.width, LANES):
             piece = (plan.columns.start + k) // LANES
@@ -497,24 +525,20 @@
     return lax.optimization_barrier((*values, *marks))[: len(values)]
 
 
-def reduce_kernels(plans, weights, vec, sides):
+def reduce_kernels(plans, sides, vec, width):
     full = vec.shape[1]
-    held = {plan: weights for plan in plans}
-    got = {}
+    held, got = {}, {}
     marks = ()
     for plan in plans:
-        (weights_late,) = after(marks, weights)
-        (sent,) = marks = call(
-            functools.partial(first_kernel, plan=plan), [((plan.rows, plan.width), BF)],
-            near(weights_late), name="first",
-        )
+        held[plan], sent = sides.weights(plan, marks)
+        marks = (sent,)
         got[plan] = permute_by(sent, plan.core_bit, plan.core_bit, plan.core_bit)
     state = sides.early(marks)
     marks = (state,)
     shapes = [(vec.shape, F32), (state.shape, BF)]
     for step in range(plans[0].steps):
         if step == 1:
-            marks = sides.late(marks)
+            (nodes,) = marks = sides.late(marks)
         for plan in plans:
             half = plan.rows >> (step + 1)
             source, came = after(marks, held[plan], got[plan])
@@ -541,17 +565,18 @@
         near(got[carrier]), name="carried",
     )
     other = permute_by(vec, carrier.core_bit, carrier.core_bit, carrier.core_bit)
-    sides.last(state)
     pairs = [near(a) for plan in plans for a in (held[plan], got[plan])]
-    out, vectors = call(
+    out, vectors, nodes = call(
         functools.partial(close_kernel, plans=plans),
         [
-            ((plans[0].block * weights.shape[1] // LANES, LANES), F32),
+            ((plans[0].block * width // LANES, LANES), F32),
             ((vec.size // LANES, LANES), F32),
+            (nodes.shape, F32),
         ],
-        near(vec), near(other), *pairs, name="close", plain=(0, 1),
-    )
-    return out.reshape(-1), vectors.reshape(-1)
+        sides.last, near(nodes), near(state), near(vec), near(other), *pairs, name="close",
+        plain=(0, 1, 2),
+    )
+    return out.reshape(-1), vectors.reshape(-1), nodes
 
 
 def make_plans(rows, width, slots):
@@ -609,18 +634,20 @@
     low = ring(out_high, 1)
     high = ring(out_low, -1)
 
-    part, own, pick, turned = call(
+    part, npart, pick, turned = call(
         table_kernel,
         [
             ((edge_count, hidden_width), F32),
-            ((2 * count, hidden_width), BF),
+            ((count, hidden_width), F32),
             ((edge_count, picked), BF),
             ((picked, edge_count), BF),
         ],
         senders.reshape(1, -1), receivers.reshape(1, -1), edge_shift, nodes, edge_inner, edges,
-        name="table", flops=2 * (edge_count + 2 * count) * width * hidden_width,
-    )
-    hidden, slope, normed, invstd, pulled, partial, node_weights, node_sums = call(
+        node_inner, node_shift,
+        name="table", flops=4 * edge_count * width * hidden_width,
+        scratch=[pltpu.VMEM((2 * count, hidden_width), BF)],
+    )
+    hidden, slope, normed, invstd, pulled, partial, node_sums, *node_terms = call(
         functools.partial(forward_kernel, scale=node_norm),
         [
             ((edge_count, hidden_width), BF),
@@ -629,28 +656,45 @@
             ((edge_count, 1), F32),
             ((count, width), BF),
             ((count, width), F32),
-            ((weight_rows - edge_rows, hidden_width), F32),
             ((3, width), F32),
+            ((count, width), BF),
+            ((count, hidden_width), BF),
+            ((count, hidden_width), BF),
+            ((count, width), BF),
         ],
-        near(part), near(own), near(pick), near(turned), near(low), near(high), edges, nodes,
-        edge_inner, edge_outer, edge_offset, edge_gain, node_shift, node_offset, node_gain,
+        near(part), near(npart), near(pick), near(turned), near(low), near(high), edges,
+        edge_inner, edge_outer, edge_offset, edge_gain, node_offset, node_gain,
         node_inner, node_outer, node_cotan, name="forward", flops=5 << 30,
     )
-    fresh, preact, spread, weights, sums = call(
+    fresh, preact, spread, sums, linear = call(
         functools.partial(backward_kernel, scale=edge_norm),
         [
             ((edge_count, width), F32),
             ((edge_count, hidden_width), BF),
             ((2 * count + slots, hidden_width), BF),
-            ((weight_rows, hidden_width), F32),
             ((6, width), F32),
+            ((edge_count, width), BF),
         ],
-        near(pick), near(turned), edges, edge_cotan, nodes, near(low),
-        near(high), near(hidden), near(slope), near(normed), near(invstd), near(pulled),
-        edge_outer, edge_gain, near(node_sums), near(node_weights),
-        name="backward", flops=5 << 30,
-        scratch=[pltpu.VMEM((edge_count, width), BF)],
-    )
+        near(pick), near(turned), edge_cotan, near(normed), near(invstd), near(slope), near(pulled),
+        edge_outer, edge_gain, near(node_sums),
+        name="backward", flops=3 << 30,
+    )
+
+    def weights_of(plan, marks):
+        preact_late, linear_late = after(marks, preact, linear)
+        columns = plan.columns if plan else slice(0, hidden_width)
+        chunk = columns.stop - columns.start
+        sends = [((plan.rows, chunk), BF)] if plan else []
+        return call(
+            functools.partial(
+                weights_kernel, columns=columns, scales=(edge_norm, node_norm), plan=plan
+            ),
+            [((weight_rows, chunk), F32)] + sends,
+            edges, nodes, near(low), near(high), near(hidden), near(preact_late), near(linear_late),
+            near(spread), *[near(a) for a in node_terms],
+            name="weights", flops=chunk << 22,
+        )
+
     results = {}
 
     def rim_side(marks):
@@ -671,22 +715,20 @@
         )
         return (results["nodes"],)
 
-    def halo_side(back):
-        (results["nodes"],) = call(
-            rims_kernel, [((count, width), F32)], lists, near(results["nodes"]), near(back),
-            name="rims", plain=(0,), limit=4 << 20,
-        )
-
     if plans:
-        sides = Sides(rim_side, grads_side, halo_side)
-        grad_weights, grad_vectors = reduce_kernels(plans, weights, sums, sides)
+        grad_weights, grad_vectors, grad_nodes = reduce_kernels(
+            plans, Sides(weights_of, rim_side, grads_side, lists), sums, hidden_width
+        )
     else:
-        grad_weights, grad_vectors = reduce_all(weights, sums)
+        grad_weights, grad_vectors = reduce_all(weights_of(None, ())[0], sums)
         rims = rim_side((sums,))
         back = jnp.concatenate([ring(rims[:half], 1), ring(rims[half:], -1)])
         grads_side((sums,))
-        halo_side(back)
-    return (results["nodes"], results["edges"], grad_weights, grad_vectors)
+        (grad_nodes,) = call(
+            rims_kernel, [((count, width), F32)], lists, near(results["nodes"]), near(back),
+            name="rims", plain=(0,), limit=4 << 20,
+        )
+    return (grad_nodes, results["edges"], grad_weights, grad_vectors)
 
 
 def solution(mesh):

time: 57.3 us -> 55.1 us (0.962)
  Pallas kernels: 18.8 us -> 17.3 us
  starting transfers between devices: 19.2 us -> 18.6 us
    pallas_call x27 -> x26, Pallas kernels: 18.8 us -> 17.3 us  [call(): pl.pallas_call(body, out_shape=shapes, in_specs=[anywhere if i in hbm els...]
    ppermute x11, starting transfers between devices: 13.1 us -> 12.4 us  [permute_by(): return lax.ppermute(values, AXES, pairs)]
  transfers between devices with their start and end apart: 13 -> 13, of which waited for: 9 -> 10; matrix products, arithmetic and copies ran while one was open for 0% -> 0% of each run, Pallas kernels for 10% -> 12%
where the time goes in v6:
time: 55.1 us; the launch traced here: 54.9 us
  starting transfers between devices  18.6 us (34%)
  waiting for transfers between devices  18 us (33%)
  Pallas kernels  17.3 us (31%)
  between operations  1.03 us (2%)
    ppermute x11, waiting for transfers between devices, permute_by(): return lax.ppermute(values, AXES, pairs)  18 us
    pallas_call x26, Pallas kernels, call(): pl.pallas_call(body, out_shape=shapes, in_specs=[anywhere if i in hbm els...  17.3 us
    ppermute x11, starting transfers between devices, permute_by(): return lax.ppermute(values, AXES, pairs)  12.4 us
    ppermute x2, starting transfers between devices, ring(): lax.ppermute(values, 'patch', [(i, (i + step) % count) for i in range(cou...  6.12 us
  transfers between devices with their start and end apart: 13, of which 10 were waited for; matrix products, arithmetic and copies ran while one was open for 0% of the time, Pallas kernels for 12%

profile of v6, /device:TPU:0, one launch (start us, length us, event | category | flops | bytes accessed | tf_op | source)
XLA Modules:
  0.0 54.9 jit_solution(13362925693092882979)
XLA Ops:
  0.7 1.3 %pick.1 = (bf16[32,512]{1,0:T(8,128)(2,1)S(1)}, bf16[32,512]{1,0:T(8,128)(2,1)S(1)}) custom-call(s32[2,32]{1,0:T(2,128)} %bitcast.11, bf16[256,512]{1,0:T(8,128)(2,1)} %nodes_ref.5), custom_call_target="tpu_custom_call" | custom-call | flops 21474836480 | bytes 65536 | tf_op jit(solution)/shard_map/pick/pallas_call | solution.py:42
  2.2 3.0 %collective-permute-start = (bf16[32,512]{1,0:T(8,128)(2,1)S(1)}, bf16[32,512]{1,0:T(8,128)(2,1)S(1)}, u32[]{:S(2)}, u32[]{:S(2)}) collective-permute-start(bf16[32,512]{1,0:T(8,128)(2,1)S(1)} %get-tuple-element.92), channel_id=1, source_target_pairs={{0,1},{1,2},{2,3},{3,4},{4,5},{5,6},{6,7},{7,0},{8,9},{9,10},{10,1... | collective-permute-start | bytes 98312 | tf_op jit(solution)/shard_map/ppermute | solution.py:302
  5.2 3.1 %collective-permute-start.1 = (bf16[32,512]{1,0:T(8,128)(2,1)S(1)}, bf16[32,512]{1,0:T(8,128)(2,1)S(1)}, u32[]{:S(2)}, u32[]{:S(2)}) collective-permute-start(bf16[32,512]{1,0:T(8,128)(2,1)S(1)} %get-tuple-element.93), channel_id=1, source_target_pairs={{0,7},{1,0},{2,1},{3,2},{4,3},{5,4},{6,5},{7,6},{8,15},{9,8},{10,9... | collective-permute-start | bytes 98312 | tf_op jit(solution)/shard_map/ppermute | solution.py:302
  8.3 1.9 %table.1 = (f32[1024,512]{1,0:T(8,128)S(1)}, f32[256,512]{1,0:T(8,128)S(1)}, bf16[1024,640]{1,0:T(8,128)(2,1)S(1)}, bf16[640,1024]{1,0:T(8,128)(2,1)S(1)}) custom-call(s32[1,1024]{1,0:T(1,128)S(1)} %bitcast.13, s32[1,1024]{1,0:T(1,128)S(1)} %bitcast.14, f32[1,512]{1,0:T(1,128)S(1)} %bitcast.15, bf16[256,512]{1,0:T(8,128)(2,1)S(1)} %copy-done.2, ...), custom_call_target="tpu_custom_call" | custom-call | flops 1073741824 | bytes 5242880 | tf_op jit(solution)/shard_map/table/pallas_call | solution.py:42
  10.3 4.1 %forward.1 = (bf16[1024,512]{1,0:T(8,128)(2,1)S(1)}, f32[1024,512]{1,0:T(8,128)S(1)}, f32[1024,512]{1,0:T(8,128)S(1)}, f32[1024,1]{1,0:T(8,128)S(1)}, bf16[256,5...) custom-call(f32[1024,512]{1,0:T(8,128)S(1)} %get-tuple-element.90.pa, ...), custom_call_target="tpu_custom_call" | custom-call | flops 5368709120 | bytes 7088128 | tf_op jit(solution)/shard_map/forward/pallas_call | solution.py:42
  14.4 2.6 %backward.1 = (f32[1024,512]{1,0:T(8,128)S(1)}, bf16[1024,512]{1,0:T(8,128)(2,1)S(1)}, bf16[576,512]{1,0:T(8,128)(2,1)S(1)}, f32[6,512]{1,0:T(8,128)S(1)}, bf16[1024,512]{1,0:T(8,128)(2,1)S(1)}) custom-call(bf16[1024,640]{1,0:T(8,128)(2,1)S(1)} %get-tuple-element.88.pick_ref, bf16[640,1024]{1,0:T(8,128)(2,1)S(1)} %get-tuple-element.89.turned_ref, ...), custom_call_target="tpu_custom_call" | custom-call | flops 3221225472 | bytes 4796416 | tf_op jit(solution)/shard_map/backward/pallas_call | solution.py:42
  17.1 1.5 %weights.2 = (f32[3584,256]{1,0:T(8,128)S(1)}, bf16[1792,256]{1,0:T(8,128)(2,1)S(1)}) custom-call(bf16[1024,512]{1,0:T(8,128)(2,1)S(1)} %copy-done, bf16[256,512]{1,0:T(8,128)(2,1)S(1)} %copy-done.2, bf16[32,512]{1,0:T(8,128)(2,1)S(1)} %collective-permute-done.low_ref, bf16[32,512]{1,0:T(8,128)(2,1)S(1)} %collective-permute-done.1.high_ref, ...), custom_call_target="tpu_custom_call" | custom-call | flops 1073741824 | bytes 4587520 | tf_op jit(solution)/shard_map/weights/pallas_call | solution.py:42
  18.7 1.5 %weights.3 = (f32[3584,256]{1,0:T(8,128)S(1)}, bf16[1792,256]{1,0:T(8,128)(2,1)S(1)}) custom-call(bf16[1024,512]{1,0:T(8,128)(2,1)S(1)} %copy-done, bf16[256,512]{1,0:T(8,128)(2,1)S(1)} %copy-done.2, bf16[32,512]{1,0:T(8,128)(2,1)S(1)} %collective-permute-done.low_ref, bf16[32,512]{1,0:T(8,128)(2,1)S(1)} %collective-permute-done.1.high_ref, ...), custom_call_target="tpu_custom_call" | custom-call | flops 1073741824 | bytes 4587520 | tf_op jit(solution)/shard_map/weights/pallas_call | solution.py:42
  20.2 0.5 collective-permute-start.2
  20.8 0.3 rim.1.refs_1_
  21.0 0.1 collective-permute-done.3.got_ref
  21.2 0.1 send0.2
  21.3 1.7 %collective-permute-start.4 = (bf16[1056,256]{1,0:T(8,128)(2,1)S(1)}, bf16[1056,256]{1,0:T(8,128)(2,1)S(1)}, u32[]{:S(2)}, u32[]{:S(2)}) collective-permute-start(bf16[1056,256]{1,0:T(8,128)(2,1)S(1)} %get-tuple-element.120), channel_id=1, source_target_pairs={{0,16},{1,17},{2,18},{3,19},{4,20},{5,21},{6,22},{7,23},{8,9},{9,8... | collective-permute-start | bytes 1622024 | tf_op jit(solution)/shard_map/ppermute | solution.py:315
  23.0 1.6 %collective-permute-start.6 = (bf16[896,256]{1,0:T(8,128)(2,1)S(1)}, bf16[896,256]{1,0:T(8,128)(2,1)S(1)}, u32[]{:S(2)}, u32[]{:S(2)}) collective-permute-start(bf16[896,256]{1,0:T(8,128)(2,1)S(1)} %send0.3), channel_id=1, source_target_pairs={{0,16},{1,17},{2,18},{3,19},{4,20},{5,21},{6,22},{7,23},{8,9},{9,8... | collective-permute-start | bytes 1376264 | tf_op jit(solution)/shard_map/ppermute | solution.py:315
  24.7 2.0 %grads.1 = (f32[256,512]{1,0:T(8,128)S(1)}, bf16[1024,512]{1,0:T(8,128)(2,1)}) custom-call(bf16[576,512]{1,0:T(8,128)(2,1)S(1)} %get-tuple-element.123.spread_ref, bf16[1536,512]{1,0:T(8,128)(2,1)S(1)} %copy-done.1, f32[256,512]{1,0:T(8,128)S(1)} %get-tuple-element.124.partial_ref, f32[1024,512]{1,0:T(8,128)S(1)} %get-tuple-element.125.fresh_ref, ...), custom_call_target="tpu_custom_call" | custom-call | flops 2147483648 | bytes 1572864 | tf_op jit(solution)/shard_map/grads/pallas_call | solution.py:42
  26.7 4.0 %collective-permute-done.4.got_ref = bf16[1056,256]{1,0:T(8,128)(2,1)S(1)} collective-permute-done((bf16[1056,256]{1,0:T(8,128)(2,1)S(1)}, bf16[1056,256]{1,0:T(8,128)(2,1)S(1)}, u32[]{:S(2)}, u32[]{:S(2)}) %collective-permute-start.4) | collective-permute-done | bytes 540704 | tf_op jit(solution)/shard_map/ppermute | solution.py:315
  30.8 1.3 %collective-permute-start.5 = (bf16[608,256]{1,0:T(8,128)(2,1)S(1)}, bf16[608,256]{1,0:T(8,128)(2,1)S(1)}, u32[]{:S(2)}, u32[]{:S(2)}) collective-permute-start(bf16[608,256]{1,0:T(8,128)(2,1)S(1)} %get-tuple-element.133), channel_id=1, source_target_pairs={{0,1},{1,0},{2,3},{3,2},{4,5},{5,4},{6,7},{7,6},{8,10},{9,11},{10,... | collective-permute-start | bytes 933896 | tf_op jit(solution)/shard_map/ppermute | solution.py:315
  32.1 0.1 keep0.3.src_ref
  32.1 3.5 %collective-permute-done.6.got_ref = bf16[896,256]{1,0:T(8,128)(2,1)S(1)} collective-permute-done((bf16[896,256]{1,0:T(8,128)(2,1)S(1)}, bf16[896,256]{1,0:T(8,128)(2,1)S(1)}, u32[]{:S(2)}, u32[]{:S(2)}) %collective-permute-start.6) | collective-permute-done | bytes 458784 | tf_op jit(solution)/shard_map/ppermute | solution.py:315
  35.6 1.3 %collective-permute-start.8 = (bf16[448,256]{1,0:T(8,128)(2,1)S(1)}, bf16[448,256]{1,0:T(8,128)(2,1)S(1)}, u32[]{:S(2)}, u32[]{:S(2)}) collective-permute-start(bf16[448,256]{1,0:T(8,128)(2,1)S(1)} %send1.3), channel_id=1, source_target_pairs={{0,1},{1,0},{2,3},{3,2},{4,5},{5,4},{6,7},{7,6},{8,10},{9,11},{10,... | collective-permute-start | bytes 688136 | tf_op jit(solution)/shard_map/ppermute | solution.py:315
  37.0 1.1 %collective-permute-done.5.got_ref = bf16[608,256]{1,0:T(8,128)(2,1)S(1)} collective-permute-done((bf16[608,256]{1,0:T(8,128)(2,1)S(1)}, bf16[608,256]{1,0:T(8,128)(2,1)S(1)}, u32[]{:S(2)}, u32[]{:S(2)}) %collective-permute-start.5) | collective-permute-done | bytes 311328 | tf_op jit(solution)/shard_map/ppermute | solution.py:315
  38.2 1.1 %collective-permute-start.7 = (bf16[320,256]{1,0:T(8,128)(2,1)S(1)}, bf16[320,256]{1,0:T(8,128)(2,1)S(1)}, u32[]{:S(2)}, u32[]{:S(2)}) collective-permute-start(bf16[320,256]{1,0:T(8,128)(2,1)S(1)} %get-tuple-element.144), channel_id=1, source_target_pairs={{0,2},{1,3},{2,0},{3,1},{4,6},{5,7},{6,4},{7,5},{8,24},{9,25},{10,... | collective-permute-start | bytes 491528 | tf_op jit(solution)/shard_map/ppermute | solution.py:315
  39.4 2.4 %collective-permute-done.8.got_ref = bf16[448,256]{1,0:T(8,128)(2,1)S(1)} collective-permute-done((bf16[448,256]{1,0:T(8,128)(2,1)S(1)}, bf16[448,256]{1,0:T(8,128)(2,1)S(1)}, u32[]{:S(2)}, u32[]{:S(2)}) %collective-permute-start.8) | collective-permute-done | bytes 229408 | tf_op jit(solution)/shard_map/ppermute | solution.py:315
  41.8 0.8 %collective-permute-start.11 = (bf16[224,256]{1,0:T(8,128)(2,1)S(1)}, bf16[224,256]{1,0:T(8,128)(2,1)S(1)}, u32[]{:S(2)}, u32[]{:S(2)}) collective-permute-start(bf16[224,256]{1,0:T(8,128)(2,1)S(1)} %send2.3), channel_id=1, source_target_pairs={{0,2},{1,3},{2,0},{3,1},{4,6},{5,7},{6,4},{7,5},{8,24},{9,25},{10,... | collective-permute-start | bytes 344072 | tf_op jit(solution)/shard_map/ppermute | solution.py:315
  42.6 0.9 %collective-permute-done.7.got_ref = bf16[320,256]{1,0:T(8,128)(2,1)S(1)} collective-permute-done((bf16[320,256]{1,0:T(8,128)(2,1)S(1)}, bf16[320,256]{1,0:T(8,128)(2,1)S(1)}, u32[]{:S(2)}, u32[]{:S(2)}) %collective-permute-start.7) | collective-permute-done | bytes 163872 | tf_op jit(solution)/shard_map/ppermute | solution.py:315
  43.6 2.1 %collective-permute-start.9 = (bf16[208,256]{1,0:T(8,128)(2,1)S(1)}, bf16[208,256]{1,0:T(8,128)(2,1)S(1)}, u32[]{:S(2)}, u32[]{:S(2)}) collective-permute-start(bf16[208,256]{1,0:T(8,128)(2,1)S(1)} %get-tuple-element.157), channel_id=1, source_target_pairs={{0,4},{1,5},{2,6},{3,7},{4,0},{5,1},{6,2},{7,3},{8,12},{9,13},{10,... | collective-permute-start | bytes 319496 | tf_op jit(solution)/shard_map/ppermute | solution.py:315
  45.8 2.0 %collective-permute-done.11.got_ref = bf16[224,256]{1,0:T(8,128)(2,1)S(1)} collective-permute-done((bf16[224,256]{1,0:T(8,128)(2,1)S(1)}, bf16[224,256]{1,0:T(8,128)(2,1)S(1)}, u32[]{:S(2)}, u32[]{:S(2)}) %collective-permute-start.11) | collective-permute-done | bytes 114720 | tf_op jit(solution)/shard_map/ppermute | solution.py:315
  47.8 1.8 %collective-permute-start.12 = (bf16[112,256]{1,0:T(8,128)(2,1)S(1)}, bf16[112,256]{1,0:T(8,128)(2,1)S(1)}, u32[]{:S(2)}, u32[]{:S(2)}) collective-permute-start(bf16[112,256]{1,0:T(8,128)(2,1)S(1)} %send3.3), channel_id=1, source_target_pairs={{0,4},{1,5},{2,6},{3,7},{4,0},{5,1},{6,2},{7,3},{8,12},{9,13},{10,... | collective-permute-start | bytes 172040 | tf_op jit(solution)/shard_map/ppermute | solution.py:315
  49.6 2.9 %collective-permute-done.9.got_ref.refs_1_ = bf16[208,256]{1,0:T(8,128)(2,1)S(1)} collective-permute-done((bf16[208,256]{1,0:T(8,128)(2,1)S(1)}, bf16[208,256]{1,0:T(8,128)(2,1)S(1)}, u32[]{:S(2)}, u32[]{:S(2)}) %collective-permute-start.9) | collective-permute-done | bytes 106528 | tf_op jit(solution)/shard_map/ppermute | solution.py:315
  52.7 0.4 collective-permute-done.12.refs_3_
  53.2 0.7 %collective-permute-done.10.other_ref = f32[6,512]{1,0:T(8,128)S(1)} collective-permute-done((f32[6,512]{1,0:T(8,128)S(1)}, f32[6,512]{1,0:T(8,128)S(1)}, u32[]{:S(2)}, u32[]{:S(2)}) %collective-permute-start.10) | collective-permute-done | bytes 12320 | tf_op jit(solution)/shard_map/ppermute | solution.py:315
  53.8 1.1 %close.1 = (f32[448,128]{1,0:T(8,128)}, f32[24,128]{1,0:T(8,128)}, f32[256,512]{1,0:T(8,128)}) custom-call(s32[2,32]{1,0:T(2,128)S(1)} %bitcast.12, f32[256,512]{1,0:T(8,128)S(1)} %get-tuple-element.126.partial_ref, bf16[64,512]{1,0:T(8,128)(2,1)S(1)} %get-tuple-element.158.back_ref, f32[6,512]{1,0:T(8,128)S(1)} %get-tuple-element.159.vec_ref, ...), custom_call_target="tpu_custom_call" | custom-call | bytes 765952 | tf_op jit(solution)/shard_map/close/pallas_call | solution.py:42
  (54 shorter events, 0.9 us)
Async XLA Ops:
  0.6 7.6 %copy-start = (bf16[1024,512]{1,0:T(8,128)(2,1)S(1)}, bf16[1024,512]{1,0:T(8,128)(2,1)}, u32[]{:S(2)}) copy-start(bf16[1024,512]{1,0:T(8,128)(2,1)} %edges_ref.7) | copy-start | bytes 3145732
  0.6 7.6 %copy-start.1 = (bf16[1536,512]{1,0:T(8,128)(2,1)S(1)}, bf16[1536,512]{1,0:T(8,128)(2,1)}, u32[]{:S(2)}) copy-start(bf16[1536,512]{1,0:T(8,128)(2,1)} %inner_ref.5) | copy-start | bytes 4718596
  0.7 7.6 %copy-start.2 = (bf16[256,512]{1,0:T(8,128)(2,1)S(1)}, bf16[256,512]{1,0:T(8,128)(2,1)}, u32[]{:S(2)}) copy-start(bf16[256,512]{1,0:T(8,128)(2,1)} %nodes_ref.5) | copy-start | bytes 786436
  0.7 7.6 %copy-start.4 = (bf16[1024,512]{1,0:T(8,128)(2,1)S(1)}, bf16[1024,512]{1,0:T(8,128)(2,1)}, u32[]{:S(2)}) copy-start(bf16[1024,512]{1,0:T(8,128)(2,1)} %ninner_ref.3) | copy-start | bytes 3145732
  0.7 7.6 %copy-start.9 = (s32[1024]{0:T(1024)S(1)}, s32[1024]{0:T(1024)}, u32[]{:S(2)}) copy-start(s32[1024]{0:T(1024)} %param.32) | copy-start | bytes 12292
  0.7 7.6 %copy-start.10 = (s32[1024]{0:T(1024)S(1)}, s32[1024]{0:T(1024)}, u32[]{:S(2)}) copy-start(s32[1024]{0:T(1024)} %param.33) | copy-start | bytes 12292
  0.7 7.6 %copy-start.11 = (f32[512]{0:T(512)S(1)}, f32[512]{0:T(512)}, u32[]{:S(2)}) copy-start(f32[512]{0:T(512)} %param.25) | copy-start | bytes 6148
  0.7 7.6 %copy-start.12 = (f32[512]{0:T(512)S(1)}, f32[512]{0:T(512)}, u32[]{:S(2)}) copy-start(f32[512]{0:T(512)} %param.28) | copy-start | bytes 6148
  2.1 8.2 %copy-start.6 = (bf16[512,512]{1,0:T(8,128)(2,1)S(1)}, bf16[512,512]{1,0:T(8,128)(2,1)}, u32[]{:S(2)}) copy-start(bf16[512,512]{1,0:T(8,128)(2,1)} %nouter_ref.1) | copy-start | bytes 1572868
  2.1 8.2 %copy-start.7 = (bf16[512,512]{1,0:T(8,128)(2,1)S(1)}, bf16[512,512]{1,0:T(8,128)(2,1)}, u32[]{:S(2)}) copy-start(bf16[512,512]{1,0:T(8,128)(2,1)} %eouter_ref.3) | copy-start | bytes 1572868
  2.1 8.2 %copy-start.8 = (bf16[256,512]{1,0:T(8,128)(2,1)S(1)}, bf16[256,512]{1,0:T(8,128)(2,1)}, u32[]{:S(2)}) copy-start(bf16[256,512]{1,0:T(8,128)(2,1)} %cotan_ref.1) | copy-start | bytes 786436
  2.1 8.2 %copy-start.13 = (f32[512]{0:T(512)S(1)}, f32[512]{0:T(512)}, u32[]{:S(2)}) copy-start(f32[512]{0:T(512)} %param.26) | copy-start | bytes 6148
  2.1 8.2 %copy-start.14 = (f32[512]{0:T(512)S(1)}, f32[512]{0:T(512)}, u32[]{:S(2)}) copy-start(f32[512]{0:T(512)} %param.29) | copy-start | bytes 6148
  2.1 8.2 %copy-start.15 = (f32[512]{0:T(512)S(1)}, f32[512]{0:T(512)}, u32[]{:S(2)}) copy-start(f32[512]{0:T(512)} %param.30) | copy-start | bytes 6148
  2.1 8.2 %copy-start.16 = (f32[512]{0:T(512)S(1)}, f32[512]{0:T(512)}, u32[]{:S(2)}) copy-start(f32[512]{0:T(512)} %param.27) | copy-start | bytes 6148
  2.2 8.1 %collective-permute-start = (bf16[32,512]{1,0:T(8,128)(2,1)S(1)}, bf16[32,512]{1,0:T(8,128)(2,1)S(1)}, u32[]{:S(2)}, u32[]{:S(2)}) collective-permute-start(bf16[32,512]{1,0:T(8,128)(2,1)S(1)} %get-tuple-element.92), channel_id=1, source_target_pairs={{0,1},{1,2},{2,3},{3,4},{4,5},{5,6},{6,7},{7,0},{8,9},{9,10},{10,1... | collective-permute-start | bytes 98312 | tf_op jit(solution)/shard_map/ppermute | solution.py:302
  5.2 5.1 %collective-permute-start.1 = (bf16[32,512]{1,0:T(8,128)(2,1)S(1)}, bf16[32,512]{1,0:T(8,128)(2,1)S(1)}, u32[]{:S(2)}, u32[]{:S(2)}) collective-permute-start(bf16[32,512]{1,0:T(8,128)(2,1)S(1)} %get-tuple-element.93), channel_id=1, source_target_pairs={{0,7},{1,0},{2,1},{3,2},{4,3},{5,4},{6,5},{7,6},{8,15},{9,8},{10,9... | collective-permute-start | bytes 98312 | tf_op jit(solution)/shard_map/ppermute | solution.py:302
  10.3 4.1 %copy-start.5 = (bf16[1024,512]{1,0:T(8,128)(2,1)S(1)}, bf16[1024,512]{1,0:T(8,128)(2,1)}, u32[]{:S(2)}) copy-start(bf16[1024,512]{1,0:T(8,128)(2,1)} %ecotan_ref.1) | copy-start | bytes 3145732
  18.6 2.5 %collective-permute-start.3 = (bf16[1792,256]{1,0:T(8,128)(2,1)S(1)}, bf16[1792,256]{1,0:T(8,128)(2,1)S(1)}, u32[]{:S(2)}, u32[]{:S(2)}) collective-permute-start(bf16[1792,256]{1,0:T(8,128)(2,1)S(1)} %get-tuple-element.110), channel_id=1, source_target_pairs={{0,8},{1,9},{2,10},{3,11},{4,12},{5,13},{6,14},{7,15},{8,0},{9,1},... | collective-permute-start | bytes 2752520 | tf_op jit(solution)/shard_map/ppermute | solution.py:315
  20.2 2.7 %collective-permute-start.2 = (bf16[1792,256]{1,0:T(8,128)(2,1)S(1)}, bf16[1792,256]{1,0:T(8,128)(2,1)S(1)}, u32[]{:S(2)}, u32[]{:S(2)}) collective-permute-start(bf16[1792,256]{1,0:T(8,128)(2,1)S(1)} %get-tuple-element.114), channel_id=1, source_target_pairs={{0,8},{1,9},{2,10},{3,11},{4,12},{5,13},{6,14},{7,15},{8,0},{9,1},... | collective-permute-start | bytes 2752520 | tf_op jit(solution)/shard_map/ppermute | solution.py:315
  21.3 9.4 %collective-permute-start.4 = (bf16[1056,256]{1,0:T(8,128)(2,1)S(1)}, bf16[1056,256]{1,0:T(8,128)(2,1)S(1)}, u32[]{:S(2)}, u32[]{:S(2)}) collective-permute-start(bf16[1056,256]{1,0:T(8,128)(2,1)S(1)} %get-tuple-element.120), channel_id=1, source_target_pairs={{0,16},{1,17},{2,18},{3,19},{4,20},{5,21},{6,22},{7,23},{8,9},{9,8... | collective-permute-start | bytes 1622024 | tf_op jit(solution)/shard_map/ppermute | solution.py:315
  23.0 12.6 %collective-permute-start.6 = (bf16[896,256]{1,0:T(8,128)(2,1)S(1)}, bf16[896,256]{1,0:T(8,128)(2,1)S(1)}, u32[]{:S(2)}, u32[]{:S(2)}) collective-permute-start(bf16[896,256]{1,0:T(8,128)(2,1)S(1)} %send0.3), channel_id=1, source_target_pairs={{0,16},{1,17},{2,18},{3,19},{4,20},{5,21},{6,22},{7,23},{8,9},{9,8... | collective-permute-start | bytes 1376264 | tf_op jit(solution)/shard_map/ppermute | solution.py:315
  30.8 7.3 %collective-permute-start.5 = (bf16[608,256]{1,0:T(8,128)(2,1)S(1)}, bf16[608,256]{1,0:T(8,128)(2,1)S(1)}, u32[]{:S(2)}, u32[]{:S(2)}) collective-permute-start(bf16[608,256]{1,0:T(8,128)(2,1)S(1)} %get-tuple-element.133), channel_id=1, source_target_pairs={{0,1},{1,0},{2,3},{3,2},{4,5},{5,4},{6,7},{7,6},{8,10},{9,11},{10,... | collective-permute-start | bytes 933896 | tf_op jit(solution)/shard_map/ppermute | solution.py:315
  35.6 6.1 %collective-permute-start.8 = (bf16[448,256]{1,0:T(8,128)(2,1)S(1)}, bf16[448,256]{1,0:T(8,128)(2,1)S(1)}, u32[]{:S(2)}, u32[]{:S(2)}) collective-permute-start(bf16[448,256]{1,0:T(8,128)(2,1)S(1)} %send1.3), channel_id=1, source_target_pairs={{0,1},{1,0},{2,3},{3,2},{4,5},{5,4},{6,7},{7,6},{8,10},{9,11},{10,... | collective-permute-start | bytes 688136 | tf_op jit(solution)/shard_map/ppermute | solution.py:315
  38.2 5.4 %collective-permute-start.7 = (bf16[320,256]{1,0:T(8,128)(2,1)S(1)}, bf16[320,256]{1,0:T(8,128)(2,1)S(1)}, u32[]{:S(2)}, u32[]{:S(2)}) collective-permute-start(bf16[320,256]{1,0:T(8,128)(2,1)S(1)} %get-tuple-element.144), channel_id=1, source_target_pairs={{0,2},{1,3},{2,0},{3,1},{4,6},{5,7},{6,4},{7,5},{8,24},{9,25},{10,... | collective-permute-start | bytes 491528 | tf_op jit(solution)/shard_map/ppermute | solution.py:315
  41.8 12.1 %copy-start.3 = (s32[1,1,2,32]{3,2,1,0:T(2,128)S(1)}, s32[1,1,2,32]{3,2,1,0:T(2,128)}, u32[]{:S(2)}) copy-start(s32[1,1,2,32]{3,2,1,0:T(2,128)} %param.31) | copy-start | bytes 772
  41.8 6.0 %collective-permute-start.11 = (bf16[224,256]{1,0:T(8,128)(2,1)S(1)}, bf16[224,256]{1,0:T(8,128)(2,1)S(1)}, u32[]{:S(2)}, u32[]{:S(2)}) collective-permute-start(bf16[224,256]{1,0:T(8,128)(2,1)S(1)} %send2.3), channel_id=1, source_target_pairs={{0,2},{1,3},{2,0},{3,1},{4,6},{5,7},{6,4},{7,5},{8,24},{9,25},{10,... | collective-permute-start | bytes 344072 | tf_op jit(solution)/shard_map/ppermute | solution.py:315
  43.6 8.9 %collective-permute-start.9 = (bf16[208,256]{1,0:T(8,128)(2,1)S(1)}, bf16[208,256]{1,0:T(8,128)(2,1)S(1)}, u32[]{:S(2)}, u32[]{:S(2)}) collective-permute-start(bf16[208,256]{1,0:T(8,128)(2,1)S(1)} %get-tuple-element.157), channel_id=1, source_target_pairs={{0,4},{1,5},{2,6},{3,7},{4,0},{5,1},{6,2},{7,3},{8,12},{9,13},{10,... | collective-permute-start | bytes 319496 | tf_op jit(solution)/shard_map/ppermute | solution.py:315
  47.8 5.4 %collective-permute-start.12 = (bf16[112,256]{1,0:T(8,128)(2,1)S(1)}, bf16[112,256]{1,0:T(8,128)(2,1)S(1)}, u32[]{:S(2)}, u32[]{:S(2)}) collective-permute-start(bf16[112,256]{1,0:T(8,128)(2,1)S(1)} %send3.3), channel_id=1, source_target_pairs={{0,4},{1,5},{2,6},{3,7},{4,0},{5,1},{6,2},{7,3},{8,12},{9,13},{10,... | collective-permute-start | bytes 172040 | tf_op jit(solution)/shard_map/ppermute | solution.py:315
  52.6 1.2 %collective-permute-start.10 = (f32[6,512]{1,0:T(8,128)S(1)}, f32[6,512]{1,0:T(8,128)S(1)}, u32[]{:S(2)}, u32[]{:S(2)}) collective-permute-start(f32[6,512]{1,0:T(8,128)S(1)} %get-tuple-element.159.vec_ref), channel_id=1, source_target_pairs={{0,8},{1,9},{2,10},{3,11},{4,12},{5,13},{6,14},{7,15},{8,0},{9,1},... | collective-permute-start | bytes 36872 | tf_op jit(solution)/shard_map/ppermute | solution.py:315

commit v7 on v6

--- a/solution.py
+++ b/solution.py
@@ -306,7 +306,7 @@
     core_bit = lax.axis_size("patch")
     high = [core_bit << k for k in range(1, lax.axis_size("region").bit_length() - 1)]
     low = [1 << k for k in range(core_bit.bit_length() - 1)]
-    return core_bit, high + low, low[:-1] + high + low[-1:]
+    return core_bit, high + low, low + high
 
 
 def permute_by(values, first, second, core_bit):
@@ -584,8 +584,8 @@
     core_bit, first, second = halving_orders()
     if rows % (16 * count) or width % (4 * LANES) or slots % 32:
         return []
-    high = [b for b in first if b > core_bit]
-    low = [b for b in first if b < core_bit]
+    high = [b for b in sorted(first) if b > core_bit]
+    low = [b for b in sorted(first) if b < core_bit]
     turned = low[1:-1] + high + low[:1] + low[-1:]
     quarter = width // 4
     chunks = CHUNKS

time: 55.1 us -> 53.3 us (0.967)
  waiting for transfers between devices: 18 us -> 15.2 us
  starting transfers between devices: 18.6 us -> 19.6 us
    ppermute x11, waiting for transfers between devices: 18 us -> 15.2 us  [permute_by(): return lax.ppermute(values, AXES, pairs)]
    ppermute x11, starting transfers between devices: 12.4 us -> 13.4 us  [permute_by(): return lax.ppermute(values, AXES, pairs)]
  transfers between devices with their start and end apart: 13 -> 13, of which waited for: 10 -> 9; matrix products, arithmetic and copies ran while one was open for 0% -> 0% of each run, Pallas kernels for 12% -> 12%
where the time goes in v7:
time: 53.3 us; the launch traced here: 53.2 us
  starting transfers between devices  19.6 us (37%)
  Pallas kernels  17.4 us (33%)
  waiting for transfers between devices  15.2 us (29%)
  between operations  1.03 us (2%)
    pallas_call x26, Pallas kernels, call(): pl.pallas_call(body, out_shape=shapes, in_specs=[anywhere if i in hbm els...  17.4 us
    ppermute x11, waiting for transfers between devices, permute_by(): return lax.ppermute(values, AXES, pairs)  15.2 us
    ppermute x11, starting transfers between devices, permute_by(): return lax.ppermute(values, AXES, pairs)  13.4 us
    ppermute x2, starting transfers between devices, ring(): lax.ppermute(values, 'patch', [(i, (i + step) % count) for i in range(cou...  6.12 us
  transfers between devices with their start and end apart: 13, of which 9 were waited for; matrix products, arithmetic and copies ran while one was open for 0% of the time, Pallas kernels for 12%

profile of v7, /device:TPU:0, one launch (start us, length us, event | category | flops | bytes accessed | tf_op | source)
XLA Modules:
  0.0 53.2 jit_solution(12585115743732136830)
XLA Ops:
  0.7 1.3 %pick.1 = (bf16[32,512]{1,0:T(8,128)(2,1)S(1)}, bf16[32,512]{1,0:T(8,128)(2,1)S(1)}) custom-call(s32[2,32]{1,0:T(2,128)} %bitcast.11, bf16[256,512]{1,0:T(8,128)(2,1)} %nodes_ref.5), custom_call_target="tpu_custom_call" | custom-call | flops 21474836480 | bytes 65536 | tf_op jit(solution)/shard_map/pick/pallas_call | solution.py:42
  2.2 3.0 %collective-permute-start = (bf16[32,512]{1,0:T(8,128)(2,1)S(1)}, bf16[32,512]{1,0:T(8,128)(2,1)S(1)}, u32[]{:S(2)}, u32[]{:S(2)}) collective-permute-start(bf16[32,512]{1,0:T(8,128)(2,1)S(1)} %get-tuple-element.92), channel_id=1, source_target_pairs={{0,1},{1,2},{2,3},{3,4},{4,5},{5,6},{6,7},{7,0},{8,9},{9,10},{10,1... | collective-permute-start | bytes 98312 | tf_op jit(solution)/shard_map/ppermute | solution.py:302
  5.2 3.1 %collective-permute-start.1 = (bf16[32,512]{1,0:T(8,128)(2,1)S(1)}, bf16[32,512]{1,0:T(8,128)(2,1)S(1)}, u32[]{:S(2)}, u32[]{:S(2)}) collective-permute-start(bf16[32,512]{1,0:T(8,128)(2,1)S(1)} %get-tuple-element.93), channel_id=1, source_target_pairs={{0,7},{1,0},{2,1},{3,2},{4,3},{5,4},{6,5},{7,6},{8,15},{9,8},{10,9... | collective-permute-start | bytes 98312 | tf_op jit(solution)/shard_map/ppermute | solution.py:302
  8.3 1.9 %table.1 = (f32[1024,512]{1,0:T(8,128)S(1)}, f32[256,512]{1,0:T(8,128)S(1)}, bf16[1024,640]{1,0:T(8,128)(2,1)S(1)}, bf16[640,1024]{1,0:T(8,128)(2,1)S(1)}) custom-call(s32[1,1024]{1,0:T(1,128)S(1)} %bitcast.13, s32[1,1024]{1,0:T(1,128)S(1)} %bitcast.14, f32[1,512]{1,0:T(1,128)S(1)} %bitcast.15, bf16[256,512]{1,0:T(8,128)(2,1)S(1)} %copy-done.2, ...), custom_call_target="tpu_custom_call" | custom-call | flops 1073741824 | bytes 5242880 | tf_op jit(solution)/shard_map/table/pallas_call | solution.py:42
  10.3 4.1 %forward.1 = (bf16[1024,512]{1,0:T(8,128)(2,1)S(1)}, f32[1024,512]{1,0:T(8,128)S(1)}, f32[1024,512]{1,0:T(8,128)S(1)}, f32[1024,1]{1,0:T(8,128)S(1)}, bf16[256,5...) custom-call(f32[1024,512]{1,0:T(8,128)S(1)} %get-tuple-element.90.pa, ...), custom_call_target="tpu_custom_call" | custom-call | flops 5368709120 | bytes 7088128 | tf_op jit(solution)/shard_map/forward/pallas_call | solution.py:42
  14.4 2.6 %backward.1 = (f32[1024,512]{1,0:T(8,128)S(1)}, bf16[1024,512]{1,0:T(8,128)(2,1)S(1)}, bf16[576,512]{1,0:T(8,128)(2,1)S(1)}, f32[6,512]{1,0:T(8,128)S(1)}, bf16[1024,512]{1,0:T(8,128)(2,1)S(1)}) custom-call(bf16[1024,640]{1,0:T(8,128)(2,1)S(1)} %get-tuple-element.88.pick_ref, bf16[640,1024]{1,0:T(8,128)(2,1)S(1)} %get-tuple-element.89.turned_ref, ...), custom_call_target="tpu_custom_call" | custom-call | flops 3221225472 | bytes 4796416 | tf_op jit(solution)/shard_map/backward/pallas_call | solution.py:42
  17.1 1.6 %weights.2 = (f32[3584,256]{1,0:T(8,128)S(1)}, bf16[1792,256]{1,0:T(8,128)(2,1)S(1)}) custom-call(bf16[1024,512]{1,0:T(8,128)(2,1)S(1)} %copy-done, bf16[256,512]{1,0:T(8,128)(2,1)S(1)} %copy-done.2, bf16[32,512]{1,0:T(8,128)(2,1)S(1)} %collective-permute-done.low_ref, bf16[32,512]{1,0:T(8,128)(2,1)S(1)} %collective-permute-done.1.high_ref, ...), custom_call_target="tpu_custom_call" | custom-call | flops 1073741824 | bytes 4587520 | tf_op jit(solution)/shard_map/weights/pallas_call | solution.py:42
  18.8 1.6 %weights.3 = (f32[3584,256]{1,0:T(8,128)S(1)}, bf16[1792,256]{1,0:T(8,128)(2,1)S(1)}) custom-call(bf16[1024,512]{1,0:T(8,128)(2,1)S(1)} %copy-done, bf16[256,512]{1,0:T(8,128)(2,1)S(1)} %copy-done.2, bf16[32,512]{1,0:T(8,128)(2,1)S(1)} %collective-permute-done.low_ref, bf16[32,512]{1,0:T(8,128)(2,1)S(1)} %collective-permute-done.1.high_ref, ...), custom_call_target="tpu_custom_call" | custom-call | flops 1073741824 | bytes 4587520 | tf_op jit(solution)/shard_map/weights/pallas_call | solution.py:42
  20.3 0.5 %collective-permute-start.2 = (bf16[1792,256]{1,0:T(8,128)(2,1)S(1)}, bf16[1792,256]{1,0:T(8,128)(2,1)S(1)}, u32[]{:S(2)}, u32[]{:S(2)}) collective-permute-start(bf16[1792,256]{1,0:T(8,128)(2,1)S(1)} %get-tuple-element.114), channel_id=1, source_target_pairs={{0,8},{1,9},{2,10},{3,11},{4,12},{5,13},{6,14},{7,15},{8,0},{9,1},... | collective-permute-start | bytes 2752520 | tf_op jit(solution)/shard_map/ppermute | solution.py:315
  20.9 0.3 rim.1.refs_1_
  21.2 0.1 send0.2
  21.3 1.7 %collective-permute-start.4 = (bf16[1056,256]{1,0:T(8,128)(2,1)S(1)}, bf16[1056,256]{1,0:T(8,128)(2,1)S(1)}, u32[]{:S(2)}, u32[]{:S(2)}) collective-permute-start(bf16[1056,256]{1,0:T(8,128)(2,1)S(1)} %get-tuple-element.120), channel_id=1, source_target_pairs={{0,16},{1,17},{2,18},{3,19},{4,20},{5,21},{6,22},{7,23},{8,9},{9,8... | collective-permute-start | bytes 1622024 | tf_op jit(solution)/shard_map/ppermute | solution.py:315
  23.0 0.1 send0.3
  23.1 1.6 %collective-permute-start.6 = (bf16[896,256]{1,0:T(8,128)(2,1)S(1)}, bf16[896,256]{1,0:T(8,128)(2,1)S(1)}, u32[]{:S(2)}, u32[]{:S(2)}) collective-permute-start(bf16[896,256]{1,0:T(8,128)(2,1)S(1)} %send0.3), channel_id=1, source_target_pairs={{0,16},{1,17},{2,18},{3,19},{4,20},{5,21},{6,22},{7,23},{8,9},{9,8... | collective-permute-start | bytes 1376264 | tf_op jit(solution)/shard_map/ppermute | solution.py:315
  24.7 0.1 keep0.2.src_ref
  24.8 2.0 %grads.1 = (f32[256,512]{1,0:T(8,128)S(1)}, bf16[1024,512]{1,0:T(8,128)(2,1)}) custom-call(bf16[576,512]{1,0:T(8,128)(2,1)S(1)} %get-tuple-element.123.spread_ref, bf16[1536,512]{1,0:T(8,128)(2,1)S(1)} %copy-done.1, f32[256,512]{1,0:T(8,128)S(1)} %get-tuple-element.124.partial_ref, f32[1024,512]{1,0:T(8,128)S(1)} %get-tuple-element.125.fresh_ref, ...), custom_call_target="tpu_custom_call" | custom-call | flops 2147483648 | bytes 1572864 | tf_op jit(solution)/shard_map/grads/pallas_call | solution.py:42
  26.8 3.9 %collective-permute-done.4.got_ref = bf16[1056,256]{1,0:T(8,128)(2,1)S(1)} collective-permute-done((bf16[1056,256]{1,0:T(8,128)(2,1)S(1)}, bf16[1056,256]{1,0:T(8,128)(2,1)S(1)}, u32[]{:S(2)}, u32[]{:S(2)}) %collective-permute-start.4) | collective-permute-done | bytes 540704 | tf_op jit(solution)/shard_map/ppermute | solution.py:315
  30.8 1.3 %collective-permute-start.5 = (bf16[608,256]{1,0:T(8,128)(2,1)S(1)}, bf16[608,256]{1,0:T(8,128)(2,1)S(1)}, u32[]{:S(2)}, u32[]{:S(2)}) collective-permute-start(bf16[608,256]{1,0:T(8,128)(2,1)S(1)} %get-tuple-element.133), channel_id=1, source_target_pairs={{0,1},{1,0},{2,3},{3,2},{4,5},{5,4},{6,7},{7,6},{8,10},{9,11},{10,... | collective-permute-start | bytes 933896 | tf_op jit(solution)/shard_map/ppermute | solution.py:315
  32.1 0.1 keep0.3.src_ref
  32.2 3.5 %collective-permute-done.6.got_ref = bf16[896,256]{1,0:T(8,128)(2,1)S(1)} collective-permute-done((bf16[896,256]{1,0:T(8,128)(2,1)S(1)}, bf16[896,256]{1,0:T(8,128)(2,1)S(1)}, u32[]{:S(2)}, u32[]{:S(2)}) %collective-permute-start.6) | collective-permute-done | bytes 458784 | tf_op jit(solution)/shard_map/ppermute | solution.py:315
  35.7 1.3 %collective-permute-start.8 = (bf16[448,256]{1,0:T(8,128)(2,1)S(1)}, bf16[448,256]{1,0:T(8,128)(2,1)S(1)}, u32[]{:S(2)}, u32[]{:S(2)}) collective-permute-start(bf16[448,256]{1,0:T(8,128)(2,1)S(1)} %send1.3), channel_id=1, source_target_pairs={{0,1},{1,0},{2,3},{3,2},{4,5},{5,4},{6,7},{7,6},{8,10},{9,11},{10,... | collective-permute-start | bytes 688136 | tf_op jit(solution)/shard_map/ppermute | solution.py:315
  37.0 1.1 %collective-permute-done.5.got_ref = bf16[608,256]{1,0:T(8,128)(2,1)S(1)} collective-permute-done((bf16[608,256]{1,0:T(8,128)(2,1)S(1)}, bf16[608,256]{1,0:T(8,128)(2,1)S(1)}, u32[]{:S(2)}, u32[]{:S(2)}) %collective-permute-start.5) | collective-permute-done | bytes 311328 | tf_op jit(solution)/shard_map/ppermute | solution.py:315
  38.2 1.1 %collective-permute-start.7 = (bf16[320,256]{1,0:T(8,128)(2,1)S(1)}, bf16[320,256]{1,0:T(8,128)(2,1)S(1)}, u32[]{:S(2)}, u32[]{:S(2)}) collective-permute-start(bf16[320,256]{1,0:T(8,128)(2,1)S(1)} %get-tuple-element.144), channel_id=1, source_target_pairs={{0,2},{1,3},{2,0},{3,1},{4,6},{5,7},{6,4},{7,5},{8,12},{9,13},{10,... | collective-permute-start | bytes 491528 | tf_op jit(solution)/shard_map/ppermute | solution.py:315
  39.4 2.4 %collective-permute-done.8.got_ref = bf16[448,256]{1,0:T(8,128)(2,1)S(1)} collective-permute-done((bf16[448,256]{1,0:T(8,128)(2,1)S(1)}, bf16[448,256]{1,0:T(8,128)(2,1)S(1)}, u32[]{:S(2)}, u32[]{:S(2)}) %collective-permute-start.8) | collective-permute-done | bytes 229408 | tf_op jit(solution)/shard_map/ppermute | solution.py:315
  41.8 0.8 %collective-permute-start.11 = (bf16[224,256]{1,0:T(8,128)(2,1)S(1)}, bf16[224,256]{1,0:T(8,128)(2,1)S(1)}, u32[]{:S(2)}, u32[]{:S(2)}) collective-permute-start(bf16[224,256]{1,0:T(8,128)(2,1)S(1)} %send2.3), channel_id=1, source_target_pairs={{0,2},{1,3},{2,0},{3,1},{4,6},{5,7},{6,4},{7,5},{8,12},{9,13},{10,... | collective-permute-start | bytes 344072 | tf_op jit(solution)/shard_map/ppermute | solution.py:315
  42.7 1.2 %collective-permute-done.7.got_ref = bf16[320,256]{1,0:T(8,128)(2,1)S(1)} collective-permute-done((bf16[320,256]{1,0:T(8,128)(2,1)S(1)}, bf16[320,256]{1,0:T(8,128)(2,1)S(1)}, u32[]{:S(2)}, u32[]{:S(2)}) %collective-permute-start.7) | collective-permute-done | bytes 163872 | tf_op jit(solution)/shard_map/ppermute | solution.py:315
  44.0 2.6 %collective-permute-start.9 = (bf16[208,256]{1,0:T(8,128)(2,1)S(1)}, bf16[208,256]{1,0:T(8,128)(2,1)S(1)}, u32[]{:S(2)}, u32[]{:S(2)}) collective-permute-start(bf16[208,256]{1,0:T(8,128)(2,1)S(1)} %get-tuple-element.157), channel_id=1, source_target_pairs={{0,4},{1,5},{2,6},{3,7},{4,0},{5,1},{6,2},{7,3},{8,24},{9,25},{10,... | collective-permute-start | bytes 319496 | tf_op jit(solution)/shard_map/ppermute | solution.py:315
  46.6 0.3 collective-permute-done.11.got_ref
  47.0 2.3 %collective-permute-start.12 = (bf16[112,256]{1,0:T(8,128)(2,1)S(1)}, bf16[112,256]{1,0:T(8,128)(2,1)S(1)}, u32[]{:S(2)}, u32[]{:S(2)}) collective-permute-start(bf16[112,256]{1,0:T(8,128)(2,1)S(1)} %send3.3), channel_id=1, source_target_pairs={{0,4},{1,5},{2,6},{3,7},{4,0},{5,1},{6,2},{7,3},{8,24},{9,25},{10,... | collective-permute-start | bytes 172040 | tf_op jit(solution)/shard_map/ppermute | solution.py:315
  49.3 0.4 collective-permute-done.9.got_ref.refs_1_
  49.9 2.2 %collective-permute-done.12.refs_3_ = bf16[112,256]{1,0:T(8,128)(2,1)S(1)} collective-permute-done((bf16[112,256]{1,0:T(8,128)(2,1)S(1)}, bf16[112,256]{1,0:T(8,128)(2,1)S(1)}, u32[]{:S(2)}, u32[]{:S(2)}) %collective-permute-start.12) | collective-permute-done | bytes 57376 | tf_op jit(solution)/shard_map/ppermute | solution.py:315
  52.1 1.1 %close.1 = (f32[448,128]{1,0:T(8,128)}, f32[24,128]{1,0:T(8,128)}, f32[256,512]{1,0:T(8,128)}) custom-call(s32[2,32]{1,0:T(2,128)S(1)} %bitcast.12, f32[256,512]{1,0:T(8,128)S(1)} %get-tuple-element.126.partial_ref, bf16[64,512]{1,0:T(8,128)(2,1)S(1)} %get-tuple-element.158.back_ref, f32[6,512]{1,0:T(8,128)S(1)} %get-tuple-element.159.vec_ref, ...), custom_call_target="tpu_custom_call" | custom-call | bytes 765952 | tf_op jit(solution)/shard_map/close/pallas_call | solution.py:42
  (54 shorter events, 0.8 us)
Async XLA Ops:
  0.6 7.6 %copy-start = (bf16[1024,512]{1,0:T(8,128)(2,1)S(1)}, bf16[1024,512]{1,0:T(8,128)(2,1)}, u32[]{:S(2)}) copy-start(bf16[1024,512]{1,0:T(8,128)(2,1)} %edges_ref.7) | copy-start | bytes 3145732
  0.6 7.6 %copy-start.1 = (bf16[1536,512]{1,0:T(8,128)(2,1)S(1)}, bf16[1536,512]{1,0:T(8,128)(2,1)}, u32[]{:S(2)}) copy-start(bf16[1536,512]{1,0:T(8,128)(2,1)} %inner_ref.5) | copy-start | bytes 4718596
  0.7 7.6 %copy-start.2 = (bf16[256,512]{1,0:T(8,128)(2,1)S(1)}, bf16[256,512]{1,0:T(8,128)(2,1)}, u32[]{:S(2)}) copy-start(bf16[256,512]{1,0:T(8,128)(2,1)} %nodes_ref.5) | copy-start | bytes 786436
  0.7 7.6 %copy-start.4 = (bf16[1024,512]{1,0:T(8,128)(2,1)S(1)}, bf16[1024,512]{1,0:T(8,128)(2,1)}, u32[]{:S(2)}) copy-start(bf16[1024,512]{1,0:T(8,128)(2,1)} %ninner_ref.3) | copy-start | bytes 3145732
  0.7 7.6 %copy-start.9 = (s32[1024]{0:T(1024)S(1)}, s32[1024]{0:T(1024)}, u32[]{:S(2)}) copy-start(s32[1024]{0:T(1024)} %param.32) | copy-start | bytes 12292
  0.7 7.6 %copy-start.10 = (s32[1024]{0:T(1024)S(1)}, s32[1024]{0:T(1024)}, u32[]{:S(2)}) copy-start(s32[1024]{0:T(1024)} %param.33) | copy-start | bytes 12292
  0.7 7.6 %copy-start.11 = (f32[512]{0:T(512)S(1)}, f32[512]{0:T(512)}, u32[]{:S(2)}) copy-start(f32[512]{0:T(512)} %param.25) | copy-start | bytes 6148
  0.7 7.6 %copy-start.12 = (f32[512]{0:T(512)S(1)}, f32[512]{0:T(512)}, u32[]{:S(2)}) copy-start(f32[512]{0:T(512)} %param.28) | copy-start | bytes 6148
  2.1 8.2 %copy-start.6 = (bf16[512,512]{1,0:T(8,128)(2,1)S(1)}, bf16[512,512]{1,0:T(8,128)(2,1)}, u32[]{:S(2)}) copy-start(bf16[512,512]{1,0:T(8,128)(2,1)} %nouter_ref.1) | copy-start | bytes 1572868
  2.1 8.2 %copy-start.7 = (bf16[512,512]{1,0:T(8,128)(2,1)S(1)}, bf16[512,512]{1,0:T(8,128)(2,1)}, u32[]{:S(2)}) copy-start(bf16[512,512]{1,0:T(8,128)(2,1)} %eouter_ref.3) | copy-start | bytes 1572868
  2.1 8.2 %copy-start.8 = (bf16[256,512]{1,0:T(8,128)(2,1)S(1)}, bf16[256,512]{1,0:T(8,128)(2,1)}, u32[]{:S(2)}) copy-start(bf16[256,512]{1,0:T(8,128)(2,1)} %cotan_ref.1) | copy-start | bytes 786436
  2.1 8.2 %copy-start.13 = (f32[512]{0:T(512)S(1)}, f32[512]{0:T(512)}, u32[]{:S(2)}) copy-start(f32[512]{0:T(512)} %param.26) | copy-start | bytes 6148
  2.1 8.2 %copy-start.14 = (f32[512]{0:T(512)S(1)}, f32[512]{0:T(512)}, u32[]{:S(2)}) copy-start(f32[512]{0:T(512)} %param.29) | copy-start | bytes 6148
  2.1 8.2 %copy-start.15 = (f32[512]{0:T(512)S(1)}, f32[512]{0:T(512)}, u32[]{:S(2)}) copy-start(f32[512]{0:T(512)} %param.30) | copy-start | bytes 6148
  2.1 8.2 %copy-start.16 = (f32[512]{0:T(512)S(1)}, f32[512]{0:T(512)}, u32[]{:S(2)}) copy-start(f32[512]{0:T(512)} %param.27) | copy-start | bytes 6148
  2.2 8.1 %collective-permute-start = (bf16[32,512]{1,0:T(8,128)(2,1)S(1)}, bf16[32,512]{1,0:T(8,128)(2,1)S(1)}, u32[]{:S(2)}, u32[]{:S(2)}) collective-permute-start(bf16[32,512]{1,0:T(8,128)(2,1)S(1)} %get-tuple-element.92), channel_id=1, source_target_pairs={{0,1},{1,2},{2,3},{3,4},{4,5},{5,6},{6,7},{7,0},{8,9},{9,10},{10,1... | collective-permute-start | bytes 98312 | tf_op jit(solution)/shard_map/ppermute | solution.py:302
  5.2 5.1 %collective-permute-start.1 = (bf16[32,512]{1,0:T(8,128)(2,1)S(1)}, bf16[32,512]{1,0:T(8,128)(2,1)S(1)}, u32[]{:S(2)}, u32[]{:S(2)}) collective-permute-start(bf16[32,512]{1,0:T(8,128)(2,1)S(1)} %get-tuple-element.93), channel_id=1, source_target_pairs={{0,7},{1,0},{2,1},{3,2},{4,3},{5,4},{6,5},{7,6},{8,15},{9,8},{10,9... | collective-permute-start | bytes 98312 | tf_op jit(solution)/shard_map/ppermute | solution.py:302
  10.3 4.1 %copy-start.5 = (bf16[1024,512]{1,0:T(8,128)(2,1)S(1)}, bf16[1024,512]{1,0:T(8,128)(2,1)}, u32[]{:S(2)}) copy-start(bf16[1024,512]{1,0:T(8,128)(2,1)} %ecotan_ref.1) | copy-start | bytes 3145732
  18.7 2.5 %collective-permute-start.3 = (bf16[1792,256]{1,0:T(8,128)(2,1)S(1)}, bf16[1792,256]{1,0:T(8,128)(2,1)S(1)}, u32[]{:S(2)}, u32[]{:S(2)}) collective-permute-start(bf16[1792,256]{1,0:T(8,128)(2,1)S(1)} %get-tuple-element.110), channel_id=1, source_target_pairs={{0,8},{1,9},{2,10},{3,11},{4,12},{5,13},{6,14},{7,15},{8,0},{9,1},... | collective-permute-start | bytes 2752520 | tf_op jit(solution)/shard_map/ppermute | solution.py:315
  20.3 2.6 %collective-permute-start.2 = (bf16[1792,256]{1,0:T(8,128)(2,1)S(1)}, bf16[1792,256]{1,0:T(8,128)(2,1)S(1)}, u32[]{:S(2)}, u32[]{:S(2)}) collective-permute-start(bf16[1792,256]{1,0:T(8,128)(2,1)S(1)} %get-tuple-element.114), channel_id=1, source_target_pairs={{0,8},{1,9},{2,10},{3,11},{4,12},{5,13},{6,14},{7,15},{8,0},{9,1},... | collective-permute-start | bytes 2752520 | tf_op jit(solution)/shard_map/ppermute | solution.py:315
  21.3 9.4 %collective-permute-start.4 = (bf16[1056,256]{1,0:T(8,128)(2,1)S(1)}, bf16[1056,256]{1,0:T(8,128)(2,1)S(1)}, u32[]{:S(2)}, u32[]{:S(2)}) collective-permute-start(bf16[1056,256]{1,0:T(8,128)(2,1)S(1)} %get-tuple-element.120), channel_id=1, source_target_pairs={{0,16},{1,17},{2,18},{3,19},{4,20},{5,21},{6,22},{7,23},{8,9},{9,8... | collective-permute-start | bytes 1622024 | tf_op jit(solution)/shard_map/ppermute | solution.py:315
  23.1 12.6 %collective-permute-start.6 = (bf16[896,256]{1,0:T(8,128)(2,1)S(1)}, bf16[896,256]{1,0:T(8,128)(2,1)S(1)}, u32[]{:S(2)}, u32[]{:S(2)}) collective-permute-start(bf16[896,256]{1,0:T(8,128)(2,1)S(1)} %send0.3), channel_id=1, source_target_pairs={{0,16},{1,17},{2,18},{3,19},{4,20},{5,21},{6,22},{7,23},{8,9},{9,8... | collective-permute-start | bytes 1376264 | tf_op jit(solution)/shard_map/ppermute | solution.py:315
  30.8 7.3 %collective-permute-start.5 = (bf16[608,256]{1,0:T(8,128)(2,1)S(1)}, bf16[608,256]{1,0:T(8,128)(2,1)S(1)}, u32[]{:S(2)}, u32[]{:S(2)}) collective-permute-start(bf16[608,256]{1,0:T(8,128)(2,1)S(1)} %get-tuple-element.133), channel_id=1, source_target_pairs={{0,1},{1,0},{2,3},{3,2},{4,5},{5,4},{6,7},{7,6},{8,10},{9,11},{10,... | collective-permute-start | bytes 933896 | tf_op jit(solution)/shard_map/ppermute | solution.py:315
  35.7 6.1 %collective-permute-start.8 = (bf16[448,256]{1,0:T(8,128)(2,1)S(1)}, bf16[448,256]{1,0:T(8,128)(2,1)S(1)}, u32[]{:S(2)}, u32[]{:S(2)}) collective-permute-start(bf16[448,256]{1,0:T(8,128)(2,1)S(1)} %send1.3), channel_id=1, source_target_pairs={{0,1},{1,0},{2,3},{3,2},{4,5},{5,4},{6,7},{7,6},{8,10},{9,11},{10,... | collective-permute-start | bytes 688136 | tf_op jit(solution)/shard_map/ppermute | solution.py:315
  38.2 5.7 %collective-permute-start.7 = (bf16[320,256]{1,0:T(8,128)(2,1)S(1)}, bf16[320,256]{1,0:T(8,128)(2,1)S(1)}, u32[]{:S(2)}, u32[]{:S(2)}) collective-permute-start(bf16[320,256]{1,0:T(8,128)(2,1)S(1)} %get-tuple-element.144), channel_id=1, source_target_pairs={{0,2},{1,3},{2,0},{3,1},{4,6},{5,7},{6,4},{7,5},{8,12},{9,13},{10,... | collective-permute-start | bytes 491528 | tf_op jit(solution)/shard_map/ppermute | solution.py:315
  41.8 10.3 %copy-start.3 = (s32[1,1,2,32]{3,2,1,0:T(2,128)S(1)}, s32[1,1,2,32]{3,2,1,0:T(2,128)}, u32[]{:S(2)}) copy-start(s32[1,1,2,32]{3,2,1,0:T(2,128)} %param.31) | copy-start | bytes 772
  41.8 5.1 %collective-permute-start.11 = (bf16[224,256]{1,0:T(8,128)(2,1)S(1)}, bf16[224,256]{1,0:T(8,128)(2,1)S(1)}, u32[]{:S(2)}, u32[]{:S(2)}) collective-permute-start(bf16[224,256]{1,0:T(8,128)(2,1)S(1)} %send2.3), channel_id=1, source_target_pairs={{0,2},{1,3},{2,0},{3,1},{4,6},{5,7},{6,4},{7,5},{8,12},{9,13},{10,... | collective-permute-start | bytes 344072 | tf_op jit(solution)/shard_map/ppermute | solution.py:315
  44.0 5.7 %collective-permute-start.9 = (bf16[208,256]{1,0:T(8,128)(2,1)S(1)}, bf16[208,256]{1,0:T(8,128)(2,1)S(1)}, u32[]{:S(2)}, u32[]{:S(2)}) collective-permute-start(bf16[208,256]{1,0:T(8,128)(2,1)S(1)} %get-tuple-element.157), channel_id=1, source_target_pairs={{0,4},{1,5},{2,6},{3,7},{4,0},{5,1},{6,2},{7,3},{8,24},{9,25},{10,... | collective-permute-start | bytes 319496 | tf_op jit(solution)/shard_map/ppermute | solution.py:315
  47.0 5.1 %collective-permute-start.12 = (bf16[112,256]{1,0:T(8,128)(2,1)S(1)}, bf16[112,256]{1,0:T(8,128)(2,1)S(1)}, u32[]{:S(2)}, u32[]{:S(2)}) collective-permute-start(bf16[112,256]{1,0:T(8,128)(2,1)S(1)} %send3.3), channel_id=1, source_target_pairs={{0,4},{1,5},{2,6},{3,7},{4,0},{5,1},{6,2},{7,3},{8,24},{9,25},{10,... | collective-permute-start | bytes 172040 | tf_op jit(solution)/shard_map/ppermute | solution.py:315
  49.7 2.4 %collective-permute-start.10 = (f32[6,512]{1,0:T(8,128)S(1)}, f32[6,512]{1,0:T(8,128)S(1)}, u32[]{:S(2)}, u32[]{:S(2)}) collective-permute-start(f32[6,512]{1,0:T(8,128)S(1)} %get-tuple-element.159.vec_ref), channel_id=1, source_target_pairs={{0,8},{1,9},{2,10},{3,11},{4,12},{5,13},{6,14},{7,15},{8,0},{9,1},... | collective-permute-start | bytes 36872 | tf_op jit(solution)/shard_map/ppermute | solution.py:315

commit v8 on v7

--- a/solution.py
+++ b/solution.py
@@ -103,7 +103,7 @@
 
 def table_kernel(
     senders_ref, receivers_ref, shift_ref, nodes_ref, inner_ref, edges_ref, ninner_ref, nshift_ref,
-    part_ref, npart_ref, pick_ref, turned_ref, own_ref,
+    part_ref, npart_ref, pick_ref, turned_ref, edges_turned_ref, own_ref,
 ):
     edge_count, width = edges_ref.shape
     count = nodes_ref.shape[0]
@@ -132,6 +132,7 @@
             + shift_ref[...]
         )
     npart_ref[...] = mm(nodes, ninner_ref[:width, :]) + nshift_ref[...]
+    edges_turned_ref[...] = edges_ref[...].T
 
 
 def forward_kernel(
@@ -234,7 +235,7 @@
 
 
 def weights_kernel(
-    edges_ref, nodes_ref, low_ref, high_ref, hidden_ref, preact_ref, linear_ref, spread_ref,
+    edges_turned_ref, nodes_ref, low_ref, high_ref, hidden_ref, preact_ref, linear_ref, spread_ref,
     aggregate_ref, node_hidden_ref, node_preact_ref, node_linear_ref,
     weights_ref, *sends, columns, scales, plan,
 ):
@@ -242,17 +243,24 @@
     nodes = nodes_ref[...]
     rim = jnp.concatenate([low_ref[...], high_ref[...]], axis=0)
     node_preact = node_preact_ref[:, columns]
+    chunk = columns.stop - columns.start
+    by_nodes = mm_tn(
+        nodes,
+        jnp.concatenate(
+            [spread_ref[:count, columns], spread_ref[count : 2 * count, columns], node_preact], axis=1
+        ),
+    )
     start = 0
-    for scale, terms in (
-        (scales[0], [(edges_ref[...], preact_ref[:, columns])]),
-        (scales[0], [(nodes, spread_ref[:count, columns]), (rim, spread_ref[2 * count :, columns])]),
-        (scales[0], [(nodes, spread_ref[count : 2 * count, columns])]),
-        (scales[0], [(hidden_ref[...], linear_ref[:, columns])]),
-        (scales[1], [(nodes, node_preact)]),
-        (scales[1], [(aggregate_ref[...], node_preact)]),
-        (scales[1], [(node_hidden_ref[...], node_linear_ref[:, columns])]),
+    for scale, term in (
+        (scales[0], mm(edges_turned_ref[...], preact_ref[:, columns])),
+        (scales[0], by_nodes[:, :chunk] + mm_tn(rim, spread_ref[2 * count :, columns])),
+        (scales[0], by_nodes[:, chunk : 2 * chunk]),
+        (scales[0], mm_tn(hidden_ref[...], linear_ref[:, columns])),
+        (scales[1], by_nodes[:, 2 * chunk :]),
+        (scales[1], mm_tn(aggregate_ref[...], node_preact)),
+        (scales[1], mm_tn(node_hidden_ref[...], node_linear_ref[:, columns])),
     ):
-        value = sum(mm_tn(a, b) for a, b in terms) * scale
+        value = term * scale
         weights_ref[start : start + value.shape[0], :] = value
         start += value.shape[0]
     for send_ref in sends:
@@ -507,9 +515,8 @@
     moved_ref[...] = move_halo(state_ref, got_ref, start, plan, plan.steps - 1).astype(BF)
 
 
-def close_kernel(lists_ref, partial_ref, back_ref, vec_ref, other_ref, *refs, plans):
-    *refs, out_ref, vectors_ref, nodes_ref = refs
-    rims_kernel(lists_ref, partial_ref, back_ref, nodes_ref)
+def close_kernel(vec_ref, other_ref, *refs, plans):
+    *refs, out_ref, vectors_ref = refs
     pieces = out_ref.shape[0] // plans[0].block
     for plan, held_ref, got_ref in zip(plans, refs[0::2], refs[1::2]):
         total = held_ref[...] + got_ref[: plan.block, :]
@@ -528,13 +535,14 @@
 def reduce_kernels(plans, sides, vec, width):
     full = vec.shape[1]
     held, got = {}, {}
-    marks = ()
+    marks, state = (), None
     for plan in plans:
         held[plan], sent = sides.weights(plan, marks)
         marks = (sent,)
         got[plan] = permute_by(sent, plan.core_bit, plan.core_bit, plan.core_bit)
-    state = sides.early(marks)
-    marks = (state,)
+        if state is None:
+            state = sides.early(marks)
+            marks = (state,)
     shapes = [(vec.shape, F32), (state.shape, BF)]
     for step in range(plans[0].steps):
         if step == 1:
@@ -566,15 +574,17 @@
     )
     other = permute_by(vec, carrier.core_bit, carrier.core_bit, carrier.core_bit)
     pairs = [near(a) for plan in plans for a in (held[plan], got[plan])]
-    out, vectors, nodes = call(
+    (nodes,) = call(
+        rims_kernel, [(nodes.shape, F32)], sides.last, near(nodes), near(state), name="rims",
+        plain=(0,), limit=4 << 20,
+    )
+    out, vectors = call(
         functools.partial(close_kernel, plans=plans),
         [
             ((plans[0].block * width // LANES, LANES), F32),
             ((vec.size // LANES, LANES), F32),
-            (nodes.shape, F32),
         ],
-        sides.last, near(nodes), near(state), near(vec), near(other), *pairs, name="close",
-        plain=(0, 1, 2),
+        near(vec), near(other), *pairs, name="close", plain=(0, 1),
     )
     return out.reshape(-1), vectors.reshape(-1), nodes
 
@@ -634,13 +644,14 @@
     low = ring(out_high, 1)
     high = ring(out_low, -1)
 
-    part, npart, pick, turned = call(
+    part, npart, pick, turned, edges_turned = call(
         table_kernel,
         [
             ((edge_count, hidden_width), F32),
             ((count, hidden_width), F32),
             ((edge_count, picked), BF),
             ((picked, edge_count), BF),
+            ((width, edge_count), BF),
         ],
         senders.reshape(1, -1), receivers.reshape(1, -1), edge_shift, nodes, edge_inner, edges,
         node_inner, node_shift,
@@ -690,7 +701,7 @@
                 weights_kernel, columns=columns, scales=(edge_norm, node_norm), plan=plan
             ),
             [((weight_rows, chunk), F32)] + sends,
-            edges, nodes, near(low), near(high), near(hidden), near(preact_late), near(linear_late),
+            near(edges_turned), nodes, near(low), near(high), near(hidden), near(preact_late), near(linear_late),
             near(spread), *[near(a) for a in node_terms],
             name="weights", flops=chunk << 22,
         )

time: 53.3 us -> 53 us (level)
  waiting for transfers between devices: 15.2 us -> 14.2 us
  Pallas kernels: 17.4 us -> 18.1 us
    ppermute x11, waiting for transfers between devices: 15.2 us -> 14.2 us  [permute_by(): return lax.ppermute(values, AXES, pairs)]
    pallas_call x26 -> x27, Pallas kernels: 17.4 us -> 18.1 us  [call(): pl.pallas_call(body, out_shape=shapes, in_specs=[anywhere if i in hbm els...]
  transfers between devices with their start and end apart: 13 -> 13, of which waited for: 9 -> 10; matrix products, arithmetic and copies ran while one was open for 0% -> 0% of each run, Pallas kernels for 12% -> 15%
where the time goes in v8:
time: 53 us; the launch traced here: 52.8 us
  starting transfers between devices  19.5 us (37%)
  Pallas kernels  18.1 us (34%)
  waiting for transfers between devices  14.2 us (27%)
  between operations  1.04 us (2%)
    pallas_call x27, Pallas kernels, call(): pl.pallas_call(body, out_shape=shapes, in_specs=[anywhere if i in hbm els...  18.1 us
    ppermute x11, waiting for transfers between devices, permute_by(): return lax.ppermute(values, AXES, pairs)  14.2 us
    ppermute x11, starting transfers between devices, permute_by(): return lax.ppermute(values, AXES, pairs)  13.4 us
    ppermute x2, starting transfers between devices, ring(): lax.ppermute(values, 'patch', [(i, (i + step) % count) for i in range(cou...  6.12 us
  transfers between devices with their start and end apart: 13, of which 10 were waited for; matrix products, arithmetic and copies ran while one was open for 0% of the time, Pallas kernels for 15%

profile of v8, /device:TPU:0, one launch (start us, length us, event | category | flops | bytes accessed | tf_op | source)
XLA Modules:
  0.0 52.8 jit_solution(11327132875048353752)
XLA Ops:
  0.7 1.3 %pick.1 = (bf16[32,512]{1,0:T(8,128)(2,1)S(1)}, bf16[32,512]{1,0:T(8,128)(2,1)S(1)}) custom-call(s32[2,32]{1,0:T(2,128)} %bitcast.11, bf16[256,512]{1,0:T(8,128)(2,1)} %nodes_ref.5), custom_call_target="tpu_custom_call" | custom-call | flops 21474836480 | bytes 65536 | tf_op jit(solution)/shard_map/pick/pallas_call | solution.py:42
  2.2 3.0 %collective-permute-start = (bf16[32,512]{1,0:T(8,128)(2,1)S(1)}, bf16[32,512]{1,0:T(8,128)(2,1)S(1)}, u32[]{:S(2)}, u32[]{:S(2)}) collective-permute-start(bf16[32,512]{1,0:T(8,128)(2,1)S(1)} %get-tuple-element.92), channel_id=1, source_target_pairs={{0,1},{1,2},{2,3},{3,4},{4,5},{5,6},{6,7},{7,0},{8,9},{9,10},{10,1... | collective-permute-start | bytes 98312 | tf_op jit(solution)/shard_map/ppermute | solution.py:310
  5.2 3.1 %collective-permute-start.1 = (bf16[32,512]{1,0:T(8,128)(2,1)S(1)}, bf16[32,512]{1,0:T(8,128)(2,1)S(1)}, u32[]{:S(2)}, u32[]{:S(2)}) collective-permute-start(bf16[32,512]{1,0:T(8,128)(2,1)S(1)} %get-tuple-element.93), channel_id=1, source_target_pairs={{0,7},{1,0},{2,1},{3,2},{4,3},{5,4},{6,5},{7,6},{8,15},{9,8},{10,9... | collective-permute-start | bytes 98312 | tf_op jit(solution)/shard_map/ppermute | solution.py:310
  8.3 1.9 %table.1 = (f32[1024,512]{1,0:T(8,128)S(1)}, f32[256,512]{1,0:T(8,128)S(1)}, bf16[1024,640]{1,0:T(8,128)(2,1)S(1)}, bf16[640,1024]{1,0:T(8,128)(2,1)S(1)}, bf16[512,1024]{1,0:T(8,128)(2,1)S(1)}) custom-call(s32[1,1024]{1,0:T(1,128)S(1)} %bitcast.13, s32[1,1024]{1,0:T(1,128)S(1)} %bitcast.14, f32[1,512]{1,0:T(1,128)S(1)} %bitcast.15, ...), custom_call_target="tpu_custom_call" | custom-call | flops 1073741824 | bytes 6291456 | tf_op jit(solution)/shard_map/table/pallas_call | solution.py:42
  10.4 4.1 %forward.1 = (bf16[1024,512]{1,0:T(8,128)(2,1)S(1)}, f32[1024,512]{1,0:T(8,128)S(1)}, f32[1024,512]{1,0:T(8,128)S(1)}, f32[1024,1]{1,0:T(8,128)S(1)}, bf16[256,5...) custom-call(f32[1024,512]{1,0:T(8,128)S(1)} %get-tuple-element.90.pa, ...), custom_call_target="tpu_custom_call" | custom-call | flops 5368709120 | bytes 7088128 | tf_op jit(solution)/shard_map/forward/pallas_call | solution.py:42
  14.4 2.7 %backward.1 = (f32[1024,512]{1,0:T(8,128)S(1)}, bf16[1024,512]{1,0:T(8,128)(2,1)S(1)}, bf16[576,512]{1,0:T(8,128)(2,1)S(1)}, f32[6,512]{1,0:T(8,128)S(1)}, bf16[1024,512]{1,0:T(8,128)(2,1)S(1)}) custom-call(bf16[1024,640]{1,0:T(8,128)(2,1)S(1)} %get-tuple-element.88.pick_ref, bf16[640,1024]{1,0:T(8,128)(2,1)S(1)} %get-tuple-element.89.turned_ref, ...), custom_call_target="tpu_custom_call" | custom-call | flops 3221225472 | bytes 4796416 | tf_op jit(solution)/shard_map/backward/pallas_call | solution.py:42
  17.2 1.5 %weights.2 = (f32[3584,256]{1,0:T(8,128)S(1)}, bf16[1792,256]{1,0:T(8,128)(2,1)S(1)}) custom-call(bf16[512,1024]{1,0:T(8,128)(2,1)S(1)} %get-tuple-element.101.edges_turned_ref, bf16[256,512]{1,0:T(8,128)(2,1)S(1)} %copy-done.1, bf16[32,512]{1,0:T(8,128)(2,1)S(1)} %collective-permute-done.low_ref, bf16[32,512]{1,0:T(8,128)(2,1)S(1)} %collective-permute-done.1.high_ref, ...), custom_call_target="tpu_custom_call" | custom-call | flops 1073741824 | bytes 4587520 | tf_op jit(solution)/shard_map/weights/pallas_call | solution.py:42
  18.8 0.3 rim.1.refs_1_
  19.1 1.5 %weights.3 = (f32[3584,256]{1,0:T(8,128)S(1)}, bf16[1792,256]{1,0:T(8,128)(2,1)S(1)}) custom-call(bf16[512,1024]{1,0:T(8,128)(2,1)S(1)} %get-tuple-element.101.edges_turned_ref, bf16[256,512]{1,0:T(8,128)(2,1)S(1)} %copy-done.1, bf16[32,512]{1,0:T(8,128)(2,1)S(1)} %collective-permute-done.low_ref, bf16[32,512]{1,0:T(8,128)(2,1)S(1)} %collective-permute-done.1.high_ref, ...), custom_call_target="tpu_custom_call" | custom-call | flops 1073741824 | bytes 4587520 | tf_op jit(solution)/shard_map/weights/pallas_call | solution.py:42
  20.6 0.5 collective-permute-start.2
  21.1 0.1 collective-permute-done.3.got_ref
  21.2 0.1 send0.2
  21.3 1.7 %collective-permute-start.4 = (bf16[1056,256]{1,0:T(8,128)(2,1)S(1)}, bf16[1056,256]{1,0:T(8,128)(2,1)S(1)}, u32[]{:S(2)}, u32[]{:S(2)}) collective-permute-start(bf16[1056,256]{1,0:T(8,128)(2,1)S(1)} %get-tuple-element.121), channel_id=1, source_target_pairs={{0,16},{1,17},{2,18},{3,19},{4,20},{5,21},{6,22},{7,23},{8,9},{9,8... | collective-permute-start | bytes 1622024 | tf_op jit(solution)/shard_map/ppermute | solution.py:323
  23.0 0.2 collective-permute-done.2.got_ref
  23.3 1.7 %collective-permute-start.6 = (bf16[896,256]{1,0:T(8,128)(2,1)S(1)}, bf16[896,256]{1,0:T(8,128)(2,1)S(1)}, u32[]{:S(2)}, u32[]{:S(2)}) collective-permute-start(bf16[896,256]{1,0:T(8,128)(2,1)S(1)} %send0.3), channel_id=1, source_target_pairs={{0,16},{1,17},{2,18},{3,19},{4,20},{5,21},{6,22},{7,23},{8,9},{9,8... | collective-permute-start | bytes 1376264 | tf_op jit(solution)/shard_map/ppermute | solution.py:323
  25.1 2.0 %grads.1 = (f32[256,512]{1,0:T(8,128)S(1)}, bf16[1024,512]{1,0:T(8,128)(2,1)}) custom-call(bf16[576,512]{1,0:T(8,128)(2,1)S(1)} %get-tuple-element.124.spread_ref, bf16[1536,512]{1,0:T(8,128)(2,1)S(1)} %copy-done, f32[256,512]{1,0:T(8,128)S(1)} %get-tuple-element.125.partial_ref, f32[1024,512]{1,0:T(8,128)S(1)} %get-tuple-element.126.fresh_ref, ...), custom_call_target="tpu_custom_call" | custom-call | flops 2147483648 | bytes 1572864 | tf_op jit(solution)/shard_map/grads/pallas_call | solution.py:42
  27.1 3.7 %collective-permute-done.4.got_ref = bf16[1056,256]{1,0:T(8,128)(2,1)S(1)} collective-permute-done((bf16[1056,256]{1,0:T(8,128)(2,1)S(1)}, bf16[1056,256]{1,0:T(8,128)(2,1)S(1)}, u32[]{:S(2)}, u32[]{:S(2)}) %collective-permute-start.4) | collective-permute-done | bytes 540704 | tf_op jit(solution)/shard_map/ppermute | solution.py:323
  30.8 1.3 %collective-permute-start.5 = (bf16[608,256]{1,0:T(8,128)(2,1)S(1)}, bf16[608,256]{1,0:T(8,128)(2,1)S(1)}, u32[]{:S(2)}, u32[]{:S(2)}) collective-permute-start(bf16[608,256]{1,0:T(8,128)(2,1)S(1)} %get-tuple-element.134), channel_id=1, source_target_pairs={{0,1},{1,0},{2,3},{3,2},{4,5},{5,4},{6,7},{7,6},{8,10},{9,11},{10,... | collective-permute-start | bytes 933896 | tf_op jit(solution)/shard_map/ppermute | solution.py:323
  32.2 3.5 %collective-permute-done.6.got_ref = bf16[896,256]{1,0:T(8,128)(2,1)S(1)} collective-permute-done((bf16[896,256]{1,0:T(8,128)(2,1)S(1)}, bf16[896,256]{1,0:T(8,128)(2,1)S(1)}, u32[]{:S(2)}, u32[]{:S(2)}) %collective-permute-start.6) | collective-permute-done | bytes 458784 | tf_op jit(solution)/shard_map/ppermute | solution.py:323
  35.7 1.3 %collective-permute-start.8 = (bf16[448,256]{1,0:T(8,128)(2,1)S(1)}, bf16[448,256]{1,0:T(8,128)(2,1)S(1)}, u32[]{:S(2)}, u32[]{:S(2)}) collective-permute-start(bf16[448,256]{1,0:T(8,128)(2,1)S(1)} %send1.3), channel_id=1, source_target_pairs={{0,1},{1,0},{2,3},{3,2},{4,5},{5,4},{6,7},{7,6},{8,10},{9,11},{10,... | collective-permute-start | bytes 688136 | tf_op jit(solution)/shard_map/ppermute | solution.py:323
  37.0 1.1 %collective-permute-done.5.got_ref = bf16[608,256]{1,0:T(8,128)(2,1)S(1)} collective-permute-done((bf16[608,256]{1,0:T(8,128)(2,1)S(1)}, bf16[608,256]{1,0:T(8,128)(2,1)S(1)}, u32[]{:S(2)}, u32[]{:S(2)}) %collective-permute-start.5) | collective-permute-done | bytes 311328 | tf_op jit(solution)/shard_map/ppermute | solution.py:323
  38.3 1.1 %collective-permute-start.7 = (bf16[320,256]{1,0:T(8,128)(2,1)S(1)}, bf16[320,256]{1,0:T(8,128)(2,1)S(1)}, u32[]{:S(2)}, u32[]{:S(2)}) collective-permute-start(bf16[320,256]{1,0:T(8,128)(2,1)S(1)} %get-tuple-element.145), channel_id=1, source_target_pairs={{0,2},{1,3},{2,0},{3,1},{4,6},{5,7},{6,4},{7,5},{8,12},{9,13},{10,... | collective-permute-start | bytes 491528 | tf_op jit(solution)/shard_map/ppermute | solution.py:323
  39.4 2.4 %collective-permute-done.8.got_ref = bf16[448,256]{1,0:T(8,128)(2,1)S(1)} collective-permute-done((bf16[448,256]{1,0:T(8,128)(2,1)S(1)}, bf16[448,256]{1,0:T(8,128)(2,1)S(1)}, u32[]{:S(2)}, u32[]{:S(2)}) %collective-permute-start.8) | collective-permute-done | bytes 229408 | tf_op jit(solution)/shard_map/ppermute | solution.py:323
  41.8 0.8 %collective-permute-start.11 = (bf16[224,256]{1,0:T(8,128)(2,1)S(1)}, bf16[224,256]{1,0:T(8,128)(2,1)S(1)}, u32[]{:S(2)}, u32[]{:S(2)}) collective-permute-start(bf16[224,256]{1,0:T(8,128)(2,1)S(1)} %send2.3), channel_id=1, source_target_pairs={{0,2},{1,3},{2,0},{3,1},{4,6},{5,7},{6,4},{7,5},{8,12},{9,13},{10,... | collective-permute-start | bytes 344072 | tf_op jit(solution)/shard_map/ppermute | solution.py:323
  42.7 1.2 %collective-permute-done.7.got_ref = bf16[320,256]{1,0:T(8,128)(2,1)S(1)} collective-permute-done((bf16[320,256]{1,0:T(8,128)(2,1)S(1)}, bf16[320,256]{1,0:T(8,128)(2,1)S(1)}, u32[]{:S(2)}, u32[]{:S(2)}) %collective-permute-start.7) | collective-permute-done | bytes 163872 | tf_op jit(solution)/shard_map/ppermute | solution.py:323
  44.0 2.6 %collective-permute-start.9 = (bf16[208,256]{1,0:T(8,128)(2,1)S(1)}, bf16[208,256]{1,0:T(8,128)(2,1)S(1)}, u32[]{:S(2)}, u32[]{:S(2)}) collective-permute-start(bf16[208,256]{1,0:T(8,128)(2,1)S(1)} %get-tuple-element.158), channel_id=1, source_target_pairs={{0,4},{1,5},{2,6},{3,7},{4,0},{5,1},{6,2},{7,3},{8,24},{9,25},{10,... | collective-permute-start | bytes 319496 | tf_op jit(solution)/shard_map/ppermute | solution.py:323
  46.6 0.3 collective-permute-done.11.got_ref
  47.0 2.3 %collective-permute-start.12 = (bf16[112,256]{1,0:T(8,128)(2,1)S(1)}, bf16[112,256]{1,0:T(8,128)(2,1)S(1)}, u32[]{:S(2)}, u32[]{:S(2)}) collective-permute-start(bf16[112,256]{1,0:T(8,128)(2,1)S(1)} %send3.3), channel_id=1, source_target_pairs={{0,4},{1,5},{2,6},{3,7},{4,0},{5,1},{6,2},{7,3},{8,24},{9,25},{10,... | collective-permute-start | bytes 172040 | tf_op jit(solution)/shard_map/ppermute | solution.py:323
  49.3 0.4 collective-permute-done.9.got_ref.refs_1_
  49.9 1.1 %rims.1 = f32[256,512]{1,0:T(8,128)} custom-call(s32[2,32]{1,0:T(2,128)S(1)} %bitcast.12, f32[256,512]{1,0:T(8,128)S(1)} %get-tuple-element.127.partial_ref, bf16[64,512]{1,0:T(8,128)(2,1)S(1)} %get-tuple-element.159.back_ref), custom_call_target="tpu_custom_call" | custom-call | bytes 524288 | tf_op jit(solution)/shard_map/rims/pallas_call | solution.py:42
  51.0 1.1 %collective-permute-done.12.refs_3_ = bf16[112,256]{1,0:T(8,128)(2,1)S(1)} collective-permute-done((bf16[112,256]{1,0:T(8,128)(2,1)S(1)}, bf16[112,256]{1,0:T(8,128)(2,1)S(1)}, u32[]{:S(2)}, u32[]{:S(2)}) %collective-permute-start.12) | collective-permute-done | bytes 57376 | tf_op jit(solution)/shard_map/ppermute | solution.py:323
  52.1 0.7 %close.1 = (f32[448,128]{1,0:T(8,128)}, f32[24,128]{1,0:T(8,128)}) custom-call(f32[6,512]{1,0:T(8,128)S(1)} %get-tuple-element.161.vec_ref, f32[6,512]{1,0:T(8,128)S(1)} %collective-permute-done.10.other_ref, f32[112,256]{1,0:T(8,128)S(1)} %keep3.2.refs_0_, bf16[208,256]{1,0:T(8,128)(2,1)S(1)} %collective-permute-done.9.got_ref.refs_1_, ...), custom_call_target="tpu_custom_call" | custom-call | bytes 241664 | tf_op jit(solution)/shard_map/close/pallas_call | solution.py:42
  (55 shorter events, 1.0 us)
Async XLA Ops:
  0.6 7.6 %copy-start = (bf16[1536,512]{1,0:T(8,128)(2,1)S(1)}, bf16[1536,512]{1,0:T(8,128)(2,1)}, u32[]{:S(2)}) copy-start(bf16[1536,512]{1,0:T(8,128)(2,1)} %inner_ref.5) | copy-start | bytes 4718596
  0.6 7.6 %copy-start.1 = (bf16[256,512]{1,0:T(8,128)(2,1)S(1)}, bf16[256,512]{1,0:T(8,128)(2,1)}, u32[]{:S(2)}) copy-start(bf16[256,512]{1,0:T(8,128)(2,1)} %nodes_ref.5) | copy-start | bytes 786436
  0.7 7.6 %copy-start.3 = (bf16[1024,512]{1,0:T(8,128)(2,1)S(1)}, bf16[1024,512]{1,0:T(8,128)(2,1)}, u32[]{:S(2)}) copy-start(bf16[1024,512]{1,0:T(8,128)(2,1)} %edges_ref.3) | copy-start | bytes 3145732
  0.7 7.6 %copy-start.4 = (bf16[1024,512]{1,0:T(8,128)(2,1)S(1)}, bf16[1024,512]{1,0:T(8,128)(2,1)}, u32[]{:S(2)}) copy-start(bf16[1024,512]{1,0:T(8,128)(2,1)} %ninner_ref.3) | copy-start | bytes 3145732
  0.7 7.6 %copy-start.9 = (s32[1024]{0:T(1024)S(1)}, s32[1024]{0:T(1024)}, u32[]{:S(2)}) copy-start(s32[1024]{0:T(1024)} %param.32) | copy-start | bytes 12292
  0.7 7.6 %copy-start.10 = (s32[1024]{0:T(1024)S(1)}, s32[1024]{0:T(1024)}, u32[]{:S(2)}) copy-start(s32[1024]{0:T(1024)} %param.33) | copy-start | bytes 12292
  0.7 7.6 %copy-start.11 = (f32[512]{0:T(512)S(1)}, f32[512]{0:T(512)}, u32[]{:S(2)}) copy-start(f32[512]{0:T(512)} %param.25) | copy-start | bytes 6148
  0.7 7.6 %copy-start.12 = (f32[512]{0:T(512)S(1)}, f32[512]{0:T(512)}, u32[]{:S(2)}) copy-start(f32[512]{0:T(512)} %param.28) | copy-start | bytes 6148
  2.1 8.2 %copy-start.6 = (bf16[512,512]{1,0:T(8,128)(2,1)S(1)}, bf16[512,512]{1,0:T(8,128)(2,1)}, u32[]{:S(2)}) copy-start(bf16[512,512]{1,0:T(8,128)(2,1)} %nouter_ref.1) | copy-start | bytes 1572868
  2.1 8.2 %copy-start.7 = (bf16[512,512]{1,0:T(8,128)(2,1)S(1)}, bf16[512,512]{1,0:T(8,128)(2,1)}, u32[]{:S(2)}) copy-start(bf16[512,512]{1,0:T(8,128)(2,1)} %eouter_ref.3) | copy-start | bytes 1572868
  2.1 8.2 %copy-start.8 = (bf16[256,512]{1,0:T(8,128)(2,1)S(1)}, bf16[256,512]{1,0:T(8,128)(2,1)}, u32[]{:S(2)}) copy-start(bf16[256,512]{1,0:T(8,128)(2,1)} %cotan_ref.1) | copy-start | bytes 786436
  2.1 8.2 %copy-start.13 = (f32[512]{0:T(512)S(1)}, f32[512]{0:T(512)}, u32[]{:S(2)}) copy-start(f32[512]{0:T(512)} %param.26) | copy-start | bytes 6148
  2.1 8.2 %copy-start.14 = (f32[512]{0:T(512)S(1)}, f32[512]{0:T(512)}, u32[]{:S(2)}) copy-start(f32[512]{0:T(512)} %param.29) | copy-start | bytes 6148
  2.1 8.2 %copy-start.15 = (f32[512]{0:T(512)S(1)}, f32[512]{0:T(512)}, u32[]{:S(2)}) copy-start(f32[512]{0:T(512)} %param.30) | copy-start | bytes 6148
  2.1 8.2 %copy-start.16 = (f32[512]{0:T(512)S(1)}, f32[512]{0:T(512)}, u32[]{:S(2)}) copy-start(f32[512]{0:T(512)} %param.27) | copy-start | bytes 6148
  2.2 8.1 %collective-permute-start = (bf16[32,512]{1,0:T(8,128)(2,1)S(1)}, bf16[32,512]{1,0:T(8,128)(2,1)S(1)}, u32[]{:S(2)}, u32[]{:S(2)}) collective-permute-start(bf16[32,512]{1,0:T(8,128)(2,1)S(1)} %get-tuple-element.92), channel_id=1, source_target_pairs={{0,1},{1,2},{2,3},{3,4},{4,5},{5,6},{6,7},{7,0},{8,9},{9,10},{10,1... | collective-permute-start | bytes 98312 | tf_op jit(solution)/shard_map/ppermute | solution.py:310
  5.2 5.1 %collective-permute-start.1 = (bf16[32,512]{1,0:T(8,128)(2,1)S(1)}, bf16[32,512]{1,0:T(8,128)(2,1)S(1)}, u32[]{:S(2)}, u32[]{:S(2)}) collective-permute-start(bf16[32,512]{1,0:T(8,128)(2,1)S(1)} %get-tuple-element.93), channel_id=1, source_target_pairs={{0,7},{1,0},{2,1},{3,2},{4,3},{5,4},{6,5},{7,6},{8,15},{9,8},{10,9... | collective-permute-start | bytes 98312 | tf_op jit(solution)/shard_map/ppermute | solution.py:310
  10.4 4.1 %copy-start.5 = (bf16[1024,512]{1,0:T(8,128)(2,1)S(1)}, bf16[1024,512]{1,0:T(8,128)(2,1)}, u32[]{:S(2)}) copy-start(bf16[1024,512]{1,0:T(8,128)(2,1)} %ecotan_ref.1) | copy-start | bytes 3145732
  18.7 2.5 %collective-permute-start.3 = (bf16[1792,256]{1,0:T(8,128)(2,1)S(1)}, bf16[1792,256]{1,0:T(8,128)(2,1)S(1)}, u32[]{:S(2)}, u32[]{:S(2)}) collective-permute-start(bf16[1792,256]{1,0:T(8,128)(2,1)S(1)} %get-tuple-element.111), channel_id=1, source_target_pairs={{0,8},{1,9},{2,10},{3,11},{4,12},{5,13},{6,14},{7,15},{8,0},{9,1},... | collective-permute-start | bytes 2752520 | tf_op jit(solution)/shard_map/ppermute | solution.py:323
  20.6 2.6 %collective-permute-start.2 = (bf16[1792,256]{1,0:T(8,128)(2,1)S(1)}, bf16[1792,256]{1,0:T(8,128)(2,1)S(1)}, u32[]{:S(2)}, u32[]{:S(2)}) collective-permute-start(bf16[1792,256]{1,0:T(8,128)(2,1)S(1)} %get-tuple-element.116), channel_id=1, source_target_pairs={{0,8},{1,9},{2,10},{3,11},{4,12},{5,13},{6,14},{7,15},{8,0},{9,1},... | collective-permute-start | bytes 2752520 | tf_op jit(solution)/shard_map/ppermute | solution.py:323
  21.3 9.4 %collective-permute-start.4 = (bf16[1056,256]{1,0:T(8,128)(2,1)S(1)}, bf16[1056,256]{1,0:T(8,128)(2,1)S(1)}, u32[]{:S(2)}, u32[]{:S(2)}) collective-permute-start(bf16[1056,256]{1,0:T(8,128)(2,1)S(1)} %get-tuple-element.121), channel_id=1, source_target_pairs={{0,16},{1,17},{2,18},{3,19},{4,20},{5,21},{6,22},{7,23},{8,9},{9,8... | collective-permute-start | bytes 1622024 | tf_op jit(solution)/shard_map/ppermute | solution.py:323
  23.3 12.3 %collective-permute-start.6 = (bf16[896,256]{1,0:T(8,128)(2,1)S(1)}, bf16[896,256]{1,0:T(8,128)(2,1)S(1)}, u32[]{:S(2)}, u32[]{:S(2)}) collective-permute-start(bf16[896,256]{1,0:T(8,128)(2,1)S(1)} %send0.3), channel_id=1, source_target_pairs={{0,16},{1,17},{2,18},{3,19},{4,20},{5,21},{6,22},{7,23},{8,9},{9,8... | collective-permute-start | bytes 1376264 | tf_op jit(solution)/shard_map/ppermute | solution.py:323
  30.8 7.3 %collective-permute-start.5 = (bf16[608,256]{1,0:T(8,128)(2,1)S(1)}, bf16[608,256]{1,0:T(8,128)(2,1)S(1)}, u32[]{:S(2)}, u32[]{:S(2)}) collective-permute-start(bf16[608,256]{1,0:T(8,128)(2,1)S(1)} %get-tuple-element.134), channel_id=1, source_target_pairs={{0,1},{1,0},{2,3},{3,2},{4,5},{5,4},{6,7},{7,6},{8,10},{9,11},{10,... | collective-permute-start | bytes 933896 | tf_op jit(solution)/shard_map/ppermute | solution.py:323
  35.7 6.1 %collective-permute-start.8 = (bf16[448,256]{1,0:T(8,128)(2,1)S(1)}, bf16[448,256]{1,0:T(8,128)(2,1)S(1)}, u32[]{:S(2)}, u32[]{:S(2)}) collective-permute-start(bf16[448,256]{1,0:T(8,128)(2,1)S(1)} %send1.3), channel_id=1, source_target_pairs={{0,1},{1,0},{2,3},{3,2},{4,5},{5,4},{6,7},{7,6},{8,10},{9,11},{10,... | collective-permute-start | bytes 688136 | tf_op jit(solution)/shard_map/ppermute | solution.py:323
  38.3 5.7 %collective-permute-start.7 = (bf16[320,256]{1,0:T(8,128)(2,1)S(1)}, bf16[320,256]{1,0:T(8,128)(2,1)S(1)}, u32[]{:S(2)}, u32[]{:S(2)}) collective-permute-start(bf16[320,256]{1,0:T(8,128)(2,1)S(1)} %get-tuple-element.145), channel_id=1, source_target_pairs={{0,2},{1,3},{2,0},{3,1},{4,6},{5,7},{6,4},{7,5},{8,12},{9,13},{10,... | collective-permute-start | bytes 491528 | tf_op jit(solution)/shard_map/ppermute | solution.py:323
  41.8 8.1 %copy-start.2 = (s32[1,1,2,32]{3,2,1,0:T(2,128)S(1)}, s32[1,1,2,32]{3,2,1,0:T(2,128)}, u32[]{:S(2)}) copy-start(s32[1,1,2,32]{3,2,1,0:T(2,128)} %param.31) | copy-start | bytes 772
  41.8 5.1 %collective-permute-start.11 = (bf16[224,256]{1,0:T(8,128)(2,1)S(1)}, bf16[224,256]{1,0:T(8,128)(2,1)S(1)}, u32[]{:S(2)}, u32[]{:S(2)}) collective-permute-start(bf16[224,256]{1,0:T(8,128)(2,1)S(1)} %send2.3), channel_id=1, source_target_pairs={{0,2},{1,3},{2,0},{3,1},{4,6},{5,7},{6,4},{7,5},{8,12},{9,13},{10,... | collective-permute-start | bytes 344072 | tf_op jit(solution)/shard_map/ppermute | solution.py:323
  44.0 5.7 %collective-permute-start.9 = (bf16[208,256]{1,0:T(8,128)(2,1)S(1)}, bf16[208,256]{1,0:T(8,128)(2,1)S(1)}, u32[]{:S(2)}, u32[]{:S(2)}) collective-permute-start(bf16[208,256]{1,0:T(8,128)(2,1)S(1)} %get-tuple-element.158), channel_id=1, source_target_pairs={{0,4},{1,5},{2,6},{3,7},{4,0},{5,1},{6,2},{7,3},{8,24},{9,25},{10,... | collective-permute-start | bytes 319496 | tf_op jit(solution)/shard_map/ppermute | solution.py:323
  47.0 5.1 %collective-permute-start.12 = (bf16[112,256]{1,0:T(8,128)(2,1)S(1)}, bf16[112,256]{1,0:T(8,128)(2,1)S(1)}, u32[]{:S(2)}, u32[]{:S(2)}) collective-permute-start(bf16[112,256]{1,0:T(8,128)(2,1)S(1)} %send3.3), channel_id=1, source_target_pairs={{0,4},{1,5},{2,6},{3,7},{4,0},{5,1},{6,2},{7,3},{8,24},{9,25},{10,... | collective-permute-start | bytes 172040 | tf_op jit(solution)/shard_map/ppermute | solution.py:323
  49.7 2.4 %collective-permute-start.10 = (f32[6,512]{1,0:T(8,128)S(1)}, f32[6,512]{1,0:T(8,128)S(1)}, u32[]{:S(2)}, u32[]{:S(2)}) collective-permute-start(f32[6,512]{1,0:T(8,128)S(1)} %get-tuple-element.161.vec_ref), channel_id=1, source_target_pairs={{0,8},{1,9},{2,10},{3,11},{4,12},{5,13},{6,14},{7,15},{8,0},{9,1},... | collective-permute-start | bytes 36872 | tf_op jit(solution)/shard_map/ppermute | solution.py:323

commit v9 on v8

--- a/solution.py
+++ b/solution.py
@@ -148,7 +148,7 @@
     rim = jnp.concatenate([low_ref[...], high_ref[...]], axis=0)
     far = mm(rim, einner_ref[width : 2 * width, :]).astype(BF)
     slots = rim.shape[0]
-    tile = edge_count // 2
+    tile = edge_count // 1
     tiles = [slice(start, start + tile) for start in range(0, edge_count, tile)]
 
     def first(rows):
@@ -199,7 +199,7 @@
 ):
     edge_count = ecotan_ref.shape[0]
     count = pulled_ref.shape[0]
-    tile = edge_count // 2
+    tile = edge_count // 1
     tiles = [slice(start, start + tile) for start in range(0, edge_count, tile)]
     sums = [0.0, 0.0, 0.0]
 

time: 53 us -> 52.8 us (level)
  no operation moved by 1% of the time
where the time goes in v9:
time: 52.8 us; the launch traced here: 52.7 us
  starting transfers between devices  19.5 us (37%)
  Pallas kernels  17.9 us (34%)
  waiting for transfers between devices  14.2 us (27%)
  between operations  1.04 us (2%)
    pallas_call x27, Pallas kernels, call(): pl.pallas_call(body, out_shape=shapes, in_specs=[anywhere if i in hbm els...  17.9 us
    ppermute x11, waiting for transfers between devices, permute_by(): return lax.ppermute(values, AXES, pairs)  14.2 us
    ppermute x11, starting transfers between devices, permute_by(): return lax.ppermute(values, AXES, pairs)  13.3 us
    ppermute x2, starting transfers between devices, ring(): lax.ppermute(values, 'patch', [(i, (i + step) % count) for i in range(cou...  6.12 us
  transfers between devices with their start and end apart: 13, of which 10 were waited for; matrix products, arithmetic and copies ran while one was open for 0% of the time, Pallas kernels for 15%

profile of v9, /device:TPU:0, one launch (start us, length us, event | category | flops | bytes accessed | tf_op | source)
XLA Modules:
  0.0 52.7 jit_solution(17340138471857480668)
XLA Ops:
  0.7 1.3 %pick.1 = (bf16[32,512]{1,0:T(8,128)(2,1)S(1)}, bf16[32,512]{1,0:T(8,128)(2,1)S(1)}) custom-call(s32[2,32]{1,0:T(2,128)} %bitcast.11, bf16[256,512]{1,0:T(8,128)(2,1)} %nodes_ref.5), custom_call_target="tpu_custom_call" | custom-call | flops 21474836480 | bytes 65536 | tf_op jit(solution)/shard_map/pick/pallas_call | solution.py:42
  2.2 3.0 %collective-permute-start = (bf16[32,512]{1,0:T(8,128)(2,1)S(1)}, bf16[32,512]{1,0:T(8,128)(2,1)S(1)}, u32[]{:S(2)}, u32[]{:S(2)}) collective-permute-start(bf16[32,512]{1,0:T(8,128)(2,1)S(1)} %get-tuple-element.92), channel_id=1, source_target_pairs={{0,1},{1,2},{2,3},{3,4},{4,5},{5,6},{6,7},{7,0},{8,9},{9,10},{10,1... | collective-permute-start | bytes 98312 | tf_op jit(solution)/shard_map/ppermute | solution.py:310
  5.2 3.1 %collective-permute-start.1 = (bf16[32,512]{1,0:T(8,128)(2,1)S(1)}, bf16[32,512]{1,0:T(8,128)(2,1)S(1)}, u32[]{:S(2)}, u32[]{:S(2)}) collective-permute-start(bf16[32,512]{1,0:T(8,128)(2,1)S(1)} %get-tuple-element.93), channel_id=1, source_target_pairs={{0,7},{1,0},{2,1},{3,2},{4,3},{5,4},{6,5},{7,6},{8,15},{9,8},{10,9... | collective-permute-start | bytes 98312 | tf_op jit(solution)/shard_map/ppermute | solution.py:310
  8.3 1.9 %table.1 = (f32[1024,512]{1,0:T(8,128)S(1)}, f32[256,512]{1,0:T(8,128)S(1)}, bf16[1024,640]{1,0:T(8,128)(2,1)S(1)}, bf16[640,1024]{1,0:T(8,128)(2,1)S(1)}, bf16[512,1024]{1,0:T(8,128)(2,1)S(1)}) custom-call(s32[1,1024]{1,0:T(1,128)S(1)} %bitcast.13, s32[1,1024]{1,0:T(1,128)S(1)} %bitcast.14, f32[1,512]{1,0:T(1,128)S(1)} %bitcast.15, ...), custom_call_target="tpu_custom_call" | custom-call | flops 1073741824 | bytes 6291456 | tf_op jit(solution)/shard_map/table/pallas_call | solution.py:42
  10.4 3.9 %forward.1 = (bf16[1024,512]{1,0:T(8,128)(2,1)S(1)}, f32[1024,512]{1,0:T(8,128)S(1)}, f32[1024,512]{1,0:T(8,128)S(1)}, f32[1024,1]{1,0:T(8,128)S(1)}, bf16[256,5...) custom-call(f32[1024,512]{1,0:T(8,128)S(1)} %get-tuple-element.90.pa, ...), custom_call_target="tpu_custom_call" | custom-call | flops 5368709120 | bytes 7088128 | tf_op jit(solution)/shard_map/forward/pallas_call | solution.py:42
  14.3 2.7 %backward.1 = (f32[1024,512]{1,0:T(8,128)S(1)}, bf16[1024,512]{1,0:T(8,128)(2,1)S(1)}, bf16[576,512]{1,0:T(8,128)(2,1)S(1)}, f32[6,512]{1,0:T(8,128)S(1)}, bf16[1024,512]{1,0:T(8,128)(2,1)S(1)}) custom-call(bf16[1024,640]{1,0:T(8,128)(2,1)S(1)} %get-tuple-element.88.pick_ref, bf16[640,1024]{1,0:T(8,128)(2,1)S(1)} %get-tuple-element.89.turned_ref, ...), custom_call_target="tpu_custom_call" | custom-call | flops 3221225472 | bytes 4796416 | tf_op jit(solution)/shard_map/backward/pallas_call | solution.py:42
  17.0 1.5 %weights.2 = (f32[3584,256]{1,0:T(8,128)S(1)}, bf16[1792,256]{1,0:T(8,128)(2,1)S(1)}) custom-call(bf16[512,1024]{1,0:T(8,128)(2,1)S(1)} %get-tuple-element.101.edges_turned_ref, bf16[256,512]{1,0:T(8,128)(2,1)S(1)} %copy-done.1, bf16[32,512]{1,0:T(8,128)(2,1)S(1)} %collective-permute-done.low_ref, bf16[32,512]{1,0:T(8,128)(2,1)S(1)} %collective-permute-done.1.high_ref, ...), custom_call_target="tpu_custom_call" | custom-call | flops 1073741824 | bytes 4587520 | tf_op jit(solution)/shard_map/weights/pallas_call | solution.py:42
  18.6 0.3 rim.1.refs_1_
  18.9 1.5 %weights.3 = (f32[3584,256]{1,0:T(8,128)S(1)}, bf16[1792,256]{1,0:T(8,128)(2,1)S(1)}) custom-call(bf16[512,1024]{1,0:T(8,128)(2,1)S(1)} %get-tuple-element.101.edges_turned_ref, bf16[256,512]{1,0:T(8,128)(2,1)S(1)} %copy-done.1, bf16[32,512]{1,0:T(8,128)(2,1)S(1)} %collective-permute-done.low_ref, bf16[32,512]{1,0:T(8,128)(2,1)S(1)} %collective-permute-done.1.high_ref, ...), custom_call_target="tpu_custom_call" | custom-call | flops 1073741824 | bytes 4587520 | tf_op jit(solution)/shard_map/weights/pallas_call | solution.py:42
  20.5 0.5 collective-permute-start.2
  21.0 0.1 collective-permute-done.3.got_ref
  21.1 0.1 send0.2
  21.2 1.7 %collective-permute-start.4 = (bf16[1056,256]{1,0:T(8,128)(2,1)S(1)}, bf16[1056,256]{1,0:T(8,128)(2,1)S(1)}, u32[]{:S(2)}, u32[]{:S(2)}) collective-permute-start(bf16[1056,256]{1,0:T(8,128)(2,1)S(1)} %get-tuple-element.121), channel_id=1, source_target_pairs={{0,16},{1,17},{2,18},{3,19},{4,20},{5,21},{6,22},{7,23},{8,9},{9,8... | collective-permute-start | bytes 1622024 | tf_op jit(solution)/shard_map/ppermute | solution.py:323
  22.9 0.2 collective-permute-done.2.got_ref
  23.2 1.7 %collective-permute-start.6 = (bf16[896,256]{1,0:T(8,128)(2,1)S(1)}, bf16[896,256]{1,0:T(8,128)(2,1)S(1)}, u32[]{:S(2)}, u32[]{:S(2)}) collective-permute-start(bf16[896,256]{1,0:T(8,128)(2,1)S(1)} %send0.3), channel_id=1, source_target_pairs={{0,16},{1,17},{2,18},{3,19},{4,20},{5,21},{6,22},{7,23},{8,9},{9,8... | collective-permute-start | bytes 1376264 | tf_op jit(solution)/shard_map/ppermute | solution.py:323
  24.9 2.0 %grads.1 = (f32[256,512]{1,0:T(8,128)S(1)}, bf16[1024,512]{1,0:T(8,128)(2,1)}) custom-call(bf16[576,512]{1,0:T(8,128)(2,1)S(1)} %get-tuple-element.124.spread_ref, bf16[1536,512]{1,0:T(8,128)(2,1)S(1)} %copy-done, f32[256,512]{1,0:T(8,128)S(1)} %get-tuple-element.125.partial_ref, f32[1024,512]{1,0:T(8,128)S(1)} %get-tuple-element.126.fresh_ref, ...), custom_call_target="tpu_custom_call" | custom-call | flops 2147483648 | bytes 1572864 | tf_op jit(solution)/shard_map/grads/pallas_call | solution.py:42
  26.9 3.7 %collective-permute-done.4.got_ref = bf16[1056,256]{1,0:T(8,128)(2,1)S(1)} collective-permute-done((bf16[1056,256]{1,0:T(8,128)(2,1)S(1)}, bf16[1056,256]{1,0:T(8,128)(2,1)S(1)}, u32[]{:S(2)}, u32[]{:S(2)}) %collective-permute-start.4) | collective-permute-done | bytes 540704 | tf_op jit(solution)/shard_map/ppermute | solution.py:323
  30.7 1.3 %collective-permute-start.5 = (bf16[608,256]{1,0:T(8,128)(2,1)S(1)}, bf16[608,256]{1,0:T(8,128)(2,1)S(1)}, u32[]{:S(2)}, u32[]{:S(2)}) collective-permute-start(bf16[608,256]{1,0:T(8,128)(2,1)S(1)} %get-tuple-element.134), channel_id=1, source_target_pairs={{0,1},{1,0},{2,3},{3,2},{4,5},{5,4},{6,7},{7,6},{8,10},{9,11},{10,... | collective-permute-start | bytes 933896 | tf_op jit(solution)/shard_map/ppermute | solution.py:323
  32.1 3.5 %collective-permute-done.6.got_ref = bf16[896,256]{1,0:T(8,128)(2,1)S(1)} collective-permute-done((bf16[896,256]{1,0:T(8,128)(2,1)S(1)}, bf16[896,256]{1,0:T(8,128)(2,1)S(1)}, u32[]{:S(2)}, u32[]{:S(2)}) %collective-permute-start.6) | collective-permute-done | bytes 458784 | tf_op jit(solution)/shard_map/ppermute | solution.py:323
  35.6 1.3 %collective-permute-start.8 = (bf16[448,256]{1,0:T(8,128)(2,1)S(1)}, bf16[448,256]{1,0:T(8,128)(2,1)S(1)}, u32[]{:S(2)}, u32[]{:S(2)}) collective-permute-start(bf16[448,256]{1,0:T(8,128)(2,1)S(1)} %send1.3), channel_id=1, source_target_pairs={{0,1},{1,0},{2,3},{3,2},{4,5},{5,4},{6,7},{7,6},{8,10},{9,11},{10,... | collective-permute-start | bytes 688136 | tf_op jit(solution)/shard_map/ppermute | solution.py:323
  36.9 1.1 %collective-permute-done.5.got_ref = bf16[608,256]{1,0:T(8,128)(2,1)S(1)} collective-permute-done((bf16[608,256]{1,0:T(8,128)(2,1)S(1)}, bf16[608,256]{1,0:T(8,128)(2,1)S(1)}, u32[]{:S(2)}, u32[]{:S(2)}) %collective-permute-start.5) | collective-permute-done | bytes 311328 | tf_op jit(solution)/shard_map/ppermute | solution.py:323
  38.1 1.1 %collective-permute-start.7 = (bf16[320,256]{1,0:T(8,128)(2,1)S(1)}, bf16[320,256]{1,0:T(8,128)(2,1)S(1)}, u32[]{:S(2)}, u32[]{:S(2)}) collective-permute-start(bf16[320,256]{1,0:T(8,128)(2,1)S(1)} %get-tuple-element.145), channel_id=1, source_target_pairs={{0,2},{1,3},{2,0},{3,1},{4,6},{5,7},{6,4},{7,5},{8,12},{9,13},{10,... | collective-permute-start | bytes 491528 | tf_op jit(solution)/shard_map/ppermute | solution.py:323
  39.3 2.4 %collective-permute-done.8.got_ref = bf16[448,256]{1,0:T(8,128)(2,1)S(1)} collective-permute-done((bf16[448,256]{1,0:T(8,128)(2,1)S(1)}, bf16[448,256]{1,0:T(8,128)(2,1)S(1)}, u32[]{:S(2)}, u32[]{:S(2)}) %collective-permute-start.8) | collective-permute-done | bytes 229408 | tf_op jit(solution)/shard_map/ppermute | solution.py:323
  41.7 0.8 %collective-permute-start.11 = (bf16[224,256]{1,0:T(8,128)(2,1)S(1)}, bf16[224,256]{1,0:T(8,128)(2,1)S(1)}, u32[]{:S(2)}, u32[]{:S(2)}) collective-permute-start(bf16[224,256]{1,0:T(8,128)(2,1)S(1)} %send2.3), channel_id=1, source_target_pairs={{0,2},{1,3},{2,0},{3,1},{4,6},{5,7},{6,4},{7,5},{8,12},{9,13},{10,... | collective-permute-start | bytes 344072 | tf_op jit(solution)/shard_map/ppermute | solution.py:323
  42.6 1.2 %collective-permute-done.7.got_ref = bf16[320,256]{1,0:T(8,128)(2,1)S(1)} collective-permute-done((bf16[320,256]{1,0:T(8,128)(2,1)S(1)}, bf16[320,256]{1,0:T(8,128)(2,1)S(1)}, u32[]{:S(2)}, u32[]{:S(2)}) %collective-permute-start.7) | collective-permute-done | bytes 163872 | tf_op jit(solution)/shard_map/ppermute | solution.py:323
  43.9 2.6 %collective-permute-start.9 = (bf16[208,256]{1,0:T(8,128)(2,1)S(1)}, bf16[208,256]{1,0:T(8,128)(2,1)S(1)}, u32[]{:S(2)}, u32[]{:S(2)}) collective-permute-start(bf16[208,256]{1,0:T(8,128)(2,1)S(1)} %get-tuple-element.158), channel_id=1, source_target_pairs={{0,4},{1,5},{2,6},{3,7},{4,0},{5,1},{6,2},{7,3},{8,24},{9,25},{10,... | collective-permute-start | bytes 319496 | tf_op jit(solution)/shard_map/ppermute | solution.py:323
  46.5 0.3 collective-permute-done.11.got_ref
  46.8 2.3 %collective-permute-start.12 = (bf16[112,256]{1,0:T(8,128)(2,1)S(1)}, bf16[112,256]{1,0:T(8,128)(2,1)S(1)}, u32[]{:S(2)}, u32[]{:S(2)}) collective-permute-start(bf16[112,256]{1,0:T(8,128)(2,1)S(1)} %send3.3), channel_id=1, source_target_pairs={{0,4},{1,5},{2,6},{3,7},{4,0},{5,1},{6,2},{7,3},{8,24},{9,25},{10,... | collective-permute-start | bytes 172040 | tf_op jit(solution)/shard_map/ppermute | solution.py:323
  49.1 0.4 collective-permute-done.9.got_ref.refs_1_
  49.8 1.1 %rims.1 = f32[256,512]{1,0:T(8,128)} custom-call(s32[2,32]{1,0:T(2,128)S(1)} %bitcast.12, f32[256,512]{1,0:T(8,128)S(1)} %get-tuple-element.127.partial_ref, bf16[64,512]{1,0:T(8,128)(2,1)S(1)} %get-tuple-element.159.back_ref), custom_call_target="tpu_custom_call" | custom-call | bytes 524288 | tf_op jit(solution)/shard_map/rims/pallas_call | solution.py:42
  50.8 1.1 %collective-permute-done.12.refs_3_ = bf16[112,256]{1,0:T(8,128)(2,1)S(1)} collective-permute-done((bf16[112,256]{1,0:T(8,128)(2,1)S(1)}, bf16[112,256]{1,0:T(8,128)(2,1)S(1)}, u32[]{:S(2)}, u32[]{:S(2)}) %collective-permute-start.12) | collective-permute-done | bytes 57376 | tf_op jit(solution)/shard_map/ppermute | solution.py:323
  52.0 0.7 %close.1 = (f32[448,128]{1,0:T(8,128)}, f32[24,128]{1,0:T(8,128)}) custom-call(f32[6,512]{1,0:T(8,128)S(1)} %get-tuple-element.161.vec_ref, f32[6,512]{1,0:T(8,128)S(1)} %collective-permute-done.10.other_ref, f32[112,256]{1,0:T(8,128)S(1)} %keep3.2.refs_0_, bf16[208,256]{1,0:T(8,128)(2,1)S(1)} %collective-permute-done.9.got_ref.refs_1_, ...), custom_call_target="tpu_custom_call" | custom-call | bytes 241664 | tf_op jit(solution)/shard_map/close/pallas_call | solution.py:42
  (55 shorter events, 1.0 us)
Async XLA Ops:
  0.6 7.6 %copy-start = (bf16[1536,512]{1,0:T(8,128)(2,1)S(1)}, bf16[1536,512]{1,0:T(8,128)(2,1)}, u32[]{:S(2)}) copy-start(bf16[1536,512]{1,0:T(8,128)(2,1)} %inner_ref.5) | copy-start | bytes 4718596
  0.6 7.6 %copy-start.1 = (bf16[256,512]{1,0:T(8,128)(2,1)S(1)}, bf16[256,512]{1,0:T(8,128)(2,1)}, u32[]{:S(2)}) copy-start(bf16[256,512]{1,0:T(8,128)(2,1)} %nodes_ref.5) | copy-start | bytes 786436
  0.7 7.6 %copy-start.3 = (bf16[1024,512]{1,0:T(8,128)(2,1)S(1)}, bf16[1024,512]{1,0:T(8,128)(2,1)}, u32[]{:S(2)}) copy-start(bf16[1024,512]{1,0:T(8,128)(2,1)} %edges_ref.3) | copy-start | bytes 3145732
  0.7 7.6 %copy-start.4 = (bf16[1024,512]{1,0:T(8,128)(2,1)S(1)}, bf16[1024,512]{1,0:T(8,128)(2,1)}, u32[]{:S(2)}) copy-start(bf16[1024,512]{1,0:T(8,128)(2,1)} %ninner_ref.3) | copy-start | bytes 3145732
  0.7 7.6 %copy-start.9 = (s32[1024]{0:T(1024)S(1)}, s32[1024]{0:T(1024)}, u32[]{:S(2)}) copy-start(s32[1024]{0:T(1024)} %param.32) | copy-start | bytes 12292
  0.7 7.6 %copy-start.10 = (s32[1024]{0:T(1024)S(1)}, s32[1024]{0:T(1024)}, u32[]{:S(2)}) copy-start(s32[1024]{0:T(1024)} %param.33) | copy-start | bytes 12292
  0.7 7.6 %copy-start.11 = (f32[512]{0:T(512)S(1)}, f32[512]{0:T(512)}, u32[]{:S(2)}) copy-start(f32[512]{0:T(512)} %param.25) | copy-start | bytes 6148
  0.7 7.6 %copy-start.12 = (f32[512]{0:T(512)S(1)}, f32[512]{0:T(512)}, u32[]{:S(2)}) copy-start(f32[512]{0:T(512)} %param.28) | copy-start | bytes 6148
  2.1 8.2 %copy-start.6 = (bf16[512,512]{1,0:T(8,128)(2,1)S(1)}, bf16[512,512]{1,0:T(8,128)(2,1)}, u32[]{:S(2)}) copy-start(bf16[512,512]{1,0:T(8,128)(2,1)} %nouter_ref.1) | copy-start | bytes 1572868
  2.1 8.2 %copy-start.7 = (bf16[512,512]{1,0:T(8,128)(2,1)S(1)}, bf16[512,512]{1,0:T(8,128)(2,1)}, u32[]{:S(2)}) copy-start(bf16[512,512]{1,0:T(8,128)(2,1)} %eouter_ref.3) | copy-start | bytes 1572868
  2.1 8.2 %copy-start.8 = (bf16[256,512]{1,0:T(8,128)(2,1)S(1)}, bf16[256,512]{1,0:T(8,128)(2,1)}, u32[]{:S(2)}) copy-start(bf16[256,512]{1,0:T(8,128)(2,1)} %cotan_ref.1) | copy-start | bytes 786436
  2.1 8.2 %copy-start.13 = (f32[512]{0:T(512)S(1)}, f32[512]{0:T(512)}, u32[]{:S(2)}) copy-start(f32[512]{0:T(512)} %param.26) | copy-start | bytes 6148
  2.1 8.2 %copy-start.14 = (f32[512]{0:T(512)S(1)}, f32[512]{0:T(512)}, u32[]{:S(2)}) copy-start(f32[512]{0:T(512)} %param.29) | copy-start | bytes 6148
  2.1 8.2 %copy-start.15 = (f32[512]{0:T(512)S(1)}, f32[512]{0:T(512)}, u32[]{:S(2)}) copy-start(f32[512]{0:T(512)} %param.30) | copy-start | bytes 6148
  2.1 8.2 %copy-start.16 = (f32[512]{0:T(512)S(1)}, f32[512]{0:T(512)}, u32[]{:S(2)}) copy-start(f32[512]{0:T(512)} %param.27) | copy-start | bytes 6148
  2.2 8.1 %collective-permute-start = (bf16[32,512]{1,0:T(8,128)(2,1)S(1)}, bf16[32,512]{1,0:T(8,128)(2,1)S(1)}, u32[]{:S(2)}, u32[]{:S(2)}) collective-permute-start(bf16[32,512]{1,0:T(8,128)(2,1)S(1)} %get-tuple-element.92), channel_id=1, source_target_pairs={{0,1},{1,2},{2,3},{3,4},{4,5},{5,6},{6,7},{7,0},{8,9},{9,10},{10,1... | collective-permute-start | bytes 98312 | tf_op jit(solution)/shard_map/ppermute | solution.py:310
  5.2 5.1 %collective-permute-start.1 = (bf16[32,512]{1,0:T(8,128)(2,1)S(1)}, bf16[32,512]{1,0:T(8,128)(2,1)S(1)}, u32[]{:S(2)}, u32[]{:S(2)}) collective-permute-start(bf16[32,512]{1,0:T(8,128)(2,1)S(1)} %get-tuple-element.93), channel_id=1, source_target_pairs={{0,7},{1,0},{2,1},{3,2},{4,3},{5,4},{6,5},{7,6},{8,15},{9,8},{10,9... | collective-permute-start | bytes 98312 | tf_op jit(solution)/shard_map/ppermute | solution.py:310
  10.4 3.9 %copy-start.5 = (bf16[1024,512]{1,0:T(8,128)(2,1)S(1)}, bf16[1024,512]{1,0:T(8,128)(2,1)}, u32[]{:S(2)}) copy-start(bf16[1024,512]{1,0:T(8,128)(2,1)} %ecotan_ref.1) | copy-start | bytes 3145732
  18.6 2.5 %collective-permute-start.3 = (bf16[1792,256]{1,0:T(8,128)(2,1)S(1)}, bf16[1792,256]{1,0:T(8,128)(2,1)S(1)}, u32[]{:S(2)}, u32[]{:S(2)}) collective-permute-start(bf16[1792,256]{1,0:T(8,128)(2,1)S(1)} %get-tuple-element.111), channel_id=1, source_target_pairs={{0,8},{1,9},{2,10},{3,11},{4,12},{5,13},{6,14},{7,15},{8,0},{9,1},... | collective-permute-start | bytes 2752520 | tf_op jit(solution)/shard_map/ppermute | solution.py:323
  20.5 2.6 %collective-permute-start.2 = (bf16[1792,256]{1,0:T(8,128)(2,1)S(1)}, bf16[1792,256]{1,0:T(8,128)(2,1)S(1)}, u32[]{:S(2)}, u32[]{:S(2)}) collective-permute-start(bf16[1792,256]{1,0:T(8,128)(2,1)S(1)} %get-tuple-element.116), channel_id=1, source_target_pairs={{0,8},{1,9},{2,10},{3,11},{4,12},{5,13},{6,14},{7,15},{8,0},{9,1},... | collective-permute-start | bytes 2752520 | tf_op jit(solution)/shard_map/ppermute | solution.py:323
  21.2 9.4 %collective-permute-start.4 = (bf16[1056,256]{1,0:T(8,128)(2,1)S(1)}, bf16[1056,256]{1,0:T(8,128)(2,1)S(1)}, u32[]{:S(2)}, u32[]{:S(2)}) collective-permute-start(bf16[1056,256]{1,0:T(8,128)(2,1)S(1)} %get-tuple-element.121), channel_id=1, source_target_pairs={{0,16},{1,17},{2,18},{3,19},{4,20},{5,21},{6,22},{7,23},{8,9},{9,8... | collective-permute-start | bytes 1622024 | tf_op jit(solution)/shard_map/ppermute | solution.py:323
  23.2 12.3 %collective-permute-start.6 = (bf16[896,256]{1,0:T(8,128)(2,1)S(1)}, bf16[896,256]{1,0:T(8,128)(2,1)S(1)}, u32[]{:S(2)}, u32[]{:S(2)}) collective-permute-start(bf16[896,256]{1,0:T(8,128)(2,1)S(1)} %send0.3), channel_id=1, source_target_pairs={{0,16},{1,17},{2,18},{3,19},{4,20},{5,21},{6,22},{7,23},{8,9},{9,8... | collective-permute-start | bytes 1376264 | tf_op jit(solution)/shard_map/ppermute | solution.py:323
  30.7 7.3 %collective-permute-start.5 = (bf16[608,256]{1,0:T(8,128)(2,1)S(1)}, bf16[608,256]{1,0:T(8,128)(2,1)S(1)}, u32[]{:S(2)}, u32[]{:S(2)}) collective-permute-start(bf16[608,256]{1,0:T(8,128)(2,1)S(1)} %get-tuple-element.134), channel_id=1, source_target_pairs={{0,1},{1,0},{2,3},{3,2},{4,5},{5,4},{6,7},{7,6},{8,10},{9,11},{10,... | collective-permute-start | bytes 933896 | tf_op jit(solution)/shard_map/ppermute | solution.py:323
  35.6 6.1 %collective-permute-start.8 = (bf16[448,256]{1,0:T(8,128)(2,1)S(1)}, bf16[448,256]{1,0:T(8,128)(2,1)S(1)}, u32[]{:S(2)}, u32[]{:S(2)}) collective-permute-start(bf16[448,256]{1,0:T(8,128)(2,1)S(1)} %send1.3), channel_id=1, source_target_pairs={{0,1},{1,0},{2,3},{3,2},{4,5},{5,4},{6,7},{7,6},{8,10},{9,11},{10,... | collective-permute-start | bytes 688136 | tf_op jit(solution)/shard_map/ppermute | solution.py:323
  38.1 5.7 %collective-permute-start.7 = (bf16[320,256]{1,0:T(8,128)(2,1)S(1)}, bf16[320,256]{1,0:T(8,128)(2,1)S(1)}, u32[]{:S(2)}, u32[]{:S(2)}) collective-permute-start(bf16[320,256]{1,0:T(8,128)(2,1)S(1)} %get-tuple-element.145), channel_id=1, source_target_pairs={{0,2},{1,3},{2,0},{3,1},{4,6},{5,7},{6,4},{7,5},{8,12},{9,13},{10,... | collective-permute-start | bytes 491528 | tf_op jit(solution)/shard_map/ppermute | solution.py:323
  41.7 8.1 %copy-start.2 = (s32[1,1,2,32]{3,2,1,0:T(2,128)S(1)}, s32[1,1,2,32]{3,2,1,0:T(2,128)}, u32[]{:S(2)}) copy-start(s32[1,1,2,32]{3,2,1,0:T(2,128)} %param.31) | copy-start | bytes 772
  41.7 5.1 %collective-permute-start.11 = (bf16[224,256]{1,0:T(8,128)(2,1)S(1)}, bf16[224,256]{1,0:T(8,128)(2,1)S(1)}, u32[]{:S(2)}, u32[]{:S(2)}) collective-permute-start(bf16[224,256]{1,0:T(8,128)(2,1)S(1)} %send2.3), channel_id=1, source_target_pairs={{0,2},{1,3},{2,0},{3,1},{4,6},{5,7},{6,4},{7,5},{8,12},{9,13},{10,... | collective-permute-start | bytes 344072 | tf_op jit(solution)/shard_map/ppermute | solution.py:323
  43.9 5.7 %collective-permute-start.9 = (bf16[208,256]{1,0:T(8,128)(2,1)S(1)}, bf16[208,256]{1,0:T(8,128)(2,1)S(1)}, u32[]{:S(2)}, u32[]{:S(2)}) collective-permute-start(bf16[208,256]{1,0:T(8,128)(2,1)S(1)} %get-tuple-element.158), channel_id=1, source_target_pairs={{0,4},{1,5},{2,6},{3,7},{4,0},{5,1},{6,2},{7,3},{8,24},{9,25},{10,... | collective-permute-start | bytes 319496 | tf_op jit(solution)/shard_map/ppermute | solution.py:323
  46.8 5.1 %collective-permute-start.12 = (bf16[112,256]{1,0:T(8,128)(2,1)S(1)}, bf16[112,256]{1,0:T(8,128)(2,1)S(1)}, u32[]{:S(2)}, u32[]{:S(2)}) collective-permute-start(bf16[112,256]{1,0:T(8,128)(2,1)S(1)} %send3.3), channel_id=1, source_target_pairs={{0,4},{1,5},{2,6},{3,7},{4,0},{5,1},{6,2},{7,3},{8,24},{9,25},{10,... | collective-permute-start | bytes 172040 | tf_op jit(solution)/shard_map/ppermute | solution.py:323
  49.6 2.4 %collective-permute-start.10 = (f32[6,512]{1,0:T(8,128)S(1)}, f32[6,512]{1,0:T(8,128)S(1)}, u32[]{:S(2)}, u32[]{:S(2)}) collective-permute-start(f32[6,512]{1,0:T(8,128)S(1)} %get-tuple-element.161.vec_ref), channel_id=1, source_target_pairs={{0,8},{1,9},{2,10},{3,11},{4,12},{5,13},{6,14},{7,15},{8,0},{9,1},... | collective-permute-start | bytes 36872 | tf_op jit(solution)/shard_map/ppermute | solution.py:323

commit v10 on v9

--- a/solution.py
+++ b/solution.py
@@ -194,8 +194,8 @@
 
 def backward_kernel(
     pick_ref, turned_ref, ecotan_ref, normed_ref, invstd_ref, slope_ref, pulled_ref, eouter_ref,
-    egain_ref, node_sums_ref,
-    fresh_ref, preact_ref, spread_ref, sums_ref, linear_ref, *, scale,
+    egain_ref, node_sums_ref, einner_ref,
+    fresh_ref, preact_ref, spread_ref, sums_ref, linear_ref, rim_ref, *, scale,
 ):
     edge_count = ecotan_ref.shape[0]
     count = pulled_ref.shape[0]
@@ -232,6 +232,7 @@
     sums_ref[3:, :] = node_sums_ref[...]
     used = spread_ref.shape[0]
     spread_ref[...] = mm(turned_ref[:used, :], preact_ref[...]).astype(BF)
+    rim_kernel(spread_ref, einner_ref, rim_ref, count=count)
 
 
 def weights_kernel(
@@ -541,8 +542,7 @@
         marks = (sent,)
         got[plan] = permute_by(sent, plan.core_bit, plan.core_bit, plan.core_bit)
         if state is None:
-            state = sides.early(marks)
-            marks = (state,)
+            state = sides.early
     shapes = [(vec.shape, F32), (state.shape, BF)]
     for step in range(plans[0].steps):
         if step == 1:
@@ -677,7 +677,7 @@
         edge_inner, edge_outer, edge_offset, edge_gain, node_offset, node_gain,
         node_inner, node_outer, node_cotan, name="forward", flops=5 << 30,
     )
-    fresh, preact, spread, sums, linear = call(
+    fresh, preact, spread, sums, linear, rims = call(
         functools.partial(backward_kernel, scale=edge_norm),
         [
             ((edge_count, width), F32),
@@ -685,9 +685,10 @@
             ((2 * count + slots, hidden_width), BF),
             ((6, width), F32),
             ((edge_count, width), BF),
+            ((slots, width), BF),
         ],
         near(pick), near(turned), edge_cotan, near(normed), near(invstd), near(slope), near(pulled),
-        edge_outer, edge_gain, near(node_sums),
+        edge_outer, edge_gain, near(node_sums), edge_inner,
         name="backward", flops=3 << 30,
     )
 
@@ -708,14 +709,6 @@
 
     results = {}
 
-    def rim_side(marks):
-        (spread_late,) = after(marks, spread)
-        (rims,) = call(
-            functools.partial(rim_kernel, count=count), [((slots, width), BF)],
-            near(spread_late), edge_inner, name="rim", limit=4 << 20,
-        )
-        return rims
-
     def grads_side(marks):
         spread_late, fresh_late = after(marks, spread, fresh)
         results["nodes"], results["edges"] = call(
@@ -728,11 +721,10 @@
 
     if plans:
         grad_weights, grad_vectors, grad_nodes = reduce_kernels(
-            plans, Sides(weights_of, rim_side, grads_side, lists), sums, hidden_width
+            plans, Sides(weights_of, rims, grads_side, lists), sums, hidden_width
         )
     else:
         grad_weights, grad_vectors = reduce_all(weights_of(None, ())[0], sums)
-        rims = rim_side((sums,))
         back = jnp.concatenate([ring(rims[:half], 1), ring(rims[half:], -1)])
         grads_side((sums,))
         (grad_nodes,) = call(

time: 52.8 us -> 53 us (level)
    pallas_call x27 -> x26, Pallas kernels: 17.9 us -> 17.8 us  [call(): pl.pallas_call(body, out_shape=shapes, in_specs=[anywhere if i in hbm els...]
  transfers between devices with their start and end apart: 13 -> 13, of which waited for: 10 -> 9; matrix products, arithmetic and copies ran while one was open for 0% -> 0% of each run, Pallas kernels for 15% -> 14%
where the time goes in v10:
time: 53 us; the launch traced here: 52.8 us
  starting transfers between devices  19.4 us (37%)
  Pallas kernels  17.8 us (34%)
  waiting for transfers between devices  14.5 us (27%)
  between operations  1.04 us (2%)
    pallas_call x26, Pallas kernels, call(): pl.pallas_call(body, out_shape=shapes, in_specs=[anywhere if i in hbm els...  17.8 us
    ppermute x11, waiting for transfers between devices, permute_by(): return lax.ppermute(values, AXES, pairs)  14.5 us
    ppermute x11, starting transfers between devices, permute_by(): return lax.ppermute(values, AXES, pairs)  13.3 us
    ppermute x2, starting transfers between devices, ring(): lax.ppermute(values, 'patch', [(i, (i + step) % count) for i in range(cou...  6.12 us
  transfers between devices with their start and end apart: 13, of which 9 were waited for; matrix products, arithmetic and copies ran while one was open for 0% of the time, Pallas kernels for 14%

profile of v10, /device:TPU:0, one launch (start us, length us, event | category | flops | bytes accessed | tf_op | source)
XLA Modules:
  0.0 52.8 jit_solution(4986438727487904820)
XLA Ops:
  0.7 1.4 %pick.1 = (bf16[32,512]{1,0:T(8,128)(2,1)S(1)}, bf16[32,512]{1,0:T(8,128)(2,1)S(1)}) custom-call(s32[2,32]{1,0:T(2,128)} %bitcast.11, bf16[256,512]{1,0:T(8,128)(2,1)} %nodes_ref.5), custom_call_target="tpu_custom_call" | custom-call | flops 21474836480 | bytes 65536 | tf_op jit(solution)/shard_map/pick/pallas_call | solution.py:42
  2.2 3.0 %collective-permute-start = (bf16[32,512]{1,0:T(8,128)(2,1)S(1)}, bf16[32,512]{1,0:T(8,128)(2,1)S(1)}, u32[]{:S(2)}, u32[]{:S(2)}) collective-permute-start(bf16[32,512]{1,0:T(8,128)(2,1)S(1)} %get-tuple-element.92), channel_id=1, source_target_pairs={{0,1},{1,2},{2,3},{3,4},{4,5},{5,6},{6,7},{7,0},{8,9},{9,10},{10,1... | collective-permute-start | bytes 98312 | tf_op jit(solution)/shard_map/ppermute | solution.py:311
  5.2 3.1 %collective-permute-start.1 = (bf16[32,512]{1,0:T(8,128)(2,1)S(1)}, bf16[32,512]{1,0:T(8,128)(2,1)S(1)}, u32[]{:S(2)}, u32[]{:S(2)}) collective-permute-start(bf16[32,512]{1,0:T(8,128)(2,1)S(1)} %get-tuple-element.93), channel_id=1, source_target_pairs={{0,7},{1,0},{2,1},{3,2},{4,3},{5,4},{6,5},{7,6},{8,15},{9,8},{10,9... | collective-permute-start | bytes 98312 | tf_op jit(solution)/shard_map/ppermute | solution.py:311
  8.3 1.9 %table.1 = (f32[1024,512]{1,0:T(8,128)S(1)}, f32[256,512]{1,0:T(8,128)S(1)}, bf16[1024,640]{1,0:T(8,128)(2,1)S(1)}, bf16[640,1024]{1,0:T(8,128)(2,1)S(1)}, bf16[512,1024]{1,0:T(8,128)(2,1)S(1)}) custom-call(s32[1,1024]{1,0:T(1,128)S(1)} %bitcast.13, s32[1,1024]{1,0:T(1,128)S(1)} %bitcast.14, f32[1,512]{1,0:T(1,128)S(1)} %bitcast.15, ...), custom_call_target="tpu_custom_call" | custom-call | flops 1073741824 | bytes 6291456 | tf_op jit(solution)/shard_map/table/pallas_call | solution.py:42
  10.4 3.9 %forward.1 = (bf16[1024,512]{1,0:T(8,128)(2,1)S(1)}, f32[1024,512]{1,0:T(8,128)S(1)}, f32[1024,512]{1,0:T(8,128)S(1)}, f32[1024,1]{1,0:T(8,128)S(1)}, bf16[256,5...) custom-call(f32[1024,512]{1,0:T(8,128)S(1)} %get-tuple-element.90.pa, ...), custom_call_target="tpu_custom_call" | custom-call | flops 5368709120 | bytes 7088128 | tf_op jit(solution)/shard_map/forward/pallas_call | solution.py:42
  14.3 2.8 %backward.1 = (f32[1024,512]{1,0:T(8,128)S(1)}, bf16[1024,512]{1,0:T(8,128)(2,1)S(1)}, bf16[576,512]{1,0:T(8,128)(2,1)S(1)}, f32[6,512]{1,0:T(8,128)S(1)}, bf16[...) custom-call(bf16[1024,640]{1,0:T(8,128)(2,1)S(1)} %get-tuple-element.88.pick_ref, ...), custom_call_target="tpu_custom_call" | custom-call | flops 3221225472 | bytes 4861952 | tf_op jit(solution)/shard_map/backward/pallas_call | solution.py:42
  17.1 1.6 %weights.2 = (f32[3584,256]{1,0:T(8,128)S(1)}, bf16[1792,256]{1,0:T(8,128)(2,1)S(1)}) custom-call(bf16[512,1024]{1,0:T(8,128)(2,1)S(1)} %get-tuple-element.101.edges_turned_ref, bf16[256,512]{1,0:T(8,128)(2,1)S(1)} %copy-done, bf16[32,512]{1,0:T(8,128)(2,1)S(1)} %collective-permute-done.low_ref, bf16[32,512]{1,0:T(8,128)(2,1)S(1)} %collective-permute-done.1.high_ref, ...), custom_call_target="tpu_custom_call" | custom-call | flops 1073741824 | bytes 4587520 | tf_op jit(solution)/shard_map/weights/pallas_call | solution.py:42
  18.8 1.6 %weights.3 = (f32[3584,256]{1,0:T(8,128)S(1)}, bf16[1792,256]{1,0:T(8,128)(2,1)S(1)}) custom-call(bf16[512,1024]{1,0:T(8,128)(2,1)S(1)} %get-tuple-element.101.edges_turned_ref, bf16[256,512]{1,0:T(8,128)(2,1)S(1)} %copy-done, bf16[32,512]{1,0:T(8,128)(2,1)S(1)} %collective-permute-done.low_ref, bf16[32,512]{1,0:T(8,128)(2,1)S(1)} %collective-permute-done.1.high_ref, ...), custom_call_target="tpu_custom_call" | custom-call | flops 1073741824 | bytes 4587520 | tf_op jit(solution)/shard_map/weights/pallas_call | solution.py:42
  20.3 0.5 collective-permute-start.2
  20.9 0.4 collective-permute-done.3.got_ref
  21.2 0.1 send0.2
  21.3 1.7 %collective-permute-start.4 = (bf16[1056,256]{1,0:T(8,128)(2,1)S(1)}, bf16[1056,256]{1,0:T(8,128)(2,1)S(1)}, u32[]{:S(2)}, u32[]{:S(2)}) collective-permute-start(bf16[1056,256]{1,0:T(8,128)(2,1)S(1)} %get-tuple-element.121), channel_id=1, source_target_pairs={{0,16},{1,17},{2,18},{3,19},{4,20},{5,21},{6,22},{7,23},{8,9},{9,8... | collective-permute-start | bytes 1622024 | tf_op jit(solution)/shard_map/ppermute | solution.py:324
  23.1 1.6 %collective-permute-start.6 = (bf16[896,256]{1,0:T(8,128)(2,1)S(1)}, bf16[896,256]{1,0:T(8,128)(2,1)S(1)}, u32[]{:S(2)}, u32[]{:S(2)}) collective-permute-start(bf16[896,256]{1,0:T(8,128)(2,1)S(1)} %send0.3), channel_id=1, source_target_pairs={{0,16},{1,17},{2,18},{3,19},{4,20},{5,21},{6,22},{7,23},{8,9},{9,8... | collective-permute-start | bytes 1376264 | tf_op jit(solution)/shard_map/ppermute | solution.py:324
  24.7 0.1 keep0.2.src_ref
  24.8 2.0 %grads.1 = (f32[256,512]{1,0:T(8,128)S(1)}, bf16[1024,512]{1,0:T(8,128)(2,1)}) custom-call(bf16[576,512]{1,0:T(8,128)(2,1)S(1)} %get-tuple-element.124.spread_ref, bf16[1536,512]{1,0:T(8,128)(2,1)S(1)} %copy-done.2, f32[256,512]{1,0:T(8,128)S(1)} %get-tuple-element.125.partial_ref, f32[1024,512]{1,0:T(8,128)S(1)} %get-tuple-element.126.fresh_ref, ...), custom_call_target="tpu_custom_call" | custom-call | flops 2147483648 | bytes 1572864 | tf_op jit(solution)/shard_map/grads/pallas_call | solution.py:42
  26.8 3.9 %collective-permute-done.4.got_ref = bf16[1056,256]{1,0:T(8,128)(2,1)S(1)} collective-permute-done((bf16[1056,256]{1,0:T(8,128)(2,1)S(1)}, bf16[1056,256]{1,0:T(8,128)(2,1)S(1)}, u32[]{:S(2)}, u32[]{:S(2)}) %collective-permute-start.4) | collective-permute-done | bytes 540704 | tf_op jit(solution)/shard_map/ppermute | solution.py:324
  30.8 1.3 %collective-permute-start.5 = (bf16[608,256]{1,0:T(8,128)(2,1)S(1)}, bf16[608,256]{1,0:T(8,128)(2,1)S(1)}, u32[]{:S(2)}, u32[]{:S(2)}) collective-permute-start(bf16[608,256]{1,0:T(8,128)(2,1)S(1)} %get-tuple-element.134), channel_id=1, source_target_pairs={{0,1},{1,0},{2,3},{3,2},{4,5},{5,4},{6,7},{7,6},{8,10},{9,11},{10,... | collective-permute-start | bytes 933896 | tf_op jit(solution)/shard_map/ppermute | solution.py:324
  32.1 0.1 keep0.3.src_ref
  32.2 3.5 %collective-permute-done.6.got_ref = bf16[896,256]{1,0:T(8,128)(2,1)S(1)} collective-permute-done((bf16[896,256]{1,0:T(8,128)(2,1)S(1)}, bf16[896,256]{1,0:T(8,128)(2,1)S(1)}, u32[]{:S(2)}, u32[]{:S(2)}) %collective-permute-start.6) | collective-permute-done | bytes 458784 | tf_op jit(solution)/shard_map/ppermute | solution.py:324
  35.7 1.3 %collective-permute-start.8 = (bf16[448,256]{1,0:T(8,128)(2,1)S(1)}, bf16[448,256]{1,0:T(8,128)(2,1)S(1)}, u32[]{:S(2)}, u32[]{:S(2)}) collective-permute-start(bf16[448,256]{1,0:T(8,128)(2,1)S(1)} %send1.3), channel_id=1, source_target_pairs={{0,1},{1,0},{2,3},{3,2},{4,5},{5,4},{6,7},{7,6},{8,10},{9,11},{10,... | collective-permute-start | bytes 688136 | tf_op jit(solution)/shard_map/ppermute | solution.py:324
  37.0 1.1 %collective-permute-done.5.got_ref = bf16[608,256]{1,0:T(8,128)(2,1)S(1)} collective-permute-done((bf16[608,256]{1,0:T(8,128)(2,1)S(1)}, bf16[608,256]{1,0:T(8,128)(2,1)S(1)}, u32[]{:S(2)}, u32[]{:S(2)}) %collective-permute-start.5) | collective-permute-done | bytes 311328 | tf_op jit(solution)/shard_map/ppermute | solution.py:324
  38.2 1.1 %collective-permute-start.7 = (bf16[320,256]{1,0:T(8,128)(2,1)S(1)}, bf16[320,256]{1,0:T(8,128)(2,1)S(1)}, u32[]{:S(2)}, u32[]{:S(2)}) collective-permute-start(bf16[320,256]{1,0:T(8,128)(2,1)S(1)} %get-tuple-element.145), channel_id=1, source_target_pairs={{0,2},{1,3},{2,0},{3,1},{4,6},{5,7},{6,4},{7,5},{8,12},{9,13},{10,... | collective-permute-start | bytes 491528 | tf_op jit(solution)/shard_map/ppermute | solution.py:324
  39.4 2.4 %collective-permute-done.8.got_ref = bf16[448,256]{1,0:T(8,128)(2,1)S(1)} collective-permute-done((bf16[448,256]{1,0:T(8,128)(2,1)S(1)}, bf16[448,256]{1,0:T(8,128)(2,1)S(1)}, u32[]{:S(2)}, u32[]{:S(2)}) %collective-permute-start.8) | collective-permute-done | bytes 229408 | tf_op jit(solution)/shard_map/ppermute | solution.py:324
  41.8 0.8 %collective-permute-start.11 = (bf16[224,256]{1,0:T(8,128)(2,1)S(1)}, bf16[224,256]{1,0:T(8,128)(2,1)S(1)}, u32[]{:S(2)}, u32[]{:S(2)}) collective-permute-start(bf16[224,256]{1,0:T(8,128)(2,1)S(1)} %send2.3), channel_id=1, source_target_pairs={{0,2},{1,3},{2,0},{3,1},{4,6},{5,7},{6,4},{7,5},{8,12},{9,13},{10,... | collective-permute-start | bytes 344072 | tf_op jit(solution)/shard_map/ppermute | solution.py:324
  42.7 1.2 %collective-permute-done.7.got_ref = bf16[320,256]{1,0:T(8,128)(2,1)S(1)} collective-permute-done((bf16[320,256]{1,0:T(8,128)(2,1)S(1)}, bf16[320,256]{1,0:T(8,128)(2,1)S(1)}, u32[]{:S(2)}, u32[]{:S(2)}) %collective-permute-start.7) | collective-permute-done | bytes 163872 | tf_op jit(solution)/shard_map/ppermute | solution.py:324
  44.0 2.6 %collective-permute-start.9 = (bf16[208,256]{1,0:T(8,128)(2,1)S(1)}, bf16[208,256]{1,0:T(8,128)(2,1)S(1)}, u32[]{:S(2)}, u32[]{:S(2)}) collective-permute-start(bf16[208,256]{1,0:T(8,128)(2,1)S(1)} %get-tuple-element.158), channel_id=1, source_target_pairs={{0,4},{1,5},{2,6},{3,7},{4,0},{5,1},{6,2},{7,3},{8,24},{9,25},{10,... | collective-permute-start | bytes 319496 | tf_op jit(solution)/shard_map/ppermute | solution.py:324
  46.6 0.3 collective-permute-done.11.got_ref
  47.0 2.3 %collective-permute-start.12 = (bf16[112,256]{1,0:T(8,128)(2,1)S(1)}, bf16[112,256]{1,0:T(8,128)(2,1)S(1)}, u32[]{:S(2)}, u32[]{:S(2)}) collective-permute-start(bf16[112,256]{1,0:T(8,128)(2,1)S(1)} %send3.3), channel_id=1, source_target_pairs={{0,4},{1,5},{2,6},{3,7},{4,0},{5,1},{6,2},{7,3},{8,24},{9,25},{10,... | collective-permute-start | bytes 172040 | tf_op jit(solution)/shard_map/ppermute | solution.py:324
  49.2 0.4 collective-permute-done.9.got_ref.refs_1_
  49.9 1.1 %rims.1 = f32[256,512]{1,0:T(8,128)} custom-call(s32[2,32]{1,0:T(2,128)S(1)} %bitcast.12, f32[256,512]{1,0:T(8,128)S(1)} %get-tuple-element.127.partial_ref, bf16[64,512]{1,0:T(8,128)(2,1)S(1)} %get-tuple-element.159.back_ref), custom_call_target="tpu_custom_call" | custom-call | bytes 524288 | tf_op jit(solution)/shard_map/rims/pallas_call | solution.py:42
  51.0 1.1 %collective-permute-done.12.refs_3_ = bf16[112,256]{1,0:T(8,128)(2,1)S(1)} collective-permute-done((bf16[112,256]{1,0:T(8,128)(2,1)S(1)}, bf16[112,256]{1,0:T(8,128)(2,1)S(1)}, u32[]{:S(2)}, u32[]{:S(2)}) %collective-permute-start.12) | collective-permute-done | bytes 57376 | tf_op jit(solution)/shard_map/ppermute | solution.py:324
  52.1 0.7 %close.1 = (f32[448,128]{1,0:T(8,128)}, f32[24,128]{1,0:T(8,128)}) custom-call(f32[6,512]{1,0:T(8,128)S(1)} %get-tuple-element.161.vec_ref, f32[6,512]{1,0:T(8,128)S(1)} %collective-permute-done.10.other_ref, f32[112,256]{1,0:T(8,128)S(1)} %keep3.2.refs_0_, bf16[208,256]{1,0:T(8,128)(2,1)S(1)} %collective-permute-done.9.got_ref.refs_1_, ...), custom_call_target="tpu_custom_call" | custom-call | bytes 241664 | tf_op jit(solution)/shard_map/close/pallas_call | solution.py:42
  (54 shorter events, 0.9 us)
Async XLA Ops:
  0.6 7.7 %copy-start = (bf16[256,512]{1,0:T(8,128)(2,1)S(1)}, bf16[256,512]{1,0:T(8,128)(2,1)}, u32[]{:S(2)}) copy-start(bf16[256,512]{1,0:T(8,128)(2,1)} %nodes_ref.5) | copy-start | bytes 786436
  0.6 7.7 %copy-start.2 = (bf16[1536,512]{1,0:T(8,128)(2,1)S(1)}, bf16[1536,512]{1,0:T(8,128)(2,1)}, u32[]{:S(2)}) copy-start(bf16[1536,512]{1,0:T(8,128)(2,1)} %inner_ref.3) | copy-start | bytes 4718596
  0.7 7.6 %copy-start.3 = (bf16[1024,512]{1,0:T(8,128)(2,1)S(1)}, bf16[1024,512]{1,0:T(8,128)(2,1)}, u32[]{:S(2)}) copy-start(bf16[1024,512]{1,0:T(8,128)(2,1)} %edges_ref.3) | copy-start | bytes 3145732
  0.7 7.6 %copy-start.4 = (bf16[1024,512]{1,0:T(8,128)(2,1)S(1)}, bf16[1024,512]{1,0:T(8,128)(2,1)}, u32[]{:S(2)}) copy-start(bf16[1024,512]{1,0:T(8,128)(2,1)} %ninner_ref.3) | copy-start | bytes 3145732
  0.7 7.6 %copy-start.9 = (s32[1024]{0:T(1024)S(1)}, s32[1024]{0:T(1024)}, u32[]{:S(2)}) copy-start(s32[1024]{0:T(1024)} %param.32) | copy-start | bytes 12292
  0.7 7.6 %copy-start.10 = (s32[1024]{0:T(1024)S(1)}, s32[1024]{0:T(1024)}, u32[]{:S(2)}) copy-start(s32[1024]{0:T(1024)} %param.33) | copy-start | bytes 12292
  0.7 7.6 %copy-start.11 = (f32[512]{0:T(512)S(1)}, f32[512]{0:T(512)}, u32[]{:S(2)}) copy-start(f32[512]{0:T(512)} %param.25) | copy-start | bytes 6148
  0.7 7.6 %copy-start.12 = (f32[512]{0:T(512)S(1)}, f32[512]{0:T(512)}, u32[]{:S(2)}) copy-start(f32[512]{0:T(512)} %param.28) | copy-start | bytes 6148
  2.1 8.2 %copy-start.6 = (bf16[512,512]{1,0:T(8,128)(2,1)S(1)}, bf16[512,512]{1,0:T(8,128)(2,1)}, u32[]{:S(2)}) copy-start(bf16[512,512]{1,0:T(8,128)(2,1)} %nouter_ref.1) | copy-start | bytes 1572868
  2.1 8.2 %copy-start.7 = (bf16[512,512]{1,0:T(8,128)(2,1)S(1)}, bf16[512,512]{1,0:T(8,128)(2,1)}, u32[]{:S(2)}) copy-start(bf16[512,512]{1,0:T(8,128)(2,1)} %eouter_ref.3) | copy-start | bytes 1572868
  2.1 8.2 %copy-start.8 = (bf16[256,512]{1,0:T(8,128)(2,1)S(1)}, bf16[256,512]{1,0:T(8,128)(2,1)}, u32[]{:S(2)}) copy-start(bf16[256,512]{1,0:T(8,128)(2,1)} %cotan_ref.1) | copy-start | bytes 786436
  2.1 8.2 %copy-start.13 = (f32[512]{0:T(512)S(1)}, f32[512]{0:T(512)}, u32[]{:S(2)}) copy-start(f32[512]{0:T(512)} %param.26) | copy-start | bytes 6148
  2.1 8.2 %copy-start.14 = (f32[512]{0:T(512)S(1)}, f32[512]{0:T(512)}, u32[]{:S(2)}) copy-start(f32[512]{0:T(512)} %param.29) | copy-start | bytes 6148
  2.1 8.2 %copy-start.15 = (f32[512]{0:T(512)S(1)}, f32[512]{0:T(512)}, u32[]{:S(2)}) copy-start(f32[512]{0:T(512)} %param.30) | copy-start | bytes 6148
  2.2 8.2 %copy-start.16 = (f32[512]{0:T(512)S(1)}, f32[512]{0:T(512)}, u32[]{:S(2)}) copy-start(f32[512]{0:T(512)} %param.27) | copy-start | bytes 6148
  2.2 8.1 %collective-permute-start = (bf16[32,512]{1,0:T(8,128)(2,1)S(1)}, bf16[32,512]{1,0:T(8,128)(2,1)S(1)}, u32[]{:S(2)}, u32[]{:S(2)}) collective-permute-start(bf16[32,512]{1,0:T(8,128)(2,1)S(1)} %get-tuple-element.92), channel_id=1, source_target_pairs={{0,1},{1,2},{2,3},{3,4},{4,5},{5,6},{6,7},{7,0},{8,9},{9,10},{10,1... | collective-permute-start | bytes 98312 | tf_op jit(solution)/shard_map/ppermute | solution.py:311
  5.2 5.1 %collective-permute-start.1 = (bf16[32,512]{1,0:T(8,128)(2,1)S(1)}, bf16[32,512]{1,0:T(8,128)(2,1)S(1)}, u32[]{:S(2)}, u32[]{:S(2)}) collective-permute-start(bf16[32,512]{1,0:T(8,128)(2,1)S(1)} %get-tuple-element.93), channel_id=1, source_target_pairs={{0,7},{1,0},{2,1},{3,2},{4,3},{5,4},{6,5},{7,6},{8,15},{9,8},{10,9... | collective-permute-start | bytes 98312 | tf_op jit(solution)/shard_map/ppermute | solution.py:311
  10.4 3.9 %copy-start.5 = (bf16[1024,512]{1,0:T(8,128)(2,1)S(1)}, bf16[1024,512]{1,0:T(8,128)(2,1)}, u32[]{:S(2)}) copy-start(bf16[1024,512]{1,0:T(8,128)(2,1)} %ecotan_ref.1) | copy-start | bytes 3145732
  18.7 2.5 %collective-permute-start.3 = (bf16[1792,256]{1,0:T(8,128)(2,1)S(1)}, bf16[1792,256]{1,0:T(8,128)(2,1)S(1)}, u32[]{:S(2)}, u32[]{:S(2)}) collective-permute-start(bf16[1792,256]{1,0:T(8,128)(2,1)S(1)} %get-tuple-element.111), channel_id=1, source_target_pairs={{0,8},{1,9},{2,10},{3,11},{4,12},{5,13},{6,14},{7,15},{8,0},{9,1},... | collective-permute-start | bytes 2752520 | tf_op jit(solution)/shard_map/ppermute | solution.py:324
  20.3 2.6 %collective-permute-start.2 = (bf16[1792,256]{1,0:T(8,128)(2,1)S(1)}, bf16[1792,256]{1,0:T(8,128)(2,1)S(1)}, u32[]{:S(2)}, u32[]{:S(2)}) collective-permute-start(bf16[1792,256]{1,0:T(8,128)(2,1)S(1)} %get-tuple-element.115), channel_id=1, source_target_pairs={{0,8},{1,9},{2,10},{3,11},{4,12},{5,13},{6,14},{7,15},{8,0},{9,1},... | collective-permute-start | bytes 2752520 | tf_op jit(solution)/shard_map/ppermute | solution.py:324
  21.3 9.4 %collective-permute-start.4 = (bf16[1056,256]{1,0:T(8,128)(2,1)S(1)}, bf16[1056,256]{1,0:T(8,128)(2,1)S(1)}, u32[]{:S(2)}, u32[]{:S(2)}) collective-permute-start(bf16[1056,256]{1,0:T(8,128)(2,1)S(1)} %get-tuple-element.121), channel_id=1, source_target_pairs={{0,16},{1,17},{2,18},{3,19},{4,20},{5,21},{6,22},{7,23},{8,9},{9,8... | collective-permute-start | bytes 1622024 | tf_op jit(solution)/shard_map/ppermute | solution.py:324
  23.1 12.6 %collective-permute-start.6 = (bf16[896,256]{1,0:T(8,128)(2,1)S(1)}, bf16[896,256]{1,0:T(8,128)(2,1)S(1)}, u32[]{:S(2)}, u32[]{:S(2)}) collective-permute-start(bf16[896,256]{1,0:T(8,128)(2,1)S(1)} %send0.3), channel_id=1, source_target_pairs={{0,16},{1,17},{2,18},{3,19},{4,20},{5,21},{6,22},{7,23},{8,9},{9,8... | collective-permute-start | bytes 1376264 | tf_op jit(solution)/shard_map/ppermute | solution.py:324
  30.8 7.3 %collective-permute-start.5 = (bf16[608,256]{1,0:T(8,128)(2,1)S(1)}, bf16[608,256]{1,0:T(8,128)(2,1)S(1)}, u32[]{:S(2)}, u32[]{:S(2)}) collective-permute-start(bf16[608,256]{1,0:T(8,128)(2,1)S(1)} %get-tuple-element.134), channel_id=1, source_target_pairs={{0,1},{1,0},{2,3},{3,2},{4,5},{5,4},{6,7},{7,6},{8,10},{9,11},{10,... | collective-permute-start | bytes 933896 | tf_op jit(solution)/shard_map/ppermute | solution.py:324
  35.7 6.1 %collective-permute-start.8 = (bf16[448,256]{1,0:T(8,128)(2,1)S(1)}, bf16[448,256]{1,0:T(8,128)(2,1)S(1)}, u32[]{:S(2)}, u32[]{:S(2)}) collective-permute-start(bf16[448,256]{1,0:T(8,128)(2,1)S(1)} %send1.3), channel_id=1, source_target_pairs={{0,1},{1,0},{2,3},{3,2},{4,5},{5,4},{6,7},{7,6},{8,10},{9,11},{10,... | collective-permute-start | bytes 688136 | tf_op jit(solution)/shard_map/ppermute | solution.py:324
  38.2 5.7 %collective-permute-start.7 = (bf16[320,256]{1,0:T(8,128)(2,1)S(1)}, bf16[320,256]{1,0:T(8,128)(2,1)S(1)}, u32[]{:S(2)}, u32[]{:S(2)}) collective-permute-start(bf16[320,256]{1,0:T(8,128)(2,1)S(1)} %get-tuple-element.145), channel_id=1, source_target_pairs={{0,2},{1,3},{2,0},{3,1},{4,6},{5,7},{6,4},{7,5},{8,12},{9,13},{10,... | collective-permute-start | bytes 491528 | tf_op jit(solution)/shard_map/ppermute | solution.py:324
  41.8 8.1 %copy-start.1 = (s32[1,1,2,32]{3,2,1,0:T(2,128)S(1)}, s32[1,1,2,32]{3,2,1,0:T(2,128)}, u32[]{:S(2)}) copy-start(s32[1,1,2,32]{3,2,1,0:T(2,128)} %param.31) | copy-start | bytes 772
  41.8 5.1 %collective-permute-start.11 = (bf16[224,256]{1,0:T(8,128)(2,1)S(1)}, bf16[224,256]{1,0:T(8,128)(2,1)S(1)}, u32[]{:S(2)}, u32[]{:S(2)}) collective-permute-start(bf16[224,256]{1,0:T(8,128)(2,1)S(1)} %send2.3), channel_id=1, source_target_pairs={{0,2},{1,3},{2,0},{3,1},{4,6},{5,7},{6,4},{7,5},{8,12},{9,13},{10,... | collective-permute-start | bytes 344072 | tf_op jit(solution)/shard_map/ppermute | solution.py:324
  44.0 5.7 %collective-permute-start.9 = (bf16[208,256]{1,0:T(8,128)(2,1)S(1)}, bf16[208,256]{1,0:T(8,128)(2,1)S(1)}, u32[]{:S(2)}, u32[]{:S(2)}) collective-permute-start(bf16[208,256]{1,0:T(8,128)(2,1)S(1)} %get-tuple-element.158), channel_id=1, source_target_pairs={{0,4},{1,5},{2,6},{3,7},{4,0},{5,1},{6,2},{7,3},{8,24},{9,25},{10,... | collective-permute-start | bytes 319496 | tf_op jit(solution)/shard_map/ppermute | solution.py:324
  47.0 5.1 %collective-permute-start.12 = (bf16[112,256]{1,0:T(8,128)(2,1)S(1)}, bf16[112,256]{1,0:T(8,128)(2,1)S(1)}, u32[]{:S(2)}, u32[]{:S(2)}) collective-permute-start(bf16[112,256]{1,0:T(8,128)(2,1)S(1)} %send3.3), channel_id=1, source_target_pairs={{0,4},{1,5},{2,6},{3,7},{4,0},{5,1},{6,2},{7,3},{8,24},{9,25},{10,... | collective-permute-start | bytes 172040 | tf_op jit(solution)/shard_map/ppermute | solution.py:324
  49.7 2.4 %collective-permute-start.10 = (f32[6,512]{1,0:T(8,128)S(1)}, f32[6,512]{1,0:T(8,128)S(1)}, u32[]{:S(2)}, u32[]{:S(2)}) collective-permute-start(f32[6,512]{1,0:T(8,128)S(1)} %get-tuple-element.161.vec_ref), channel_id=1, source_target_pairs={{0,8},{1,9},{2,10},{3,11},{4,12},{5,13},{6,14},{7,15},{8,0},{9,1},... | collective-permute-start | bytes 36872 | tf_op jit(solution)/shard_map/ppermute | solution.py:324

commit v11 on v9

--- a/solution.py
+++ b/solution.py
@@ -82,7 +82,7 @@
 
 
 def silu_and_slope(preact):
-    gate = 1.0 / (1.0 + jnp.exp(-preact))
+    gate = 0.5 * jnp.tanh(0.5 * preact) + 0.5
     hidden = preact * gate
     return hidden, gate + hidden * (1.0 - gate)
 

time: 52.8 us -> 52.8 us (level)
  no operation moved by 1% of the time
where the time goes in v11:
time: 52.8 us; the launch traced here: 52.7 us
  starting transfers between devices  19.4 us (37%)
  Pallas kernels  17.9 us (34%)
  waiting for transfers between devices  14.3 us (27%)
  between operations  1.04 us (2%)
    pallas_call x27, Pallas kernels, call(): pl.pallas_call(body, out_shape=shapes, in_specs=[anywhere if i in hbm els...  17.9 us
    ppermute x11, waiting for transfers between devices, permute_by(): return lax.ppermute(values, AXES, pairs)  14.3 us
    ppermute x11, starting transfers between devices, permute_by(): return lax.ppermute(values, AXES, pairs)  13.3 us
    ppermute x2, starting transfers between devices, ring(): lax.ppermute(values, 'patch', [(i, (i + step) % count) for i in range(cou...  6.12 us
  transfers between devices with their start and end apart: 13, of which 10 were waited for; matrix products, arithmetic and copies ran while one was open for 0% of the time, Pallas kernels for 15%

profile of v11, /device:TPU:0, one launch (start us, length us, event | category | flops | bytes accessed | tf_op | source)
XLA Modules:
  0.0 52.7 jit_solution(9932301177415747229)
XLA Ops:
  0.7 1.3 %pick.1 = (bf16[32,512]{1,0:T(8,128)(2,1)S(1)}, bf16[32,512]{1,0:T(8,128)(2,1)S(1)}) custom-call(s32[2,32]{1,0:T(2,128)} %bitcast.11, bf16[256,512]{1,0:T(8,128)(2,1)} %nodes_ref.5), custom_call_target="tpu_custom_call" | custom-call | flops 21474836480 | bytes 65536 | tf_op jit(solution)/shard_map/pick/pallas_call | solution.py:42
  2.2 3.0 %collective-permute-start = (bf16[32,512]{1,0:T(8,128)(2,1)S(1)}, bf16[32,512]{1,0:T(8,128)(2,1)S(1)}, u32[]{:S(2)}, u32[]{:S(2)}) collective-permute-start(bf16[32,512]{1,0:T(8,128)(2,1)S(1)} %get-tuple-element.92), channel_id=1, source_target_pairs={{0,1},{1,2},{2,3},{3,4},{4,5},{5,6},{6,7},{7,0},{8,9},{9,10},{10,1... | collective-permute-start | bytes 98312 | tf_op jit(solution)/shard_map/ppermute | solution.py:310
  5.2 3.1 %collective-permute-start.1 = (bf16[32,512]{1,0:T(8,128)(2,1)S(1)}, bf16[32,512]{1,0:T(8,128)(2,1)S(1)}, u32[]{:S(2)}, u32[]{:S(2)}) collective-permute-start(bf16[32,512]{1,0:T(8,128)(2,1)S(1)} %get-tuple-element.93), channel_id=1, source_target_pairs={{0,7},{1,0},{2,1},{3,2},{4,3},{5,4},{6,5},{7,6},{8,15},{9,8},{10,9... | collective-permute-start | bytes 98312 | tf_op jit(solution)/shard_map/ppermute | solution.py:310
  8.3 1.9 %table.1 = (f32[1024,512]{1,0:T(8,128)S(1)}, f32[256,512]{1,0:T(8,128)S(1)}, bf16[1024,640]{1,0:T(8,128)(2,1)S(1)}, bf16[640,1024]{1,0:T(8,128)(2,1)S(1)}, bf16[512,1024]{1,0:T(8,128)(2,1)S(1)}) custom-call(s32[1,1024]{1,0:T(1,128)S(1)} %bitcast.13, s32[1,1024]{1,0:T(1,128)S(1)} %bitcast.14, f32[1,512]{1,0:T(1,128)S(1)} %bitcast.15, ...), custom_call_target="tpu_custom_call" | custom-call | flops 1073741824 | bytes 6291456 | tf_op jit(solution)/shard_map/table/pallas_call | solution.py:42
  10.4 3.9 %forward.1 = (bf16[1024,512]{1,0:T(8,128)(2,1)S(1)}, f32[1024,512]{1,0:T(8,128)S(1)}, f32[1024,512]{1,0:T(8,128)S(1)}, f32[1024,1]{1,0:T(8,128)S(1)}, bf16[256,5...) custom-call(f32[1024,512]{1,0:T(8,128)S(1)} %get-tuple-element.90.pa, ...), custom_call_target="tpu_custom_call" | custom-call | flops 5368709120 | bytes 7088128 | tf_op jit(solution)/shard_map/forward/pallas_call | solution.py:42
  14.3 2.7 %backward.1 = (f32[1024,512]{1,0:T(8,128)S(1)}, bf16[1024,512]{1,0:T(8,128)(2,1)S(1)}, bf16[576,512]{1,0:T(8,128)(2,1)S(1)}, f32[6,512]{1,0:T(8,128)S(1)}, bf16[1024,512]{1,0:T(8,128)(2,1)S(1)}) custom-call(bf16[1024,640]{1,0:T(8,128)(2,1)S(1)} %get-tuple-element.88.pick_ref, bf16[640,1024]{1,0:T(8,128)(2,1)S(1)} %get-tuple-element.89.turned_ref, ...), custom_call_target="tpu_custom_call" | custom-call | flops 3221225472 | bytes 4796416 | tf_op jit(solution)/shard_map/backward/pallas_call | solution.py:42
  17.0 1.5 %weights.2 = (f32[3584,256]{1,0:T(8,128)S(1)}, bf16[1792,256]{1,0:T(8,128)(2,1)S(1)}) custom-call(bf16[512,1024]{1,0:T(8,128)(2,1)S(1)} %get-tuple-element.101.edges_turned_ref, bf16[256,512]{1,0:T(8,128)(2,1)S(1)} %copy-done.1, bf16[32,512]{1,0:T(8,128)(2,1)S(1)} %collective-permute-done.low_ref, bf16[32,512]{1,0:T(8,128)(2,1)S(1)} %collective-permute-done.1.high_ref, ...), custom_call_target="tpu_custom_call" | custom-call | flops 1073741824 | bytes 4587520 | tf_op jit(solution)/shard_map/weights/pallas_call | solution.py:42
  18.6 0.3 rim.1.refs_1_
  18.9 1.5 %weights.3 = (f32[3584,256]{1,0:T(8,128)S(1)}, bf16[1792,256]{1,0:T(8,128)(2,1)S(1)}) custom-call(bf16[512,1024]{1,0:T(8,128)(2,1)S(1)} %get-tuple-element.101.edges_turned_ref, bf16[256,512]{1,0:T(8,128)(2,1)S(1)} %copy-done.1, bf16[32,512]{1,0:T(8,128)(2,1)S(1)} %collective-permute-done.low_ref, bf16[32,512]{1,0:T(8,128)(2,1)S(1)} %collective-permute-done.1.high_ref, ...), custom_call_target="tpu_custom_call" | custom-call | flops 1073741824 | bytes 4587520 | tf_op jit(solution)/shard_map/weights/pallas_call | solution.py:42
  20.5 0.5 collective-permute-start.2
  21.0 0.1 collective-permute-done.3.got_ref
  21.1 0.1 send0.2
  21.2 1.7 %collective-permute-start.4 = (bf16[1056,256]{1,0:T(8,128)(2,1)S(1)}, bf16[1056,256]{1,0:T(8,128)(2,1)S(1)}, u32[]{:S(2)}, u32[]{:S(2)}) collective-permute-start(bf16[1056,256]{1,0:T(8,128)(2,1)S(1)} %get-tuple-element.121), channel_id=1, source_target_pairs={{0,16},{1,17},{2,18},{3,19},{4,20},{5,21},{6,22},{7,23},{8,9},{9,8... | collective-permute-start | bytes 1622024 | tf_op jit(solution)/shard_map/ppermute | solution.py:323
  22.8 0.2 collective-permute-done.2.got_ref
  23.2 1.7 %collective-permute-start.6 = (bf16[896,256]{1,0:T(8,128)(2,1)S(1)}, bf16[896,256]{1,0:T(8,128)(2,1)S(1)}, u32[]{:S(2)}, u32[]{:S(2)}) collective-permute-start(bf16[896,256]{1,0:T(8,128)(2,1)S(1)} %send0.3), channel_id=1, source_target_pairs={{0,16},{1,17},{2,18},{3,19},{4,20},{5,21},{6,22},{7,23},{8,9},{9,8... | collective-permute-start | bytes 1376264 | tf_op jit(solution)/shard_map/ppermute | solution.py:323
  24.9 2.0 %grads.1 = (f32[256,512]{1,0:T(8,128)S(1)}, bf16[1024,512]{1,0:T(8,128)(2,1)}) custom-call(bf16[576,512]{1,0:T(8,128)(2,1)S(1)} %get-tuple-element.124.spread_ref, bf16[1536,512]{1,0:T(8,128)(2,1)S(1)} %copy-done, f32[256,512]{1,0:T(8,128)S(1)} %get-tuple-element.125.partial_ref, f32[1024,512]{1,0:T(8,128)S(1)} %get-tuple-element.126.fresh_ref, ...), custom_call_target="tpu_custom_call" | custom-call | flops 2147483648 | bytes 1572864 | tf_op jit(solution)/shard_map/grads/pallas_call | solution.py:42
  26.9 3.7 %collective-permute-done.4.got_ref = bf16[1056,256]{1,0:T(8,128)(2,1)S(1)} collective-permute-done((bf16[1056,256]{1,0:T(8,128)(2,1)S(1)}, bf16[1056,256]{1,0:T(8,128)(2,1)S(1)}, u32[]{:S(2)}, u32[]{:S(2)}) %collective-permute-start.4) | collective-permute-done | bytes 540704 | tf_op jit(solution)/shard_map/ppermute | solution.py:323
  30.7 1.3 %collective-permute-start.5 = (bf16[608,256]{1,0:T(8,128)(2,1)S(1)}, bf16[608,256]{1,0:T(8,128)(2,1)S(1)}, u32[]{:S(2)}, u32[]{:S(2)}) collective-permute-start(bf16[608,256]{1,0:T(8,128)(2,1)S(1)} %get-tuple-element.134), channel_id=1, source_target_pairs={{0,1},{1,0},{2,3},{3,2},{4,5},{5,4},{6,7},{7,6},{8,10},{9,11},{10,... | collective-permute-start | bytes 933896 | tf_op jit(solution)/shard_map/ppermute | solution.py:323
  32.0 3.5 %collective-permute-done.6.got_ref = bf16[896,256]{1,0:T(8,128)(2,1)S(1)} collective-permute-done((bf16[896,256]{1,0:T(8,128)(2,1)S(1)}, bf16[896,256]{1,0:T(8,128)(2,1)S(1)}, u32[]{:S(2)}, u32[]{:S(2)}) %collective-permute-start.6) | collective-permute-done | bytes 458784 | tf_op jit(solution)/shard_map/ppermute | solution.py:323
  35.6 1.3 %collective-permute-start.8 = (bf16[448,256]{1,0:T(8,128)(2,1)S(1)}, bf16[448,256]{1,0:T(8,128)(2,1)S(1)}, u32[]{:S(2)}, u32[]{:S(2)}) collective-permute-start(bf16[448,256]{1,0:T(8,128)(2,1)S(1)} %send1.3), channel_id=1, source_target_pairs={{0,1},{1,0},{2,3},{3,2},{4,5},{5,4},{6,7},{7,6},{8,10},{9,11},{10,... | collective-permute-start | bytes 688136 | tf_op jit(solution)/shard_map/ppermute | solution.py:323
  36.9 1.2 %collective-permute-done.5.got_ref = bf16[608,256]{1,0:T(8,128)(2,1)S(1)} collective-permute-done((bf16[608,256]{1,0:T(8,128)(2,1)S(1)}, bf16[608,256]{1,0:T(8,128)(2,1)S(1)}, u32[]{:S(2)}, u32[]{:S(2)}) %collective-permute-start.5) | collective-permute-done | bytes 311328 | tf_op jit(solution)/shard_map/ppermute | solution.py:323
  38.1 1.1 %collective-permute-start.7 = (bf16[320,256]{1,0:T(8,128)(2,1)S(1)}, bf16[320,256]{1,0:T(8,128)(2,1)S(1)}, u32[]{:S(2)}, u32[]{:S(2)}) collective-permute-start(bf16[320,256]{1,0:T(8,128)(2,1)S(1)} %get-tuple-element.145), channel_id=1, source_target_pairs={{0,2},{1,3},{2,0},{3,1},{4,6},{5,7},{6,4},{7,5},{8,12},{9,13},{10,... | collective-permute-start | bytes 491528 | tf_op jit(solution)/shard_map/ppermute | solution.py:323
  39.2 2.4 %collective-permute-done.8.got_ref = bf16[448,256]{1,0:T(8,128)(2,1)S(1)} collective-permute-done((bf16[448,256]{1,0:T(8,128)(2,1)S(1)}, bf16[448,256]{1,0:T(8,128)(2,1)S(1)}, u32[]{:S(2)}, u32[]{:S(2)}) %collective-permute-start.8) | collective-permute-done | bytes 229408 | tf_op jit(solution)/shard_map/ppermute | solution.py:323
  41.7 0.8 %collective-permute-start.11 = (bf16[224,256]{1,0:T(8,128)(2,1)S(1)}, bf16[224,256]{1,0:T(8,128)(2,1)S(1)}, u32[]{:S(2)}, u32[]{:S(2)}) collective-permute-start(bf16[224,256]{1,0:T(8,128)(2,1)S(1)} %send2.3), channel_id=1, source_target_pairs={{0,2},{1,3},{2,0},{3,1},{4,6},{5,7},{6,4},{7,5},{8,12},{9,13},{10,... | collective-permute-start | bytes 344072 | tf_op jit(solution)/shard_map/ppermute | solution.py:323
  42.5 1.3 %collective-permute-done.7.got_ref = bf16[320,256]{1,0:T(8,128)(2,1)S(1)} collective-permute-done((bf16[320,256]{1,0:T(8,128)(2,1)S(1)}, bf16[320,256]{1,0:T(8,128)(2,1)S(1)}, u32[]{:S(2)}, u32[]{:S(2)}) %collective-permute-start.7) | collective-permute-done | bytes 163872 | tf_op jit(solution)/shard_map/ppermute | solution.py:323
  43.9 2.6 %collective-permute-start.9 = (bf16[208,256]{1,0:T(8,128)(2,1)S(1)}, bf16[208,256]{1,0:T(8,128)(2,1)S(1)}, u32[]{:S(2)}, u32[]{:S(2)}) collective-permute-start(bf16[208,256]{1,0:T(8,128)(2,1)S(1)} %get-tuple-element.158), channel_id=1, source_target_pairs={{0,4},{1,5},{2,6},{3,7},{4,0},{5,1},{6,2},{7,3},{8,24},{9,25},{10,... | collective-permute-start | bytes 319496 | tf_op jit(solution)/shard_map/ppermute | solution.py:323
  46.5 0.3 collective-permute-done.11.got_ref
  46.8 2.3 %collective-permute-start.12 = (bf16[112,256]{1,0:T(8,128)(2,1)S(1)}, bf16[112,256]{1,0:T(8,128)(2,1)S(1)}, u32[]{:S(2)}, u32[]{:S(2)}) collective-permute-start(bf16[112,256]{1,0:T(8,128)(2,1)S(1)} %send3.3), channel_id=1, source_target_pairs={{0,4},{1,5},{2,6},{3,7},{4,0},{5,1},{6,2},{7,3},{8,24},{9,25},{10,... | collective-permute-start | bytes 172040 | tf_op jit(solution)/shard_map/ppermute | solution.py:323
  49.1 0.4 collective-permute-done.9.got_ref.refs_1_
  49.8 1.1 %rims.1 = f32[256,512]{1,0:T(8,128)} custom-call(s32[2,32]{1,0:T(2,128)S(1)} %bitcast.12, f32[256,512]{1,0:T(8,128)S(1)} %get-tuple-element.127.partial_ref, bf16[64,512]{1,0:T(8,128)(2,1)S(1)} %get-tuple-element.159.back_ref), custom_call_target="tpu_custom_call" | custom-call | bytes 524288 | tf_op jit(solution)/shard_map/rims/pallas_call | solution.py:42
  50.8 1.1 %collective-permute-done.12.refs_3_ = bf16[112,256]{1,0:T(8,128)(2,1)S(1)} collective-permute-done((bf16[112,256]{1,0:T(8,128)(2,1)S(1)}, bf16[112,256]{1,0:T(8,128)(2,1)S(1)}, u32[]{:S(2)}, u32[]{:S(2)}) %collective-permute-start.12) | collective-permute-done | bytes 57376 | tf_op jit(solution)/shard_map/ppermute | solution.py:323
  52.0 0.7 %close.1 = (f32[448,128]{1,0:T(8,128)}, f32[24,128]{1,0:T(8,128)}) custom-call(f32[6,512]{1,0:T(8,128)S(1)} %get-tuple-element.161.vec_ref, f32[6,512]{1,0:T(8,128)S(1)} %collective-permute-done.10.other_ref, f32[112,256]{1,0:T(8,128)S(1)} %keep3.2.refs_0_, bf16[208,256]{1,0:T(8,128)(2,1)S(1)} %collective-permute-done.9.got_ref.refs_1_, ...), custom_call_target="tpu_custom_call" | custom-call | bytes 241664 | tf_op jit(solution)/shard_map/close/pallas_call | solution.py:42
  (55 shorter events, 1.0 us)
Async XLA Ops:
  0.6 7.6 %copy-start = (bf16[1536,512]{1,0:T(8,128)(2,1)S(1)}, bf16[1536,512]{1,0:T(8,128)(2,1)}, u32[]{:S(2)}) copy-start(bf16[1536,512]{1,0:T(8,128)(2,1)} %inner_ref.5) | copy-start | bytes 4718596
  0.6 7.6 %copy-start.1 = (bf16[256,512]{1,0:T(8,128)(2,1)S(1)}, bf16[256,512]{1,0:T(8,128)(2,1)}, u32[]{:S(2)}) copy-start(bf16[256,512]{1,0:T(8,128)(2,1)} %nodes_ref.5) | copy-start | bytes 786436
  0.7 7.6 %copy-start.3 = (bf16[1024,512]{1,0:T(8,128)(2,1)S(1)}, bf16[1024,512]{1,0:T(8,128)(2,1)}, u32[]{:S(2)}) copy-start(bf16[1024,512]{1,0:T(8,128)(2,1)} %edges_ref.3) | copy-start | bytes 3145732
  0.7 7.6 %copy-start.4 = (bf16[1024,512]{1,0:T(8,128)(2,1)S(1)}, bf16[1024,512]{1,0:T(8,128)(2,1)}, u32[]{:S(2)}) copy-start(bf16[1024,512]{1,0:T(8,128)(2,1)} %ninner_ref.3) | copy-start | bytes 3145732
  0.7 7.6 %copy-start.9 = (s32[1024]{0:T(1024)S(1)}, s32[1024]{0:T(1024)}, u32[]{:S(2)}) copy-start(s32[1024]{0:T(1024)} %param.32) | copy-start | bytes 12292
  0.7 7.6 %copy-start.10 = (s32[1024]{0:T(1024)S(1)}, s32[1024]{0:T(1024)}, u32[]{:S(2)}) copy-start(s32[1024]{0:T(1024)} %param.33) | copy-start | bytes 12292
  0.7 7.6 %copy-start.11 = (f32[512]{0:T(512)S(1)}, f32[512]{0:T(512)}, u32[]{:S(2)}) copy-start(f32[512]{0:T(512)} %param.25) | copy-start | bytes 6148
  0.7 7.6 %copy-start.12 = (f32[512]{0:T(512)S(1)}, f32[512]{0:T(512)}, u32[]{:S(2)}) copy-start(f32[512]{0:T(512)} %param.28) | copy-start | bytes 6148
  2.1 8.2 %copy-start.6 = (bf16[512,512]{1,0:T(8,128)(2,1)S(1)}, bf16[512,512]{1,0:T(8,128)(2,1)}, u32[]{:S(2)}) copy-start(bf16[512,512]{1,0:T(8,128)(2,1)} %nouter_ref.1) | copy-start | bytes 1572868
  2.1 8.2 %copy-start.7 = (bf16[512,512]{1,0:T(8,128)(2,1)S(1)}, bf16[512,512]{1,0:T(8,128)(2,1)}, u32[]{:S(2)}) copy-start(bf16[512,512]{1,0:T(8,128)(2,1)} %eouter_ref.3) | copy-start | bytes 1572868
  2.1 8.2 %copy-start.8 = (bf16[256,512]{1,0:T(8,128)(2,1)S(1)}, bf16[256,512]{1,0:T(8,128)(2,1)}, u32[]{:S(2)}) copy-start(bf16[256,512]{1,0:T(8,128)(2,1)} %cotan_ref.1) | copy-start | bytes 786436
  2.1 8.2 %copy-start.13 = (f32[512]{0:T(512)S(1)}, f32[512]{0:T(512)}, u32[]{:S(2)}) copy-start(f32[512]{0:T(512)} %param.26) | copy-start | bytes 6148
  2.1 8.2 %copy-start.14 = (f32[512]{0:T(512)S(1)}, f32[512]{0:T(512)}, u32[]{:S(2)}) copy-start(f32[512]{0:T(512)} %param.29) | copy-start | bytes 6148
  2.1 8.2 %copy-start.15 = (f32[512]{0:T(512)S(1)}, f32[512]{0:T(512)}, u32[]{:S(2)}) copy-start(f32[512]{0:T(512)} %param.30) | copy-start | bytes 6148
  2.1 8.2 %copy-start.16 = (f32[512]{0:T(512)S(1)}, f32[512]{0:T(512)}, u32[]{:S(2)}) copy-start(f32[512]{0:T(512)} %param.27) | copy-start | bytes 6148
  2.2 8.1 %collective-permute-start = (bf16[32,512]{1,0:T(8,128)(2,1)S(1)}, bf16[32,512]{1,0:T(8,128)(2,1)S(1)}, u32[]{:S(2)}, u32[]{:S(2)}) collective-permute-start(bf16[32,512]{1,0:T(8,128)(2,1)S(1)} %get-tuple-element.92), channel_id=1, source_target_pairs={{0,1},{1,2},{2,3},{3,4},{4,5},{5,6},{6,7},{7,0},{8,9},{9,10},{10,1... | collective-permute-start | bytes 98312 | tf_op jit(solution)/shard_map/ppermute | solution.py:310
  5.2 5.1 %collective-permute-start.1 = (bf16[32,512]{1,0:T(8,128)(2,1)S(1)}, bf16[32,512]{1,0:T(8,128)(2,1)S(1)}, u32[]{:S(2)}, u32[]{:S(2)}) collective-permute-start(bf16[32,512]{1,0:T(8,128)(2,1)S(1)} %get-tuple-element.93), channel_id=1, source_target_pairs={{0,7},{1,0},{2,1},{3,2},{4,3},{5,4},{6,5},{7,6},{8,15},{9,8},{10,9... | collective-permute-start | bytes 98312 | tf_op jit(solution)/shard_map/ppermute | solution.py:310
  10.4 3.9 %copy-start.5 = (bf16[1024,512]{1,0:T(8,128)(2,1)S(1)}, bf16[1024,512]{1,0:T(8,128)(2,1)}, u32[]{:S(2)}) copy-start(bf16[1024,512]{1,0:T(8,128)(2,1)} %ecotan_ref.1) | copy-start | bytes 3145732
  18.5 2.5 %collective-permute-start.3 = (bf16[1792,256]{1,0:T(8,128)(2,1)S(1)}, bf16[1792,256]{1,0:T(8,128)(2,1)S(1)}, u32[]{:S(2)}, u32[]{:S(2)}) collective-permute-start(bf16[1792,256]{1,0:T(8,128)(2,1)S(1)} %get-tuple-element.111), channel_id=1, source_target_pairs={{0,8},{1,9},{2,10},{3,11},{4,12},{5,13},{6,14},{7,15},{8,0},{9,1},... | collective-permute-start | bytes 2752520 | tf_op jit(solution)/shard_map/ppermute | solution.py:323
  20.5 2.6 %collective-permute-start.2 = (bf16[1792,256]{1,0:T(8,128)(2,1)S(1)}, bf16[1792,256]{1,0:T(8,128)(2,1)S(1)}, u32[]{:S(2)}, u32[]{:S(2)}) collective-permute-start(bf16[1792,256]{1,0:T(8,128)(2,1)S(1)} %get-tuple-element.116), channel_id=1, source_target_pairs={{0,8},{1,9},{2,10},{3,11},{4,12},{5,13},{6,14},{7,15},{8,0},{9,1},... | collective-permute-start | bytes 2752520 | tf_op jit(solution)/shard_map/ppermute | solution.py:323
  21.2 9.4 %collective-permute-start.4 = (bf16[1056,256]{1,0:T(8,128)(2,1)S(1)}, bf16[1056,256]{1,0:T(8,128)(2,1)S(1)}, u32[]{:S(2)}, u32[]{:S(2)}) collective-permute-start(bf16[1056,256]{1,0:T(8,128)(2,1)S(1)} %get-tuple-element.121), channel_id=1, source_target_pairs={{0,16},{1,17},{2,18},{3,19},{4,20},{5,21},{6,22},{7,23},{8,9},{9,8... | collective-permute-start | bytes 1622024 | tf_op jit(solution)/shard_map/ppermute | solution.py:323
  23.2 12.3 %collective-permute-start.6 = (bf16[896,256]{1,0:T(8,128)(2,1)S(1)}, bf16[896,256]{1,0:T(8,128)(2,1)S(1)}, u32[]{:S(2)}, u32[]{:S(2)}) collective-permute-start(bf16[896,256]{1,0:T(8,128)(2,1)S(1)} %send0.3), channel_id=1, source_target_pairs={{0,16},{1,17},{2,18},{3,19},{4,20},{5,21},{6,22},{7,23},{8,9},{9,8... | collective-permute-start | bytes 1376264 | tf_op jit(solution)/shard_map/ppermute | solution.py:323
  30.7 7.3 %collective-permute-start.5 = (bf16[608,256]{1,0:T(8,128)(2,1)S(1)}, bf16[608,256]{1,0:T(8,128)(2,1)S(1)}, u32[]{:S(2)}, u32[]{:S(2)}) collective-permute-start(bf16[608,256]{1,0:T(8,128)(2,1)S(1)} %get-tuple-element.134), channel_id=1, source_target_pairs={{0,1},{1,0},{2,3},{3,2},{4,5},{5,4},{6,7},{7,6},{8,10},{9,11},{10,... | collective-permute-start | bytes 933896 | tf_op jit(solution)/shard_map/ppermute | solution.py:323
  35.6 6.1 %collective-permute-start.8 = (bf16[448,256]{1,0:T(8,128)(2,1)S(1)}, bf16[448,256]{1,0:T(8,128)(2,1)S(1)}, u32[]{:S(2)}, u32[]{:S(2)}) collective-permute-start(bf16[448,256]{1,0:T(8,128)(2,1)S(1)} %send1.3), channel_id=1, source_target_pairs={{0,1},{1,0},{2,3},{3,2},{4,5},{5,4},{6,7},{7,6},{8,10},{9,11},{10,... | collective-permute-start | bytes 688136 | tf_op jit(solution)/shard_map/ppermute | solution.py:323
  38.1 5.7 %collective-permute-start.7 = (bf16[320,256]{1,0:T(8,128)(2,1)S(1)}, bf16[320,256]{1,0:T(8,128)(2,1)S(1)}, u32[]{:S(2)}, u32[]{:S(2)}) collective-permute-start(bf16[320,256]{1,0:T(8,128)(2,1)S(1)} %get-tuple-element.145), channel_id=1, source_target_pairs={{0,2},{1,3},{2,0},{3,1},{4,6},{5,7},{6,4},{7,5},{8,12},{9,13},{10,... | collective-permute-start | bytes 491528 | tf_op jit(solution)/shard_map/ppermute | solution.py:323
  41.7 8.1 %copy-start.2 = (s32[1,1,2,32]{3,2,1,0:T(2,128)S(1)}, s32[1,1,2,32]{3,2,1,0:T(2,128)}, u32[]{:S(2)}) copy-start(s32[1,1,2,32]{3,2,1,0:T(2,128)} %param.31) | copy-start | bytes 772
  41.7 5.1 %collective-permute-start.11 = (bf16[224,256]{1,0:T(8,128)(2,1)S(1)}, bf16[224,256]{1,0:T(8,128)(2,1)S(1)}, u32[]{:S(2)}, u32[]{:S(2)}) collective-permute-start(bf16[224,256]{1,0:T(8,128)(2,1)S(1)} %send2.3), channel_id=1, source_target_pairs={{0,2},{1,3},{2,0},{3,1},{4,6},{5,7},{6,4},{7,5},{8,12},{9,13},{10,... | collective-permute-start | bytes 344072 | tf_op jit(solution)/shard_map/ppermute | solution.py:323
  43.9 5.7 %collective-permute-start.9 = (bf16[208,256]{1,0:T(8,128)(2,1)S(1)}, bf16[208,256]{1,0:T(8,128)(2,1)S(1)}, u32[]{:S(2)}, u32[]{:S(2)}) collective-permute-start(bf16[208,256]{1,0:T(8,128)(2,1)S(1)} %get-tuple-element.158), channel_id=1, source_target_pairs={{0,4},{1,5},{2,6},{3,7},{4,0},{5,1},{6,2},{7,3},{8,24},{9,25},{10,... | collective-permute-start | bytes 319496 | tf_op jit(solution)/shard_map/ppermute | solution.py:323
  46.8 5.1 %collective-permute-start.12 = (bf16[112,256]{1,0:T(8,128)(2,1)S(1)}, bf16[112,256]{1,0:T(8,128)(2,1)S(1)}, u32[]{:S(2)}, u32[]{:S(2)}) collective-permute-start(bf16[112,256]{1,0:T(8,128)(2,1)S(1)} %send3.3), channel_id=1, source_target_pairs={{0,4},{1,5},{2,6},{3,7},{4,0},{5,1},{6,2},{7,3},{8,24},{9,25},{10,... | collective-permute-start | bytes 172040 | tf_op jit(solution)/shard_map/ppermute | solution.py:323
  49.6 2.4 %collective-permute-start.10 = (f32[6,512]{1,0:T(8,128)S(1)}, f32[6,512]{1,0:T(8,128)S(1)}, u32[]{:S(2)}, u32[]{:S(2)}) collective-permute-start(f32[6,512]{1,0:T(8,128)S(1)} %get-tuple-element.161.vec_ref), channel_id=1, source_target_pairs={{0,8},{1,9},{2,10},{3,11},{4,12},{5,13},{6,14},{7,15},{8,0},{9,1},... | collective-permute-start | bytes 36872 | tf_op jit(solution)/shard_map/ppermute | solution.py:323
